TPU v7x, 32 devices: a whole 2x2x4 slice. The times are simulated.
32 devices in a mesh: groups: 2 (over y), patch: 4 (over z), sub: 2 (over x), half: 2 (over core).
Axes of the slice: x: 2, y: 2, z: 4, core: 2. Of those that a mesh axis runs over, the one named last changes fastest.
Arguments:
- vectors: float32 [2, 8192, 256], P(None, ('groups', 'patch', 'sub', 'half')), parts along dimension 1, may hold values from -600 to 600
- prestress: bfloat16 [8192, 3, 256], P(('groups', 'patch', 'sub', 'half')), parts along dimension 0, may hold values from -4 to 4
- thickness: float32 [8192, 256], P(('groups', 'patch', 'sub', 'half')), parts along dimension 0, may hold values from 0.5 to 2
- foundation: float32 [8192, 256], P(('groups', 'patch', 'sub', 'half')), parts along dimension 0, may hold values from 2 to 6
- patch_rows: int32 [64], P(('groups', 'patch', 'sub', 'half')), parts along dimension 0, may hold values from 64 to 128, as said below
- matched: int32 [64], P(('groups', 'patch', 'sub', 'half')), parts along dimension 0, may hold values from 0 to 31, as said below
- elem_row: int32 [8192], P(('groups', 'patch', 'sub', 'half')), parts along dimension 0, may hold values from 0 to 4095, as said below
Outputs:
- modes: float32 [2, 8192, 256], P(None, ('groups', 'patch', 'sub', 'half')), parts along dimension 1
There are 2 independent parts, one for each index of `groups`. A program takes and returns all parts, laid end to end along the dimension named above; each array names one. Nothing has to cross between parts.
Inputs may be any that keep to these rules, and one draw needn't show every extreme that they name: `patch_rows`: the largest value is reached by some patch in every draw. A permutation of the patches; the patch matched to a patch lies on the device with the same sub and half indices and a patch index one above or one below, cyclically. `elem_row`: a permutation of the rows; of each device's rows, those in positions k * 16 to (k + 1) * 16 - 1 belong to patches of the device with index k along patch+sub+half.
All inputs are finite; a program needn't handle non-finite values.
Results may differ from a plain program's by a relative error of at most 0.0003.
Values may be sent and summed in bfloat16 or wider, within the bound.
No kernel may reach another device: no remote copies, remote signals or barrier semaphores. Data moves between devices by JAX's collectives and lax.ppermute only.
A program may use at most 64 MiB of HBM per device.

v0:
```python
import jax
import jax.numpy as jnp
from jax import lax
from jax.sharding import PartitionSpec as P

ITERS = 2


step_size = 1.0
norm_scale = 16.0
penalty_value = 8.0
penalty_slope = 4.0


def passed_along(array, axis, by):
    peers = lax.axis_size(axis)
    return lax.ppermute(array, axis, [(i, (i + by) % peers) for i in range(peers)])


def second_rows(field):
    padded = jnp.pad(field, [(0, 0)] * (field.ndim - 2) + [(1, 1), (0, 0)])
    return padded[..., :-2, :] - 2.0 * field + padded[..., 2:, :]


def second_cols(field):
    padded = jnp.pad(field, [(0, 0)] * (field.ndim - 1) + [(1, 1)])
    return padded[..., :-2] - 2.0 * field + padded[..., 2:]


def forward_rows(field):
    zeros = jnp.zeros_like(field[..., :1, :])
    return jnp.concatenate([field[..., 1:, :], zeros], axis=-2) - field


def backward_rows(field):
    zeros = jnp.zeros_like(field[..., :1, :])
    return jnp.concatenate([zeros, field[..., :-1, :]], axis=-2) - field


def forward_cols(field):
    zeros = jnp.zeros_like(field[..., :1])
    return jnp.concatenate([field[..., 1:], zeros], axis=-1) - field


def backward_cols(field):
    zeros = jnp.zeros_like(field[..., :1])
    return jnp.concatenate([zeros, field[..., :-1]], axis=-1) - field


def stiffness(field, live, thickness, foundation):
    bend_rows = thickness * live * second_rows(field)
    bend_cols = thickness * second_cols(field)
    return live * (foundation * field + second_rows(bend_rows) + second_cols(bend_cols))


def geometric(field, live, stress):
    along_rows = forward_rows(field)
    along_cols = forward_cols(field)
    nuu = stress[:, :, 0, :]
    nvv = stress[:, :, 1, :]
    nuv = stress[:, :, 2, :]
    total = backward_rows(nuu * along_rows + nuv * along_cols) + backward_cols(
        nvv * along_cols + nuv * along_rows
    )
    return live * total


def edges(field, lengths):

    def row_pick(index):
        where_rows = jnp.broadcast_to(
            index[None, :, None, None], (field.shape[0], field.shape[1], 1, field.shape[3])
        )
        return jnp.take_along_axis(field, where_rows, axis=2)[:, :, 0, :]

    top = jnp.stack([row_pick(lengths - 2), row_pick(lengths - 1)], axis=2)
    bottom = field[:, :, 0:2, :]
    return (top, bottom)


def interface(field, lengths, top, bottom, partner_top, partner_bottom):
    jump_top = top[:, :, 1, :] - partner_bottom[:, :, 0, :]
    slope_top = (
        top[:, :, 1, :]
        - top[:, :, 0, :]
        - (partner_bottom[:, :, 1, :] - partner_bottom[:, :, 0, :])
    )
    jump_bottom = partner_top[:, :, 1, :] - bottom[:, :, 0, :]
    slope_bottom = (
        partner_top[:, :, 1, :]
        - partner_top[:, :, 0, :]
        - (bottom[:, :, 1, :] - bottom[:, :, 0, :])
    )
    rows = jnp.arange(field.shape[2], dtype=jnp.int32)[None, :, None]
    last = lengths[:, None, None] - 1
    added = jnp.where(
        rows == last, (penalty_value * jump_top + penalty_slope * slope_top)[:, :, None, :], 0.0
    )
    added = added + jnp.where(rows == last - 1, (-penalty_slope * slope_top)[:, :, None, :], 0.0)
    added = added + jnp.where(
        rows == 0, (-penalty_value * jump_bottom + penalty_slope * slope_bottom)[:, :, None, :], 0.0
    )
    added = added + jnp.where(rows == 1, (-penalty_slope * slope_bottom)[:, :, None, :], 0.0)
    return added


def products(field, kfield, gfield):
    return jnp.stack(
        [
            jnp.sum(field[0] * kfield[0]),
            jnp.sum(field[0] * kfield[1]),
            jnp.sum(field[1] * kfield[1]),
            jnp.sum(field[0] * gfield[0]),
            jnp.sum(field[0] * gfield[1]),
            jnp.sum(field[1] * gfield[1]),
        ]
    )


def advance(field, kfield, gfield, totals, precond, cells):
    first_a = totals[0]
    cross_k = totals[1]
    second_a = totals[2]
    first_g = totals[3]
    cross_g = totals[4]
    second_g = totals[5]
    ratio = cross_k / first_a
    other = field[1] - ratio * field[0]
    other_k = kfield[1] - ratio * kfield[0]
    other_g = gfield[1] - ratio * gfield[0]
    other_a = second_a - ratio * cross_k
    other_q = second_g - 2.0 * ratio * cross_g + ratio * ratio * first_g
    first_mu = first_g / first_a
    other_mu = other_q / other_a
    new_first = (field[0] + step_size * precond * (gfield[0] - first_mu * kfield[0])) * jnp.sqrt(
        norm_scale * cells / first_a
    )
    new_other = (other + step_size * precond * (other_g - other_mu * other_k)) * jnp.sqrt(
        norm_scale * cells / other_a
    )
    return jnp.stack([new_first, new_other])


def choose(candidates, wanted, labels):
    match = labels[None, :] == wanted[:, None]
    return jnp.sum(jnp.where(match[None, :, :, None, None], candidates[:, None], 0.0), axis=2)


def per_device(vectors, prestress, thickness, foundation, patch_rows, matched, elem_row):
    owners = lax.axis_size("patch")
    inner = lax.axis_size(("sub", "half"))
    slots = patch_rows.shape[0]
    rows_dev = thickness.shape[0]
    prows = rows_dev // slots
    ncol = thickness.shape[1]
    per_peer = rows_dev // (owners * inner)
    blocks = prestress.reshape(owners, inner, per_peer, 3, ncol)
    targets = (elem_row % rows_dev).reshape(owners, inner, per_peer)
    arrived, arrived_rows = (
        lax.all_to_all(
            lax.all_to_all(blocks, "patch", split_axis=0, concat_axis=0, tiled=True),
            ("sub", "half"),
            split_axis=1,
            concat_axis=1,
            tiled=True,
        ),
        lax.all_to_all(
            lax.all_to_all(targets, "patch", split_axis=0, concat_axis=0, tiled=True),
            ("sub", "half"),
            split_axis=1,
            concat_axis=1,
            tiled=True,
        ),
    )
    placed = (
        jnp.zeros((rows_dev, 3, ncol), jnp.bfloat16)
        .at[arrived_rows.reshape(-1)]
        .set(arrived.reshape(-1, 3, ncol))
    )
    stress = placed.astype(jnp.float32).reshape(slots, prows, 3, ncol)
    rows = jnp.arange(prows, dtype=jnp.int32)[None, :]
    live = (rows < patch_rows[:, None]).astype(jnp.float32)[:, :, None]
    thick = thickness.reshape(slots, prows, ncol)
    support = foundation.reshape(slots, prows, ncol)
    precond = live / (support + 12.0 * thick)
    own_ids = lax.axis_index(("patch", "sub", "half")) * slots + jnp.arange(slots, dtype=jnp.int32)
    labels = jnp.stack([own_ids, matched])
    field = vectors.reshape(2, slots, prows, ncol) * live
    cells = jnp.float32(owners * inner * rows_dev * ncol)
    for step in range(ITERS):
        top, bottom = edges(field, patch_rows)
        strips = jnp.stack([top, bottom])
        below = passed_along((strips, labels), "patch", 1)
        above = passed_along((strips, labels), "patch", -1)
        got_strips = jnp.stack([below[0], above[0]])
        got_labels = jnp.stack([below[1], above[1]])
        count = got_strips.shape[0] * slots
        cand_top = jnp.moveaxis(got_strips[:, 0], 0, 1).reshape(2, count, 2, ncol)
        cand_bottom = jnp.moveaxis(got_strips[:, 1], 0, 1).reshape(2, count, 2, ncol)
        cand_ids = got_labels[:, 0].reshape(-1)
        cand_next = got_labels[:, 1].reshape(-1)
        partner_bottom = choose(cand_bottom, matched, cand_ids)
        partner_top = choose(cand_top, own_ids, cand_next)
        kfield = stiffness(field, live, thick, support) + interface(
            field, patch_rows, top, bottom, partner_top, partner_bottom
        )
        gfield = geometric(field, live, stress)
        totals = lax.psum(products(field, kfield, gfield), ("patch", "sub", "half"))
        field = advance(field, kfield, gfield, totals, precond, cells)
    return field.reshape(2, rows_dev, ncol)


def solution(mesh):
    in_specs = (
        P(None, ("groups", "patch", "sub", "half"), None),
        P(("groups", "patch", "sub", "half"), None, None),
        P(("groups", "patch", "sub", "half"), None),
        P(("groups", "patch", "sub", "half"), None),
        P(("groups", "patch", "sub", "half")),
        P(("groups", "patch", "sub", "half")),
        P(("groups", "patch", "sub", "half")),
    )
    out_specs = P(None, ("groups", "patch", "sub", "half"), None)
    return jax.shard_map(
        per_device, mesh=mesh, in_specs=in_specs, out_specs=out_specs, check_vma=False
    )
```

profile of v0, /device:TPU:0, one launch (start us, length us, event | category | flops | bytes accessed | tf_op | source)
XLA Modules:
  0.0 211.1 jit_solution(15988298672852159609)
XLA Ops:
  1.1 1.1 broadcast_multiply_fusion
  2.2 12.3 %gather_fusion = f32[1024]{0:T(1024)S(1)} fusion(f32[2,2,128,256]{3,2,1,0:T(8,128)S(1)} %broadcast_multiply_fusion, s32[1024]{0:T(1024)S(1)} %bitcast.210), kind=kCustom, calls=%fused_computation.clone | custom fusion | bytes 24576 | tf_op jit(solution)/shard_map/jit(take_along_axis)/gather | solution.py:74
  14.6 12.3 %gather_fusion.1 = f32[1024]{0:T(1024)S(1)} fusion(f32[2,2,128,256]{3,2,1,0:T(8,128)S(1)} %broadcast_multiply_fusion, s32[1024]{0:T(1024)S(1)} %bitcast.212), kind=kCustom, calls=%fused_computation.1.clone | custom fusion | bytes 24576 | tf_op jit(solution)/shard_map/jit(take_along_axis)/gather | solution.py:74
  27.1 3.1 %collective-permute-start.2 = (f32[2,2,2,2,256]{4,3,2,1,0:T(2,128)S(1)}, f32[2,2,2,2,256]{4,3,2,1,0:T(2,128)S(1)}, u32[]{:S(2)}, u32[]{:S(2)}) collective-permute-start(f32[2,2,2,2,256]{4,3,2,1,0:T(2,128)S(1)} %pad_maximum_fusion.4), channel_id=1, source_target_pairs={{0,4},{4,8},{8,12},{12,0},{1,5},{5,9},{9,13},{13,1},{2,6},{6,10},{... | collective-permute-start | bytes 49160 | tf_op jit(solution)/shard_map/ppermute | solution.py:17
  30.1 2.1 collective-permute-start.3
  33.0 3.8 %collective-permute-start.1 = (s32[2,2]{1,0:T(2,128)S(1)}, s32[2,2]{1,0:T(2,128)S(1)}, u32[]{:S(2)}, u32[]{:S(2)}) collective-permute-start(s32[2,2]{1,0:T(2,128)S(1)} %pad_add_fusion.4), channel_id=1, source_target_pairs={{0,12},{4,0},{8,4},{12,8},{1,13},{5,1},{9,5},{13,9},{2,14},{6,2},{... | collective-permute-start | bytes 56 | tf_op jit(solution)/shard_map/ppermute | solution.py:17
  37.5 3.2 %all-to-all-start = ((s32[4,4,16]{2,1,0:T(4,128)}), s32[4,4,16]{2,1,0:T(4,128)S(1)}, u32[]{:S(2)}, u32[]{:S(2)}) async-start(s32[4,4,16]{2,1,0:T(4,128)} %reshape.291), calls=%async_computation | async-start | bytes 16384 | tf_op jit(solution)/shard_map/all_to_all | solution.py:168
  43.8 2.4 %all-to-all-done = s32[4,4,16]{2,1,0:T(4,128)S(1)} async-done(((s32[4,4,16]{2,1,0:T(4,128)}), s32[4,4,16]{2,1,0:T(4,128)S(1)}, u32[]{:S(2)}, u32[]{:S(2)}) %all-to-all-start) | async-done | bytes 1056 | tf_op jit(solution)/shard_map/all_to_all | solution.py:168
  46.9 3.2 %all-to-all-start.1 = ((s32[4,4,16]{2,0,1:T(4,128)}), s32[4,4,16]{2,0,1:T(4,128)S(1)}, u32[]{:S(2)}, u32[]{:S(2)}) async-start(s32[4,4,16]{2,0,1:T(4,128)} %copy.28), calls=%async_computation.1 | async-start | bytes 16384 | tf_op jit(solution)/shard_map/all_to_all | solution.py:167
  50.2 3.7 %all-to-all-done.1 = s32[4,4,16]{2,0,1:T(4,128)S(1)} async-done(((s32[4,4,16]{2,0,1:T(4,128)}), s32[4,4,16]{2,0,1:T(4,128)S(1)}, u32[]{:S(2)}, u32[]{:S(2)}) %all-to-all-start.1) | async-done | bytes 1056 | tf_op jit(solution)/shard_map/all_to_all | solution.py:167
  53.9 3.5 %all-to-all-start.2 = ((bf16[4,4,16,3,256]{4,2,1,3,0:T(8,128)(2,1)}), bf16[4,4,16,3,256]{4,2,1,3,0:T(8,128)(2,1)S(1)}, u32[]{:S(2)}, u32[]{:S(2)}) async-start(bf16[4,4,16,3,256]{4,2,1,3,0:T(8,128)(2,1)} %copy.30), calls=%async_computation.2 | async-start | bytes 786432 | tf_op jit(solution)/shard_map/all_to_all | solution.py:161
  57.8 11.4 %all-to-all-done.2 = bf16[4,4,16,3,256]{4,2,1,3,0:T(8,128)(2,1)S(1)} async-done(((bf16[4,4,16,3,256]{4,2,1,3,0:T(8,128)(2,1)}), bf16[4,4,16,3,256]{4,2,1,3,0:T(8,128)(2,1)S(1)}, u32[]{:S(2)}, u32[]{:S(2)}) %all-to-all-start.2) | async-done | bytes 393248 | tf_op jit(solution)/shard_map/all_to_all | solution.py:161
  70.0 3.5 %all-to-all-start.3 = ((bf16[4,4,16,3,256]{4,2,0,3,1:T(8,128)(2,1)}), bf16[4,4,16,3,256]{4,2,0,3,1:T(8,128)(2,1)S(1)}, u32[]{:S(2)}, u32[]{:S(2)}) async-start(bf16[4,4,16,3,256]{4,2,0,3,1:T(8,128)(2,1)} %copy.31), calls=%async_computation.3 | async-start | bytes 786432 | tf_op jit(solution)/shard_map/all_to_all | solution.py:160
  73.6 7.3 %all-to-all-done.3 = bf16[4,4,16,3,256]{4,2,0,3,1:T(8,128)(2,1)S(1)} async-done(((bf16[4,4,16,3,256]{4,2,0,3,1:T(8,128)(2,1)}), bf16[4,4,16,3,256]{4,2,0,3,1:T(8,128)(2,1)S(1)}, u32[]{:S(2)}, u32[]{:S(2)}) %all-to-all-start.3) | async-done | bytes 393248 | tf_op jit(solution)/shard_map/all_to_all | solution.py:160
  81.4 7.0 %scatter_fusion = bf16[256,3,256]{2,1,0:T(4,128)(2,1)S(1)} fusion(bf16[256,3,256]{2,1,0:T(4,128)(2,1)S(1)} %broadcast_in_dim.225, s32[256]{0:T(256)S(1)} %bitcast.260, bf16[256,3,256]{2,1,0:T(4,128)(2,1)S(1)} %copy.33), kind=kCustom, calls=%fused_computation.4 | custom fusion | bytes 1180672 | tf_op jit(solution)/shard_map/scatter | solution.py:178
  89.1 1.2 copy-done.7
  93.0 3.8 %stack.135 = f32[6]{0:T(128)S(1)} concatenate(f32[1]{0:T(128)} %bitcast.30, f32[1]{0:T(128)} %bitcast.32, f32[1]{0:T(128)} %bitcast.34, f32[1]{0:T(128)} %bitcast.36, f32[1]{0:T(128)} %bitcast.38, f32[1]{0:T(128)} %bitcast.39), dimensions={0} | concatenate | bytes 48 | tf_op jit(solution)/shard_map/stack | solution.py:108
  96.8 30.2 %psum.14 = f32[6]{0:T(128)S(1)} all-reduce(f32[6]{0:T(128)S(1)} %stack.135), channel_id=1, replica_groups=mesh['groups'=2,'patch'=4,'sub'=2,'half'=2] {'patch','sub','half'}, use_global_device_ids=true, to_apply=%region_9.11 | all-reduce | flops 6 | bytes 48 | tf_op jit(solution)/shard_map/psum | solution.py:208
  136.7 12.3 %gather_fusion.3 = f32[1024]{0:T(1024)S(1)} fusion(f32[2,2,128,256]{3,2,1,0:T(8,128)S(1)} %get-tuple-element.46, s32[1024]{0:T(1024)S(1)} %bitcast.213), kind=kCustom, calls=%fused_computation.3.clone | custom fusion | bytes 24576 | tf_op jit(solution)/shard_map/jit(take_along_axis)/gather | solution.py:74
  149.1 12.3 %gather_fusion.2 = f32[1024]{0:T(1024)S(1)} fusion(f32[2,2,128,256]{3,2,1,0:T(8,128)S(1)} %get-tuple-element.46, s32[1024]{0:T(1024)S(1)} %bitcast.211), kind=kCustom, calls=%fused_computation.2.clone | custom fusion | bytes 24576 | tf_op jit(solution)/shard_map/jit(take_along_axis)/gather | solution.py:74
  161.6 3.8 %collective-permute-start.5 = (f32[2,2,2,2,256]{4,3,2,1,0:T(2,128)S(1)}, f32[2,2,2,2,256]{4,3,2,1,0:T(2,128)S(1)}, u32[]{:S(2)}, u32[]{:S(2)}) collective-permute-start(f32[2,2,2,2,256]{4,3,2,1,0:T(2,128)S(1)} %pad_maximum_fusion.5), channel_id=1, source_target_pairs={{0,12},{4,0},{8,4},{12,8},{1,13},{5,1},{9,5},{13,9},{2,14},{6,2},{... | collective-permute-start | bytes 49160 | tf_op jit(solution)/shard_map/ppermute | solution.py:17
  166.1 1.1 collective-permute-done.4
  169.5 3.8 %stack.150 = f32[6]{0:T(128)S(1)} concatenate(f32[1]{0:T(128)} %bitcast.59, f32[1]{0:T(128)} %bitcast.61, f32[1]{0:T(128)} %bitcast.62, f32[1]{0:T(128)} %bitcast.64, f32[1]{0:T(128)} %bitcast.66, f32[1]{0:T(128)} %bitcast.67), dimensions={0} | concatenate | bytes 48 | tf_op jit(solution)/shard_map/stack | solution.py:108
  173.4 29.5 %psum.15 = f32[6]{0:T(128)S(1)} all-reduce(f32[6]{0:T(128)S(1)} %stack.150), channel_id=1, replica_groups=mesh['groups'=2,'patch'=4,'sub'=2,'half'=2] {'patch','sub','half'}, use_global_device_ids=true, to_apply=%region_18.20 | all-reduce | flops 6 | bytes 48 | tf_op jit(solution)/shard_map/psum | solution.py:208
  (130 shorter events, 19.5 us)
Async XLA Ops:
  0.0 0.7 copy-start.12
  27.1 30.4 %collective-permute-start.2 = (f32[2,2,2,2,256]{4,3,2,1,0:T(2,128)S(1)}, f32[2,2,2,2,256]{4,3,2,1,0:T(2,128)S(1)}, u32[]{:S(2)}, u32[]{:S(2)}) collective-permute-start(f32[2,2,2,2,256]{4,3,2,1,0:T(2,128)S(1)} %pad_maximum_fusion.4), channel_id=1, source_target_pairs={{0,4},{4,8},{8,12},{12,0},{1,5},{5,9},{9,13},{13,1},{2,6},{6,10},{... | collective-permute-start | bytes 49160 | tf_op jit(solution)/shard_map/ppermute | solution.py:17
  30.1 27.3 %collective-permute-start.3 = (f32[2,2,2,2,256]{4,3,2,1,0:T(2,128)S(1)}, f32[2,2,2,2,256]{4,3,2,1,0:T(2,128)S(1)}, u32[]{:S(2)}, u32[]{:S(2)}) collective-permute-start(f32[2,2,2,2,256]{4,3,2,1,0:T(2,128)S(1)} %pad_maximum_fusion.4), channel_id=1, source_target_pairs={{0,12},{4,0},{8,4},{12,8},{1,13},{5,1},{9,5},{13,9},{2,14},{6,2},{... | collective-permute-start | bytes 49160 | tf_op jit(solution)/shard_map/ppermute | solution.py:17
  32.2 0.7 copy-start.13
  32.9 3.9 %copy-start.11 = (s32[256]{0:T(256)S(1)}, s32[256]{0:T(256)}, u32[]{:S(2)}) copy-start(s32[256]{0:T(256)} %param.15) | copy-start | bytes 3076
  32.9 10.7 %collective-permute-start = (s32[2,2]{1,0:T(2,128)S(1)}, s32[2,2]{1,0:T(2,128)S(1)}, u32[]{:S(2)}, u32[]{:S(2)}) collective-permute-start(s32[2,2]{1,0:T(2,128)S(1)} %pad_add_fusion.4), channel_id=1, source_target_pairs={{0,4},{4,8},{8,12},{12,0},{1,5},{5,9},{9,13},{13,1},{2,6},{6,10},{... | collective-permute-start | bytes 56 | tf_op jit(solution)/shard_map/ppermute | solution.py:17
  33.0 10.6 %collective-permute-start.1 = (s32[2,2]{1,0:T(2,128)S(1)}, s32[2,2]{1,0:T(2,128)S(1)}, u32[]{:S(2)}, u32[]{:S(2)}) collective-permute-start(s32[2,2]{1,0:T(2,128)S(1)} %pad_add_fusion.4), channel_id=1, source_target_pairs={{0,12},{4,0},{8,4},{12,8},{1,13},{5,1},{9,5},{13,9},{2,14},{6,2},{... | collective-permute-start | bytes 56 | tf_op jit(solution)/shard_map/ppermute | solution.py:17
  37.5 8.8 %all-to-all-start = ((s32[4,4,16]{2,1,0:T(4,128)}), s32[4,4,16]{2,1,0:T(4,128)S(1)}, u32[]{:S(2)}, u32[]{:S(2)}) async-start(s32[4,4,16]{2,1,0:T(4,128)} %reshape.291), calls=%async_computation | async-start | bytes 16384 | tf_op jit(solution)/shard_map/all_to_all | solution.py:168
  40.8 1.1 copy-start
  41.8 1.0 copy-start.10
  46.9 7.0 %all-to-all-start.1 = ((s32[4,4,16]{2,0,1:T(4,128)}), s32[4,4,16]{2,0,1:T(4,128)S(1)}, u32[]{:S(2)}, u32[]{:S(2)}) async-start(s32[4,4,16]{2,0,1:T(4,128)} %copy.28), calls=%async_computation.1 | async-start | bytes 16384 | tf_op jit(solution)/shard_map/all_to_all | solution.py:167
  53.9 15.4 %all-to-all-start.2 = ((bf16[4,4,16,3,256]{4,2,1,3,0:T(8,128)(2,1)}), bf16[4,4,16,3,256]{4,2,1,3,0:T(8,128)(2,1)S(1)}, u32[]{:S(2)}, u32[]{:S(2)}) async-start(bf16[4,4,16,3,256]{4,2,1,3,0:T(8,128)(2,1)} %copy.30), calls=%async_computation.2 | async-start | bytes 786432 | tf_op jit(solution)/shard_map/all_to_all | solution.py:161
  70.0 10.9 %all-to-all-start.3 = ((bf16[4,4,16,3,256]{4,2,0,3,1:T(8,128)(2,1)}), bf16[4,4,16,3,256]{4,2,0,3,1:T(8,128)(2,1)S(1)}, u32[]{:S(2)}, u32[]{:S(2)}) async-start(bf16[4,4,16,3,256]{4,2,0,3,1:T(8,128)(2,1)} %copy.31), calls=%async_computation.3 | async-start | bytes 786432 | tf_op jit(solution)/shard_map/all_to_all | solution.py:160
  89.0 1.2 copy-start.7
  89.0 1.6 copy-start.2
  89.0 1.6 copy-start.4
  90.2 0.9 copy-start.1
  90.2 1.1 copy-start.6
  135.5 1.0 copy-start.3
  135.5 1.0 copy-start.5
  161.6 5.6 %collective-permute-start.4 = (f32[2,2,2,2,256]{4,3,2,1,0:T(2,128)S(1)}, f32[2,2,2,2,256]{4,3,2,1,0:T(2,128)S(1)}, u32[]{:S(2)}, u32[]{:S(2)}) collective-permute-start(f32[2,2,2,2,256]{4,3,2,1,0:T(2,128)S(1)} %pad_maximum_fusion.5), channel_id=1, source_target_pairs={{0,4},{4,8},{8,12},{12,0},{1,5},{5,9},{9,13},{13,1},{2,6},{6,10},{... | collective-permute-start | bytes 49160 | tf_op jit(solution)/shard_map/ppermute | solution.py:17
  161.6 5.5 %collective-permute-start.5 = (f32[2,2,2,2,256]{4,3,2,1,0:T(2,128)S(1)}, f32[2,2,2,2,256]{4,3,2,1,0:T(2,128)S(1)}, u32[]{:S(2)}, u32[]{:S(2)}) collective-permute-start(f32[2,2,2,2,256]{4,3,2,1,0:T(2,128)S(1)} %pad_maximum_fusion.5), channel_id=1, source_target_pairs={{0,12},{4,0},{8,4},{12,8},{1,13},{5,1},{9,5},{13,9},{2,14},{6,2},{... | collective-permute-start | bytes 49160 | tf_op jit(solution)/shard_map/ppermute | solution.py:17
  167.6 1.0 copy-start.8
  167.7 1.0 copy-start.9
where the time goes:
time: 212 us; the launch traced here: 211 us
  local copies, waits for them, and re-layouts  75.2 us (35%)
  blocking collectives  59.7 us (28%)
  starting transfers between devices  26.3 us (12%)
  waiting for transfers between devices  26 us (12%)
  between operations  13.6 us (6%)
  other arithmetic  10.3 us (5%)
    psum x2, blocking collectives, per_device(): totals = lax.psum(products(field, kfield, gfield), ('patch', 'sub', 'half'))  59.7 us
    gather x4, local copies, waits for them, and re-layouts, row_pick(): return jnp.take_along_axis(field, where_rows, axis=2)[:, :, 0, :]  49.2 us
    ppermute x6, starting transfers between devices, passed_along(): lax.ppermute(array, axis, [(i, (i + by) % peers) for i in range(peers)])  12.9 us
    all_to_all x1, waiting for transfers between devices, per_device(): lax.all_to_all(blocks, 'patch', split_axis=0, concat_axis=0, tiled=True)  11.4 us
    another operation x2, local copies, waits for them, and re-layouts, products(): jnp.stack([jnp.sum(field[0] * kfield[0]), jnp.sum(field[0] * kfield[1]),...  7.63 us
    all_to_all x1, waiting for transfers between devices, per_device(): lax.all_to_all(lax.all_to_all(blocks, 'patch', split_axis=0, concat_axis=...  7.33 us
    scatter x1, local copies, waits for them, and re-layouts, per_device(): placed = jnp.zeros((rows_dev, 3, ncol), jnp.bfloat16).at[arrived_rows.res...  6.97 us
    unnamed x40, local copies, waits for them, and re-layouts  4.77 us
  transfers between devices with their start and end apart: 10, of which 5 were waited for; matrix products, arithmetic and copies ran while one was open for 2% of the time, Pallas kernels for 0%

commit v1 on v0

v1 whole, which is shorter than its diff:
```python
import functools

import jax
import jax.numpy as jnp
from jax import lax
from jax.experimental import pallas as pl
from jax.experimental.pallas import tpu as pltpu
from jax.sharding import PartitionSpec as P

norm_scale = 16.0
penalty_value = 8.0
penalty_slope = 4.0
LANES = 128

UU = [(a, b) for a in range(4) for b in range(a, 4)]
NAMES = (
    [("kuu", a, b) for a, b in UU]
    + [("guu", a, b) for a, b in UU]
    + [("kxx", 0, 0), ("kxx", 0, 1), ("kxx", 1, 1)]
    + [("gxx", 0, 0), ("gxx", 0, 1), ("gxx", 1, 1)]
    + [("kpk", 0, 0), ("kpk", 0, 1), ("kpk", 1, 1)]
    + [("kpg", a, b) for a in range(2) for b in range(2)]
    + [("gpg", 0, 0), ("gpg", 0, 1), ("gpg", 1, 1)]
)
AT = {name: k for k, name in enumerate(NAMES)}
SUMS = 40
TILES = SUMS // 8


def passed_along(array, axis, by):
    peers = lax.axis_size(axis)
    return lax.ppermute(array, axis, [(i, (i + by) % peers) for i in range(peers)])


def summed_over(array, axis):
    total = array
    for by in range(1, lax.axis_size(axis)):
        total = total + passed_along(array, axis, by)
    return total


def iota(shape, axis):
    return lax.broadcasted_iota(jnp.int32, shape, axis)


def row_after(w):
    n = w.shape[0]
    return jnp.where(iota(w.shape, 0) < n - 1, pltpu.roll(w, n - 1, 0), 0.0)


def row_before(w):
    return jnp.where(iota(w.shape, 0) > 0, pltpu.roll(w, 1, 0), 0.0)


def col_after(w):
    n = w.shape[1]
    return jnp.where(iota(w.shape, 1) < n - 1, pltpu.roll(w, n - 1, 1), 0.0)


def col_before(w):
    return jnp.where(iota(w.shape, 1) > 0, pltpu.roll(w, 1, 1), 0.0)


def second_rows(w):
    return row_before(w) + row_after(w) - 2.0 * w


def second_cols(w):
    return col_before(w) + col_after(w) - 2.0 * w


def stiffness(w, live, thick, support):
    bend_rows = jnp.where(live, thick * second_rows(w), 0.0)
    bend_cols = thick * second_cols(w)
    return jnp.where(live, support * w + second_rows(bend_rows) + second_cols(bend_cols), 0.0)


def geometric(w, live, nuu, nvv, nuv):
    along_rows = row_after(w) - w
    along_cols = col_after(w) - w
    rows = nuu * along_rows + nuv * along_cols
    cols = nvv * along_cols + nuv * along_rows
    return jnp.where(live, row_before(rows) - rows + col_before(cols) - cols, 0.0)


def live_of(rows_ref, slot, shape):
    return iota(shape, 0) < rows_ref[slot]


def column_sums(product):
    return jnp.sum(product, axis=0, keepdims=True)


def packed(sums):
    totals = jnp.sum(sums, axis=1, keepdims=True)
    lane = iota((8, LANES), 1)
    out = jnp.zeros((8, LANES), jnp.float32)
    for tile in range(TILES):
        out = jnp.where(lane == tile, totals[8 * tile : 8 * tile + 8], out)
    return out


def pack_kernel(rows_ref, mine_ref, match_ref, stress_ref, elem_ref, vec_ref, pay_ref, edge_ref):
    rows_dev, ncol = stress_ref.shape[1:]
    slots = rows_ref.shape[0]
    prows = rows_dev // slots
    for j in range(3):
        pay_ref[:, j * ncol : (j + 1) * ncol] = stress_ref[j]
    square = (rows_dev, rows_dev)
    spread = jnp.broadcast_to(elem_ref[...].astype(jnp.float32), square)
    column = jnp.sum(
        jnp.where(iota(square, 0) == iota(square, 1), spread, 0.0), axis=1, keepdims=True
    )
    pay_ref[:, 3 * ncol :] = jnp.broadcast_to(column, (rows_dev, LANES)).astype(jnp.bfloat16)
    for s in range(slots):
        last = s * prows + rows_ref[s] - 1
        for v in range(2):
            at = 4 * (2 * s + v)
            edge_ref[at : at + 1, :] = vec_ref[v, pl.ds(last - 1, 1), :]
            edge_ref[at + 1 : at + 2, :] = vec_ref[v, pl.ds(last, 1), :]
            edge_ref[at + 2 : at + 4, :] = vec_ref[v, s * prows : s * prows + 2, :]
        at = 8 * slots
        edge_ref[at + s : at + s + 1, :] = jnp.full((1, ncol), mine_ref[s], jnp.int32).astype(jnp.float32)
        edge_ref[at + slots + s : at + slots + s + 1, :] = jnp.full((1, ncol), match_ref[s], jnp.int32).astype(jnp.float32)
    used = 10 * slots
    edge_ref[used:, :] = jnp.zeros((edge_ref.shape[0] - used, ncol), jnp.float32)


def stiff_kernel(
    rows_ref, mine_ref, match_ref, vec_ref, thick_ref, support_ref, edge_ref, below_ref, above_ref,
    k_ref, uk_ref, prec_ref,
):
    slots = rows_ref.shape[0]
    rows_dev, ncol = thick_ref.shape
    prows = rows_dev // slots
    for s in range(slots):
        at = slice(s * prows, (s + 1) * prows)
        live = live_of(rows_ref, s, (prows, ncol))
        thick, support = thick_ref[at, :], support_ref[at, :]
        prec = jnp.where(live, 1.0 / (support + 12.0 * thick), 0.0)
        prec_ref[at, :] = prec
        for v in range(2):
            w = jnp.where(live, vec_ref[v, at, :], 0.0)
            k_ref[v, at, :] = stiffness(w, live, thick, support)
        last = s * prows + rows_ref[s] - 1
        first = s * prows
        for v in range(2):
            own = edge_ref[4 * (2 * s + v) : 4 * (2 * s + v) + 4, :]
            top = jnp.zeros((2, ncol), jnp.float32)
            bottom = jnp.zeros((2, ncol), jnp.float32)
            for ref in (below_ref, above_ref):
                for t in range(slots):
                    strip = ref[4 * (2 * t + v) : 4 * (2 * t + v) + 4, :]
                    label = ref[8 * slots + t : 8 * slots + t + 1, :]
                    wants = ref[9 * slots + t : 9 * slots + t + 1, :]
                    top = top + jnp.where(wants == mine_ref[s].astype(jnp.float32), strip[0:2], 0.0)
                    bottom = bottom + jnp.where(label == match_ref[s].astype(jnp.float32), strip[2:4], 0.0)
            jump_t = own[1:2] - bottom[0:1]
            slope_t = own[1:2] - own[0:1] - (bottom[1:2] - bottom[0:1])
            jump_b = top[1:2] - own[2:3]
            slope_b = top[1:2] - top[0:1] - (own[3:4] - own[2:3])
            k_ref[v, pl.ds(last, 1), :] += penalty_value * jump_t + penalty_slope * slope_t
            k_ref[v, pl.ds(last - 1, 1), :] += -penalty_slope * slope_t
            k_ref[v, first : first + 1, :] += -penalty_value * jump_b + penalty_slope * slope_b
            k_ref[v, first + 1 : first + 2, :] += -penalty_slope * slope_b
        for v in range(2):
            uk_ref[v, at, :] = prec * k_ref[v, at, :]


def gram_kernel(
    rows_ref, match_ref, arrived_ref, vec_ref, thick_ref, support_ref, prec_ref, k_ref, uk_ref,
    ug_ref, stress_ref, out_ref, sums_ref, g_ref,
):
    slots = rows_ref.shape[0]
    rows_dev, ncol = thick_ref.shape
    prows = rows_dev // slots
    index = arrived_ref[:, 3 * ncol :].astype(jnp.float32)
    lane = iota(index.shape, 1).astype(jnp.float32)
    pick = jnp.concatenate(
        [
            jnp.where(index == lane + float(h * LANES), 1.0, 0.0).astype(jnp.bfloat16)
            for h in range(rows_dev // LANES)
        ],
        axis=1,
    )
    placed = lax.dot_general(
        pick, arrived_ref[:, : 3 * ncol], (((0,), (0,)), ((), ())), preferred_element_type=jnp.float32
    )
    for j in range(3):
        stress_ref[j] = placed[:, j * ncol : (j + 1) * ncol]
    sums_ref[...] = jnp.zeros_like(sums_ref)

    def add(name, product):
        k = AT[name]
        sums_ref[k : k + 1, :] += column_sums(product)

    for s in range(slots):
        at = slice(s * prows, (s + 1) * prows)
        shape = (prows, ncol)
        live = live_of(rows_ref, s, shape)
        thick, support, prec = thick_ref[at, :], support_ref[at, :], prec_ref[at, :]
        nuu, nvv, nuv = (stress_ref[j, at, :] for j in range(3))
        for v in range(2):
            w = jnp.where(live, vec_ref[v, at, :], 0.0)
            g_ref[v] = geometric(w, live, nuu, nvv, nuv)
            ug_ref[v, at, :] = prec * g_ref[v]
        for a in range(2):
            wa = jnp.where(live, vec_ref[a, at, :], 0.0)
            for b in range(a, 2):
                add(("kxx", a, b), wa * k_ref[b, at, :])
                add(("gxx", a, b), wa * g_ref[b])
                add(("kpk", a, b), k_ref[a, at, :] * uk_ref[b, at, :])
                add(("gpg", a, b), g_ref[a] * ug_ref[b, at, :])
            for b in range(2):
                add(("kpg", a, b), k_ref[a, at, :] * ug_ref[b, at, :])
        basis = [(ug_ref, 0), (ug_ref, 1), (uk_ref, 0), (uk_ref, 1)]
        for a in range(4):
            ref, v = basis[a]
            w = ref[v, at, :]
            kw = stiffness(w, live, thick, support)
            gw = geometric(w, live, nuu, nvv, nuv)
            for b in range(a + 1):
                ref, v = basis[b]
                other = ref[v, at, :]
                add(("kuu", b, a), other * kw)
                add(("guu", b, a), other * gw)
        last = s * prows + rows_ref[s] - 1
        for a in range(4):
            ref, v = basis[a]
            to = 4 * (4 * s + a)
            out_ref[to : to + 1, :] = ref[v, pl.ds(last - 1, 1), :]
            out_ref[to + 1 : to + 2, :] = ref[v, pl.ds(last, 1), :]
            out_ref[to + 2 : to + 4, :] = ref[v, s * prows : s * prows + 2, :]
    to = 16 * slots
    out_ref[to : to + 8, :LANES] = packed(sums_ref[...])
    for s in range(slots):
        out_ref[to + s : to + s + 1, LANES:] = jnp.full((1, ncol - LANES), match_ref[s], jnp.int32).astype(jnp.float32)


def apply_kernel(
    rows_ref, thick_ref, support_ref, prec_ref, stress_ref, ug_ref, uk_ref, pk_ref, pg_ref,
):
    slots = rows_ref.shape[0]
    rows_dev, ncol = thick_ref.shape
    prows = rows_dev // slots
    for s in range(slots):
        at = slice(s * prows, (s + 1) * prows)
        live = live_of(rows_ref, s, (prows, ncol))
        thick, support, prec = thick_ref[at, :], support_ref[at, :], prec_ref[at, :]
        nuu, nvv, nuv = (stress_ref[j, at, :] for j in range(3))
        for a, (ref, v) in enumerate([(ug_ref, 0), (ug_ref, 1), (uk_ref, 0), (uk_ref, 1)]):
            w = ref[v, at, :]
            pk_ref[a, at, :] = prec * stiffness(w, live, thick, support)
            pg_ref[a, at, :] = prec * geometric(w, live, nuu, nvv, nuv)


def line_kernel(slots, line_ref, out_ref, sums_ref):
    owners, _, ncol = line_ref.shape
    tag = 16 * slots
    total = line_ref[0, tag : tag + 8, :LANES]
    for z in range(1, owners):
        total = total + line_ref[z, tag : tag + 8, :LANES]
    sums_ref[...] = jnp.zeros_like(sums_ref)
    for z in range(owners):
        for s in range(slots):
            wanted = line_ref[z, tag + s : tag + s + 1, LANES : 2 * LANES][:, :1]
            jumps, slopes = [], []
            for a in range(4):
                own = line_ref[z, 4 * (4 * s + a) : 4 * (4 * s + a) + 2, :]
                bottom = jnp.zeros((2, ncol), jnp.float32)
                for near in {(z + 1) % owners, (z - 1) % owners}:
                    for t in range(slots):
                        strip = line_ref[near, 4 * (4 * t + a) + 2 : 4 * (4 * t + a) + 4, :]
                        bottom = bottom + jnp.where(wanted == float(near * slots + t), strip, 0.0)
                jumps.append(own[1:2] - bottom[0:1])
                slopes.append(own[1:2] - own[0:1] - (bottom[1:2] - bottom[0:1]))
            for a, b in UU:
                k = AT["kuu", a, b]
                sums_ref[k : k + 1, :] += (
                    penalty_value * jumps[a] * jumps[b] + penalty_slope * slopes[a] * slopes[b]
                )
    out_ref[...] = total + packed(sums_ref[...])


def form(table, left, right):
    total = None
    for i, c in left.items():
        for j, d in right.items():
            term = c * d * table[i, j]
            total = term if total is None else total + term
    return total


def final_kernel(
    cells, rows_ref, mine_ref, match_ref, total_ref, vec_ref, ug_ref, uk_ref, prec_ref, pk_ref, pg_ref,
    edge_ref, below_ref, above_ref, sent_ref, line_ref, out_ref,
):
    slots = rows_ref.shape[0]
    rows_dev, ncol = prec_ref.shape
    prows = rows_dev // slots
    owners = line_ref.shape[0]
    total = total_ref[...]

    def value(*name):
        k = AT[name]
        return total[k % 8 : k % 8 + 1, k // 8 : k // 8 + 1]

    k_table, g_table = {}, {}

    def put(table, i, j, what):
        table[i, j] = what
        table[j, i] = what

    for a in range(2):
        for b in range(2):
            lo, hi = min(a, b), max(a, b)
            put(k_table, a, b, value("kxx", lo, hi))
            put(g_table, a, b, value("gxx", lo, hi))
            put(k_table, a, 2 + b, value("kpg", a, b))
            put(k_table, a, 4 + b, value("kpk", lo, hi))
            put(g_table, a, 2 + b, value("gpg", lo, hi))
            put(g_table, a, 4 + b, value("kpg", b, a))
    for a, b in UU:
        put(k_table, 2 + a, 2 + b, value("kuu", a, b))
        put(g_table, 2 + a, 2 + b, value("guu", a, b))

    first_a, cross_k, second_a = k_table[0, 0], k_table[0, 1], k_table[1, 1]
    first_g, cross_g, second_g = g_table[0, 0], g_table[0, 1], g_table[1, 1]
    ratio = cross_k / first_a
    other_a = second_a - ratio * cross_k
    other_q = second_g - 2.0 * ratio * cross_g + ratio * ratio * first_g
    mu_first = first_g / first_a
    mu_other = other_q / other_a
    scale_first = jnp.sqrt(norm_scale * cells / first_a)
    scale_other = jnp.sqrt(norm_scale * cells / other_a)
    one = jnp.ones_like(ratio)
    new_first = {0: scale_first, 2: scale_first, 4: -scale_first * mu_first}
    new_second = {
        0: -scale_other * ratio,
        1: scale_other,
        2: -scale_other * ratio,
        3: scale_other,
        4: scale_other * mu_other * ratio,
        5: -scale_other * mu_other,
    }
    a1 = form(k_table, new_first, new_first)
    c = form(k_table, new_first, new_second)
    a2 = form(k_table, new_second, new_second)
    g1 = form(g_table, new_first, new_first)
    h = form(g_table, new_first, new_second)
    g2 = form(g_table, new_second, new_second)
    r = c / a1
    b2 = a2 - r * c
    q2 = g2 - 2.0 * r * h + r * r * g1
    mus = [g1 / a1, q2 / b2]
    scales = [jnp.sqrt(norm_scale * cells / a1), jnp.sqrt(norm_scale * cells / b2)]
    zero = jnp.zeros_like(one)
    lead = [new_first, {i: new_second[i] - r * new_first.get(i, zero) for i in new_second}]
    for s in range(slots):
        at = slice(s * prows, (s + 1) * prows)
        live = live_of(rows_ref, s, (prows, ncol))
        basis = [jnp.where(live, vec_ref[v, at, :], 0.0) for v in range(2)]
        basis += [ug_ref[v, at, :] for v in range(2)] + [uk_ref[v, at, :] for v in range(2)]
        for v in range(2):
            acc = None
            coef = dict(lead[v])
            for i in (0, 1):
                if i in lead[v]:
                    coef[2 + i] = coef.get(2 + i, zero) + lead[v][i]
                    coef[4 + i] = coef.get(4 + i, zero) - mus[v] * lead[v][i]
            for i, f in coef.items():
                term = (scales[v] * f) * basis[i]
                acc = term if acc is None else acc + term
            for i in range(2, 6):
                if i in lead[v]:
                    f = scales[v] * lead[v][i]
                    acc = acc + f * pg_ref[i - 2, at, :] - (f * mus[v]) * pk_ref[i - 2, at, :]
            out_ref[v, at, :] = acc
    for s in range(slots):
        own_id = mine_ref[s].astype(jnp.float32)
        want_id = match_ref[s].astype(jnp.float32)
        last = s * prows + rows_ref[s] - 1
        first = s * prows
        own, top, bottom = [], [], []
        for a in range(4):
            own.append(sent_ref[4 * (4 * s + a) : 4 * (4 * s + a) + 4, :])
            t_part = jnp.zeros((2, ncol), jnp.float32)
            b_part = jnp.zeros((2, ncol), jnp.float32)
            for z in range(owners):
                for t in range(slots):
                    strip = line_ref[z, 4 * (4 * t + a) : 4 * (4 * t + a) + 4, :]
                    wants = line_ref[z, 16 * slots + t : 16 * slots + t + 1, LANES : 2 * LANES][:, :1]
                    t_part = t_part + jnp.where(wants == own_id, strip[0:2], 0.0)
                    b_part = b_part + jnp.where(want_id == float(z * slots + t), strip[2:4], 0.0)
            top.append(t_part)
            bottom.append(b_part)
        for v in range(2):
            sides = []
            for strips in (own, top, bottom):
                acc = None
                for i in range(2, 6):
                    if i in lead[v]:
                        term = lead[v][i] * strips[i - 2]
                        acc = term if acc is None else acc + term
                sides.append(acc)
            o, t, b = sides
            jump_t = o[1:2] - b[0:1]
            slope_t = o[1:2] - o[0:1] - (b[1:2] - b[0:1])
            jump_b = t[1:2] - o[2:3]
            slope_b = t[1:2] - t[0:1] - (o[3:4] - o[2:3])
            gain = -scales[v] * mus[v]

            def put_row(row, what):
                out_ref[v, pl.ds(row, 1), :] += gain * prec_ref[pl.ds(row, 1), :] * what

            put_row(last, penalty_value * jump_t + penalty_slope * slope_t)
            put_row(last - 1, -penalty_slope * slope_t)
            put_row(first, -penalty_value * jump_b + penalty_slope * slope_b)
            put_row(first + 1, -penalty_slope * slope_b)


def call(body, outs, kinds, scratch=(), flops=1_000_000):
    spaces = {"s": pltpu.SMEM, "v": pltpu.VMEM}
    return pl.pallas_call(
        body,
        out_shape=[jax.ShapeDtypeStruct(s, d) for s, d in outs],
        in_specs=[pl.BlockSpec(memory_space=spaces[k]) for k in kinds],
        out_specs=[pl.BlockSpec(memory_space=pltpu.VMEM) for _ in outs],
        scratch_shapes=[pltpu.VMEM(s, jnp.float32) for s in scratch],
        compiler_params=pltpu.CompilerParams(vmem_limit_bytes=32 * 1024 * 1024),
        cost_estimate=pl.CostEstimate(flops=flops, bytes_accessed=2_000_000, transcendentals=0),
    )


def per_device(vectors, prestress, thickness, foundation, patch_rows, matched, elem_row):
    owners = lax.axis_size("patch")
    inner = lax.axis_size(("sub", "half"))
    slots = patch_rows.shape[0]
    rows_dev, ncol = thickness.shape
    f32 = jnp.float32
    mine = lax.axis_index("patch") * slots + jnp.arange(slots, dtype=jnp.int32)
    match = matched // (inner * slots) * slots + matched % slots
    local_row = (elem_row % rows_dev).reshape(1, rows_dev)
    cells = float(owners * inner * rows_dev * ncol)

    width = 3 * ncol + LANES
    edge_rows = -(-10 * slots // 8) * 8
    payload, edges = call(
        pack_kernel,
        [((rows_dev, width), jnp.bfloat16), ((edge_rows, ncol), f32)],
        "sssvvv",
    )(patch_rows, mine, match, jnp.transpose(prestress, (1, 0, 2)), local_row, vectors)
    arrived = lax.all_to_all(
        payload, ("patch", "sub", "half"), split_axis=0, concat_axis=0, tiled=True
    )
    below = passed_along(edges, "patch", 1)
    above = passed_along(edges, "patch", -1)
    field = ((2, rows_dev, ncol), f32)
    four = ((4, rows_dev, ncol), f32)
    one = ((rows_dev, ncol), f32)
    k_x, u_k, prec = call(stiff_kernel, [field, field, one], "sssvvvvvv")(
        patch_rows, mine, match, vectors, thickness, foundation, edges, below, above
    )
    sent_rows = 16 * slots + 8
    u_g, stress, sent = call(
        gram_kernel,
        [field, ((3, rows_dev, ncol), f32), ((sent_rows, ncol), f32)],
        "ssvvvvvvv",
        [(SUMS, ncol), (2, rows_dev // slots, ncol)],
    )(patch_rows, match, arrived, vectors, thickness, foundation, prec, k_x, u_k)
    line = lax.all_to_all(
        jnp.broadcast_to(sent[None], (owners, sent_rows, ncol)), "patch", split_axis=0, concat_axis=0, tiled=True
    )
    pk, pg = call(apply_kernel, [four, four], "svvvvvv")(
        patch_rows, thickness, foundation, prec, stress, u_g, u_k
    )
    (total,) = call(
        functools.partial(line_kernel, slots), [((8, LANES), f32)], "v", [(SUMS, ncol)]
    )(line)
    total = summed_over(summed_over(total, "half"), "sub")
    (modes,) = call(functools.partial(final_kernel, cells), [field], "sssvvvvvvvvvvvv")(
        patch_rows, mine, match, total, vectors, u_g, u_k, prec, pk, pg, edges, below, above, sent, line
    )
    return modes


def solution(mesh):
    in_specs = (
        P(None, ("groups", "patch", "sub", "half"), None),
        P(("groups", "patch", "sub", "half"), None, None),
        P(("groups", "patch", "sub", "half"), None),
        P(("groups", "patch", "sub", "half"), None),
        P(("groups", "patch", "sub", "half")),
        P(("groups", "patch", "sub", "half")),
        P(("groups", "patch", "sub", "half")),
    )
    out_specs = P(None, ("groups", "patch", "sub", "half"), None)
    return jax.shard_map(
        per_device, mesh=mesh, in_specs=in_specs, out_specs=out_specs, check_vma=False
    )
```

time: 212 us -> 51.8 us (0.24)
  local copies, waits for them, and re-layouts: 75.2 us -> 4.04 us
  blocking collectives: 59.7 us -> 10.1 us
  waiting for transfers between devices: 26 us -> 10.4 us
  Pallas kernels: 0 us -> 13.9 us
  starting transfers between devices: 26.3 us -> 12.8 us
  between operations: 13.6 us -> 0.1 us
  other arithmetic: 10.3 us -> 0.03 us
    psum x2 -> x0, blocking collectives: 59.7 us -> none  [per_device(): totals = lax.psum(products(field, kfield, gfield), ('patch', 'sub', 'half'))]
    gather x4 -> x0, local copies, waits for them, and re-layouts: 49.2 us -> none  [row_pick(): return jnp.take_along_axis(field, where_rows, axis=2)[:, :, 0, :]]
    all_to_all x4 -> x1, waiting for transfers between devices: 24.9 us -> 0.01 us  [per_device(): lax.all_to_all(payload, ('patch', 'sub', 'half'), split_axis=0, concat_ax...]
    pallas_call x0 -> x6, Pallas kernels: none -> 13.9 us  [the longest x1 4.63 us: per_device(): call(gram_kernel, [field, ((3, rows_dev, ncol), f32), ((sent_rows, ncol),...]
    all_to_all x0 -> x1, blocking collectives: none -> 10.1 us  [per_device(): lax.all_to_all(jnp.broadcast_to(sent[None], (owners, sent_rows, ncol)), '...]
    ppermute x6 -> x4, waiting for transfers between devices: 1.1 us -> 10.4 us  [passed_along(): lax.ppermute(array, axis, [(i, (i + by) % peers) for i in range(peers)])]
    another operation x6 -> x0, local copies, waits for them, and re-layouts: 7.64 us -> none  [the longest x2 7.63 us: products(): jnp.stack([jnp.sum(field[0] * kfield[0]), jnp.sum(field[0] * kfield[1]),...]
    ppermute x6 -> x4, starting transfers between devices: 12.9 us -> 5.34 us  [passed_along(): lax.ppermute(array, axis, [(i, (i + by) % peers) for i in range(peers)])]
  transfers between devices with their start and end apart: 10 -> 5, of which waited for: 5 -> 2; matrix products, arithmetic and copies ran while one was open for 2% -> 0% of each run, Pallas kernels for 0% -> 10%
where the time goes in v1:
time: 51.8 us; the launch traced here: 51.4 us
  Pallas kernels  13.9 us (27%)
  starting transfers between devices  12.8 us (25%)
  waiting for transfers between devices  10.4 us (20%)
  blocking collectives  10.1 us (19%)
  local copies, waits for them, and re-layouts  4.04 us (8%)
    ppermute x4, waiting for transfers between devices, passed_along(): lax.ppermute(array, axis, [(i, (i + by) % peers) for i in range(peers)])  10.4 us
    all_to_all x1, blocking collectives, per_device(): lax.all_to_all(jnp.broadcast_to(sent[None], (owners, sent_rows, ncol)), '...  10.1 us
    all_to_all x1, starting transfers between devices, per_device(): lax.all_to_all(payload, ('patch', 'sub', 'half'), split_axis=0, concat_ax...  7.49 us
    ppermute x4, starting transfers between devices, passed_along(): lax.ppermute(array, axis, [(i, (i + by) % peers) for i in range(peers)])  5.34 us
    pallas_call x1, Pallas kernels, per_device(): call(gram_kernel, [field, ((3, rows_dev, ncol), f32), ((sent_rows, ncol),...  4.63 us
    unnamed x16, local copies, waits for them, and re-layouts  4.03 us
    pallas_call x1, Pallas kernels, per_device(): call(apply_kernel, [four, four], 'svvvvvv')  3.34 us
    pallas_call x1, Pallas kernels, per_device(): call(functools.partial(final_kernel, cells), [field], 'sssvvvvvvvvvvvv')  2.38 us
  transfers between devices with their start and end apart: 5, of which 2 were waited for; matrix products, arithmetic and copies ran while one was open for 0% of the time, Pallas kernels for 10%

profile of v1, /device:TPU:0, one launch (start us, length us, event | category | flops | bytes accessed | tf_op | source)
XLA Modules:
  0.0 51.4 jit_solution(12727462187592522190)
XLA Ops:
  0.0 0.7 %copy-done.6 = s32[256]{0:T(256)S(1)} copy-done((s32[256]{0:T(256)S(1)}, s32[256]{0:T(256)}, u32[]{:S(2)}) %copy-start.6) | copy-done | bytes 1048
  0.7 0.6 %copy-done.7 = s32[2]{0:T(128)S(1)} copy-done((s32[2]{0:T(128)S(1)}, s32[2]{0:T(128)}, u32[]{:S(2)}) %copy-start.7) | copy-done | bytes 32
  1.4 0.0 copy-start.5
  1.4 0.6 %copy-done.5 = s32[2]{0:T(128)S(1)} copy-done((s32[2]{0:T(128)S(1)}, s32[2]{0:T(128)}, u32[]{:S(2)}) %copy-start.5) | copy-done | bytes 32
  2.0 1.0 %copy-done = f32[2,256,256]{2,1,0:T(8,128)S(1)} copy-done((f32[2,256,256]{2,1,0:T(8,128)S(1)}, f32[2,256,256]{2,1,0:T(8,128)}, u32[]{:S(2)}) %copy-start) | copy-done | bytes 524312
  3.1 1.0 %copy-done.4 = bf16[256,3,256]{2,0,1:T(8,128)(2,1)S(1)} copy-done((bf16[256,3,256]{2,0,1:T(8,128)(2,1)S(1)}, bf16[256,3,256]{2,0,1:T(8,128)(2,1)}, u32[]{:S(2)}) %copy-start.4) | copy-done | bytes 393240
  4.1 1.4 %shard_map.73 = (bf16[256,896]{1,0:T(8,128)(2,1)}, f32[24,256]{1,0:T(8,128)S(1)}) custom-call(s32[2]{0:T(128)S(1)} %copy-done.5, s32[2]{0:T(128)S(1)} %get-tuple-element.26.mine_ref, s32[2]{0:T(128)S(1)} %get-tuple-element.25.match_ref, bf16[3,256,256]{2,1,0:T(8,128)(2,1)S(1)} %bitcast.5, s32[1,256]{1,0:T(1,128)S(1)} %bitcast.6, f32[2,256,256]{2,1,0:T(8,128)S(1)} %copy-done), custom_call_target="tpu_custom_call" | custom-call | flops 1000000 | bytes 2000000 | tf_op jit(solution)/shard_map/pallas_call | solution.py:448
  5.5 7.5 %all-to-all-start = ((bf16[16,16,896]{2,1,0:T(8,128)(2,1)}), bf16[16,16,896]{2,1,0:T(8,128)(2,1)S(1)}, u32[]{:S(2)}, u32[]{:S(2)}) async-start(bf16[16,16,896]{2,1,0:T(8,128)(2,1)} %bitcast.2), calls=%async_computation | async-start | bytes 917504 | tf_op jit(solution)/shard_map/all_to_all | solution.py:453
  13.0 1.9 %collective-permute-start = (f32[24,256]{1,0:T(8,128)S(1)}, f32[24,256]{1,0:T(8,128)S(1)}, u32[]{:S(2)}, u32[]{:S(2)}) collective-permute-start(f32[24,256]{1,0:T(8,128)S(1)} %get-tuple-element.16.edge_ref), channel_id=1, source_target_pairs={{0,4},{4,8},{8,12},{12,0},{1,5},{5,9},{9,13},{13,1},{2,6},{6,10},{... | collective-permute-start | bytes 73736 | tf_op jit(solution)/shard_map/ppermute | solution.py:32
  14.9 2.0 %collective-permute-start.1 = (f32[24,256]{1,0:T(8,128)S(1)}, f32[24,256]{1,0:T(8,128)S(1)}, u32[]{:S(2)}, u32[]{:S(2)}) collective-permute-start(f32[24,256]{1,0:T(8,128)S(1)} %get-tuple-element.16.edge_ref), channel_id=1, source_target_pairs={{0,12},{4,0},{8,4},{12,8},{1,13},{5,1},{9,5},{13,9},{2,14},{6,2},{... | collective-permute-start | bytes 73736 | tf_op jit(solution)/shard_map/ppermute | solution.py:32
  16.9 9.2 %collective-permute-done.below_ref = f32[24,256]{1,0:T(8,128)S(1)} collective-permute-done((f32[24,256]{1,0:T(8,128)S(1)}, f32[24,256]{1,0:T(8,128)S(1)}, u32[]{:S(2)}, u32[]{:S(2)}) %collective-permute-start) | collective-permute-done | bytes 24608 | tf_op jit(solution)/shard_map/ppermute | solution.py:32
  26.1 0.0 collective-permute-done.1.above_ref
  26.1 0.0 copy-done.3
  26.1 1.6 %shard_map.74 = (f32[2,256,256]{2,1,0:T(8,128)S(1)}, f32[2,256,256]{2,1,0:T(8,128)S(1)}, f32[256,256]{1,0:T(8,128)S(1)}) custom-call(s32[2]{0:T(128)S(1)} %copy-done.5, s32[2]{0:T(128)S(1)} %get-tuple-element.26.mine_ref, s32[2]{0:T(128)S(1)} %get-tuple-element.25.match_ref, f32[2,256,256]{2,1,0:T(8,128)S(1)} %copy-done.1, f32[256,256]{1,0:T(8,128)S(1)} %copy-done.2, ...), custom_call_target="tpu_custom_call" | custom-call | flops 1000000 | bytes 2000000 | tf_op jit(solution)/shard_map/pallas_call | solution.py:461
  27.8 0.0 all-to-all-done
  27.8 4.6 %shard_map.75 = (f32[2,256,256]{2,1,0:T(8,128)S(1)}, f32[3,256,256]{2,1,0:T(8,128)S(1)}, f32[40,256]{1,0:T(8,128)S(1)}) custom-call(s32[2]{0:T(128)S(1)} %copy-done.5, s32[2]{0:T(128)S(1)} %get-tuple-element.25.match_ref, bf16[256,896]{1,0:T(8,128)(2,1)S(1)} %bitcast.4, f32[2,256,256]{2,1,0:T(8,128)S(1)} %copy-done.1, f32[256,256]{1,0:T(8,128)S(1)} %copy-done.2, ...), custom_call_target="tpu_custom_call" | custom-call | flops 1000000 | bytes 2000000 | tf_op jit(solution)/shard_map/pallas_call | solution.py:465
  32.5 10.1 %all_to_all.16.line_ref = f32[4,40,256]{2,1,0:T(8,128)S(1)} all-to-all(f32[4,40,256]{2,1,0:T(8,128)S(1)} %broadcast_in_dim.2), channel_id=1, replica_groups=mesh['groups'=2,'patch'=4,'sub'=2,'half'=2] {'patch'}, dimensions={0} | all-to-all | bytes 327680 | tf_op jit(solution)/shard_map/all_to_all | solution.py:471
  42.6 0.5 shard_map.76
  43.1 0.0 collective-permute-start.2
  43.1 1.2 %collective-permute-done.2 = f32[8,128]{1,0:T(8,128)S(1)} collective-permute-done((f32[8,128]{1,0:T(8,128)S(1)}, f32[8,128]{1,0:T(8,128)S(1)}, u32[]{:S(2)}, u32[]{:S(2)}) %collective-permute-start.2) | collective-permute-done | bytes 4128 | tf_op jit(solution)/shard_map/ppermute | solution.py:32
  44.3 1.4 %collective-permute-start.3 = (f32[8,128]{1,0:T(8,128)S(1)}, f32[8,128]{1,0:T(8,128)S(1)}, u32[]{:S(2)}, u32[]{:S(2)}) collective-permute-start(f32[8,128]{1,0:T(8,128)S(1)} %add.33), channel_id=1, source_target_pairs={{0,2},{2,0},{1,3},{3,1},{4,6},{6,4},{5,7},{7,5},{8,10},{10,8},{9,1... | collective-permute-start | bytes 12296 | tf_op jit(solution)/shard_map/ppermute | solution.py:32
  45.7 3.3 %shard_map.77 = (f32[4,256,256]{2,1,0:T(8,128)S(1)}, f32[4,256,256]{2,1,0:T(8,128)S(1)}) custom-call(s32[2]{0:T(128)S(1)} %copy-done.5, f32[256,256]{1,0:T(8,128)S(1)} %copy-done.2, f32[256,256]{1,0:T(8,128)S(1)} %copy-done.3, f32[256,256]{1,0:T(8,128)S(1)} %get-tuple-element.17.prec_ref, f32[3,256,256]{2,1,0:T(8,128)S(1)} %get-tuple-element.22.stress_ref, ...), custom_call_target="tpu_custom_call" | custom-call | flops 1000000 | bytes 2000000 | tf_op jit(solution)/shard_map/pallas_call | solution.py:474
  49.0 0.0 collective-permute-done.3
  49.1 2.4 %shard_map.78 = f32[2,256,256]{2,1,0:T(8,128)} custom-call(s32[2]{0:T(128)S(1)} %copy-done.5, s32[2]{0:T(128)S(1)} %get-tuple-element.26.mine_ref, s32[2]{0:T(128)S(1)} %get-tuple-element.25.match_ref, f32[8,128]{1,0:T(8,128)S(1)} %add.34.total_ref, f32[2,256,256]{2,1,0:T(8,128)S(1)} %copy-done.1, f32[2,256,256]{2,1,0:T(8,128)S(1)} %get-tuple-element.21.ug_ref, ...), custom_call_target="tpu_custom_call" | custom-call | flops 1000000 | bytes 2000000 | tf_op jit(solution)/shard_map/pallas_call | solution.py:481
  (14 shorter events, 0.1 us)
Async XLA Ops:
  0.0 0.7 %copy-start.6 = (s32[256]{0:T(256)S(1)}, s32[256]{0:T(256)}, u32[]{:S(2)}) copy-start(s32[256]{0:T(256)} %param.13) | copy-start | bytes 3076
  0.7 0.7 %copy-start.7 = (s32[2]{0:T(128)S(1)}, s32[2]{0:T(128)}, u32[]{:S(2)}) copy-start(s32[2]{0:T(128)} %param.12) | copy-start | bytes 28
  1.4 0.7 %copy-start.5 = (s32[2]{0:T(128)S(1)}, s32[2]{0:T(128)}, u32[]{:S(2)}) copy-start(s32[2]{0:T(128)} %rows_ref.9) | copy-start | bytes 28
  2.0 1.0 %copy-start = (f32[2,256,256]{2,1,0:T(8,128)S(1)}, f32[2,256,256]{2,1,0:T(8,128)}, u32[]{:S(2)}) copy-start(f32[2,256,256]{2,1,0:T(8,128)} %vec_ref.7) | copy-start | bytes 1572868
  3.1 1.0 %copy-start.4 = (bf16[256,3,256]{2,0,1:T(8,128)(2,1)S(1)}, bf16[256,3,256]{2,0,1:T(8,128)(2,1)}, u32[]{:S(2)}) copy-start(bf16[256,3,256]{2,0,1:T(8,128)(2,1)} %param.8) | copy-start | bytes 1179652
  4.1 22.1 %copy-start.3 = (f32[256,256]{1,0:T(8,128)S(1)}, f32[256,256]{1,0:T(8,128)}, u32[]{:S(2)}) copy-start(f32[256,256]{1,0:T(8,128)} %support_ref.5) | copy-start | bytes 786436
  5.5 20.6 %copy-start.1 = (f32[2,256,256]{2,1,0:T(8,128)S(1)}, f32[2,256,256]{2,1,0:T(8,128)}, u32[]{:S(2)}) copy-start(f32[2,256,256]{2,1,0:T(8,128)} %vec_ref.7) | copy-start | bytes 1572868
  5.5 20.7 %copy-start.2 = (f32[256,256]{1,0:T(8,128)S(1)}, f32[256,256]{1,0:T(8,128)}, u32[]{:S(2)}) copy-start(f32[256,256]{1,0:T(8,128)} %thick_ref.5) | copy-start | bytes 786436
  5.5 22.3 %all-to-all-start = ((bf16[16,16,896]{2,1,0:T(8,128)(2,1)}), bf16[16,16,896]{2,1,0:T(8,128)(2,1)S(1)}, u32[]{:S(2)}, u32[]{:S(2)}) async-start(bf16[16,16,896]{2,1,0:T(8,128)(2,1)} %bitcast.2), calls=%async_computation | async-start | bytes 917504 | tf_op jit(solution)/shard_map/all_to_all | solution.py:453
  13.0 13.1 %collective-permute-start = (f32[24,256]{1,0:T(8,128)S(1)}, f32[24,256]{1,0:T(8,128)S(1)}, u32[]{:S(2)}, u32[]{:S(2)}) collective-permute-start(f32[24,256]{1,0:T(8,128)S(1)} %get-tuple-element.16.edge_ref), channel_id=1, source_target_pairs={{0,4},{4,8},{8,12},{12,0},{1,5},{5,9},{9,13},{13,1},{2,6},{6,10},{... | collective-permute-start | bytes 73736 | tf_op jit(solution)/shard_map/ppermute | solution.py:32
  14.9 11.2 %collective-permute-start.1 = (f32[24,256]{1,0:T(8,128)S(1)}, f32[24,256]{1,0:T(8,128)S(1)}, u32[]{:S(2)}, u32[]{:S(2)}) collective-permute-start(f32[24,256]{1,0:T(8,128)S(1)} %get-tuple-element.16.edge_ref), channel_id=1, source_target_pairs={{0,12},{4,0},{8,4},{12,8},{1,13},{5,1},{9,5},{13,9},{2,14},{6,2},{... | collective-permute-start | bytes 73736 | tf_op jit(solution)/shard_map/ppermute | solution.py:32
  43.1 1.2 %collective-permute-start.2 = (f32[8,128]{1,0:T(8,128)S(1)}, f32[8,128]{1,0:T(8,128)S(1)}, u32[]{:S(2)}, u32[]{:S(2)}) collective-permute-start(f32[8,128]{1,0:T(8,128)S(1)} %shard_map.76), channel_id=1, source_target_pairs={{0,1},{1,0},{2,3},{3,2},{4,5},{5,4},{6,7},{7,6},{8,9},{9,8},{10,11... | collective-permute-start | bytes 12296 | tf_op jit(solution)/shard_map/ppermute | solution.py:32
  44.3 4.8 %collective-permute-start.3 = (f32[8,128]{1,0:T(8,128)S(1)}, f32[8,128]{1,0:T(8,128)S(1)}, u32[]{:S(2)}, u32[]{:S(2)}) collective-permute-start(f32[8,128]{1,0:T(8,128)S(1)} %add.33), channel_id=1, source_target_pairs={{0,2},{2,0},{1,3},{3,1},{4,6},{6,4},{5,7},{7,5},{8,10},{10,8},{9,1... | collective-permute-start | bytes 12296 | tf_op jit(solution)/shard_map/ppermute | solution.py:32

commit v2 on v1

v2 whole, which is shorter than its diff:
```python
import functools

import jax
import jax.numpy as jnp
from jax import lax
from jax.experimental import pallas as pl
from jax.experimental.pallas import tpu as pltpu
from jax.sharding import PartitionSpec as P

norm_scale = 16.0
penalty_value = 8.0
penalty_slope = 4.0
LANES = 128

UU = [(a, b) for a in range(4) for b in range(a, 4)]
NAMES = (
    [("kuu", a, b) for a, b in UU]
    + [("guu", a, b) for a, b in UU]
    + [("kxx", 0, 0), ("kxx", 0, 1), ("kxx", 1, 1)]
    + [("gxx", 0, 0), ("gxx", 0, 1), ("gxx", 1, 1)]
    + [("kpk", 0, 0), ("kpk", 0, 1), ("kpk", 1, 1)]
    + [("kpg", a, b) for a in range(2) for b in range(2)]
    + [("gpg", 0, 0), ("gpg", 0, 1), ("gpg", 1, 1)]
)
AT = {name: k for k, name in enumerate(NAMES)}
SUMS = 40
TILES = SUMS // 8


def passed_along(array, axis, by):
    peers = lax.axis_size(axis)
    return lax.ppermute(array, axis, [(i, (i + by) % peers) for i in range(peers)])


def summed_over(array, axis):
    total = array
    for by in range(1, lax.axis_size(axis)):
        total = total + passed_along(array, axis, by)
    return total


def iota(shape, axis):
    return lax.broadcasted_iota(jnp.int32, shape, axis)


def row_after(w):
    n = w.shape[0]
    return jnp.where(iota(w.shape, 0) < n - 1, pltpu.roll(w, n - 1, 0), 0.0)


def row_before(w):
    return jnp.where(iota(w.shape, 0) > 0, pltpu.roll(w, 1, 0), 0.0)


def col_after(w):
    n = w.shape[1]
    return jnp.where(iota(w.shape, 1) < n - 1, pltpu.roll(w, n - 1, 1), 0.0)


def col_before(w):
    return jnp.where(iota(w.shape, 1) > 0, pltpu.roll(w, 1, 1), 0.0)


def second_rows(w):
    return row_before(w) + row_after(w) - 2.0 * w


def second_cols(w):
    return col_before(w) + col_after(w) - 2.0 * w


def stiffness(w, live, thick, support):
    bend_rows = jnp.where(live, thick * second_rows(w), 0.0)
    bend_cols = thick * second_cols(w)
    return jnp.where(live, support * w + second_rows(bend_rows) + second_cols(bend_cols), 0.0)


def geometric(w, live, nuu, nvv, nuv):
    along_rows = row_after(w) - w
    along_cols = col_after(w) - w
    rows = nuu * along_rows + nuv * along_cols
    cols = nvv * along_cols + nuv * along_rows
    return jnp.where(live, row_before(rows) - rows + col_before(cols) - cols, 0.0)


def live_of(rows_ref, slot, shape):
    return iota(shape, 0) < rows_ref[slot]


def column_sums(product):
    return jnp.sum(product, axis=0, keepdims=True)


def packed(sums):
    totals = jnp.sum(sums, axis=1, keepdims=True)
    lane = iota((8, LANES), 1)
    out = jnp.zeros((8, LANES), jnp.float32)
    for tile in range(TILES):
        out = jnp.where(lane == tile, totals[8 * tile : 8 * tile + 8], out)
    return out


def place(rows_ref, matched_ref, slots):
    inner = lax.axis_size(("sub", "half"))
    mine = [lax.axis_index("patch") * slots + s for s in range(slots)]
    match = [
        matched_ref[s] // (inner * slots) * slots + lax.rem(matched_ref[s], slots) for s in range(slots)
    ]
    return mine, match


def label(number, ncol):
    return jnp.full((1, ncol), number, jnp.int32).astype(jnp.float32)


def pack_kernel(stress_ref, elem_ref, pay_ref, elem, index, sems):
    rows_dev, ncol = stress_ref.shape[1:]
    get = pltpu.make_async_copy(elem_ref, elem, sems.at[0])
    get.start()
    planes = [
        pltpu.make_async_copy(
            stress_ref.at[j], pay_ref.at[:, pl.ds(j * ncol, ncol)], sems.at[1 + j]
        )
        for j in range(3)
    ]
    for copy in planes:
        copy.start()
    get.wait()
    square = (rows_dev, rows_dev)
    if rows_dev & (rows_dev - 1) == 0:
        local = jnp.bitwise_and(elem[...], rows_dev - 1)
    else:
        local = lax.rem(elem[...], rows_dev)
    spread = jnp.broadcast_to(local.astype(jnp.float32), square)
    column = jnp.sum(
        jnp.where(iota(square, 0) == iota(square, 1), spread, 0.0), axis=1, keepdims=True
    )
    index[...] = jnp.broadcast_to(column, (rows_dev, LANES)).astype(jnp.bfloat16)
    put = pltpu.make_async_copy(index, pay_ref.at[:, pl.ds(3 * ncol, LANES)], sems.at[4])
    put.start()
    for copy in planes:
        copy.wait()
    put.wait()


def edge_kernel(rows_ref, matched_ref, vec_ref, edge_ref):
    slots = rows_ref.shape[0]
    rows_dev, ncol = vec_ref.shape[1:]
    prows = rows_dev // slots
    mine, match = place(rows_ref, matched_ref, slots)
    for s in range(slots):
        last = s * prows + rows_ref[s] - 1
        for v in range(2):
            at = 4 * (2 * s + v)
            edge_ref[at : at + 1, :] = vec_ref[v, pl.ds(last - 1, 1), :]
            edge_ref[at + 1 : at + 2, :] = vec_ref[v, pl.ds(last, 1), :]
            edge_ref[at + 2 : at + 4, :] = vec_ref[v, s * prows : s * prows + 2, :]
        at = 8 * slots
        edge_ref[at + s : at + s + 1, :] = label(mine[s], ncol)
        edge_ref[at + slots + s : at + slots + s + 1, :] = label(match[s], ncol)
    used = 10 * slots
    edge_ref[used:, :] = jnp.zeros((edge_ref.shape[0] - used, ncol), jnp.float32)


def stiff_kernel(rows_ref, vec_ref, thick_ref, support_ref, k_ref, uk_ref, prec_ref, sums_ref):
    slots = rows_ref.shape[0]
    rows_dev, ncol = thick_ref.shape
    prows = rows_dev // slots
    sums_ref[...] = jnp.zeros_like(sums_ref)

    def add(name, product):
        k = AT[name]
        sums_ref[k : k + 1, :] += column_sums(product)

    for s in range(slots):
        at = slice(s * prows, (s + 1) * prows)
        live = live_of(rows_ref, s, (prows, ncol))
        thick, support = thick_ref[at, :], support_ref[at, :]
        prec_ref[at, :] = jnp.where(live, 1.0 / (support + 12.0 * thick), 0.0)
        for v in range(2):
            w = jnp.where(live, vec_ref[v, at, :], 0.0)
            k_ref[v, at, :] = stiffness(w, live, thick, support)
            uk_ref[v, at, :] = prec_ref[at, :] * k_ref[v, at, :]
        for a in range(2):
            wa = jnp.where(live, vec_ref[a, at, :], 0.0)
            for b in range(a, 2):
                add(("kxx", a, b), wa * k_ref[b, at, :])
                add(("kpk", a, b), k_ref[a, at, :] * uk_ref[b, at, :])


def interface_rows(own, top, bottom):
    jump_t = own[1:2] - bottom[0:1]
    slope_t = own[1:2] - own[0:1] - (bottom[1:2] - bottom[0:1])
    jump_b = top[1:2] - own[2:3]
    slope_b = top[1:2] - top[0:1] - (own[3:4] - own[2:3])
    return (
        -penalty_slope * slope_t,
        penalty_value * jump_t + penalty_slope * slope_t,
        -penalty_value * jump_b + penalty_slope * slope_b,
        -penalty_slope * slope_b,
    )


def edge_places(rows_ref, slot, prows):
    last = slot * prows + rows_ref[slot] - 1
    return (last - 1, last, slot * prows, slot * prows + 1)


def bend_kernel(
    rows_ref, matched_ref, arrived_ref, vec_ref, prec_ref, uk_ref, edge_ref, below_ref, above_ref,
    g_ref, ug_ref, stress_ref, extra_ref, out_ref,
):
    slots = rows_ref.shape[0]
    rows_dev, ncol = prec_ref.shape
    prows = rows_dev // slots
    halves = ncol // LANES
    mine, match = place(rows_ref, matched_ref, slots)
    index = arrived_ref[:, 3 * ncol :].astype(jnp.float32)
    lane = iota(index.shape, 1).astype(jnp.float32)
    pick = jnp.concatenate(
        [
            jnp.where(index == lane + float(h * LANES), 1.0, 0.0).astype(jnp.bfloat16)
            for h in range(rows_dev // LANES)
        ],
        axis=1,
    )
    placed = lax.dot_general(
        pick, arrived_ref[:, : 3 * ncol], (((0,), (0,)), ((), ())), preferred_element_type=jnp.float32
    )
    for j in range(3):
        stress_ref[j] = placed[:, j * ncol : (j + 1) * ncol]
    rows_sent = 16 * slots

    def send(to, row):
        for h in range(halves):
            out_ref[h * rows_sent + to : h * rows_sent + to + row.shape[0], :] = row[:, h * LANES : (h + 1) * LANES]

    for s in range(slots):
        at = slice(s * prows, (s + 1) * prows)
        live = live_of(rows_ref, s, (prows, ncol))
        nuu, nvv, nuv = (stress_ref[j, at, :] for j in range(3))
        for v in range(2):
            w = jnp.where(live, vec_ref[v, at, :], 0.0)
            g_ref[v, at, :] = geometric(w, live, nuu, nvv, nuv)
            ug_ref[v, at, :] = prec_ref[at, :] * g_ref[v, at, :]
        own_id, want_id = mine[s].astype(jnp.float32), match[s].astype(jnp.float32)
        places = edge_places(rows_ref, s, prows)
        for v in range(2):
            own = edge_ref[4 * (2 * s + v) : 4 * (2 * s + v) + 4, :]
            top = jnp.zeros((2, ncol), jnp.float32)
            bottom = jnp.zeros((2, ncol), jnp.float32)
            for ref in (below_ref, above_ref):
                for t in range(slots):
                    strip = ref[4 * (2 * t + v) : 4 * (2 * t + v) + 4, :]
                    label_t = ref[8 * slots + t : 8 * slots + t + 1, :]
                    wants = ref[9 * slots + t : 9 * slots + t + 1, :]
                    top = top + jnp.where(wants == own_id, strip[0:2], 0.0)
                    bottom = bottom + jnp.where(label_t == want_id, strip[2:4], 0.0)
            added = interface_rows(own, top, bottom)
            for i, row in enumerate(places):
                to = 4 * (2 * s + v) + i
                extra_ref[to : to + 1, :] = added[i]
                send(4 * (4 * s + 2 + v) + i, uk_ref[v, pl.ds(row, 1), :] + prec_ref[pl.ds(row, 1), :] * added[i])
                send(4 * (4 * s + v) + i, ug_ref[v, pl.ds(row, 1), :])
    tag = halves * rows_sent
    for s in range(slots):
        out_ref[tag + s : tag + s + 1, :] = label(match[s], LANES)
    out_ref[tag + slots :, :] = jnp.zeros((out_ref.shape[0] - tag - slots, LANES), jnp.float32)


def gram_kernel(
    rows_ref, extra_ref, vec_ref, thick_ref, support_ref, prec_ref, k_in, uk_in, sums_in,
    g_ref, ug_ref, stress_ref, uk_ref, kuk_ref, kug_ref, gu_ref, tile_ref, sums_ref, k_ref,
):
    slots = rows_ref.shape[0]
    rows_dev, ncol = thick_ref.shape
    prows = rows_dev // slots
    sums_ref[...] = sums_in[...]

    def add(name, product):
        k = AT[name]
        sums_ref[k : k + 1, :] += column_sums(product)

    for s in range(slots):
        at = slice(s * prows, (s + 1) * prows)
        live = live_of(rows_ref, s, (prows, ncol))
        thick, support, prec = thick_ref[at, :], support_ref[at, :], prec_ref[at, :]
        nuu, nvv, nuv = (stress_ref[j, at, :] for j in range(3))
        places = edge_places(rows_ref, s, prows)
        for v in range(2):
            k_ref[v, at, :] = k_in[v, at, :]
            uk_ref[v, at, :] = uk_in[v, at, :]
        add_k = [[extra_ref[4 * (2 * s + v) + i : 4 * (2 * s + v) + i + 1, :] for i in range(4)] for v in range(2)]
        for a in range(2):
            for b in range(a, 2):
                for i, row in enumerate(places):
                    p = prec_ref[pl.ds(row, 1), :]
                    ka, kb = k_in[a, pl.ds(row, 1), :], k_in[b, pl.ds(row, 1), :]
                    add(("kxx", a, b), vec_ref[a, pl.ds(row, 1), :] * add_k[b][i])
                    add(("kpk", a, b), p * (ka * add_k[b][i] + add_k[a][i] * (kb + add_k[b][i])))
        for v in range(2):
            for i, row in enumerate(places):
                k_ref[v, pl.ds(row, 1), :] += add_k[v][i]
                uk_ref[v, pl.ds(row, 1), :] += prec_ref[pl.ds(row, 1), :] * add_k[v][i]
        for v in range(2):
            kuk_ref[v, at, :] = stiffness(uk_ref[v, at, :], live, thick, support)
            kug_ref[v, at, :] = stiffness(ug_ref[v, at, :], live, thick, support)
        for a in range(2):
            wa = jnp.where(live, vec_ref[a, at, :], 0.0)
            for b in range(a, 2):
                add(("gxx", a, b), wa * g_ref[b, at, :])
                add(("gpg", a, b), g_ref[a, at, :] * ug_ref[b, at, :])
                add(("kuu", a, b), ug_ref[a, at, :] * kug_ref[b, at, :])
                add(("kuu", 2 + a, 2 + b), uk_ref[a, at, :] * kuk_ref[b, at, :])
            for b in range(2):
                add(("kpg", a, b), k_ref[a, at, :] * ug_ref[b, at, :])
                add(("kuu", a, 2 + b), ug_ref[a, at, :] * kuk_ref[b, at, :])
        basis = [(ug_ref, 0), (ug_ref, 1), (uk_ref, 0), (uk_ref, 1)]
        for a in range(4):
            ref, v = basis[a]
            gu_ref[a, at, :] = geometric(ref[v, at, :], live, nuu, nvv, nuv)
            for b in range(a + 1):
                ref, v = basis[b]
                add(("guu", b, a), ref[v, at, :] * gu_ref[a, at, :])
    tile_ref[...] = packed(sums_ref[...])


def strip_of(line_ref, z, at, rows, slots):
    halves = (line_ref.shape[1] - 1) // (16 * slots)
    return jnp.concatenate(
        [line_ref[z, h * 16 * slots + at : h * 16 * slots + at + rows, :] for h in range(halves)], axis=1
    )


def wanted_of(line_ref, z, slot, slots):
    halves = (line_ref.shape[1] - 1) // (16 * slots)
    tag = halves * 16 * slots
    return line_ref[z, tag + slot : tag + slot + 1, :1]


def line_kernel(slots, line_ref, out_ref, sums_ref):
    owners = line_ref.shape[0]
    sums_ref[...] = jnp.zeros_like(sums_ref)
    sums = {pair: None for pair in UU}
    for z in range(owners):
        for s in range(slots):
            wanted = wanted_of(line_ref, z, s, slots)
            jumps, slopes = [], []
            for a in range(4):
                own = strip_of(line_ref, z, 4 * (4 * s + a), 2, slots)
                bottom = jnp.zeros_like(own)
                for near in sorted({(z + 1) % owners, (z - 1) % owners}):
                    for t in range(slots):
                        strip = strip_of(line_ref, near, 4 * (4 * t + a) + 2, 2, slots)
                        bottom = bottom + jnp.where(wanted == float(near * slots + t), strip, 0.0)
                jumps.append(own[1:2] - bottom[0:1])
                slopes.append(own[1:2] - own[0:1] - (bottom[1:2] - bottom[0:1]))
            for a, b in UU:
                term = penalty_value * jumps[a] * jumps[b] + penalty_slope * slopes[a] * slopes[b]
                sums[a, b] = term if sums[a, b] is None else sums[a, b] + term
    for pair in UU:
        k = AT[("kuu",) + pair]
        sums_ref[k : k + 1, :] = sums[pair]
    out_ref[...] = packed(sums_ref[...])


def join_kernel(rows_ref, matched_ref, line_ref, kug_in, kuk_in, kug_ref, kuk_ref):
    kug_ref[...] = kug_in[...]
    kuk_ref[...] = kuk_in[...]
    slots = rows_ref.shape[0]
    rows_dev, ncol = kug_in.shape[1:]
    prows = rows_dev // slots
    owners = line_ref.shape[0]
    mine, match = place(rows_ref, matched_ref, slots)
    me = lax.axis_index("patch")
    for s in range(slots):
        own_id, want_id = mine[s].astype(jnp.float32), match[s].astype(jnp.float32)
        places = edge_places(rows_ref, s, prows)
        for a in range(4):
            own = jnp.zeros((4, ncol), jnp.float32)
            top = jnp.zeros((2, ncol), jnp.float32)
            bottom = jnp.zeros((2, ncol), jnp.float32)
            for z in range(owners):
                for t in range(slots):
                    strip = strip_of(line_ref, z, 4 * (4 * t + a), 4, slots)
                    top = top + jnp.where(wanted_of(line_ref, z, t, slots) == own_id, strip[0:2], 0.0)
                    bottom = bottom + jnp.where(want_id == float(z * slots + t), strip[2:4], 0.0)
                    if t == s:
                        own = own + jnp.where(me == z, strip, 0.0)
            ref = kug_ref if a < 2 else kuk_ref
            for row, added in zip(places, interface_rows(own, top, bottom)):
                ref[a % 2, pl.ds(row, 1), :] += added


def form(table, left, right):
    total = None
    for i, c in left.items():
        row = None
        for j, d in right.items():
            term = d * table[i, j]
            row = term if row is None else row + term
        total = c * row if total is None else total + c * row
    return total


def final_kernel(
    cells, rows_ref, total_ref, vec_ref, ug_ref, uk_ref, prec_ref, kug_ref, kuk_ref, gu_ref, out_ref
):
    slots = rows_ref.shape[0]
    rows_dev, ncol = prec_ref.shape
    prows = rows_dev // slots
    total = total_ref[...]

    def value(*name):
        k = AT[name]
        return total[k % 8 : k % 8 + 1, k // 8 : k // 8 + 1]

    k_table, g_table = {}, {}

    def put(table, i, j, what):
        table[i, j] = what
        table[j, i] = what

    for a in range(2):
        for b in range(2):
            lo, hi = min(a, b), max(a, b)
            put(k_table, a, b, value("kxx", lo, hi))
            put(g_table, a, b, value("gxx", lo, hi))
            put(k_table, a, 2 + b, value("kpg", a, b))
            put(k_table, a, 4 + b, value("kpk", lo, hi))
            put(g_table, a, 2 + b, value("gpg", lo, hi))
            put(g_table, a, 4 + b, value("kpg", b, a))
    for a, b in UU:
        put(k_table, 2 + a, 2 + b, value("kuu", a, b))
        put(g_table, 2 + a, 2 + b, value("guu", a, b))

    first_a, cross_k, second_a = k_table[0, 0], k_table[0, 1], k_table[1, 1]
    first_g, cross_g, second_g = g_table[0, 0], g_table[0, 1], g_table[1, 1]
    ratio = cross_k / first_a
    other_a = second_a - ratio * cross_k
    other_q = second_g - 2.0 * ratio * cross_g + ratio * ratio * first_g
    mu_first = first_g / first_a
    mu_other = other_q / other_a
    scale_first = jnp.sqrt(norm_scale * cells / first_a)
    scale_other = jnp.sqrt(norm_scale * cells / other_a)
    new_first = {0: scale_first, 2: scale_first, 4: -scale_first * mu_first}
    new_second = {
        0: -scale_other * ratio,
        1: scale_other,
        2: -scale_other * ratio,
        3: scale_other,
        4: scale_other * mu_other * ratio,
        5: -scale_other * mu_other,
    }
    a1 = form(k_table, new_first, new_first)
    c = form(k_table, new_first, new_second)
    a2 = form(k_table, new_second, new_second)
    g1 = form(g_table, new_first, new_first)
    h = form(g_table, new_first, new_second)
    g2 = form(g_table, new_second, new_second)
    r = c / a1
    b2 = a2 - r * c
    q2 = g2 - 2.0 * r * h + r * r * g1
    mus = [g1 / a1, q2 / b2]
    scales = [jnp.sqrt(norm_scale * cells / a1), jnp.sqrt(norm_scale * cells / b2)]
    lead = [
        {i: scales[0] * f for i, f in new_first.items()},
        {i: scales[1] * (f - r * new_first[i] if i in new_first else f) for i, f in new_second.items()},
    ]
    for s in range(slots):
        at = slice(s * prows, (s + 1) * prows)
        live = live_of(rows_ref, s, (prows, ncol))
        basis = [jnp.where(live, vec_ref[v, at, :], 0.0) for v in range(2)]
        basis += [ug_ref[v, at, :] for v in range(2)] + [uk_ref[v, at, :] for v in range(2)]
        for v in range(2):
            coef = dict(lead[v])
            for i in (0, 1):
                if i in lead[v]:
                    coef[2 + i] = coef[2 + i] + lead[v][i]
                    coef[4 + i] = coef[4 + i] - mus[v] * lead[v][i]
            acc = inside = None
            for i, f in coef.items():
                term = f * basis[i]
                acc = term if acc is None else acc + term
            for i in range(2, 6):
                if i in lead[v]:
                    k_part = kug_ref[i - 2, at, :] if i < 4 else kuk_ref[i - 4, at, :]
                    term = lead[v][i] * gu_ref[i - 2, at, :] - (lead[v][i] * mus[v]) * k_part
                    inside = term if inside is None else inside + term
            out_ref[v, at, :] = acc + prec_ref[at, :] * inside


def call(body, outs, kinds, scratch=(), flops=1_000_000, out_kind="v"):
    spaces = {"s": pltpu.SMEM, "v": pltpu.VMEM, "h": pltpu.HBM}
    return pl.pallas_call(
        body,
        out_shape=[jax.ShapeDtypeStruct(s, d) for s, d in outs],
        in_specs=[pl.BlockSpec(memory_space=spaces[k]) for k in kinds],
        out_specs=[pl.BlockSpec(memory_space=spaces[out_kind]) for _ in outs],
        scratch_shapes=list(scratch),
        compiler_params=pltpu.CompilerParams(vmem_limit_bytes=32 * 1024 * 1024),
        cost_estimate=pl.CostEstimate(flops=flops, bytes_accessed=2_000_000, transcendentals=0),
    )


def per_device(vectors, prestress, thickness, foundation, patch_rows, matched, elem_row):
    owners = lax.axis_size("patch")
    inner = lax.axis_size(("sub", "half"))
    slots = patch_rows.shape[0]
    rows_dev, ncol = thickness.shape
    f32, bf16 = jnp.float32, jnp.bfloat16
    cells = float(owners * inner * rows_dev * ncol)
    field = ((2, rows_dev, ncol), f32)
    one = ((rows_dev, ncol), f32)
    sums = ((SUMS, ncol), f32)
    tile = ((8, LANES), f32)

    width = 3 * ncol + LANES
    (payload,) = call(
        pack_kernel,
        [((rows_dev, width), bf16)],
        "hh",
        [
            pltpu.VMEM((1, rows_dev), jnp.int32),
            pltpu.VMEM((rows_dev, LANES), bf16),
            pltpu.SemaphoreType.DMA((5,)),
        ],
        out_kind="h",
    )(jnp.transpose(prestress, (1, 0, 2)), elem_row.reshape(1, rows_dev))
    arrived = lax.all_to_all(
        payload, ("patch", "sub", "half"), split_axis=0, concat_axis=0, tiled=True
    )
    edge_rows = -(-10 * slots // 8) * 8
    (edges,) = call(edge_kernel, [((edge_rows, ncol), f32)], "ssv")(patch_rows, matched, vectors)
    below = passed_along(edges, "patch", 1)
    above = passed_along(edges, "patch", -1)
    k_x, u_k, prec, part = call(stiff_kernel, [field, field, one, sums], "svvv")(
        patch_rows, vectors, thickness, foundation
    )
    sent_rows = (ncol // LANES) * 16 * slots + -(-slots // 8) * 8
    g_x, u_g, stress, extra, sent = call(
        bend_kernel,
        [field, field, ((3, rows_dev, ncol), f32), ((8 * slots, ncol), f32), ((sent_rows, LANES), f32)],
        "ssvvvvvvv",
    )(patch_rows, matched, arrived, vectors, prec, u_k, edges, below, above)
    line = lax.all_to_all(
        jnp.broadcast_to(sent[None], (owners, sent_rows, LANES)), "patch", split_axis=0, concat_axis=0, tiled=True
    )
    u_k, k_uk, k_ug, g_u, local = call(
        gram_kernel,
        [field, field, field, ((4, rows_dev, ncol), f32), tile],
        "svvvvvvvvvvv",
        [pltpu.VMEM((SUMS, ncol), f32), pltpu.VMEM((2, rows_dev, ncol), f32)],
    )(patch_rows, extra, vectors, thickness, foundation, prec, k_x, u_k, part, g_x, u_g, stress)
    local = summed_over(local, "patch")
    (across,) = call(
        functools.partial(line_kernel, slots), [tile], "v", [pltpu.VMEM((SUMS, ncol), f32)]
    )(line)
    total = summed_over(summed_over(local + across, "half"), "sub")
    k_ug, k_uk = call(join_kernel, [field, field], "ssvvv")(
        patch_rows, matched, line, k_ug, k_uk
    )
    (modes,) = call(functools.partial(final_kernel, cells), [field], "svvvvvvvv")(
        patch_rows, total, vectors, u_g, u_k, prec, k_ug, k_uk, g_u
    )
    return modes


def solution(mesh):
    in_specs = (
        P(None, ("groups", "patch", "sub", "half"), None),
        P(("groups", "patch", "sub", "half"), None, None),
        P(("groups", "patch", "sub", "half"), None),
        P(("groups", "patch", "sub", "half"), None),
        P(("groups", "patch", "sub", "half")),
        P(("groups", "patch", "sub", "half")),
        P(("groups", "patch", "sub", "half")),
    )
    out_specs = P(None, ("groups", "patch", "sub", "half"), None)
    return jax.shard_map(
        per_device, mesh=mesh, in_specs=in_specs, out_specs=out_specs, check_vma=False
    )
```

time: 51.8 us -> 57.8 us (1.12)
  blocking collectives: 10.1 us -> 0 us
  starting transfers between devices: 12.8 us -> 21.7 us
  local copies, waits for them, and re-layouts: 4.04 us -> 12.7 us
  Pallas kernels: 13.9 us -> 12 us
    all_to_all x1 -> x0, blocking collectives: 10.1 us -> none  [per_device(): lax.all_to_all(jnp.broadcast_to(sent[None], (owners, sent_rows, ncol)), '...]
    unnamed x16 -> x38, local copies, waits for them, and re-layouts: 4.03 us -> 12.1 us
    ppermute x4 -> x7, starting transfers between devices: 5.34 us -> 10.6 us  [passed_along(): lax.ppermute(array, axis, [(i, (i + by) % peers) for i in range(peers)])]
    all_to_all x0 -> x1, starting transfers between devices: none -> 3.66 us  [per_device(): lax.all_to_all(jnp.broadcast_to(sent[None], (owners, sent_rows, LANES)),...]
    pallas_call x6 -> x8, Pallas kernels: 13.9 us -> 12 us  [the longest x1 4.44 us: per_device(): call(gram_kernel, [field, field, field, ((4, rows_dev, ncol), f32), tile]...]
    broadcast_in_dim x1, local copies, waits for them, and re-layouts: 0.01 us -> 0.67 us  [per_device(): jnp.broadcast_to(sent[None], (owners, sent_rows, LANES))]
    ppermute x4 -> x7, waiting for transfers between devices: 10.4 us -> 9.99 us  [passed_along(): lax.ppermute(array, axis, [(i, (i + by) % peers) for i in range(peers)])]
  transfers between devices with their start and end apart: 5 -> 9, of which waited for: 2 -> 5; matrix products, arithmetic and copies ran while one was open for 0% -> 0% of each run, Pallas kernels for 10% -> 14%
where the time goes in v2:
time: 57.8 us; the launch traced here: 57.2 us
  starting transfers between devices  21.7 us (38%)
  local copies, waits for them, and re-layouts  12.7 us (22%)
  Pallas kernels  12 us (21%)
  waiting for transfers between devices  10.6 us (18%)
    unnamed x38, local copies, waits for them, and re-layouts  12.1 us
    ppermute x7, starting transfers between devices, passed_along(): lax.ppermute(array, axis, [(i, (i + by) % peers) for i in range(peers)])  10.6 us
    ppermute x7, waiting for transfers between devices, passed_along(): lax.ppermute(array, axis, [(i, (i + by) % peers) for i in range(peers)])  9.99 us
    all_to_all x1, starting transfers between devices, per_device(): lax.all_to_all(payload, ('patch', 'sub', 'half'), split_axis=0, concat_ax...  7.5 us
    pallas_call x1, Pallas kernels, per_device(): call(gram_kernel, [field, field, field, ((4, rows_dev, ncol), f32), tile]...  4.44 us
    all_to_all x1, starting transfers between devices, per_device(): lax.all_to_all(jnp.broadcast_to(sent[None], (owners, sent_rows, LANES)),...  3.66 us
    pallas_call x1, Pallas kernels, per_device(): call(functools.partial(final_kernel, cells), [field], 'svvvvvvvv')  2.2 us
    pallas_call x1, Pallas kernels, per_device(): call(stiff_kernel, [field, field, one, sums], 'svvv')  1.6 us
  transfers between devices with their start and end apart: 9, of which 5 were waited for; matrix products, arithmetic and copies ran while one was open for 0% of the time, Pallas kernels for 14%

profile of v2, /device:TPU:0, one launch (start us, length us, event | category | flops | bytes accessed | tf_op | source)
XLA Modules:
  0.0 57.2 jit_solution(4968916435794753675)
XLA Ops:
  0.7 1.0 %copy-done.15 = bf16[256,3,256]{2,0,1:T(8,128)(2,1)S(1)} copy-done((bf16[256,3,256]{2,0,1:T(8,128)(2,1)S(1)}, bf16[256,3,256]{2,0,1:T(8,128)(2,1)}, u32[]{:S(2)}) %copy-start.15) | copy-done | bytes 393240
  1.7 0.8 %shard_map.73 = bf16[256,896]{1,0:T(8,128)(2,1)} custom-call(bf16[3,256,256]{2,1,0:T(8,128)(2,1)S(1)} %bitcast.5, s32[1,256]{1,0:T(1,128)S(1)} %bitcast.6), custom_call_target="tpu_custom_call" | custom-call | flops 1000000 | bytes 2000000 | tf_op jit(solution)/shard_map/pallas_call | solution.py:519
  2.5 7.5 %all-to-all-start = ((bf16[16,16,896]{2,1,0:T(8,128)(2,1)}), bf16[16,16,896]{2,1,0:T(8,128)(2,1)S(1)}, u32[]{:S(2)}, u32[]{:S(2)}) async-start(bf16[16,16,896]{2,1,0:T(8,128)(2,1)} %bitcast.2), calls=%async_computation | async-start | bytes 917504 | tf_op jit(solution)/shard_map/all_to_all | solution.py:530
  10.7 2.0 %collective-permute-start = (f32[24,256]{1,0:T(8,128)S(1)}, f32[24,256]{1,0:T(8,128)S(1)}, u32[]{:S(2)}, u32[]{:S(2)}) collective-permute-start(f32[24,256]{1,0:T(8,128)S(1)} %shard_map.75.edge_ref), channel_id=1, source_target_pairs={{0,4},{4,8},{8,12},{12,0},{1,5},{5,9},{9,13},{13,1},{2,6},{6,10},{... | collective-permute-start | bytes 73736 | tf_op jit(solution)/shard_map/ppermute | solution.py:32
  12.6 1.9 %collective-permute-start.1 = (f32[24,256]{1,0:T(8,128)S(1)}, f32[24,256]{1,0:T(8,128)S(1)}, u32[]{:S(2)}, u32[]{:S(2)}) collective-permute-start(f32[24,256]{1,0:T(8,128)S(1)} %shard_map.75.edge_ref), channel_id=1, source_target_pairs={{0,12},{4,0},{8,4},{12,8},{1,13},{5,1},{9,5},{13,9},{2,14},{6,2},{... | collective-permute-start | bytes 73736 | tf_op jit(solution)/shard_map/ppermute | solution.py:32
  14.6 1.6 %shard_map.74 = (f32[2,256,256]{2,1,0:T(8,128)S(1)}, f32[2,256,256]{2,1,0:T(8,128)S(1)}, f32[256,256]{1,0:T(8,128)S(1)}, f32[40,256]{1,0:T(8,128)S(1)}) custom-call(s32[2]{0:T(128)S(1)} %copy-done.16, f32[2,256,256]{2,1,0:T(8,128)S(1)} %copy-done, f32[256,256]{1,0:T(8,128)S(1)} %copy-done.1, f32[256,256]{1,0:T(8,128)S(1)} %copy-done.2), custom_call_target="tpu_custom_call" | custom-call | flops 1000000 | bytes 2000000 | tf_op jit(solution)/shard_map/pallas_call | solution.py:537
  16.2 7.0 %collective-permute-done.below_ref = f32[24,256]{1,0:T(8,128)S(1)} collective-permute-done((f32[24,256]{1,0:T(8,128)S(1)}, f32[24,256]{1,0:T(8,128)S(1)}, u32[]{:S(2)}, u32[]{:S(2)}) %collective-permute-start) | collective-permute-done | bytes 24608 | tf_op jit(solution)/shard_map/ppermute | solution.py:32
  23.8 1.3 %shard_map.76 = (f32[2,256,256]{2,1,0:T(8,128)S(1)}, f32[2,256,256]{2,1,0:T(8,128)S(1)}, f32[3,256,256]{2,1,0:T(8,128)S(1)}, f32[16,256]{1,0:T(8,128)S(1)}, f32[72,128]{1,0:T(8,128)S(1)}) custom-call(s32[2]{0:T(128)S(1)} %copy-done.16, s32[2]{0:T(128)S(1)} %copy-done.17, bf16[256,896]{1,0:T(8,128)(2,1)S(1)} %bitcast.4, f32[2,256,256]{2,1,0:T(8,128)S(1)} %copy-done, ...), custom_call_target="tpu_custom_call" | custom-call | flops 1000000 | bytes 2000000 | tf_op jit(solution)/shard_map/pallas_call | solution.py:541
  25.0 0.9 %copy-done.5 = f32[3,256,256]{2,1,0:T(8,128)} copy-done((f32[3,256,256]{2,1,0:T(8,128)}, f32[3,256,256]{2,1,0:T(8,128)S(1)}, u32[]{:S(2)}) %copy-start.5) | copy-done | bytes 786456
  27.4 3.7 %all-to-all-start.1 = ((f32[4,72,128]{2,1,0:T(8,128)}), f32[4,72,128]{2,1,0:T(8,128)S(1)}, u32[]{:S(2)}, u32[]{:S(2)}) async-start(f32[4,72,128]{2,1,0:T(8,128)} %broadcast_in_dim.2), calls=%async_computation.1 | async-start | bytes 294912 | tf_op jit(solution)/shard_map/all_to_all | solution.py:546
  31.0 1.1 %copy-done.6 = f32[3,256,256]{2,1,0:T(8,128)S(1)} copy-done((f32[3,256,256]{2,1,0:T(8,128)S(1)}, f32[3,256,256]{2,1,0:T(8,128)}, u32[]{:S(2)}) %copy-start.6) | copy-done | bytes 786456
  32.2 1.0 %copy-done.8 = f32[2,256,256]{2,1,0:T(8,128)S(1)} copy-done((f32[2,256,256]{2,1,0:T(8,128)S(1)}, f32[2,256,256]{2,1,0:T(8,128)}, u32[]{:S(2)}) %copy-start.8) | copy-done | bytes 524312
  33.2 4.4 %shard_map.77 = (f32[2,256,256]{2,1,0:T(8,128)S(1)}, f32[2,256,256]{2,1,0:T(8,128)S(1)}, f32[2,256,256]{2,1,0:T(8,128)S(1)}, f32[4,256,256]{2,1,0:T(8,128)S(1)}, f32[8,128]{1,0:T(8,128)S(1)}) custom-call(s32[2]{0:T(128)S(1)} %copy-done.16, f32[16,256]{1,0:T(8,128)S(1)} %get-tuple-element.23.extra_ref, f32[2,256,256]{2,1,0:T(8,128)S(1)} %copy-done, ...), custom_call_target="tpu_custom_call" | custom-call | flops 1000000 | bytes 2000000 | tf_op jit(solution)/shard_map/pallas_call | solution.py:549
  37.7 1.0 %copy-done.3 = f32[4,256,256]{2,1,0:T(8,128)} copy-done((f32[4,256,256]{2,1,0:T(8,128)}, f32[4,256,256]{2,1,0:T(8,128)S(1)}, u32[]{:S(2)}) %copy-start.3) | copy-done | bytes 1048600
  41.0 2.0 %collective-permute-start.2 = (f32[8,128]{1,0:T(8,128)S(1)}, f32[8,128]{1,0:T(8,128)S(1)}, u32[]{:S(2)}, u32[]{:S(2)}) collective-permute-start(f32[8,128]{1,0:T(8,128)S(1)} %get-tuple-element.29), channel_id=1, source_target_pairs={{0,4},{4,8},{8,12},{12,0},{1,5},{5,9},{9,13},{13,1},{2,6},{6,10},{... | collective-permute-start | bytes 12296 | tf_op jit(solution)/shard_map/ppermute | solution.py:32
  43.0 2.4 %collective-permute-start.3 = (f32[8,128]{1,0:T(8,128)S(1)}, f32[8,128]{1,0:T(8,128)S(1)}, u32[]{:S(2)}, u32[]{:S(2)}) collective-permute-start(f32[8,128]{1,0:T(8,128)S(1)} %get-tuple-element.29), channel_id=1, source_target_pairs={{0,8},{4,12},{8,0},{12,4},{1,9},{5,13},{9,1},{13,5},{2,10},{6,14},... | collective-permute-start | bytes 12296 | tf_op jit(solution)/shard_map/ppermute | solution.py:32
  45.4 1.5 %collective-permute-start.4 = (f32[8,128]{1,0:T(8,128)S(1)}, f32[8,128]{1,0:T(8,128)S(1)}, u32[]{:S(2)}, u32[]{:S(2)}) collective-permute-start(f32[8,128]{1,0:T(8,128)S(1)} %get-tuple-element.29), channel_id=1, source_target_pairs={{0,12},{4,0},{8,4},{12,8},{1,13},{5,1},{9,5},{13,9},{2,14},{6,2},{... | collective-permute-start | bytes 12296 | tf_op jit(solution)/shard_map/ppermute | solution.py:32
  47.5 1.5 %collective-permute-done.4 = f32[8,128]{1,0:T(8,128)S(1)} collective-permute-done((f32[8,128]{1,0:T(8,128)S(1)}, f32[8,128]{1,0:T(8,128)S(1)}, u32[]{:S(2)}, u32[]{:S(2)}) %collective-permute-start.4) | collective-permute-done | bytes 4128 | tf_op jit(solution)/shard_map/ppermute | solution.py:32
  49.0 1.2 %collective-permute-done.5 = f32[8,128]{1,0:T(8,128)S(1)} collective-permute-done((f32[8,128]{1,0:T(8,128)S(1)}, f32[8,128]{1,0:T(8,128)S(1)}, u32[]{:S(2)}, u32[]{:S(2)}) %collective-permute-start.5) | collective-permute-done | bytes 4128 | tf_op jit(solution)/shard_map/ppermute | solution.py:32
  50.2 0.8 %collective-permute-start.6 = (f32[8,128]{1,0:T(8,128)S(1)}, f32[8,128]{1,0:T(8,128)S(1)}, u32[]{:S(2)}, u32[]{:S(2)}) collective-permute-start(f32[8,128]{1,0:T(8,128)S(1)} %add.22), channel_id=1, source_target_pairs={{0,2},{2,0},{1,3},{3,1},{4,6},{6,4},{5,7},{7,5},{8,10},{10,8},{9,1... | collective-permute-start | bytes 12296 | tf_op jit(solution)/shard_map/ppermute | solution.py:32
  51.0 1.0 %copy-done.10 = f32[2,256,256]{2,1,0:T(8,128)S(1)} copy-done((f32[2,256,256]{2,1,0:T(8,128)S(1)}, f32[2,256,256]{2,1,0:T(8,128)}, u32[]{:S(2)}) %copy-start.10) | copy-done | bytes 524312
  52.1 1.0 %copy-done.12 = f32[2,256,256]{2,1,0:T(8,128)S(1)} copy-done((f32[2,256,256]{2,1,0:T(8,128)S(1)}, f32[2,256,256]{2,1,0:T(8,128)}, u32[]{:S(2)}) %copy-start.12) | copy-done | bytes 524312
  53.9 1.0 %copy-done.14 = f32[2,256,256]{2,1,0:T(8,128)S(1)} copy-done((f32[2,256,256]{2,1,0:T(8,128)S(1)}, f32[2,256,256]{2,1,0:T(8,128)}, u32[]{:S(2)}) %copy-start.14) | copy-done | bytes 524312
  55.0 2.2 %shard_map.80 = f32[2,256,256]{2,1,0:T(8,128)} custom-call(s32[2]{0:T(128)S(1)} %copy-done.16, f32[8,128]{1,0:T(8,128)S(1)} %add.23.total_ref, f32[2,256,256]{2,1,0:T(8,128)S(1)} %copy-done, f32[2,256,256]{2,1,0:T(8,128)S(1)} %get-tuple-element.27.ug_ref, f32[2,256,256]{2,1,0:T(8,128)S(1)} %copy-done.14, f32[256,256]{1,0:T(8,128)S(1)} %get-tuple-element.21.prec_ref, ...), custom_call_target="tpu_custom_call" | custom-call | flops 1000000 | bytes 2000000 | tf_op jit(solution)/shard_map/pallas_call | solution.py:563
  (44 shorter events, 7.2 us)
Async XLA Ops:
  0.7 1.0 %copy-start.15 = (bf16[256,3,256]{2,0,1:T(8,128)(2,1)S(1)}, bf16[256,3,256]{2,0,1:T(8,128)(2,1)}, u32[]{:S(2)}) copy-start(bf16[256,3,256]{2,0,1:T(8,128)(2,1)} %param.8) | copy-start | bytes 1179652
  2.5 7.5 %copy-start = (f32[2,256,256]{2,1,0:T(8,128)S(1)}, f32[2,256,256]{2,1,0:T(8,128)}, u32[]{:S(2)}) copy-start(f32[2,256,256]{2,1,0:T(8,128)} %vec_ref.9) | copy-start | bytes 1572868
  2.5 7.5 %copy-start.16 = (s32[2]{0:T(128)S(1)}, s32[2]{0:T(128)}, u32[]{:S(2)}) copy-start(s32[2]{0:T(128)} %rows_ref.11) | copy-start | bytes 28
  2.5 7.5 %copy-start.17 = (s32[2]{0:T(128)S(1)}, s32[2]{0:T(128)}, u32[]{:S(2)}) copy-start(s32[2]{0:T(128)} %matched_ref.5) | copy-start | bytes 28
  2.5 21.2 %all-to-all-start = ((bf16[16,16,896]{2,1,0:T(8,128)(2,1)}), bf16[16,16,896]{2,1,0:T(8,128)(2,1)S(1)}, u32[]{:S(2)}, u32[]{:S(2)}) async-start(bf16[16,16,896]{2,1,0:T(8,128)(2,1)} %bitcast.2), calls=%async_computation | async-start | bytes 917504 | tf_op jit(solution)/shard_map/all_to_all | solution.py:530
  10.1 4.5 %copy-start.1 = (f32[256,256]{1,0:T(8,128)S(1)}, f32[256,256]{1,0:T(8,128)}, u32[]{:S(2)}) copy-start(f32[256,256]{1,0:T(8,128)} %thick_ref.3) | copy-start | bytes 786436
  10.1 4.5 %copy-start.2 = (f32[256,256]{1,0:T(8,128)S(1)}, f32[256,256]{1,0:T(8,128)}, u32[]{:S(2)}) copy-start(f32[256,256]{1,0:T(8,128)} %support_ref.3) | copy-start | bytes 786436
  10.7 12.5 %collective-permute-start = (f32[24,256]{1,0:T(8,128)S(1)}, f32[24,256]{1,0:T(8,128)S(1)}, u32[]{:S(2)}, u32[]{:S(2)}) collective-permute-start(f32[24,256]{1,0:T(8,128)S(1)} %shard_map.75.edge_ref), channel_id=1, source_target_pairs={{0,4},{4,8},{8,12},{12,0},{1,5},{5,9},{9,13},{13,1},{2,6},{6,10},{... | collective-permute-start | bytes 73736 | tf_op jit(solution)/shard_map/ppermute | solution.py:32
  12.6 10.5 %collective-permute-start.1 = (f32[24,256]{1,0:T(8,128)S(1)}, f32[24,256]{1,0:T(8,128)S(1)}, u32[]{:S(2)}, u32[]{:S(2)}) collective-permute-start(f32[24,256]{1,0:T(8,128)S(1)} %shard_map.75.edge_ref), channel_id=1, source_target_pairs={{0,12},{4,0},{8,4},{12,8},{1,13},{5,1},{9,5},{13,9},{2,14},{6,2},{... | collective-permute-start | bytes 73736 | tf_op jit(solution)/shard_map/ppermute | solution.py:32
  25.0 0.9 %copy-start.5 = (f32[3,256,256]{2,1,0:T(8,128)}, f32[3,256,256]{2,1,0:T(8,128)S(1)}, u32[]{:S(2)}) copy-start(f32[3,256,256]{2,1,0:T(8,128)S(1)} %get-tuple-element.28.stress_ref) | copy-start | bytes 2359300
  27.4 19.5 %all-to-all-start.1 = ((f32[4,72,128]{2,1,0:T(8,128)}), f32[4,72,128]{2,1,0:T(8,128)S(1)}, u32[]{:S(2)}, u32[]{:S(2)}) async-start(f32[4,72,128]{2,1,0:T(8,128)} %broadcast_in_dim.2), calls=%async_computation.1 | async-start | bytes 294912 | tf_op jit(solution)/shard_map/all_to_all | solution.py:546
  31.0 1.1 %copy-start.6 = (f32[3,256,256]{2,1,0:T(8,128)S(1)}, f32[3,256,256]{2,1,0:T(8,128)}, u32[]{:S(2)}) copy-start(f32[3,256,256]{2,1,0:T(8,128)} %copy-done.5) | copy-start | bytes 2359300
  32.2 1.0 %copy-start.8 = (f32[2,256,256]{2,1,0:T(8,128)S(1)}, f32[2,256,256]{2,1,0:T(8,128)}, u32[]{:S(2)}) copy-start(f32[2,256,256]{2,1,0:T(8,128)} %copy-done.7) | copy-start | bytes 1572868
  37.7 1.0 %copy-start.3 = (f32[4,256,256]{2,1,0:T(8,128)}, f32[4,256,256]{2,1,0:T(8,128)S(1)}, u32[]{:S(2)}) copy-start(f32[4,256,256]{2,1,0:T(8,128)S(1)} %get-tuple-element.36.gu_ref) | copy-start | bytes 3145732
  39.4 0.8 %copy-start.11 = (f32[2,256,256]{2,1,0:T(8,128)}, f32[2,256,256]{2,1,0:T(8,128)S(1)}, u32[]{:S(2)}) copy-start(f32[2,256,256]{2,1,0:T(8,128)S(1)} %get-tuple-element.32.kug_in) | copy-start | bytes 1572868
  41.0 12.9 %copy-start.4 = (f32[4,256,256]{2,1,0:T(8,128)S(1)}, f32[4,256,256]{2,1,0:T(8,128)}, u32[]{:S(2)}) copy-start(f32[4,256,256]{2,1,0:T(8,128)} %copy-done.3) | copy-start | bytes 3145732
  41.0 6.2 %collective-permute-start.2 = (f32[8,128]{1,0:T(8,128)S(1)}, f32[8,128]{1,0:T(8,128)S(1)}, u32[]{:S(2)}, u32[]{:S(2)}) collective-permute-start(f32[8,128]{1,0:T(8,128)S(1)} %get-tuple-element.29), channel_id=1, source_target_pairs={{0,4},{4,8},{8,12},{12,0},{1,5},{5,9},{9,13},{13,1},{2,6},{6,10},{... | collective-permute-start | bytes 12296 | tf_op jit(solution)/shard_map/ppermute | solution.py:32
  43.0 4.5 %collective-permute-start.3 = (f32[8,128]{1,0:T(8,128)S(1)}, f32[8,128]{1,0:T(8,128)S(1)}, u32[]{:S(2)}, u32[]{:S(2)}) collective-permute-start(f32[8,128]{1,0:T(8,128)S(1)} %get-tuple-element.29), channel_id=1, source_target_pairs={{0,8},{4,12},{8,0},{12,4},{1,9},{5,13},{9,1},{13,5},{2,10},{6,14},... | collective-permute-start | bytes 12296 | tf_op jit(solution)/shard_map/ppermute | solution.py:32
  45.4 3.6 %collective-permute-start.4 = (f32[8,128]{1,0:T(8,128)S(1)}, f32[8,128]{1,0:T(8,128)S(1)}, u32[]{:S(2)}, u32[]{:S(2)}) collective-permute-start(f32[8,128]{1,0:T(8,128)S(1)} %get-tuple-element.29), channel_id=1, source_target_pairs={{0,12},{4,0},{8,4},{12,8},{1,13},{5,1},{9,5},{13,9},{2,14},{6,2},{... | collective-permute-start | bytes 12296 | tf_op jit(solution)/shard_map/ppermute | solution.py:32
  49.0 1.2 %collective-permute-start.5 = (f32[8,128]{1,0:T(8,128)S(1)}, f32[8,128]{1,0:T(8,128)S(1)}, u32[]{:S(2)}, u32[]{:S(2)}) collective-permute-start(f32[8,128]{1,0:T(8,128)S(1)} %add_add_fusion), channel_id=1, source_target_pairs={{0,1},{1,0},{2,3},{3,2},{4,5},{5,4},{6,7},{7,6},{8,9},{9,8},{10,11... | collective-permute-start | bytes 12296 | tf_op jit(solution)/shard_map/ppermute | solution.py:32
  50.2 3.7 %collective-permute-start.6 = (f32[8,128]{1,0:T(8,128)S(1)}, f32[8,128]{1,0:T(8,128)S(1)}, u32[]{:S(2)}, u32[]{:S(2)}) collective-permute-start(f32[8,128]{1,0:T(8,128)S(1)} %add.22), channel_id=1, source_target_pairs={{0,2},{2,0},{1,3},{3,1},{4,6},{6,4},{5,7},{7,5},{8,10},{10,8},{9,1... | collective-permute-start | bytes 12296 | tf_op jit(solution)/shard_map/ppermute | solution.py:32
  51.0 1.0 %copy-start.10 = (f32[2,256,256]{2,1,0:T(8,128)S(1)}, f32[2,256,256]{2,1,0:T(8,128)}, u32[]{:S(2)}) copy-start(f32[2,256,256]{2,1,0:T(8,128)} %copy-done.9) | copy-start | bytes 1572868
  52.1 1.0 %copy-start.12 = (f32[2,256,256]{2,1,0:T(8,128)S(1)}, f32[2,256,256]{2,1,0:T(8,128)}, u32[]{:S(2)}) copy-start(f32[2,256,256]{2,1,0:T(8,128)} %copy-done.11) | copy-start | bytes 1572868
  53.9 1.0 %copy-start.14 = (f32[2,256,256]{2,1,0:T(8,128)S(1)}, f32[2,256,256]{2,1,0:T(8,128)}, u32[]{:S(2)}) copy-start(f32[2,256,256]{2,1,0:T(8,128)} %copy-done.13) | copy-start | bytes 1572868
  (4 other events, 3.1 us)

commit v3 on v2

--- a/solution.py
+++ b/solution.py
@@ -91,12 +91,14 @@
     return jnp.sum(product, axis=0, keepdims=True)
 
 
-def packed(sums):
-    totals = jnp.sum(sums, axis=1, keepdims=True)
+def packed(rows):
+    rows = list(rows)
+    rows += [jnp.zeros_like(rows[0])] * (-len(rows) % 8)
     lane = iota((8, LANES), 1)
     out = jnp.zeros((8, LANES), jnp.float32)
-    for tile in range(TILES):
-        out = jnp.where(lane == tile, totals[8 * tile : 8 * tile + 8], out)
+    for tile in range(len(rows) // 8):
+        total = jnp.sum(jnp.concatenate(rows[8 * tile : 8 * tile + 8], axis=0), axis=1, keepdims=True)
+        out = jnp.where(lane == tile, total, out)
     return out
 
 
@@ -113,14 +115,12 @@
     return jnp.full((1, ncol), number, jnp.int32).astype(jnp.float32)
 
 
-def pack_kernel(stress_ref, elem_ref, pay_ref, elem, index, sems):
+def pack_kernel(stress_ref, elem_ref, pay_ref, elem, held, sems):
     rows_dev, ncol = stress_ref.shape[1:]
     get = pltpu.make_async_copy(elem_ref, elem, sems.at[0])
     get.start()
     planes = [
-        pltpu.make_async_copy(
-            stress_ref.at[j], pay_ref.at[:, pl.ds(j * ncol, ncol)], sems.at[1 + j]
-        )
+        pltpu.make_async_copy(stress_ref.at[j], held.at[:, pl.ds(j * ncol, ncol)], sems.at[1 + j])
         for j in range(3)
     ]
     for copy in planes:
@@ -135,11 +135,11 @@
     column = jnp.sum(
         jnp.where(iota(square, 0) == iota(square, 1), spread, 0.0), axis=1, keepdims=True
     )
-    index[...] = jnp.broadcast_to(column, (rows_dev, LANES)).astype(jnp.bfloat16)
-    put = pltpu.make_async_copy(index, pay_ref.at[:, pl.ds(3 * ncol, LANES)], sems.at[4])
-    put.start()
+    held[:, 3 * ncol :] = jnp.broadcast_to(column, (rows_dev, LANES)).astype(jnp.bfloat16)
     for copy in planes:
         copy.wait()
+    put = pltpu.make_async_copy(held, pay_ref, sems.at[4])
+    put.start()
     put.wait()
 
 
@@ -162,15 +162,19 @@
     edge_ref[used:, :] = jnp.zeros((edge_ref.shape[0] - used, ncol), jnp.float32)
 
 
-def stiff_kernel(rows_ref, vec_ref, thick_ref, support_ref, k_ref, uk_ref, prec_ref, sums_ref):
+def folded(product):
+    return jnp.sum(product.reshape(product.shape[0] // 8, 8, product.shape[1]), axis=0)
+
+
+def stiff_kernel(rows_ref, vec_ref, thick_ref, support_ref, k_ref, uk_ref, kuk_ref, prec_ref, sums_ref):
     slots = rows_ref.shape[0]
     rows_dev, ncol = thick_ref.shape
     prows = rows_dev // slots
     sums_ref[...] = jnp.zeros_like(sums_ref)
 
     def add(name, product):
-        k = AT[name]
-        sums_ref[k : k + 1, :] += column_sums(product)
+        k = 8 * AT[name]
+        sums_ref[k : k + 8, :] += folded(product)
 
     for s in range(slots):
         at = slice(s * prows, (s + 1) * prows)
@@ -181,11 +185,14 @@
             w = jnp.where(live, vec_ref[v, at, :], 0.0)
             k_ref[v, at, :] = stiffness(w, live, thick, support)
             uk_ref[v, at, :] = prec_ref[at, :] * k_ref[v, at, :]
+        for v in range(2):
+            kuk_ref[v, at, :] = stiffness(uk_ref[v, at, :], live, thick, support)
         for a in range(2):
             wa = jnp.where(live, vec_ref[a, at, :], 0.0)
             for b in range(a, 2):
                 add(("kxx", a, b), wa * k_ref[b, at, :])
                 add(("kpk", a, b), k_ref[a, at, :] * uk_ref[b, at, :])
+                add(("kuu", 2 + a, 2 + b), uk_ref[a, at, :] * kuk_ref[b, at, :])
 
 
 def interface_rows(own, top, bottom):
@@ -206,9 +213,9 @@
     return (last - 1, last, slot * prows, slot * prows + 1)
 
 
-def bend_kernel(
-    rows_ref, matched_ref, arrived_ref, vec_ref, prec_ref, uk_ref, edge_ref, below_ref, above_ref,
-    g_ref, ug_ref, stress_ref, extra_ref, out_ref,
+def gram_kernel(
+    rows_ref, matched_ref, arrived_ref, vec_ref, thick_ref, support_ref, prec_ref, k_in, uk_in, kuk_in, sums_in,
+    edge_ref, below_ref, above_ref, ug_ref, uk_ref, kuk_ref, stress_ref, out_ref, sums_ref, g_ref, k_ref,
 ):
     slots = rows_ref.shape[0]
     rows_dev, ncol = prec_ref.shape
@@ -229,22 +236,28 @@
     )
     for j in range(3):
         stress_ref[j] = placed[:, j * ncol : (j + 1) * ncol]
+    sums_ref[...] = sums_in[...]
     rows_sent = 16 * slots
+
+    def add(name, product):
+        k = 8 * AT[name]
+        sums_ref[k : k + 8, :] += folded(product)
+
+    def add_row(name, product):
+        k = 8 * AT[name]
+        sums_ref[k : k + 1, :] += product
 
     def send(to, row):
         for h in range(halves):
-            out_ref[h * rows_sent + to : h * rows_sent + to + row.shape[0], :] = row[:, h * LANES : (h + 1) * LANES]
-
-    for s in range(slots):
-        at = slice(s * prows, (s + 1) * prows)
-        live = live_of(rows_ref, s, (prows, ncol))
-        nuu, nvv, nuv = (stress_ref[j, at, :] for j in range(3))
-        for v in range(2):
-            w = jnp.where(live, vec_ref[v, at, :], 0.0)
-            g_ref[v, at, :] = geometric(w, live, nuu, nvv, nuv)
-            ug_ref[v, at, :] = prec_ref[at, :] * g_ref[v, at, :]
+            out_ref[h * rows_sent + to : h * rows_sent + to + 1, :] = row[:, h * LANES : (h + 1) * LANES]
+
+    k_ref[...] = k_in[...]
+    uk_ref[...] = uk_in[...]
+    kuk_ref[...] = kuk_in[...]
+    for s in range(slots):
         own_id, want_id = mine[s].astype(jnp.float32), match[s].astype(jnp.float32)
         places = edge_places(rows_ref, s, prows)
+        added, scaled = [], []
         for v in range(2):
             own = edge_ref[4 * (2 * s + v) : 4 * (2 * s + v) + 4, :]
             top = jnp.zeros((2, ncol), jnp.float32)
@@ -256,137 +269,165 @@
                     wants = ref[9 * slots + t : 9 * slots + t + 1, :]
                     top = top + jnp.where(wants == own_id, strip[0:2], 0.0)
                     bottom = bottom + jnp.where(label_t == want_id, strip[2:4], 0.0)
-            added = interface_rows(own, top, bottom)
-            for i, row in enumerate(places):
-                to = 4 * (2 * s + v) + i
-                extra_ref[to : to + 1, :] = added[i]
-                send(4 * (4 * s + 2 + v) + i, uk_ref[v, pl.ds(row, 1), :] + prec_ref[pl.ds(row, 1), :] * added[i])
-                send(4 * (4 * s + v) + i, ug_ref[v, pl.ds(row, 1), :])
-    tag = halves * rows_sent
-    for s in range(slots):
-        out_ref[tag + s : tag + s + 1, :] = label(match[s], LANES)
-    out_ref[tag + slots :, :] = jnp.zeros((out_ref.shape[0] - tag - slots, LANES), jnp.float32)
-
-
-def gram_kernel(
-    rows_ref, extra_ref, vec_ref, thick_ref, support_ref, prec_ref, k_in, uk_in, sums_in,
-    g_ref, ug_ref, stress_ref, uk_ref, kuk_ref, kug_ref, gu_ref, tile_ref, sums_ref, k_ref,
-):
-    slots = rows_ref.shape[0]
-    rows_dev, ncol = thick_ref.shape
-    prows = rows_dev // slots
-    sums_ref[...] = sums_in[...]
-
-    def add(name, product):
-        k = AT[name]
-        sums_ref[k : k + 1, :] += column_sums(product)
-
-    for s in range(slots):
-        at = slice(s * prows, (s + 1) * prows)
-        live = live_of(rows_ref, s, (prows, ncol))
-        thick, support, prec = thick_ref[at, :], support_ref[at, :], prec_ref[at, :]
-        nuu, nvv, nuv = (stress_ref[j, at, :] for j in range(3))
-        places = edge_places(rows_ref, s, prows)
-        for v in range(2):
-            k_ref[v, at, :] = k_in[v, at, :]
-            uk_ref[v, at, :] = uk_in[v, at, :]
-        add_k = [[extra_ref[4 * (2 * s + v) + i : 4 * (2 * s + v) + i + 1, :] for i in range(4)] for v in range(2)]
+            added.append(interface_rows(own, top, bottom))
+            scaled.append([prec_ref[pl.ds(row, 1), :] * n for row, n in zip(places, added[v])])
+        last_tile = (rows_ref[s] - 1) // 8 * 8 - 8
+        for base, pair in ((0, (2, 3)), (last_tile, (0, 1))):
+            start = s * prows + base
+            at = pl.ds(pl.multiple_of(start, 8), 16)
+            row = iota((16, ncol), 0)
+            live = row + base < rows_ref[s]
+            parts = [
+                sum(jnp.where(row == places[i] - start, scaled[v][i], 0.0) for i in pair)
+                for v in range(2)
+            ]
+            thick, support = thick_ref[at, :], support_ref[at, :]
+            extra = [stiffness(part, live, thick, support) for part in parts]
+            for x in range(2):
+                for y in range(x, 2):
+                    k = 8 * AT["kuu", 2 + x, 2 + y]
+                    sums_ref[k : k + 8, :] += folded(
+                        uk_in[x, at, :] * extra[y] + parts[x] * (kuk_in[y, at, :] + extra[y])
+                    )
+            for v in range(2):
+                kuk_ref[v, at, :] += extra[v]
         for a in range(2):
             for b in range(a, 2):
                 for i, row in enumerate(places):
-                    p = prec_ref[pl.ds(row, 1), :]
                     ka, kb = k_in[a, pl.ds(row, 1), :], k_in[b, pl.ds(row, 1), :]
-                    add(("kxx", a, b), vec_ref[a, pl.ds(row, 1), :] * add_k[b][i])
-                    add(("kpk", a, b), p * (ka * add_k[b][i] + add_k[a][i] * (kb + add_k[b][i])))
+                    add_row(("kxx", a, b), vec_ref[a, pl.ds(row, 1), :] * added[b][i])
+                    add_row(("kpk", a, b), ka * scaled[b][i] + scaled[a][i] * (kb + added[b][i]))
         for v in range(2):
             for i, row in enumerate(places):
-                k_ref[v, pl.ds(row, 1), :] += add_k[v][i]
-                uk_ref[v, pl.ds(row, 1), :] += prec_ref[pl.ds(row, 1), :] * add_k[v][i]
-        for v in range(2):
-            kuk_ref[v, at, :] = stiffness(uk_ref[v, at, :], live, thick, support)
-            kug_ref[v, at, :] = stiffness(ug_ref[v, at, :], live, thick, support)
+                k_ref[v, pl.ds(row, 1), :] += added[v][i]
+                uk_ref[v, pl.ds(row, 1), :] += scaled[v][i]
+    for s in range(slots):
+        at = slice(s * prows, (s + 1) * prows)
+        live = live_of(rows_ref, s, (prows, ncol))
+        thick, support = thick_ref[at, :], support_ref[at, :]
+        nuu, nvv, nuv = (stress_ref[j, at, :] for j in range(3))
+        for v in range(2):
+            w = jnp.where(live, vec_ref[v, at, :], 0.0)
+            g_ref[v, at, :] = geometric(w, live, nuu, nvv, nuv)
+            ug_ref[v, at, :] = prec_ref[at, :] * g_ref[v, at, :]
         for a in range(2):
             wa = jnp.where(live, vec_ref[a, at, :], 0.0)
             for b in range(a, 2):
                 add(("gxx", a, b), wa * g_ref[b, at, :])
                 add(("gpg", a, b), g_ref[a, at, :] * ug_ref[b, at, :])
-                add(("kuu", a, b), ug_ref[a, at, :] * kug_ref[b, at, :])
-                add(("kuu", 2 + a, 2 + b), uk_ref[a, at, :] * kuk_ref[b, at, :])
             for b in range(2):
                 add(("kpg", a, b), k_ref[a, at, :] * ug_ref[b, at, :])
                 add(("kuu", a, 2 + b), ug_ref[a, at, :] * kuk_ref[b, at, :])
         basis = [(ug_ref, 0), (ug_ref, 1), (uk_ref, 0), (uk_ref, 1)]
-        for a in range(4):
-            ref, v = basis[a]
-            gu_ref[a, at, :] = geometric(ref[v, at, :], live, nuu, nvv, nuv)
-            for b in range(a + 1):
-                ref, v = basis[b]
-                add(("guu", b, a), ref[v, at, :] * gu_ref[a, at, :])
-    tile_ref[...] = packed(sums_ref[...])
-
-
-def strip_of(line_ref, z, at, rows, slots):
-    halves = (line_ref.shape[1] - 1) // (16 * slots)
+        bends = []
+        for v in range(2):
+            w = ug_ref[v, at, :]
+            bends.append((w, jnp.where(live, second_rows(w), 0.0), second_cols(w)))
+        for b in range(2):
+            w, r, c = bends[b]
+            sw, tr, tc = support * w, thick * r, thick * c
+            for a in range(b + 1):
+                add(("kuu", a, b), bends[a][0] * sw + bends[a][1] * tr + bends[a][2] * tc)
+        first = []
+        for ref, v in basis:
+            w = ref[v, at, :]
+            first.append((row_after(w) - w, col_after(w) - w))
+        for b in range(4):
+            r, c = first[b]
+            fr, fc = nuu * r + nuv * c, nvv * c + nuv * r
+            for a in range(b + 1):
+                add(("guu", a, b), first[a][0] * fr + first[a][1] * fc)
+        for i, row in enumerate(edge_places(rows_ref, s, prows)):
+            for a, (ref, v) in enumerate(basis):
+                send(4 * (4 * s + a) + i, ref[v, pl.ds(row, 1), :])
+    tag = halves * rows_sent
+    tile = packed([column_sums(sums_ref[8 * k : 8 * k + 8, :]) for k in range(len(NAMES))])
+    lane = iota(tile.shape, 1)
+    for s in range(slots):
+        tile = jnp.where(lane == LANES - slots + s, match[s].astype(jnp.float32), tile)
+    out_ref[tag:, :] = tile
+
+
+def apply_kernel(rows_ref, thick_ref, support_ref, stress_ref, ug_ref, uk_ref, kug_ref, gu_ref):
+    slots = rows_ref.shape[0]
+    rows_dev, ncol = thick_ref.shape
+    prows = rows_dev // slots
+    for s in range(slots):
+        at = slice(s * prows, (s + 1) * prows)
+        live = live_of(rows_ref, s, (prows, ncol))
+        thick, support = thick_ref[at, :], support_ref[at, :]
+        nuu, nvv, nuv = (stress_ref[j, at, :] for j in range(3))
+        for a, (ref, v) in enumerate([(ug_ref, 0), (ug_ref, 1), (uk_ref, 0), (uk_ref, 1)]):
+            w = ref[v, at, :]
+            gu_ref[a, at, :] = geometric(w, live, nuu, nvv, nuv)
+            if a < 2:
+                kug_ref[v, at, :] = stiffness(w, live, thick, support)
+
+
+def strip_of(ref, at, rows, slots):
+    halves = (ref.shape[0] - 8) // (16 * slots)
     return jnp.concatenate(
-        [line_ref[z, h * 16 * slots + at : h * 16 * slots + at + rows, :] for h in range(halves)], axis=1
-    )
-
-
-def wanted_of(line_ref, z, slot, slots):
-    halves = (line_ref.shape[1] - 1) // (16 * slots)
-    tag = halves * 16 * slots
-    return line_ref[z, tag + slot : tag + slot + 1, :1]
-
-
-def line_kernel(slots, line_ref, out_ref, sums_ref):
-    owners = line_ref.shape[0]
-    sums_ref[...] = jnp.zeros_like(sums_ref)
-    sums = {pair: None for pair in UU}
+        [ref[h * 16 * slots + at : h * 16 * slots + at + rows, :] for h in range(halves)], axis=1
+    )
+
+
+def wanted_of(ref, slot, slots):
+    tag = ref.shape[0] - 8
+    return ref[tag : tag + 1, LANES - slots + slot : LANES - slots + slot + 1]
+
+
+def line_kernel(slots, *refs):
+    line, out_ref = refs[:-1], refs[-1]
+    owners = len(line)
+    tag = line[0].shape[0] - 8
+    me = lax.axis_index("patch")
+    total = line[0][tag:, :]
+    for z in range(1, owners):
+        total = total + line[z][tag:, :]
+    sums = {}
     for z in range(owners):
         for s in range(slots):
-            wanted = wanted_of(line_ref, z, s, slots)
+            wanted = wanted_of(line[z], s, slots)
             jumps, slopes = [], []
             for a in range(4):
-                own = strip_of(line_ref, z, 4 * (4 * s + a), 2, slots)
+                own = strip_of(line[z], 4 * (4 * s + a), 2, slots)
                 bottom = jnp.zeros_like(own)
                 for near in sorted({(z + 1) % owners, (z - 1) % owners}):
+                    there = lax.rem(me - near + owners, owners)
                     for t in range(slots):
-                        strip = strip_of(line_ref, near, 4 * (4 * t + a) + 2, 2, slots)
-                        bottom = bottom + jnp.where(wanted == float(near * slots + t), strip, 0.0)
+                        strip = strip_of(line[near], 4 * (4 * t + a) + 2, 2, slots)
+                        is_it = wanted == (there * slots + t).astype(jnp.float32)
+                        bottom = bottom + jnp.where(is_it, strip, 0.0)
                 jumps.append(own[1:2] - bottom[0:1])
                 slopes.append(own[1:2] - own[0:1] - (bottom[1:2] - bottom[0:1]))
             for a, b in UU:
                 term = penalty_value * jumps[a] * jumps[b] + penalty_slope * slopes[a] * slopes[b]
-                sums[a, b] = term if sums[a, b] is None else sums[a, b] + term
-    for pair in UU:
-        k = AT[("kuu",) + pair]
-        sums_ref[k : k + 1, :] = sums[pair]
-    out_ref[...] = packed(sums_ref[...])
-
-
-def join_kernel(rows_ref, matched_ref, line_ref, kug_in, kuk_in, kug_ref, kuk_ref):
+                sums[a, b] = sums[a, b] + term if (a, b) in sums else term
+    out_ref[...] = total + packed([sums[pair] for pair in UU])
+
+
+def join_kernel(slots, rows_ref, matched_ref, *refs):
+    line, (kug_in, kuk_in, kug_ref, kuk_ref) = refs[:-4], refs[-4:]
     kug_ref[...] = kug_in[...]
     kuk_ref[...] = kuk_in[...]
-    slots = rows_ref.shape[0]
     rows_dev, ncol = kug_in.shape[1:]
     prows = rows_dev // slots
-    owners = line_ref.shape[0]
+    owners = len(line)
     mine, match = place(rows_ref, matched_ref, slots)
     me = lax.axis_index("patch")
     for s in range(slots):
-        own_id, want_id = mine[s].astype(jnp.float32), match[s].astype(jnp.float32)
+        own_id, want_id = mine[s].astype(jnp.float32), match[s]
         places = edge_places(rows_ref, s, prows)
         for a in range(4):
-            own = jnp.zeros((4, ncol), jnp.float32)
+            own = strip_of(line[0], 4 * (4 * s + a), 4, slots)
             top = jnp.zeros((2, ncol), jnp.float32)
             bottom = jnp.zeros((2, ncol), jnp.float32)
-            for z in range(owners):
+            for near in sorted({1, owners - 1}):
+                there = lax.rem(me - near + owners, owners)
                 for t in range(slots):
-                    strip = strip_of(line_ref, z, 4 * (4 * t + a), 4, slots)
-                    top = top + jnp.where(wanted_of(line_ref, z, t, slots) == own_id, strip[0:2], 0.0)
-                    bottom = bottom + jnp.where(want_id == float(z * slots + t), strip[2:4], 0.0)
-                    if t == s:
-                        own = own + jnp.where(me == z, strip, 0.0)
+                    strip = strip_of(line[near], 4 * (4 * t + a), 4, slots)
+                    top = top + jnp.where(wanted_of(line[near], t, slots) == own_id, strip[0:2], 0.0)
+                    bottom = bottom + jnp.where(want_id == there * slots + t, strip[2:4], 0.0)
             ref = kug_ref if a < 2 else kuk_ref
             for row, added in zip(places, interface_rows(own, top, bottom)):
                 ref[a % 2, pl.ds(row, 1), :] += added
@@ -494,7 +535,7 @@
     spaces = {"s": pltpu.SMEM, "v": pltpu.VMEM, "h": pltpu.HBM}
     return pl.pallas_call(
         body,
-        out_shape=[jax.ShapeDtypeStruct(s, d) for s, d in outs],
+        out_shape=[pltpu.HBM(s, d) if out_kind == "h" else jax.ShapeDtypeStruct(s, d) for s, d in outs],
         in_specs=[pl.BlockSpec(memory_space=spaces[k]) for k in kinds],
         out_specs=[pl.BlockSpec(memory_space=spaces[out_kind]) for _ in outs],
         scratch_shapes=list(scratch),
@@ -512,7 +553,7 @@
     cells = float(owners * inner * rows_dev * ncol)
     field = ((2, rows_dev, ncol), f32)
     one = ((rows_dev, ncol), f32)
-    sums = ((SUMS, ncol), f32)
+    sums = ((8 * SUMS, ncol), f32)
     tile = ((8, LANES), f32)
 
     width = 3 * ncol + LANES
@@ -522,11 +563,14 @@
         "hh",
         [
             pltpu.VMEM((1, rows_dev), jnp.int32),
-            pltpu.VMEM((rows_dev, LANES), bf16),
+            pltpu.VMEM((rows_dev, width), bf16),
             pltpu.SemaphoreType.DMA((5,)),
         ],
         out_kind="h",
-    )(jnp.transpose(prestress, (1, 0, 2)), elem_row.reshape(1, rows_dev))
+    )(
+        pltpu.with_memory_space_constraint(jnp.transpose(prestress, (1, 0, 2)), pltpu.HBM),
+        pltpu.with_memory_space_constraint(elem_row.reshape(1, rows_dev), pltpu.HBM),
+    )
     arrived = lax.all_to_all(
         payload, ("patch", "sub", "half"), split_axis=0, concat_axis=0, tiled=True
     )
@@ -534,31 +578,27 @@
     (edges,) = call(edge_kernel, [((edge_rows, ncol), f32)], "ssv")(patch_rows, matched, vectors)
     below = passed_along(edges, "patch", 1)
     above = passed_along(edges, "patch", -1)
-    k_x, u_k, prec, part = call(stiff_kernel, [field, field, one, sums], "svvv")(
+    k_x, u_k, k_uk, prec, part = call(stiff_kernel, [field, field, field, one, sums], "svvv")(
         patch_rows, vectors, thickness, foundation
     )
-    sent_rows = (ncol // LANES) * 16 * slots + -(-slots // 8) * 8
-    g_x, u_g, stress, extra, sent = call(
-        bend_kernel,
-        [field, field, ((3, rows_dev, ncol), f32), ((8 * slots, ncol), f32), ((sent_rows, LANES), f32)],
-        "ssvvvvvvv",
-    )(patch_rows, matched, arrived, vectors, prec, u_k, edges, below, above)
-    line = lax.all_to_all(
-        jnp.broadcast_to(sent[None], (owners, sent_rows, LANES)), "patch", split_axis=0, concat_axis=0, tiled=True
-    )
-    u_k, k_uk, k_ug, g_u, local = call(
+    sent_rows = (ncol // LANES) * 16 * slots + 8
+    u_g, u_k, k_uk, stress, sent = call(
         gram_kernel,
-        [field, field, field, ((4, rows_dev, ncol), f32), tile],
-        "svvvvvvvvvvv",
-        [pltpu.VMEM((SUMS, ncol), f32), pltpu.VMEM((2, rows_dev, ncol), f32)],
-    )(patch_rows, extra, vectors, thickness, foundation, prec, k_x, u_k, part, g_x, u_g, stress)
-    local = summed_over(local, "patch")
-    (across,) = call(
-        functools.partial(line_kernel, slots), [tile], "v", [pltpu.VMEM((SUMS, ncol), f32)]
-    )(line)
-    total = summed_over(summed_over(local + across, "half"), "sub")
-    k_ug, k_uk = call(join_kernel, [field, field], "ssvvv")(
-        patch_rows, matched, line, k_ug, k_uk
+        [field, field, field, ((3, rows_dev, ncol), f32), ((sent_rows, LANES), f32)],
+        "ssvvvvvvvvvvvv",
+        [pltpu.VMEM(sums[0], f32), pltpu.VMEM(field[0], f32), pltpu.VMEM(field[0], f32)],
+    )(
+        patch_rows, matched, arrived, vectors, thickness, foundation, prec, k_x, u_k, k_uk, part,
+        edges, below, above,
+    )
+    line = [sent] + [passed_along(sent, "patch", by) for by in range(1, owners)]
+    k_ug, g_u = call(apply_kernel, [field, ((4, rows_dev, ncol), f32)], "svvvvv")(
+        patch_rows, thickness, foundation, stress, u_g, u_k
+    )
+    (total,) = call(functools.partial(line_kernel, slots), [tile], "v" * owners)(*line)
+    total = summed_over(summed_over(total, "half"), "sub")
+    k_ug, k_uk = call(functools.partial(join_kernel, slots), [field, field], "ss" + "v" * (owners + 2))(
+        patch_rows, matched, *line, k_ug, k_uk
     )
     (modes,) = call(functools.partial(final_kernel, cells), [field], "svvvvvvvv")(
         patch_rows, total, vectors, u_g, u_k, prec, k_ug, k_uk, g_u

time: 57.8 us -> 45.9 us (0.79)
  local copies, waits for them, and re-layouts: 12.7 us -> 1.72 us
  starting transfers between devices: 21.7 us -> 17.2 us
  Pallas kernels: 12 us -> 14.9 us
  waiting for transfers between devices: 10.6 us -> 11.6 us
    unnamed x38 -> x14, local copies, waits for them, and re-layouts: 12.1 us -> 1.72 us
    all_to_all x1 -> x0, starting transfers between devices: 3.66 us -> none  [per_device(): lax.all_to_all(jnp.broadcast_to(sent[None], (owners, sent_rows, LANES)),...]
    pallas_call x5, Pallas kernels: 8.4 us -> 10.3 us  [the longest x1 3.72 us: per_device(): call(gram_kernel, [field, field, field, ((3, rows_dev, ncol), f32), ((sen...]
    ppermute x7, waiting for transfers between devices: 9.99 us -> 11.4 us  [passed_along(): lax.ppermute(array, axis, [(i, (i + by) % peers) for i in range(peers)])]
    pallas_call x1, Pallas kernels: 0.8 us -> 1.85 us  [per_device(): call(pack_kernel, [((rows_dev, width), bf16)], 'hh', [pltpu.VMEM((1, rows...]
    ppermute x7, starting transfers between devices: 10.6 us -> 9.68 us  [passed_along(): lax.ppermute(array, axis, [(i, (i + by) % peers) for i in range(peers)])]
    broadcast_in_dim x1 -> x0, local copies, waits for them, and re-layouts: 0.67 us -> none  [per_device(): jnp.broadcast_to(sent[None], (owners, sent_rows, LANES))]
  transfers between devices with their start and end apart: 9 -> 8, of which waited for: 5 -> 6; matrix products, arithmetic and copies ran while one was open for 0% -> 0% of each run, Pallas kernels for 14% -> 15%
where the time goes in v3:
time: 45.9 us; the launch traced here: 45.6 us
  starting transfers between devices  17.2 us (37%)
  Pallas kernels  14.9 us (32%)
  waiting for transfers between devices  11.6 us (25%)
  local copies, waits for them, and re-layouts  1.72 us (4%)
    ppermute x7, waiting for transfers between devices, passed_along(): lax.ppermute(array, axis, [(i, (i + by) % peers) for i in range(peers)])  11.4 us
    ppermute x7, starting transfers between devices, passed_along(): lax.ppermute(array, axis, [(i, (i + by) % peers) for i in range(peers)])  9.68 us
    all_to_all x1, starting transfers between devices, per_device(): lax.all_to_all(payload, ('patch', 'sub', 'half'), split_axis=0, concat_ax...  7.5 us
    pallas_call x1, Pallas kernels, per_device(): call(gram_kernel, [field, field, field, ((3, rows_dev, ncol), f32), ((sen...  3.72 us
    pallas_call x1, Pallas kernels, per_device(): call(stiff_kernel, [field, field, field, one, sums], 'svvv')  2.69 us
    pallas_call x1, Pallas kernels, per_device(): call(apply_kernel, [field, ((4, rows_dev, ncol), f32)], 'svvvvv')  2.68 us
    pallas_call x1, Pallas kernels, per_device(): call(functools.partial(final_kernel, cells), [field], 'svvvvvvvv')  2.24 us
    pallas_call x1, Pallas kernels, per_device(): call(pack_kernel, [((rows_dev, width), bf16)], 'hh', [pltpu.VMEM((1, rows...  1.85 us
  transfers between devices with their start and end apart: 8, of which 6 were waited for; matrix products, arithmetic and copies ran while one was open for 0% of the time, Pallas kernels for 15%

profile of v3, /device:TPU:0, one launch (start us, length us, event | category | flops | bytes accessed | tf_op | source)
XLA Modules:
  0.0 45.6 jit_solution(10576306944712791511)
XLA Ops:
  0.0 1.9 %shard_map.73 = bf16[256,896]{1,0:T(8,128)(2,1)} custom-call(bf16[3,256,256]{2,1,0:T(8,128)(2,1)} %bitcast.6, s32[1,256]{1,0:T(1,128)} %bitcast.7), custom_call_target="tpu_custom_call" | custom-call | flops 1000000 | bytes 2000000 | tf_op jit(solution)/shard_map/pallas_call | solution.py:560
  1.9 0.0 copy-start
  1.9 7.5 %all-to-all-start = ((bf16[16,16,896]{2,1,0:T(8,128)(2,1)}), bf16[16,16,896]{2,1,0:T(8,128)(2,1)S(1)}, u32[]{:S(2)}, u32[]{:S(2)}) async-start(bf16[16,16,896]{2,1,0:T(8,128)(2,1)} %bitcast.5), calls=%async_computation | async-start | bytes 917504 | tf_op jit(solution)/shard_map/all_to_all | solution.py:574
  9.5 0.6 %shard_map.75.edge_ref = f32[24,256]{1,0:T(8,128)S(1)} custom-call(s32[2]{0:T(128)S(1)} %copy-done.5, s32[2]{0:T(128)S(1)} %copy-done.6, f32[2,256,256]{2,1,0:T(8,128)S(1)} %copy-done), custom_call_target="tpu_custom_call" | custom-call | flops 1000000 | bytes 2000000 | tf_op jit(solution)/shard_map/pallas_call | solution.py:578
  10.0 3.8 %collective-permute-start.1 = (f32[24,256]{1,0:T(8,128)S(1)}, f32[24,256]{1,0:T(8,128)S(1)}, u32[]{:S(2)}, u32[]{:S(2)}) collective-permute-start(f32[24,256]{1,0:T(8,128)S(1)} %shard_map.75.edge_ref), channel_id=1, source_target_pairs={{0,12},{4,0},{8,4},{12,8},{1,13},{5,1},{9,5},{13,9},{2,14},{6,2},{... | collective-permute-start | bytes 73736 | tf_op jit(solution)/shard_map/ppermute | solution.py:32
  13.8 2.7 %shard_map.74 = (f32[2,256,256]{2,1,0:T(8,128)S(1)}, f32[2,256,256]{2,1,0:T(8,128)S(1)}, f32[2,256,256]{2,1,0:T(8,128)S(1)}, f32[256,256]{1,0:T(8,128)S(1)}, f32[320,256]{1,0:T(8,128)S(1)}) custom-call(s32[2]{0:T(128)S(1)} %copy-done.5, f32[2,256,256]{2,1,0:T(8,128)S(1)} %copy-done, f32[256,256]{1,0:T(8,128)S(1)} %copy-done.1, f32[256,256]{1,0:T(8,128)S(1)} %copy-done.2), custom_call_target="tpu_custom_call" | custom-call | flops 1000000 | bytes 2000000 | tf_op jit(solution)/shard_map/pallas_call | solution.py:581
  16.5 0.7 %copy-done.3 = f32[320,256]{1,0:T(8,128)} copy-done((f32[320,256]{1,0:T(8,128)}, f32[320,256]{1,0:T(8,128)S(1)}, u32[]{:S(2)}) %copy-start.3) | copy-done | bytes 327704
  17.3 1.3 %collective-permute-done.1.above_ref = f32[24,256]{1,0:T(8,128)S(1)} collective-permute-done((f32[24,256]{1,0:T(8,128)S(1)}, f32[24,256]{1,0:T(8,128)S(1)}, u32[]{:S(2)}, u32[]{:S(2)}) %collective-permute-start.1) | collective-permute-done | bytes 24608 | tf_op jit(solution)/shard_map/ppermute | solution.py:32
  18.6 4.3 %collective-permute-done.below_ref = f32[24,256]{1,0:T(8,128)S(1)} collective-permute-done((f32[24,256]{1,0:T(8,128)S(1)}, f32[24,256]{1,0:T(8,128)S(1)}, u32[]{:S(2)}, u32[]{:S(2)}) %collective-permute-start) | collective-permute-done | bytes 24608 | tf_op jit(solution)/shard_map/ppermute | solution.py:32
  22.9 0.2 all-to-all-done
  23.1 1.0 %copy-done.4 = f32[320,256]{1,0:T(8,128)S(1)} copy-done((f32[320,256]{1,0:T(8,128)S(1)}, f32[320,256]{1,0:T(8,128)}, u32[]{:S(2)}) %copy-start.4) | copy-done | bytes 327704
  24.1 3.7 %shard_map.76 = (f32[2,256,256]{2,1,0:T(8,128)S(1)}, f32[2,256,256]{2,1,0:T(8,128)S(1)}, f32[2,256,256]{2,1,0:T(8,128)S(1)}, f32[3,256,256]{2,1,0:T(8,128)S(1)}, f32[72,128]{1,0:T(8,128)S(1)}) custom-call(s32[2]{0:T(128)S(1)} %copy-done.5, s32[2]{0:T(128)S(1)} %copy-done.6, bf16[256,896]{1,0:T(8,128)(2,1)S(1)} %bitcast.4, f32[2,256,256]{2,1,0:T(8,128)S(1)} %copy-done, ...), custom_call_target="tpu_custom_call" | custom-call | flops 1000000 | bytes 2000000 | tf_op jit(solution)/shard_map/pallas_call | solution.py:585
  27.8 1.5 %collective-permute-start.4 = (f32[72,128]{1,0:T(8,128)S(1)}, f32[72,128]{1,0:T(8,128)S(1)}, u32[]{:S(2)}, u32[]{:S(2)}) collective-permute-start(f32[72,128]{1,0:T(8,128)S(1)} %get-tuple-element.24.refs_0_), channel_id=1, source_target_pairs={{0,12},{4,0},{8,4},{12,8},{1,13},{5,1},{9,5},{13,9},{2,14},{6,2},{... | collective-permute-start | bytes 110600 | tf_op jit(solution)/shard_map/ppermute | solution.py:32
  29.3 1.8 %collective-permute-start.3 = (f32[72,128]{1,0:T(8,128)S(1)}, f32[72,128]{1,0:T(8,128)S(1)}, u32[]{:S(2)}, u32[]{:S(2)}) collective-permute-start(f32[72,128]{1,0:T(8,128)S(1)} %get-tuple-element.24.refs_0_), channel_id=1, source_target_pairs={{0,8},{4,12},{8,0},{12,4},{1,9},{5,13},{9,1},{13,5},{2,10},{6,14},... | collective-permute-start | bytes 110600 | tf_op jit(solution)/shard_map/ppermute | solution.py:32
  31.1 1.2 %collective-permute-start.2 = (f32[72,128]{1,0:T(8,128)S(1)}, f32[72,128]{1,0:T(8,128)S(1)}, u32[]{:S(2)}, u32[]{:S(2)}) collective-permute-start(f32[72,128]{1,0:T(8,128)S(1)} %get-tuple-element.24.refs_0_), channel_id=1, source_target_pairs={{0,4},{4,8},{8,12},{12,0},{1,5},{5,9},{9,13},{13,1},{2,6},{6,10},{... | collective-permute-start | bytes 110600 | tf_op jit(solution)/shard_map/ppermute | solution.py:32
  32.2 2.3 %collective-permute-done.3.refs_2_ = f32[72,128]{1,0:T(8,128)S(1)} collective-permute-done((f32[72,128]{1,0:T(8,128)S(1)}, f32[72,128]{1,0:T(8,128)S(1)}, u32[]{:S(2)}, u32[]{:S(2)}) %collective-permute-start.3) | collective-permute-done | bytes 36896 | tf_op jit(solution)/shard_map/ppermute | solution.py:32
  34.6 2.2 %collective-permute-done.2.refs_1_ = f32[72,128]{1,0:T(8,128)S(1)} collective-permute-done((f32[72,128]{1,0:T(8,128)S(1)}, f32[72,128]{1,0:T(8,128)S(1)}, u32[]{:S(2)}, u32[]{:S(2)}) %collective-permute-start.2) | collective-permute-done | bytes 36896 | tf_op jit(solution)/shard_map/ppermute | solution.py:32
  36.8 0.4 shard_map.77
  37.2 0.0 collective-permute-start.5
  37.3 1.2 %collective-permute-done.5 = f32[8,128]{1,0:T(8,128)S(1)} collective-permute-done((f32[8,128]{1,0:T(8,128)S(1)}, f32[8,128]{1,0:T(8,128)S(1)}, u32[]{:S(2)}, u32[]{:S(2)}) %collective-permute-start.5) | collective-permute-done | bytes 4128 | tf_op jit(solution)/shard_map/ppermute | solution.py:32
  38.4 1.5 %collective-permute-start.6 = (f32[8,128]{1,0:T(8,128)S(1)}, f32[8,128]{1,0:T(8,128)S(1)}, u32[]{:S(2)}, u32[]{:S(2)}) collective-permute-start(f32[8,128]{1,0:T(8,128)S(1)} %add.6), channel_id=1, source_target_pairs={{0,2},{2,0},{1,3},{3,1},{4,6},{6,4},{5,7},{7,5},{8,10},{10,8},{9,1... | collective-permute-start | bytes 12296 | tf_op jit(solution)/shard_map/ppermute | solution.py:32
  39.9 2.7 %shard_map.78 = (f32[2,256,256]{2,1,0:T(8,128)S(1)}, f32[4,256,256]{2,1,0:T(8,128)S(1)}) custom-call(s32[2]{0:T(128)S(1)} %copy-done.5, f32[256,256]{1,0:T(8,128)S(1)} %copy-done.1, f32[256,256]{1,0:T(8,128)S(1)} %copy-done.2, f32[3,256,256]{2,1,0:T(8,128)S(1)} %get-tuple-element.27.stress_ref, f32[2,256,256]{2,1,0:T(8,128)S(1)} %get-tuple-element.25.ug_ref, ...), custom_call_target="tpu_custom_call" | custom-call | flops 1000000 | bytes 2000000 | tf_op jit(solution)/shard_map/pallas_call | solution.py:595
  42.6 0.8 %shard_map.79 = (f32[2,256,256]{2,1,0:T(8,128)S(1)}, f32[2,256,256]{2,1,0:T(8,128)S(1)}) custom-call(s32[2]{0:T(128)S(1)} %copy-done.5, s32[2]{0:T(128)S(1)} %copy-done.6, f32[72,128]{1,0:T(8,128)S(1)} %get-tuple-element.24.refs_0_, f32[72,128]{1,0:T(8,128)S(1)} %collective-permute-done.2.refs_1_, f32[72,128]{1,0:T(8,128)S(1)} %collective-permute-done.3.refs_2_, ...), custom_call_target="tpu_custom_call" | custom-call | flops 1000000 | bytes 2000000 | tf_op jit(solution)/shard_map/pallas_call | solution.py:600
  43.4 2.2 %shard_map.80 = f32[2,256,256]{2,1,0:T(8,128)} custom-call(s32[2]{0:T(128)S(1)} %copy-done.5, f32[8,128]{1,0:T(8,128)S(1)} %add.7.total_ref, f32[2,256,256]{2,1,0:T(8,128)S(1)} %copy-done, f32[2,256,256]{2,1,0:T(8,128)S(1)} %get-tuple-element.25.ug_ref, f32[2,256,256]{2,1,0:T(8,128)S(1)} %get-tuple-element.26.uk_ref, ...), custom_call_target="tpu_custom_call" | custom-call | flops 1000000 | bytes 2000000 | tf_op jit(solution)/shard_map/pallas_call | solution.py:603
  (16 shorter events, 0.0 us)
Async XLA Ops:
  1.9 7.5 %copy-start = (f32[2,256,256]{2,1,0:T(8,128)S(1)}, f32[2,256,256]{2,1,0:T(8,128)}, u32[]{:S(2)}) copy-start(f32[2,256,256]{2,1,0:T(8,128)} %vec_ref.7) | copy-start | bytes 1572868
  1.9 7.5 %copy-start.5 = (s32[2]{0:T(128)S(1)}, s32[2]{0:T(128)}, u32[]{:S(2)}) copy-start(s32[2]{0:T(128)} %rows_ref.11) | copy-start | bytes 28
  1.9 7.5 %copy-start.6 = (s32[2]{0:T(128)S(1)}, s32[2]{0:T(128)}, u32[]{:S(2)}) copy-start(s32[2]{0:T(128)} %matched_ref.5) | copy-start | bytes 28
  1.9 21.2 %all-to-all-start = ((bf16[16,16,896]{2,1,0:T(8,128)(2,1)}), bf16[16,16,896]{2,1,0:T(8,128)(2,1)S(1)}, u32[]{:S(2)}, u32[]{:S(2)}) async-start(bf16[16,16,896]{2,1,0:T(8,128)(2,1)} %bitcast.5), calls=%async_computation | async-start | bytes 917504 | tf_op jit(solution)/shard_map/all_to_all | solution.py:574
  9.4 4.4 %copy-start.1 = (f32[256,256]{1,0:T(8,128)S(1)}, f32[256,256]{1,0:T(8,128)}, u32[]{:S(2)}) copy-start(f32[256,256]{1,0:T(8,128)} %thick_ref.5) | copy-start | bytes 786436
  9.4 4.4 %copy-start.2 = (f32[256,256]{1,0:T(8,128)S(1)}, f32[256,256]{1,0:T(8,128)}, u32[]{:S(2)}) copy-start(f32[256,256]{1,0:T(8,128)} %support_ref.5) | copy-start | bytes 786436
  10.0 8.5 %collective-permute-start.1 = (f32[24,256]{1,0:T(8,128)S(1)}, f32[24,256]{1,0:T(8,128)S(1)}, u32[]{:S(2)}, u32[]{:S(2)}) collective-permute-start(f32[24,256]{1,0:T(8,128)S(1)} %shard_map.75.edge_ref), channel_id=1, source_target_pairs={{0,12},{4,0},{8,4},{12,8},{1,13},{5,1},{9,5},{13,9},{2,14},{6,2},{... | collective-permute-start | bytes 73736 | tf_op jit(solution)/shard_map/ppermute | solution.py:32
  13.8 9.1 %collective-permute-start = (f32[24,256]{1,0:T(8,128)S(1)}, f32[24,256]{1,0:T(8,128)S(1)}, u32[]{:S(2)}, u32[]{:S(2)}) collective-permute-start(f32[24,256]{1,0:T(8,128)S(1)} %shard_map.75.edge_ref), channel_id=1, source_target_pairs={{0,4},{4,8},{8,12},{12,0},{1,5},{5,9},{9,13},{13,1},{2,6},{6,10},{... | collective-permute-start | bytes 73736 | tf_op jit(solution)/shard_map/ppermute | solution.py:32
  16.5 0.7 %copy-start.3 = (f32[320,256]{1,0:T(8,128)}, f32[320,256]{1,0:T(8,128)S(1)}, u32[]{:S(2)}) copy-start(f32[320,256]{1,0:T(8,128)S(1)} %get-tuple-element.23.sums_in) | copy-start | bytes 983044
  23.1 1.0 %copy-start.4 = (f32[320,256]{1,0:T(8,128)S(1)}, f32[320,256]{1,0:T(8,128)}, u32[]{:S(2)}) copy-start(f32[320,256]{1,0:T(8,128)} %copy-done.3) | copy-start | bytes 983044
  27.8 4.4 %collective-permute-start.4 = (f32[72,128]{1,0:T(8,128)S(1)}, f32[72,128]{1,0:T(8,128)S(1)}, u32[]{:S(2)}, u32[]{:S(2)}) collective-permute-start(f32[72,128]{1,0:T(8,128)S(1)} %get-tuple-element.24.refs_0_), channel_id=1, source_target_pairs={{0,12},{4,0},{8,4},{12,8},{1,13},{5,1},{9,5},{13,9},{2,14},{6,2},{... | collective-permute-start | bytes 110600 | tf_op jit(solution)/shard_map/ppermute | solution.py:32
  29.3 5.3 %collective-permute-start.3 = (f32[72,128]{1,0:T(8,128)S(1)}, f32[72,128]{1,0:T(8,128)S(1)}, u32[]{:S(2)}, u32[]{:S(2)}) collective-permute-start(f32[72,128]{1,0:T(8,128)S(1)} %get-tuple-element.24.refs_0_), channel_id=1, source_target_pairs={{0,8},{4,12},{8,0},{12,4},{1,9},{5,13},{9,1},{13,5},{2,10},{6,14},... | collective-permute-start | bytes 110600 | tf_op jit(solution)/shard_map/ppermute | solution.py:32
  31.1 5.8 %collective-permute-start.2 = (f32[72,128]{1,0:T(8,128)S(1)}, f32[72,128]{1,0:T(8,128)S(1)}, u32[]{:S(2)}, u32[]{:S(2)}) collective-permute-start(f32[72,128]{1,0:T(8,128)S(1)} %get-tuple-element.24.refs_0_), channel_id=1, source_target_pairs={{0,4},{4,8},{8,12},{12,0},{1,5},{5,9},{9,13},{13,1},{2,6},{6,10},{... | collective-permute-start | bytes 110600 | tf_op jit(solution)/shard_map/ppermute | solution.py:32
  37.2 1.2 %collective-permute-start.5 = (f32[8,128]{1,0:T(8,128)S(1)}, f32[8,128]{1,0:T(8,128)S(1)}, u32[]{:S(2)}, u32[]{:S(2)}) collective-permute-start(f32[8,128]{1,0:T(8,128)S(1)} %shard_map.77), channel_id=1, source_target_pairs={{0,1},{1,0},{2,3},{3,2},{4,5},{5,4},{6,7},{7,6},{8,9},{9,8},{10,11... | collective-permute-start | bytes 12296 | tf_op jit(solution)/shard_map/ppermute | solution.py:32
  38.4 4.9 %collective-permute-start.6 = (f32[8,128]{1,0:T(8,128)S(1)}, f32[8,128]{1,0:T(8,128)S(1)}, u32[]{:S(2)}, u32[]{:S(2)}) collective-permute-start(f32[8,128]{1,0:T(8,128)S(1)} %add.6), channel_id=1, source_target_pairs={{0,2},{2,0},{1,3},{3,1},{4,6},{6,4},{5,7},{7,5},{8,10},{10,8},{9,1... | collective-permute-start | bytes 12296 | tf_op jit(solution)/shard_map/ppermute | solution.py:32

commit v4 on v3

--- a/solution.py
+++ b/solution.py
@@ -32,10 +32,15 @@
     return lax.ppermute(array, axis, [(i, (i + by) % peers) for i in range(peers)])
 
 
-def summed_over(array, axis):
+def summed_over_both(array, outer, inner):
+    across, within = lax.axis_size(outer), lax.axis_size(inner)
+    shifts = [(o, i) for o in range(across) for i in range(within)]
     total = array
-    for by in range(1, lax.axis_size(axis)):
-        total = total + passed_along(array, axis, by)
+    for o, i in shifts[1:]:
+        pairs = [
+            (x * within + y, (x + o) % across * within + (y + i) % within) for x, y in shifts
+        ]
+        total = total + lax.ppermute(array, (outer, inner), pairs)
     return total
 
 
@@ -44,51 +49,96 @@
 
 
 def row_after(w):
-    n = w.shape[0]
-    return jnp.where(iota(w.shape, 0) < n - 1, pltpu.roll(w, n - 1, 0), 0.0)
+    rows = w[0].shape[0]
+    zero = jnp.zeros((8, LANES), jnp.float32)
+    return [pltpu.roll(jnp.concatenate([p, zero], axis=0), rows + 7, 0)[:rows] for p in w]
 
 
 def row_before(w):
-    return jnp.where(iota(w.shape, 0) > 0, pltpu.roll(w, 1, 0), 0.0)
+    rows = w[0].shape[0]
+    zero = jnp.zeros((8, LANES), jnp.float32)
+    return [pltpu.roll(jnp.concatenate([p, zero], axis=0), 1, 0)[:rows] for p in w]
 
 
 def col_after(w):
-    n = w.shape[1]
-    return jnp.where(iota(w.shape, 1) < n - 1, pltpu.roll(w, n - 1, 1), 0.0)
+    at_end = iota(w[0].shape, 1) == LANES - 1
+    turned = [pltpu.roll(p, LANES - 1, 1) for p in w]
+    return [jnp.where(at_end, n, p) for p, n in zip(turned, turned[1:] + [0.0])]
 
 
 def col_before(w):
-    return jnp.where(iota(w.shape, 1) > 0, pltpu.roll(w, 1, 1), 0.0)
+    at_start = iota(w[0].shape, 1) == 0
+    turned = [pltpu.roll(p, 1, 1) for p in w]
+    return [jnp.where(at_start, n, p) for p, n in zip(turned, [0.0] + turned[:-1])]
+
+
+def each(f, *fields):
+    return [f(*parts) for parts in zip(*fields)]
+
+
+def minus(u, w):
+    return each(lambda a, b: a - b, u, w)
+
+
+def times(u, w):
+    return each(lambda a, b: a * b, u, w)
 
 
 def second_rows(w):
-    return row_before(w) + row_after(w) - 2.0 * w
+    return each(lambda a, b, c: a + b - (c + c), row_before(w), row_after(w), w)
 
 
 def second_cols(w):
-    return col_before(w) + col_after(w) - 2.0 * w
-
-
-def stiffness(w, live, thick, support):
-    bend_rows = jnp.where(live, thick * second_rows(w), 0.0)
-    bend_cols = thick * second_cols(w)
-    return jnp.where(live, support * w + second_rows(bend_rows) + second_cols(bend_cols), 0.0)
-
-
-def geometric(w, live, nuu, nvv, nuv):
-    along_rows = row_after(w) - w
-    along_cols = col_after(w) - w
-    rows = nuu * along_rows + nuv * along_cols
-    cols = nvv * along_cols + nuv * along_rows
-    return jnp.where(live, row_before(rows) - rows + col_before(cols) - cols, 0.0)
+    return each(lambda a, b, c: a + b - (c + c), col_before(w), col_after(w), w)
+
+
+def stiffness(w, live_thick, thick, support):
+    bend_rows = times(live_thick, second_rows(w))
+    bend_cols = times(thick, second_cols(w))
+    return each(
+        lambda f, a, r, c: f * a + (r + c), support, w, second_rows(bend_rows), second_cols(bend_cols)
+    )
+
+
+def fluxes(w, stress):
+    along_rows = minus(row_after(w), w)
+    along_cols = minus(col_after(w), w)
+    nuu, nvv, nuv = stress
+    rows = each(lambda n, r, m, c: n * r + m * c, nuu, along_rows, nuv, along_cols)
+    cols = each(lambda n, c, m, r: n * c + m * r, nvv, along_cols, nuv, along_rows)
+    return along_rows, along_cols, rows, cols
+
+
+def geometric(w, stress):
+    _, _, rows, cols = fluxes(w, stress)
+    return each(
+        lambda rb, r, cb, c: (rb - r) + (cb - c), row_before(rows), rows, col_before(cols), cols
+    )
+
+
+def cut(value):
+    return [value[:, h * LANES : (h + 1) * LANES] for h in range(value.shape[1] // LANES)]
+
+
+def joined(w):
+    return jnp.concatenate(w, axis=1)
 
 
 def live_of(rows_ref, slot, shape):
     return iota(shape, 0) < rows_ref[slot]
 
 
+def masked(live, value):
+    return [jnp.where(live, p, 0.0) for p in cut(value)]
+
+
 def column_sums(product):
     return jnp.sum(product, axis=0, keepdims=True)
+
+
+def folded(w):
+    total = sum(w[1:], w[0])
+    return jnp.sum(total.reshape(total.shape[0] // 8, 8, LANES), axis=0)
 
 
 def packed(rows):
@@ -136,11 +186,16 @@
         jnp.where(iota(square, 0) == iota(square, 1), spread, 0.0), axis=1, keepdims=True
     )
     held[:, 3 * ncol :] = jnp.broadcast_to(column, (rows_dev, LANES)).astype(jnp.bfloat16)
-    for copy in planes:
+    tail = pl.ds(3 * ncol, LANES)
+    out = [pltpu.make_async_copy(held.at[:, tail], pay_ref.at[:, tail], sems.at[4])]
+    out[0].start()
+    for j in range(3):
+        planes[j].wait()
+        part = pl.ds(j * ncol, ncol)
+        out.append(pltpu.make_async_copy(held.at[:, part], pay_ref.at[:, part], sems.at[5 + j]))
+        out[-1].start()
+    for copy in out:
         copy.wait()
-    put = pltpu.make_async_copy(held, pay_ref, sems.at[4])
-    put.start()
-    put.wait()
 
 
 def edge_kernel(rows_ref, matched_ref, vec_ref, edge_ref):
@@ -162,37 +217,40 @@
     edge_ref[used:, :] = jnp.zeros((edge_ref.shape[0] - used, ncol), jnp.float32)
 
 
-def folded(product):
-    return jnp.sum(product.reshape(product.shape[0] // 8, 8, product.shape[1]), axis=0)
+FIRST = [("kxx", 0, 0), ("kxx", 0, 1), ("kxx", 1, 1), ("kpk", 0, 0), ("kpk", 0, 1), ("kpk", 1, 1)]
+FIRST += [("kuu", 2, 2), ("kuu", 2, 3), ("kuu", 3, 3)]
 
 
 def stiff_kernel(rows_ref, vec_ref, thick_ref, support_ref, k_ref, uk_ref, kuk_ref, prec_ref, sums_ref):
     slots = rows_ref.shape[0]
     rows_dev, ncol = thick_ref.shape
     prows = rows_dev // slots
-    sums_ref[...] = jnp.zeros_like(sums_ref)
-
-    def add(name, product):
-        k = 8 * AT[name]
-        sums_ref[k : k + 8, :] += folded(product)
-
+    totals = {}
     for s in range(slots):
         at = slice(s * prows, (s + 1) * prows)
-        live = live_of(rows_ref, s, (prows, ncol))
-        thick, support = thick_ref[at, :], support_ref[at, :]
-        prec_ref[at, :] = jnp.where(live, 1.0 / (support + 12.0 * thick), 0.0)
-        for v in range(2):
-            w = jnp.where(live, vec_ref[v, at, :], 0.0)
-            k_ref[v, at, :] = stiffness(w, live, thick, support)
-            uk_ref[v, at, :] = prec_ref[at, :] * k_ref[v, at, :]
-        for v in range(2):
-            kuk_ref[v, at, :] = stiffness(uk_ref[v, at, :], live, thick, support)
+        live = live_of(rows_ref, s, (prows, LANES))
+        thick, support = cut(thick_ref[at, :]), cut(support_ref[at, :])
+        live_thick = masked(live, thick_ref[at, :])
+        prec = each(lambda f, t: jnp.where(live, 1.0 / (f + 12.0 * t), 0.0), support, thick)
+        prec_ref[at, :] = joined(prec)
+        for v in range(2):
+            kw = stiffness(masked(live, vec_ref[v, at, :]), live_thick, thick, support)
+            k_ref[v, at, :] = joined(kw)
+            uk_ref[v, at, :] = joined(times(prec, kw))
+        for v in range(2):
+            kuk_ref[v, at, :] = joined(stiffness(cut(uk_ref[v, at, :]), live_thick, thick, support))
         for a in range(2):
-            wa = jnp.where(live, vec_ref[a, at, :], 0.0)
+            wa = masked(live, vec_ref[a, at, :])
             for b in range(a, 2):
-                add(("kxx", a, b), wa * k_ref[b, at, :])
-                add(("kpk", a, b), k_ref[a, at, :] * uk_ref[b, at, :])
-                add(("kuu", 2 + a, 2 + b), uk_ref[a, at, :] * kuk_ref[b, at, :])
+                for name, product in (
+                    (("kxx", a, b), times(wa, cut(k_ref[b, at, :]))),
+                    (("kpk", a, b), times(cut(k_ref[a, at, :]), cut(uk_ref[b, at, :]))),
+                    (("kuu", 2 + a, 2 + b), times(cut(uk_ref[a, at, :]), cut(kuk_ref[b, at, :]))),
+                ):
+                    part = folded(product)
+                    totals[name] = totals[name] + part if s else part
+    for k, name in enumerate(FIRST):
+        sums_ref[8 * k : 8 * k + 8, :] = totals[name]
 
 
 def interface_rows(own, top, bottom):
@@ -215,7 +273,7 @@
 
 def gram_kernel(
     rows_ref, matched_ref, arrived_ref, vec_ref, thick_ref, support_ref, prec_ref, k_in, uk_in, kuk_in, sums_in,
-    edge_ref, below_ref, above_ref, ug_ref, uk_ref, kuk_ref, stress_ref, out_ref, sums_ref, g_ref, k_ref,
+    edge_ref, below_ref, above_ref, ug_ref, uk_ref, kuk_ref, stress_ref, out_ref, g_ref, k_ref,
 ):
     slots = rows_ref.shape[0]
     rows_dev, ncol = prec_ref.shape
@@ -236,16 +294,16 @@
     )
     for j in range(3):
         stress_ref[j] = placed[:, j * ncol : (j + 1) * ncol]
-    sums_ref[...] = sums_in[...]
     rows_sent = 16 * slots
+    totals = {name: sums_in[8 * k : 8 * k + 8, :] for k, name in enumerate(FIRST)}
+    row_totals = {}
 
     def add(name, product):
-        k = 8 * AT[name]
-        sums_ref[k : k + 8, :] += folded(product)
+        part = folded(product)
+        totals[name] = totals[name] + part if name in totals else part
 
     def add_row(name, product):
-        k = 8 * AT[name]
-        sums_ref[k : k + 1, :] += product
+        row_totals[name] = row_totals[name] + product if name in row_totals else product
 
     def send(to, row):
         for h in range(halves):
@@ -254,6 +312,7 @@
     k_ref[...] = k_in[...]
     uk_ref[...] = uk_in[...]
     kuk_ref[...] = kuk_in[...]
+    late = []
     for s in range(slots):
         own_id, want_id = mine[s].astype(jnp.float32), match[s].astype(jnp.float32)
         places = edge_places(rows_ref, s, prows)
@@ -275,22 +334,30 @@
         for base, pair in ((0, (2, 3)), (last_tile, (0, 1))):
             start = s * prows + base
             at = pl.ds(pl.multiple_of(start, 8), 16)
-            row = iota((16, ncol), 0)
+            row = iota((16, LANES), 0)
             live = row + base < rows_ref[s]
-            parts = [
-                sum(jnp.where(row == places[i] - start, scaled[v][i], 0.0) for i in pair)
-                for v in range(2)
-            ]
-            thick, support = thick_ref[at, :], support_ref[at, :]
-            extra = [stiffness(part, live, thick, support) for part in parts]
+            parts = []
+            for v in range(2):
+                rows_cut = [cut(scaled[v][i]) for i in pair]
+                parts.append(
+                    [
+                        sum(jnp.where(row == places[i] - start, rows_cut[j][h], 0.0) for j, i in enumerate(pair))
+                        for h in range(halves)
+                    ]
+                )
+            thick, support = cut(thick_ref[at, :]), cut(support_ref[at, :])
+            live_thick = masked(live, thick_ref[at, :])
+            extra = [stiffness(part, live_thick, thick, support) for part in parts]
+            kuk = [cut(kuk_in[v, at, :]) for v in range(2)]
             for x in range(2):
+                ux = cut(uk_in[x, at, :])
                 for y in range(x, 2):
-                    k = 8 * AT["kuu", 2 + x, 2 + y]
-                    sums_ref[k : k + 8, :] += folded(
-                        uk_in[x, at, :] * extra[y] + parts[x] * (kuk_in[y, at, :] + extra[y])
+                    add(
+                        ("kuu", 2 + x, 2 + y),
+                        each(lambda u, e, p, k: u * e + p * (k + e), ux, extra[y], parts[x], kuk[y]),
                     )
             for v in range(2):
-                kuk_ref[v, at, :] += extra[v]
+                late.append((kuk_ref, v, at, joined(each(lambda k, e: k + e, kuk[v], extra[v]))))
         for a in range(2):
             for b in range(a, 2):
                 for i, row in enumerate(places):
@@ -299,69 +366,92 @@
                     add_row(("kpk", a, b), ka * scaled[b][i] + scaled[a][i] * (kb + added[b][i]))
         for v in range(2):
             for i, row in enumerate(places):
-                k_ref[v, pl.ds(row, 1), :] += added[v][i]
-                uk_ref[v, pl.ds(row, 1), :] += scaled[v][i]
+                at = pl.ds(row, 1)
+                late.append((k_ref, v, at, k_in[v, at, :] + added[v][i]))
+                late.append((uk_ref, v, at, uk_in[v, at, :] + scaled[v][i]))
+    for ref, v, at, value in late:
+        ref[v, at, :] = value
+    basis = [(ug_ref, 0), (ug_ref, 1), (uk_ref, 0), (uk_ref, 1)]
     for s in range(slots):
         at = slice(s * prows, (s + 1) * prows)
-        live = live_of(rows_ref, s, (prows, ncol))
-        thick, support = thick_ref[at, :], support_ref[at, :]
-        nuu, nvv, nuv = (stress_ref[j, at, :] for j in range(3))
-        for v in range(2):
-            w = jnp.where(live, vec_ref[v, at, :], 0.0)
-            g_ref[v, at, :] = geometric(w, live, nuu, nvv, nuv)
-            ug_ref[v, at, :] = prec_ref[at, :] * g_ref[v, at, :]
+        live = live_of(rows_ref, s, (prows, LANES))
+        stress = [cut(stress_ref[j, at, :]) for j in range(3)]
+        prec = cut(prec_ref[at, :])
+        gx = []
+        for v in range(2):
+            gx.append(geometric(masked(live, vec_ref[v, at, :]), stress))
+            ug_ref[v, at, :] = joined(times(prec, gx[v]))
+            g_ref[v, at, :] = joined(gx[v])
         for a in range(2):
-            wa = jnp.where(live, vec_ref[a, at, :], 0.0)
-            for b in range(a, 2):
-                add(("gxx", a, b), wa * g_ref[b, at, :])
-                add(("gpg", a, b), g_ref[a, at, :] * ug_ref[b, at, :])
+            wa = masked(live, vec_ref[a, at, :])
+            ga, ka, ua = cut(g_ref[a, at, :]), cut(k_ref[a, at, :]), cut(ug_ref[a, at, :])
             for b in range(2):
-                add(("kpg", a, b), k_ref[a, at, :] * ug_ref[b, at, :])
-                add(("kuu", a, 2 + b), ug_ref[a, at, :] * kuk_ref[b, at, :])
-        basis = [(ug_ref, 0), (ug_ref, 1), (uk_ref, 0), (uk_ref, 1)]
+                ub = cut(ug_ref[b, at, :])
+                if b >= a:
+                    add(("gxx", a, b), times(wa, cut(g_ref[b, at, :])))
+                    add(("gpg", a, b), times(ga, ub))
+                add(("kpg", a, b), times(ka, ub))
+                add(("kuu", a, 2 + b), times(ua, cut(kuk_ref[b, at, :])))
+        thick, support = cut(thick_ref[at, :]), cut(support_ref[at, :])
+        live_thick = masked(live, thick_ref[at, :])
         bends = []
         for v in range(2):
-            w = ug_ref[v, at, :]
-            bends.append((w, jnp.where(live, second_rows(w), 0.0), second_cols(w)))
+            w = cut(ug_ref[v, at, :])
+            bends.append((w, second_rows(w), second_cols(w)))
         for b in range(2):
             w, r, c = bends[b]
-            sw, tr, tc = support * w, thick * r, thick * c
+            sw, tr, tc = times(support, w), times(live_thick, r), times(thick, c)
             for a in range(b + 1):
-                add(("kuu", a, b), bends[a][0] * sw + bends[a][1] * tr + bends[a][2] * tc)
+                add(
+                    ("kuu", a, b),
+                    each(lambda u, x, p, y, q, z: u * x + p * y + q * z, bends[a][0], sw, bends[a][1], tr, bends[a][2], tc),
+                )
         first = []
-        for ref, v in basis:
-            w = ref[v, at, :]
-            first.append((row_after(w) - w, col_after(w) - w))
         for b in range(4):
-            r, c = first[b]
-            fr, fc = nuu * r + nuv * c, nvv * c + nuv * r
+            ref, v = basis[b]
+            r, c, fr, fc = fluxes(cut(ref[v, at, :]), stress)
+            first.append((r, c))
             for a in range(b + 1):
-                add(("guu", a, b), first[a][0] * fr + first[a][1] * fc)
+                add(("guu", a, b), each(lambda p, x, q, y: p * x + q * y, first[a][0], fr, first[a][1], fc))
         for i, row in enumerate(edge_places(rows_ref, s, prows)):
             for a, (ref, v) in enumerate(basis):
                 send(4 * (4 * s + a) + i, ref[v, pl.ds(row, 1), :])
     tag = halves * rows_sent
-    tile = packed([column_sums(sums_ref[8 * k : 8 * k + 8, :]) for k in range(len(NAMES))])
+    rows = []
+    for name in NAMES:
+        row = column_sums(totals[name])
+        if name in row_totals:
+            row = row + sum(cut(row_totals[name]))
+        rows.append(row)
+    tile = packed(rows)
     lane = iota(tile.shape, 1)
     for s in range(slots):
         tile = jnp.where(lane == LANES - slots + s, match[s].astype(jnp.float32), tile)
     out_ref[tag:, :] = tile
 
 
-def apply_kernel(rows_ref, thick_ref, support_ref, stress_ref, ug_ref, uk_ref, kug_ref, gu_ref):
+def apply_kernel(
+    rows_ref, vec_ref, thick_ref, support_ref, prec_ref, stress_ref, ug_ref, uk_ref, kuk_ref,
+    a_ref, b_ref, c_ref, d_ref,
+):
     slots = rows_ref.shape[0]
     rows_dev, ncol = thick_ref.shape
     prows = rows_dev // slots
     for s in range(slots):
         at = slice(s * prows, (s + 1) * prows)
-        live = live_of(rows_ref, s, (prows, ncol))
-        thick, support = thick_ref[at, :], support_ref[at, :]
-        nuu, nvv, nuv = (stress_ref[j, at, :] for j in range(3))
-        for a, (ref, v) in enumerate([(ug_ref, 0), (ug_ref, 1), (uk_ref, 0), (uk_ref, 1)]):
-            w = ref[v, at, :]
-            gu_ref[a, at, :] = geometric(w, live, nuu, nvv, nuv)
-            if a < 2:
-                kug_ref[v, at, :] = stiffness(w, live, thick, support)
+        live = live_of(rows_ref, s, (prows, LANES))
+        thick, support = cut(thick_ref[at, :]), cut(support_ref[at, :])
+        live_thick = masked(live, thick_ref[at, :])
+        prec = cut(prec_ref[at, :])
+        stress = [cut(stress_ref[j, at, :]) for j in range(3)]
+        for v in range(2):
+            x, ug, uk = masked(live, vec_ref[v, at, :]), cut(ug_ref[v, at, :]), cut(uk_ref[v, at, :])
+            gg, gk = geometric(ug, stress), geometric(uk, stress)
+            kg = stiffness(ug, live_thick, thick, support)
+            a_ref[v, at, :] = joined(each(lambda w, u, p, g: w + (u + u) + p * g, x, ug, prec, gg))
+            b_ref[v, at, :] = joined(each(lambda u, p, g: u + p * g, uk, prec, gk))
+            c_ref[v, at, :] = joined(each(lambda u, p, k: u + p * k, uk, prec, kg))
+            d_ref[v, at, :] = joined(times(prec, cut(kuk_ref[v, at, :])))
 
 
 def strip_of(ref, at, rows, slots):
@@ -377,7 +467,7 @@
 
 
 def line_kernel(slots, *refs):
-    line, out_ref = refs[:-1], refs[-1]
+    line, out_ref = refs[:-2], refs[-1]
     owners = len(line)
     tag = line[0].shape[0] - 8
     me = lax.axis_index("patch")
@@ -406,11 +496,11 @@
     out_ref[...] = total + packed([sums[pair] for pair in UU])
 
 
-def join_kernel(slots, rows_ref, matched_ref, *refs):
-    line, (kug_in, kuk_in, kug_ref, kuk_ref) = refs[:-4], refs[-4:]
-    kug_ref[...] = kug_in[...]
-    kuk_ref[...] = kuk_in[...]
-    rows_dev, ncol = kug_in.shape[1:]
+def join_kernel(slots, rows_ref, matched_ref, prec_ref, *refs):
+    line, (c_in, d_in, c_ref, d_ref) = refs[:-4], refs[-4:]
+    c_ref[...] = c_in[...]
+    d_ref[...] = d_in[...]
+    rows_dev, ncol = c_in.shape[1:]
     prows = rows_dev // slots
     owners = len(line)
     mine, match = place(rows_ref, matched_ref, slots)
@@ -428,9 +518,9 @@
                     strip = strip_of(line[near], 4 * (4 * t + a), 4, slots)
                     top = top + jnp.where(wanted_of(line[near], t, slots) == own_id, strip[0:2], 0.0)
                     bottom = bottom + jnp.where(want_id == there * slots + t, strip[2:4], 0.0)
-            ref = kug_ref if a < 2 else kuk_ref
+            ref = c_ref if a < 2 else d_ref
             for row, added in zip(places, interface_rows(own, top, bottom)):
-                ref[a % 2, pl.ds(row, 1), :] += added
+                ref[a % 2, pl.ds(row, 1), :] += prec_ref[pl.ds(row, 1), :] * added
 
 
 def form(table, left, right):
@@ -444,12 +534,9 @@
     return total
 
 
-def final_kernel(
-    cells, rows_ref, total_ref, vec_ref, ug_ref, uk_ref, prec_ref, kug_ref, kuk_ref, gu_ref, out_ref
-):
-    slots = rows_ref.shape[0]
-    rows_dev, ncol = prec_ref.shape
-    prows = rows_dev // slots
+def final_kernel(cells, total_ref, a_ref, b_ref, c_ref, d_ref, out_ref, held, sems):
+    rows_dev, ncol = a_ref.shape[1:]
+    prows = rows_dev // 2
     total = total_ref[...]
 
     def value(*name):
@@ -508,31 +595,26 @@
         {i: scales[0] * f for i, f in new_first.items()},
         {i: scales[1] * (f - r * new_first[i] if i in new_first else f) for i, f in new_second.items()},
     ]
-    for s in range(slots):
-        at = slice(s * prows, (s + 1) * prows)
-        live = live_of(rows_ref, s, (prows, ncol))
-        basis = [jnp.where(live, vec_ref[v, at, :], 0.0) for v in range(2)]
-        basis += [ug_ref[v, at, :] for v in range(2)] + [uk_ref[v, at, :] for v in range(2)]
-        for v in range(2):
-            coef = dict(lead[v])
+    copies = []
+    for s in range(2):
+        at = pl.ds(s * prows, prows)
+        for v in range(2):
+            acc = None
             for i in (0, 1):
                 if i in lead[v]:
-                    coef[2 + i] = coef[2 + i] + lead[v][i]
-                    coef[4 + i] = coef[4 + i] - mus[v] * lead[v][i]
-            acc = inside = None
-            for i, f in coef.items():
-                term = f * basis[i]
-                acc = term if acc is None else acc + term
-            for i in range(2, 6):
-                if i in lead[v]:
-                    k_part = kug_ref[i - 2, at, :] if i < 4 else kuk_ref[i - 4, at, :]
-                    term = lead[v][i] * gu_ref[i - 2, at, :] - (lead[v][i] * mus[v]) * k_part
-                    inside = term if inside is None else inside + term
-            out_ref[v, at, :] = acc + prec_ref[at, :] * inside
+                    f, g = lead[v][i], lead[v][4 + i]
+                    term = f * a_ref[i, at, :] + g * b_ref[i, at, :]
+                    term = term - ((mus[v] * f) * c_ref[i, at, :] + (mus[v] * g) * d_ref[i, at, :])
+                    acc = term if acc is None else acc + term
+            held[v, at, :] = acc
+            copies.append(pltpu.make_async_copy(held.at[v, at, :], out_ref.at[v, at, :], sems.at[2 * s + v]))
+            copies[-1].start()
+    for copy in copies:
+        copy.wait()
 
 
 def call(body, outs, kinds, scratch=(), flops=1_000_000, out_kind="v"):
-    spaces = {"s": pltpu.SMEM, "v": pltpu.VMEM, "h": pltpu.HBM}
+    spaces = {"s": pltpu.SMEM, "v": pltpu.VMEM, "h": pltpu.HBM, "a": pl.ANY}
     return pl.pallas_call(
         body,
         out_shape=[pltpu.HBM(s, d) if out_kind == "h" else jax.ShapeDtypeStruct(s, d) for s, d in outs],
@@ -553,7 +635,7 @@
     cells = float(owners * inner * rows_dev * ncol)
     field = ((2, rows_dev, ncol), f32)
     one = ((rows_dev, ncol), f32)
-    sums = ((8 * SUMS, ncol), f32)
+    sums = ((8 * len(FIRST), LANES), f32)
     tile = ((8, LANES), f32)
 
     width = 3 * ncol + LANES
@@ -564,7 +646,7 @@
         [
             pltpu.VMEM((1, rows_dev), jnp.int32),
             pltpu.VMEM((rows_dev, width), bf16),
-            pltpu.SemaphoreType.DMA((5,)),
+            pltpu.SemaphoreType.DMA((8,)),
         ],
         out_kind="h",
     )(
@@ -586,23 +668,27 @@
         gram_kernel,
         [field, field, field, ((3, rows_dev, ncol), f32), ((sent_rows, LANES), f32)],
         "ssvvvvvvvvvvvv",
-        [pltpu.VMEM(sums[0], f32), pltpu.VMEM(field[0], f32), pltpu.VMEM(field[0], f32)],
+        [pltpu.VMEM(field[0], f32), pltpu.VMEM(field[0], f32)],
     )(
         patch_rows, matched, arrived, vectors, thickness, foundation, prec, k_x, u_k, k_uk, part,
         edges, below, above,
     )
     line = [sent] + [passed_along(sent, "patch", by) for by in range(1, owners)]
-    k_ug, g_u = call(apply_kernel, [field, ((4, rows_dev, ncol), f32)], "svvvvv")(
-        patch_rows, thickness, foundation, stress, u_g, u_k
-    )
-    (total,) = call(functools.partial(line_kernel, slots), [tile], "v" * owners)(*line)
-    total = summed_over(summed_over(total, "half"), "sub")
-    k_ug, k_uk = call(functools.partial(join_kernel, slots), [field, field], "ss" + "v" * (owners + 2))(
-        patch_rows, matched, *line, k_ug, k_uk
-    )
-    (modes,) = call(functools.partial(final_kernel, cells), [field], "svvvvvvvv")(
-        patch_rows, total, vectors, u_g, u_k, prec, k_ug, k_uk, g_u
-    )
+    a, b, c, d = call(apply_kernel, [field] * 4, "svvvvvvvv")(
+        patch_rows, vectors, thickness, foundation, prec, stress, u_g, u_k, k_uk
+    )
+    (total,) = call(functools.partial(line_kernel, slots), [tile], "v" * owners + "a")(*line, a)
+    total = summed_over_both(total, "sub", "half")
+    c, d = call(functools.partial(join_kernel, slots), [field, field], "ssv" + "v" * (owners + 2))(
+        patch_rows, matched, prec, *line, c, d
+    )
+    (modes,) = call(
+        functools.partial(final_kernel, cells),
+        [field],
+        "vvvvv",
+        [pltpu.VMEM(field[0], f32), pltpu.SemaphoreType.DMA((4,))],
+        out_kind="h",
+    )(total, a, b, c, d)
     return modes
 
 

time: 45.9 us -> 41.2 us (0.90)
  waiting for transfers between devices: 11.6 us -> 9.7 us
  local copies, waits for them, and re-layouts: 1.72 us -> 0.03 us
  Pallas kernels: 14.9 us -> 13.5 us
    ppermute x7 -> x5, waiting for transfers between devices: 11.4 us -> 8.42 us  [passed_along(): lax.ppermute(array, axis, [(i, (i + by) % peers) for i in range(peers)])]
    ppermute x0 -> x3, starting transfers between devices: none -> 1.86 us  [summed_over_both(): total = total + lax.ppermute(array, (outer, inner), pairs)]
    unnamed x14 -> x10, local copies, waits for them, and re-layouts: 1.72 us -> 0.03 us
    ppermute x7 -> x5, starting transfers between devices: 9.68 us -> 8.2 us  [passed_along(): lax.ppermute(array, axis, [(i, (i + by) % peers) for i in range(peers)])]
    ppermute x0 -> x3, waiting for transfers between devices: none -> 1.06 us  [summed_over_both(): total = total + lax.ppermute(array, (outer, inner), pairs)]
    pallas_call x4, Pallas kernels: 6.11 us -> 5.12 us  [the longest x1 2.63 us: per_device(): call(apply_kernel, [field] * 4, 'svvvvvvvv')]
  transfers between devices with their start and end apart: 8 -> 9, of which waited for: 6 -> 6; matrix products, arithmetic and copies ran while one was open for 0% -> 0% of each run, Pallas kernels for 15% -> 16%
where the time goes in v4:
time: 41.2 us; the launch traced here: 40.9 us
  starting transfers between devices  17.6 us (43%)
  Pallas kernels  13.5 us (33%)
  waiting for transfers between devices  9.7 us (24%)
    ppermute x5, waiting for transfers between devices, passed_along(): lax.ppermute(array, axis, [(i, (i + by) % peers) for i in range(peers)])  8.42 us
    ppermute x5, starting transfers between devices, passed_along(): lax.ppermute(array, axis, [(i, (i + by) % peers) for i in range(peers)])  8.2 us
    all_to_all x1, starting transfers between devices, per_device(): lax.all_to_all(payload, ('patch', 'sub', 'half'), split_axis=0, concat_ax...  7.5 us
    pallas_call x1, Pallas kernels, per_device(): call(gram_kernel, [field, field, field, ((3, rows_dev, ncol), f32), ((sen...  3.47 us
    pallas_call x1, Pallas kernels, per_device(): call(apply_kernel, [field] * 4, 'svvvvvvvv')  2.63 us
    pallas_call x1, Pallas kernels, per_device(): call(stiff_kernel, [field, field, field, one, sums], 'svvv')  2.56 us
    ppermute x3, starting transfers between devices, summed_over_both(): total = total + lax.ppermute(array, (outer, inner), pairs)  1.86 us
    pallas_call x1, Pallas kernels, per_device(): call(pack_kernel, [((rows_dev, width), bf16)], 'hh', [pltpu.VMEM((1, rows...  1.77 us
  transfers between devices with their start and end apart: 9, of which 6 were waited for; matrix products, arithmetic and copies ran while one was open for 0% of the time, Pallas kernels for 16%

profile of v4, /device:TPU:0, one launch (start us, length us, event | category | flops | bytes accessed | tf_op | source)
XLA Modules:
  0.0 40.9 jit_solution(10000873084719001618)
XLA Ops:
  0.0 1.8 %shard_map.73 = bf16[256,896]{1,0:T(8,128)(2,1)} custom-call(bf16[3,256,256]{2,1,0:T(8,128)(2,1)} %bitcast.6, s32[1,256]{1,0:T(1,128)} %bitcast.7), custom_call_target="tpu_custom_call" | custom-call | flops 1000000 | bytes 2000000 | tf_op jit(solution)/shard_map/pallas_call | solution.py:642
  1.8 0.0 copy-start.4
  1.8 7.5 %all-to-all-start = ((bf16[16,16,896]{2,1,0:T(8,128)(2,1)}), bf16[16,16,896]{2,1,0:T(8,128)(2,1)S(1)}, u32[]{:S(2)}, u32[]{:S(2)}) async-start(bf16[16,16,896]{2,1,0:T(8,128)(2,1)} %bitcast.5), calls=%async_computation | async-start | bytes 917504 | tf_op jit(solution)/shard_map/all_to_all | solution.py:656
  9.4 0.0 copy-start.1
  9.4 0.6 %shard_map.75.edge_ref = f32[24,256]{1,0:T(8,128)S(1)} custom-call(s32[2]{0:T(128)S(1)} %copy-done.3, s32[2]{0:T(128)S(1)} %copy-done.4, f32[2,256,256]{2,1,0:T(8,128)S(1)} %copy-done), custom_call_target="tpu_custom_call" | custom-call | flops 1000000 | bytes 2000000 | tf_op jit(solution)/shard_map/pallas_call | solution.py:660
  10.0 3.8 %collective-permute-start.1 = (f32[24,256]{1,0:T(8,128)S(1)}, f32[24,256]{1,0:T(8,128)S(1)}, u32[]{:S(2)}, u32[]{:S(2)}) collective-permute-start(f32[24,256]{1,0:T(8,128)S(1)} %shard_map.75.edge_ref), channel_id=1, source_target_pairs={{0,12},{4,0},{8,4},{12,8},{1,13},{5,1},{9,5},{13,9},{2,14},{6,2},{... | collective-permute-start | bytes 73736 | tf_op jit(solution)/shard_map/ppermute | solution.py:32
  13.7 2.6 %shard_map.74 = (f32[2,256,256]{2,1,0:T(8,128)S(1)}, f32[2,256,256]{2,1,0:T(8,128)S(1)}, f32[2,256,256]{2,1,0:T(8,128)S(1)}, f32[256,256]{1,0:T(8,128)S(1)}, f32[72,128]{1,0:T(8,128)S(1)}) custom-call(s32[2]{0:T(128)S(1)} %copy-done.3, f32[2,256,256]{2,1,0:T(8,128)S(1)} %copy-done, f32[256,256]{1,0:T(8,128)S(1)} %copy-done.1, f32[256,256]{1,0:T(8,128)S(1)} %copy-done.2), custom_call_target="tpu_custom_call" | custom-call | flops 1000000 | bytes 2000000 | tf_op jit(solution)/shard_map/pallas_call | solution.py:663
  16.3 2.2 %collective-permute-done.1.above_ref = f32[24,256]{1,0:T(8,128)S(1)} collective-permute-done((f32[24,256]{1,0:T(8,128)S(1)}, f32[24,256]{1,0:T(8,128)S(1)}, u32[]{:S(2)}, u32[]{:S(2)}) %collective-permute-start.1) | collective-permute-done | bytes 24608 | tf_op jit(solution)/shard_map/ppermute | solution.py:32
  18.5 4.3 %collective-permute-done.below_ref = f32[24,256]{1,0:T(8,128)S(1)} collective-permute-done((f32[24,256]{1,0:T(8,128)S(1)}, f32[24,256]{1,0:T(8,128)S(1)}, u32[]{:S(2)}, u32[]{:S(2)}) %collective-permute-start) | collective-permute-done | bytes 24608 | tf_op jit(solution)/shard_map/ppermute | solution.py:32
  22.8 0.2 all-to-all-done
  23.0 3.5 %shard_map.76 = (f32[2,256,256]{2,1,0:T(8,128)S(1)}, f32[2,256,256]{2,1,0:T(8,128)S(1)}, f32[2,256,256]{2,1,0:T(8,128)S(1)}, f32[3,256,256]{2,1,0:T(8,128)S(1)}, f32[72,128]{1,0:T(8,128)S(1)}) custom-call(s32[2]{0:T(128)S(1)} %copy-done.3, s32[2]{0:T(128)S(1)} %copy-done.4, bf16[256,896]{1,0:T(8,128)(2,1)S(1)} %bitcast.4, f32[2,256,256]{2,1,0:T(8,128)S(1)} %copy-done, ...), custom_call_target="tpu_custom_call" | custom-call | flops 1000000 | bytes 2000000 | tf_op jit(solution)/shard_map/pallas_call | solution.py:667
  26.5 1.5 %collective-permute-start.4 = (f32[72,128]{1,0:T(8,128)S(1)}, f32[72,128]{1,0:T(8,128)S(1)}, u32[]{:S(2)}, u32[]{:S(2)}) collective-permute-start(f32[72,128]{1,0:T(8,128)S(1)} %get-tuple-element.26.refs_0_), channel_id=1, source_target_pairs={{0,12},{4,0},{8,4},{12,8},{1,13},{5,1},{9,5},{13,9},{2,14},{6,2},{... | collective-permute-start | bytes 110600 | tf_op jit(solution)/shard_map/ppermute | solution.py:32
  28.0 1.8 %collective-permute-start.3 = (f32[72,128]{1,0:T(8,128)S(1)}, f32[72,128]{1,0:T(8,128)S(1)}, u32[]{:S(2)}, u32[]{:S(2)}) collective-permute-start(f32[72,128]{1,0:T(8,128)S(1)} %get-tuple-element.26.refs_0_), channel_id=1, source_target_pairs={{0,8},{4,12},{8,0},{12,4},{1,9},{5,13},{9,1},{13,5},{2,10},{6,14},... | collective-permute-start | bytes 110600 | tf_op jit(solution)/shard_map/ppermute | solution.py:32
  29.7 1.2 %collective-permute-start.2 = (f32[72,128]{1,0:T(8,128)S(1)}, f32[72,128]{1,0:T(8,128)S(1)}, u32[]{:S(2)}, u32[]{:S(2)}) collective-permute-start(f32[72,128]{1,0:T(8,128)S(1)} %get-tuple-element.26.refs_0_), channel_id=1, source_target_pairs={{0,4},{4,8},{8,12},{12,0},{1,5},{5,9},{9,13},{13,1},{2,6},{6,10},{... | collective-permute-start | bytes 110600 | tf_op jit(solution)/shard_map/ppermute | solution.py:32
  30.9 2.6 %shard_map.77 = (f32[2,256,256]{2,1,0:T(8,128)S(1)}, f32[2,256,256]{2,1,0:T(8,128)S(1)}, f32[2,256,256]{2,1,0:T(8,128)S(1)}, f32[2,256,256]{2,1,0:T(8,128)S(1)}) custom-call(s32[2]{0:T(128)S(1)} %copy-done.3, f32[2,256,256]{2,1,0:T(8,128)S(1)} %copy-done, f32[256,256]{1,0:T(8,128)S(1)} %copy-done.1, f32[256,256]{1,0:T(8,128)S(1)} %copy-done.2, ...), custom_call_target="tpu_custom_call" | custom-call | flops 1000000 | bytes 2000000 | tf_op jit(solution)/shard_map/pallas_call | solution.py:677
  33.6 1.9 %collective-permute-done.2.refs_1_ = f32[72,128]{1,0:T(8,128)S(1)} collective-permute-done((f32[72,128]{1,0:T(8,128)S(1)}, f32[72,128]{1,0:T(8,128)S(1)}, u32[]{:S(2)}, u32[]{:S(2)}) %collective-permute-start.2) | collective-permute-done | bytes 36896 | tf_op jit(solution)/shard_map/ppermute | solution.py:32
  35.5 0.4 %shard_map.78 = f32[8,128]{1,0:T(8,128)S(1)} custom-call(f32[72,128]{1,0:T(8,128)S(1)} %get-tuple-element.26.refs_0_, f32[72,128]{1,0:T(8,128)S(1)} %collective-permute-done.2.refs_1_, f32[72,128]{1,0:T(8,128)S(1)} %collective-permute-done.3.refs_2_, f32[72,128]{1,0:T(8,128)S(1)} %collective-permute-done.4.refs_3_, ...), custom_call_target="tpu_custom_call" | custom-call | flops 1000000 | bytes 2000000 | tf_op jit(solution)/shard_map/pallas_call | solution.py:680
  35.9 0.0 collective-permute-start.7
  36.0 1.5 %collective-permute-start.6 = (f32[8,128]{1,0:T(8,128)S(1)}, f32[8,128]{1,0:T(8,128)S(1)}, u32[]{:S(2)}, u32[]{:S(2)}) collective-permute-start(f32[8,128]{1,0:T(8,128)S(1)} %shard_map.78), channel_id=1, source_target_pairs={{0,2},{1,3},{2,0},{3,1},{4,6},{5,7},{6,4},{7,5},{8,10},{9,11},{10,... | collective-permute-start | bytes 12296 | tf_op jit(solution)/shard_map/ppermute | solution.py:43
  37.5 0.3 collective-permute-start.5
  37.8 0.8 %shard_map.79 = (f32[2,256,256]{2,1,0:T(8,128)S(1)}, f32[2,256,256]{2,1,0:T(8,128)S(1)}) custom-call(s32[2]{0:T(128)S(1)} %copy-done.3, s32[2]{0:T(128)S(1)} %copy-done.4, f32[256,256]{1,0:T(8,128)S(1)} %get-tuple-element.21.prec_ref, f32[72,128]{1,0:T(8,128)S(1)} %get-tuple-element.26.refs_0_, f32[72,128]{1,0:T(8,128)S(1)} %collective-permute-done.2.refs_1_, ...), custom_call_target="tpu_custom_call" | custom-call | flops 1000000 | bytes 2000000 | tf_op jit(solution)/shard_map/pallas_call | solution.py:682
  38.6 0.4 %collective-permute-done.7 = f32[8,128]{1,0:T(8,128)S(1)} collective-permute-done((f32[8,128]{1,0:T(8,128)S(1)}, f32[8,128]{1,0:T(8,128)S(1)}, u32[]{:S(2)}, u32[]{:S(2)}) %collective-permute-start.7) | collective-permute-done | bytes 4128 | tf_op jit(solution)/shard_map/ppermute | solution.py:43
  39.0 0.6 %collective-permute-done.6 = f32[8,128]{1,0:T(8,128)S(1)} collective-permute-done((f32[8,128]{1,0:T(8,128)S(1)}, f32[8,128]{1,0:T(8,128)S(1)}, u32[]{:S(2)}, u32[]{:S(2)}) %collective-permute-start.6) | collective-permute-done | bytes 4128 | tf_op jit(solution)/shard_map/ppermute | solution.py:43
  39.6 1.3 %shard_map.80 = f32[2,256,256]{2,1,0:T(8,128)} custom-call(f32[8,128]{1,0:T(8,128)S(1)} %add_add_fusion.total_ref, f32[2,256,256]{2,1,0:T(8,128)S(1)} %get-tuple-element.31.refs_4_.a_ref, f32[2,256,256]{2,1,0:T(8,128)S(1)} %get-tuple-element.32.b_ref, f32[2,256,256]{2,1,0:T(8,128)S(1)} %get-tuple-element.35.c_ref, f32[2,256,256]{2,1,0:T(8,128)S(1)} %get-tuple-element.36.d_ref), custom_call_target="tpu_custom_call" | custom-call | flops 1000000 | bytes 2000000 | tf_op jit(solution)/shard_map/pallas_call | solution.py:685
  (13 shorter events, 0.0 us)
Async XLA Ops:
  1.8 7.5 %copy-start = (f32[2,256,256]{2,1,0:T(8,128)S(1)}, f32[2,256,256]{2,1,0:T(8,128)}, u32[]{:S(2)}) copy-start(f32[2,256,256]{2,1,0:T(8,128)} %vec_ref.7) | copy-start | bytes 1572868
  1.8 7.5 %copy-start.3 = (s32[2]{0:T(128)S(1)}, s32[2]{0:T(128)}, u32[]{:S(2)}) copy-start(s32[2]{0:T(128)} %rows_ref.9) | copy-start | bytes 28
  1.8 7.5 %copy-start.4 = (s32[2]{0:T(128)S(1)}, s32[2]{0:T(128)}, u32[]{:S(2)}) copy-start(s32[2]{0:T(128)} %matched_ref.5) | copy-start | bytes 28
  1.8 21.2 %all-to-all-start = ((bf16[16,16,896]{2,1,0:T(8,128)(2,1)}), bf16[16,16,896]{2,1,0:T(8,128)(2,1)S(1)}, u32[]{:S(2)}, u32[]{:S(2)}) async-start(bf16[16,16,896]{2,1,0:T(8,128)(2,1)} %bitcast.5), calls=%async_computation | async-start | bytes 917504 | tf_op jit(solution)/shard_map/all_to_all | solution.py:656
  9.4 4.4 %copy-start.1 = (f32[256,256]{1,0:T(8,128)S(1)}, f32[256,256]{1,0:T(8,128)}, u32[]{:S(2)}) copy-start(f32[256,256]{1,0:T(8,128)} %thick_ref.5) | copy-start | bytes 786436
  9.4 4.4 %copy-start.2 = (f32[256,256]{1,0:T(8,128)S(1)}, f32[256,256]{1,0:T(8,128)}, u32[]{:S(2)}) copy-start(f32[256,256]{1,0:T(8,128)} %support_ref.5) | copy-start | bytes 786436
  10.0 8.5 %collective-permute-start.1 = (f32[24,256]{1,0:T(8,128)S(1)}, f32[24,256]{1,0:T(8,128)S(1)}, u32[]{:S(2)}, u32[]{:S(2)}) collective-permute-start(f32[24,256]{1,0:T(8,128)S(1)} %shard_map.75.edge_ref), channel_id=1, source_target_pairs={{0,12},{4,0},{8,4},{12,8},{1,13},{5,1},{9,5},{13,9},{2,14},{6,2},{... | collective-permute-start | bytes 73736 | tf_op jit(solution)/shard_map/ppermute | solution.py:32
  13.7 9.1 %collective-permute-start = (f32[24,256]{1,0:T(8,128)S(1)}, f32[24,256]{1,0:T(8,128)S(1)}, u32[]{:S(2)}, u32[]{:S(2)}) collective-permute-start(f32[24,256]{1,0:T(8,128)S(1)} %shard_map.75.edge_ref), channel_id=1, source_target_pairs={{0,4},{4,8},{8,12},{12,0},{1,5},{5,9},{9,13},{13,1},{2,6},{6,10},{... | collective-permute-start | bytes 73736 | tf_op jit(solution)/shard_map/ppermute | solution.py:32
  26.5 7.1 %collective-permute-start.4 = (f32[72,128]{1,0:T(8,128)S(1)}, f32[72,128]{1,0:T(8,128)S(1)}, u32[]{:S(2)}, u32[]{:S(2)}) collective-permute-start(f32[72,128]{1,0:T(8,128)S(1)} %get-tuple-element.26.refs_0_), channel_id=1, source_target_pairs={{0,12},{4,0},{8,4},{12,8},{1,13},{5,1},{9,5},{13,9},{2,14},{6,2},{... | collective-permute-start | bytes 110600 | tf_op jit(solution)/shard_map/ppermute | solution.py:32
  28.0 5.6 %collective-permute-start.3 = (f32[72,128]{1,0:T(8,128)S(1)}, f32[72,128]{1,0:T(8,128)S(1)}, u32[]{:S(2)}, u32[]{:S(2)}) collective-permute-start(f32[72,128]{1,0:T(8,128)S(1)} %get-tuple-element.26.refs_0_), channel_id=1, source_target_pairs={{0,8},{4,12},{8,0},{12,4},{1,9},{5,13},{9,1},{13,5},{2,10},{6,14},... | collective-permute-start | bytes 110600 | tf_op jit(solution)/shard_map/ppermute | solution.py:32
  29.7 5.8 %collective-permute-start.2 = (f32[72,128]{1,0:T(8,128)S(1)}, f32[72,128]{1,0:T(8,128)S(1)}, u32[]{:S(2)}, u32[]{:S(2)}) collective-permute-start(f32[72,128]{1,0:T(8,128)S(1)} %get-tuple-element.26.refs_0_), channel_id=1, source_target_pairs={{0,4},{4,8},{8,12},{12,0},{1,5},{5,9},{9,13},{13,1},{2,6},{6,10},{... | collective-permute-start | bytes 110600 | tf_op jit(solution)/shard_map/ppermute | solution.py:32
  35.9 3.1 %collective-permute-start.7 = (f32[8,128]{1,0:T(8,128)S(1)}, f32[8,128]{1,0:T(8,128)S(1)}, u32[]{:S(2)}, u32[]{:S(2)}) collective-permute-start(f32[8,128]{1,0:T(8,128)S(1)} %shard_map.78), channel_id=1, source_target_pairs={{0,3},{1,2},{2,1},{3,0},{4,7},{5,6},{6,5},{7,4},{8,11},{9,10},{10,... | collective-permute-start | bytes 12296 | tf_op jit(solution)/shard_map/ppermute | solution.py:43
  36.0 3.7 %collective-permute-start.6 = (f32[8,128]{1,0:T(8,128)S(1)}, f32[8,128]{1,0:T(8,128)S(1)}, u32[]{:S(2)}, u32[]{:S(2)}) collective-permute-start(f32[8,128]{1,0:T(8,128)S(1)} %shard_map.78), channel_id=1, source_target_pairs={{0,2},{1,3},{2,0},{3,1},{4,6},{5,7},{6,4},{7,5},{8,10},{9,11},{10,... | collective-permute-start | bytes 12296 | tf_op jit(solution)/shard_map/ppermute | solution.py:43
  37.5 2.1 %collective-permute-start.5 = (f32[8,128]{1,0:T(8,128)S(1)}, f32[8,128]{1,0:T(8,128)S(1)}, u32[]{:S(2)}, u32[]{:S(2)}) collective-permute-start(f32[8,128]{1,0:T(8,128)S(1)} %shard_map.78), channel_id=1, source_target_pairs={{0,1},{1,0},{2,3},{3,2},{4,5},{5,4},{6,7},{7,6},{8,9},{9,8},{10,11... | collective-permute-start | bytes 12296 | tf_op jit(solution)/shard_map/ppermute | solution.py:43

commit v5 on v4

--- a/solution.py
+++ b/solution.py
@@ -32,6 +32,15 @@
     return lax.ppermute(array, axis, [(i, (i + by) % peers) for i in range(peers)])
 
 
+def line_shared(array, axis):
+    peers = lax.axis_size(axis)
+    if peers == 4:
+        shared = [lax.ppermute(array, axis, [(i, i ^ k) for i in range(4)]) for k in (1, 2, 3)]
+        return [array] + shared, [(k ^ 1, k ^ 3) for k in range(4)]
+    shared = [passed_along(array, axis, k) for k in range(1, peers)]
+    return [array] + shared, [tuple(sorted({(k + 1) % peers, (k - 1) % peers})) for k in range(peers)]
+
+
 def summed_over_both(array, outer, inner):
     across, within = lax.axis_size(outer), lax.axis_size(inner)
     shifts = [(o, i) for o in range(across) for i in range(within)]
@@ -161,8 +170,62 @@
     return mine, match
 
 
-def label(number, ncol):
-    return jnp.full((1, ncol), number, jnp.int32).astype(jnp.float32)
+STACK = 8
+
+
+def edge_row(rows_ref, slot, side, depth, prows):
+    return slot * prows + (rows_ref[slot] - 1 - depth if side else depth)
+
+
+def stacked(rows_ref, prows):
+    return [(4 * s + 2 * v + side, v, s, side) for s in range(2) for v in range(2) for side in range(2)]
+
+
+def labels_of(rows_ref, matched_ref):
+    mine, match = place(rows_ref, matched_ref, 2)
+    row = iota((STACK, LANES), 0)
+    label = jnp.full((STACK, LANES), 0, jnp.int32)
+    for s in range(2):
+        for side, number in enumerate((mine[s], match[s])):
+            label = jnp.where((row // 4 == s) & (row % 2 == side), number, label)
+    return label.astype(jnp.float32)
+
+
+def other_side(stack):
+    row = iota(stack.shape, 0)
+    return jnp.where(row % 2 == 0, pltpu.roll(stack, STACK - 1, 0), pltpu.roll(stack, 1, 0))
+
+
+def other_vector(w):
+    row = iota(w[0].shape, 0)
+    return [jnp.where(row // 2 % 2 == 0, pltpu.roll(p, STACK - 2, 0), pltpu.roll(p, 2, 0)) for p in w]
+
+
+def opposite(label, near):
+    found = None
+    for labels, stacks in near:
+        turned, parts = other_side(labels), [[other_side(p) for p in w] for w in stacks]
+        for shift in (0, 4):
+            if shift:
+                turned, parts = pltpu.roll(turned, 4, 0), [[pltpu.roll(p, 4, 0) for p in w] for w in parts]
+            here = turned == label
+            picked = [[jnp.where(here, p, 0.0) for p in w] for w in parts]
+            found = picked if found is None else [each(lambda x, y: x + y, f, p) for f, p in zip(found, picked)]
+    return found
+
+
+def meeting(own, met):
+    jump = minus(own[0], met[0])
+    slope = each(lambda a, b, c, d: (a + b) - (c + d), own[0], met[0], own[1], met[1])
+    return jump, slope
+
+
+def interface_rows(own, met):
+    jump, slope = meeting(own, met)
+    return (
+        each(lambda j, m: penalty_value * j + penalty_slope * m, jump, slope),
+        [-penalty_slope * m for m in slope],
+    )
 
 
 def pack_kernel(stress_ref, elem_ref, pay_ref, elem, held, sems):
@@ -199,29 +262,27 @@
 
 
 def edge_kernel(rows_ref, matched_ref, vec_ref, edge_ref):
-    slots = rows_ref.shape[0]
     rows_dev, ncol = vec_ref.shape[1:]
-    prows = rows_dev // slots
-    mine, match = place(rows_ref, matched_ref, slots)
-    for s in range(slots):
-        last = s * prows + rows_ref[s] - 1
-        for v in range(2):
-            at = 4 * (2 * s + v)
-            edge_ref[at : at + 1, :] = vec_ref[v, pl.ds(last - 1, 1), :]
-            edge_ref[at + 1 : at + 2, :] = vec_ref[v, pl.ds(last, 1), :]
-            edge_ref[at + 2 : at + 4, :] = vec_ref[v, s * prows : s * prows + 2, :]
-        at = 8 * slots
-        edge_ref[at + s : at + s + 1, :] = label(mine[s], ncol)
-        edge_ref[at + slots + s : at + slots + s + 1, :] = label(match[s], ncol)
-    used = 10 * slots
-    edge_ref[used:, :] = jnp.zeros((edge_ref.shape[0] - used, ncol), jnp.float32)
+    halves = ncol // LANES
+    for depth in range(2):
+        for at, v, s, side in stacked(rows_ref, rows_dev // 2):
+            row = vec_ref[v, pl.ds(edge_row(rows_ref, s, side, depth, rows_dev // 2), 1), :]
+            for h, part in enumerate(cut(row)):
+                to = STACK * (depth * halves + h) + at
+                edge_ref[to : to + 1, :] = part
+    edge_ref[2 * STACK * halves :, :] = labels_of(rows_ref, matched_ref)
 
 
 FIRST = [("kxx", 0, 0), ("kxx", 0, 1), ("kxx", 1, 1), ("kpk", 0, 0), ("kpk", 0, 1), ("kpk", 1, 1)]
 FIRST += [("kuu", 2, 2), ("kuu", 2, 3), ("kuu", 3, 3)]
 
 
-def stiff_kernel(rows_ref, vec_ref, thick_ref, support_ref, k_ref, uk_ref, kuk_ref, prec_ref, sums_ref):
+RIM = [("prec", 2), ("thick", 3), ("support", 2), ("k", 2), ("uk", 2), ("kuk", 2)]
+RIM_AT = {name: sum(n for _, n in RIM[:i]) for i, (name, _) in enumerate(RIM)}
+RIM_STACKS = sum(n for _, n in RIM)
+
+
+def stiff_kernel(rows_ref, vec_ref, thick_ref, support_ref, k_ref, uk_ref, kuk_ref, prec_ref, sums_ref, rim_ref):
     slots = rows_ref.shape[0]
     rows_dev, ncol = thick_ref.shape
     prows = rows_dev // slots
@@ -251,35 +312,34 @@
                     totals[name] = totals[name] + part if s else part
     for k, name in enumerate(FIRST):
         sums_ref[8 * k : 8 * k + 8, :] = totals[name]
-
-
-def interface_rows(own, top, bottom):
-    jump_t = own[1:2] - bottom[0:1]
-    slope_t = own[1:2] - own[0:1] - (bottom[1:2] - bottom[0:1])
-    jump_b = top[1:2] - own[2:3]
-    slope_b = top[1:2] - top[0:1] - (own[3:4] - own[2:3])
-    return (
-        -penalty_slope * slope_t,
-        penalty_value * jump_t + penalty_slope * slope_t,
-        -penalty_value * jump_b + penalty_slope * slope_b,
-        -penalty_slope * slope_b,
-    )
-
-
-def edge_places(rows_ref, slot, prows):
-    last = slot * prows + rows_ref[slot] - 1
-    return (last - 1, last, slot * prows, slot * prows + 1)
+    sources = {"prec": prec_ref, "thick": thick_ref, "support": support_ref, "k": k_ref, "uk": uk_ref, "kuk": kuk_ref}
+    for name, depths in RIM:
+        for depth in range(depths):
+            for at, v, s, side in stacked(rows_ref, prows):
+                rows = pl.ds(edge_row(rows_ref, s, side, depth, prows), 1)
+                to = STACK * (RIM_AT[name] + depth) + at
+                ref = sources[name]
+                rim_ref[to : to + 1, :] = ref[rows, :] if len(ref.shape) == 2 else ref[v, rows, :]
+
+
+def rim_of(rim_ref, name, depth):
+    at = STACK * (RIM_AT[name] + depth)
+    return cut(rim_ref[at : at + STACK, :])
+
+
+def sent_stack(ref, kind, depth, halves):
+    at = (2 * kind + depth) * halves
+    return [ref[STACK * (at + h) : STACK * (at + h + 1), :] for h in range(halves)]
 
 
 def gram_kernel(
-    rows_ref, matched_ref, arrived_ref, vec_ref, thick_ref, support_ref, prec_ref, k_in, uk_in, kuk_in, sums_in,
+    rows_ref, arrived_ref, vec_ref, thick_ref, support_ref, prec_ref, k_in, uk_in, kuk_in, sums_in, rim_ref,
     edge_ref, below_ref, above_ref, ug_ref, uk_ref, kuk_ref, stress_ref, out_ref, g_ref, k_ref,
 ):
     slots = rows_ref.shape[0]
     rows_dev, ncol = prec_ref.shape
     prows = rows_dev // slots
     halves = ncol // LANES
-    mine, match = place(rows_ref, matched_ref, slots)
     index = arrived_ref[:, 3 * ncol :].astype(jnp.float32)
     lane = iota(index.shape, 1).astype(jnp.float32)
     pick = jnp.concatenate(
@@ -294,83 +354,67 @@
     )
     for j in range(3):
         stress_ref[j] = placed[:, j * ncol : (j + 1) * ncol]
-    rows_sent = 16 * slots
     totals = {name: sums_in[8 * k : 8 * k + 8, :] for k, name in enumerate(FIRST)}
-    row_totals = {}
 
     def add(name, product):
         part = folded(product)
         totals[name] = totals[name] + part if name in totals else part
 
-    def add_row(name, product):
-        row_totals[name] = row_totals[name] + product if name in row_totals else product
-
-    def send(to, row):
-        for h in range(halves):
-            out_ref[h * rows_sent + to : h * rows_sent + to + 1, :] = row[:, h * LANES : (h + 1) * LANES]
+    def add_stack(first, second, product):
+        part = sum(product[1:], product[0])
+        vector = iota(part.shape, 0) // 2 % 2
+        totals[first] = totals[first] + jnp.where(vector == 0, part, 0.0)
+        if second is not None:
+            totals[second] = totals[second] + jnp.where(vector == 1, part, 0.0)
 
     k_ref[...] = k_in[...]
     uk_ref[...] = uk_in[...]
     kuk_ref[...] = kuk_in[...]
-    late = []
-    for s in range(slots):
-        own_id, want_id = mine[s].astype(jnp.float32), match[s].astype(jnp.float32)
-        places = edge_places(rows_ref, s, prows)
-        added, scaled = [], []
-        for v in range(2):
-            own = edge_ref[4 * (2 * s + v) : 4 * (2 * s + v) + 4, :]
-            top = jnp.zeros((2, ncol), jnp.float32)
-            bottom = jnp.zeros((2, ncol), jnp.float32)
-            for ref in (below_ref, above_ref):
-                for t in range(slots):
-                    strip = ref[4 * (2 * t + v) : 4 * (2 * t + v) + 4, :]
-                    label_t = ref[8 * slots + t : 8 * slots + t + 1, :]
-                    wants = ref[9 * slots + t : 9 * slots + t + 1, :]
-                    top = top + jnp.where(wants == own_id, strip[0:2], 0.0)
-                    bottom = bottom + jnp.where(label_t == want_id, strip[2:4], 0.0)
-            added.append(interface_rows(own, top, bottom))
-            scaled.append([prec_ref[pl.ds(row, 1), :] * n for row, n in zip(places, added[v])])
-        last_tile = (rows_ref[s] - 1) // 8 * 8 - 8
-        for base, pair in ((0, (2, 3)), (last_tile, (0, 1))):
-            start = s * prows + base
-            at = pl.ds(pl.multiple_of(start, 8), 16)
-            row = iota((16, LANES), 0)
-            live = row + base < rows_ref[s]
-            parts = []
-            for v in range(2):
-                rows_cut = [cut(scaled[v][i]) for i in pair]
-                parts.append(
-                    [
-                        sum(jnp.where(row == places[i] - start, rows_cut[j][h], 0.0) for j, i in enumerate(pair))
-                        for h in range(halves)
-                    ]
-                )
-            thick, support = cut(thick_ref[at, :]), cut(support_ref[at, :])
-            live_thick = masked(live, thick_ref[at, :])
-            extra = [stiffness(part, live_thick, thick, support) for part in parts]
-            kuk = [cut(kuk_in[v, at, :]) for v in range(2)]
-            for x in range(2):
-                ux = cut(uk_in[x, at, :])
-                for y in range(x, 2):
-                    add(
-                        ("kuu", 2 + x, 2 + y),
-                        each(lambda u, e, p, k: u * e + p * (k + e), ux, extra[y], parts[x], kuk[y]),
-                    )
-            for v in range(2):
-                late.append((kuk_ref, v, at, joined(each(lambda k, e: k + e, kuk[v], extra[v]))))
-        for a in range(2):
-            for b in range(a, 2):
-                for i, row in enumerate(places):
-                    ka, kb = k_in[a, pl.ds(row, 1), :], k_in[b, pl.ds(row, 1), :]
-                    add_row(("kxx", a, b), vec_ref[a, pl.ds(row, 1), :] * added[b][i])
-                    add_row(("kpk", a, b), ka * scaled[b][i] + scaled[a][i] * (kb + added[b][i]))
-        for v in range(2):
-            for i, row in enumerate(places):
-                at = pl.ds(row, 1)
-                late.append((k_ref, v, at, k_in[v, at, :] + added[v][i]))
-                late.append((uk_ref, v, at, uk_in[v, at, :] + scaled[v][i]))
-    for ref, v, at, value in late:
-        ref[v, at, :] = value
+    label = edge_ref[2 * STACK * halves :, :]
+
+    def depths_of(ref):
+        return [[ref[STACK * (d * halves + h) : STACK * (d * halves + h + 1), :] for h in range(halves)] for d in range(2)]
+
+    own = depths_of(edge_ref)
+    met = opposite(label, [(ref[2 * STACK * halves :, :], depths_of(ref)) for ref in (below_ref, above_ref)])
+    added = interface_rows(own, met)
+    scaled = [times(rim_of(rim_ref, "prec", d), added[d]) for d in range(2)]
+    bend = [
+        each(lambda t, y, x: t * (y - (x + x)), rim_of(rim_ref, "thick", 0), scaled[1], scaled[0]),
+        each(lambda t, y, x: t * (y - (x + x)), rim_of(rim_ref, "thick", 1), scaled[0], scaled[1]),
+        times(rim_of(rim_ref, "thick", 2), scaled[1]),
+    ]
+    across = [second_cols(times(rim_of(rim_ref, "thick", d), second_cols(scaled[d]))) for d in range(2)]
+    extra = [
+        each(
+            lambda f, z, p, q, c: f * z + (p - (q + q)) + c,
+            rim_of(rim_ref, "support", 0), scaled[0], bend[1], bend[0], across[0],
+        ),
+        each(
+            lambda f, z, p, q, r, c: f * z + (p - (q + q) + r) + c,
+            rim_of(rim_ref, "support", 1), scaled[1], bend[0], bend[1], bend[2], across[1],
+        ),
+        each(lambda p, q: p - (q + q), bend[1], bend[2]),
+        bend[2],
+    ]
+    for d in range(2):
+        n, z, e, x = added[d], scaled[d], extra[d], own[d]
+        k, kuk = rim_of(rim_ref, "k", d), rim_of(rim_ref, "kuk", d)
+        add_stack(("kxx", 0, 0), ("kxx", 1, 1), times(x, n))
+        add_stack(("kxx", 0, 1), None, times(x, other_vector(n)))
+        z_turned = other_vector(z)
+        for key, base, more in (("kpk", k, n), ("kuu", kuk, e)):
+            lo = 2 if key == "kuu" else 0
+            turned = other_vector(each(lambda p, q: p + q, base, more))
+            add_stack((key, lo, lo), (key, lo + 1, lo + 1), each(lambda r, p, q: r * (p + p + q), z, base, more))
+            add_stack((key, lo, lo + 1), None, each(lambda r, t, p, w: r * t + p * w, z, turned, base, z_turned))
+    for d in range(4):
+        for at, v, s, side in stacked(rows_ref, prows):
+            rows = pl.ds(edge_row(rows_ref, s, side, d, prows), 1)
+            kuk_ref[v, rows, :] += joined([p[at : at + 1] for p in extra[d]])
+            if d < 2:
+                k_ref[v, rows, :] += joined([p[at : at + 1] for p in added[d]])
+                uk_ref[v, rows, :] += joined([p[at : at + 1] for p in scaled[d]])
     basis = [(ug_ref, 0), (ug_ref, 1), (uk_ref, 0), (uk_ref, 1)]
     for s in range(slots):
         at = slice(s * prows, (s + 1) * prows)
@@ -413,21 +457,17 @@
             first.append((r, c))
             for a in range(b + 1):
                 add(("guu", a, b), each(lambda p, x, q, y: p * x + q * y, first[a][0], fr, first[a][1], fc))
-        for i, row in enumerate(edge_places(rows_ref, s, prows)):
-            for a, (ref, v) in enumerate(basis):
-                send(4 * (4 * s + a) + i, ref[v, pl.ds(row, 1), :])
-    tag = halves * rows_sent
-    rows = []
-    for name in NAMES:
-        row = column_sums(totals[name])
-        if name in row_totals:
-            row = row + sum(cut(row_totals[name]))
-        rows.append(row)
-    tile = packed(rows)
-    lane = iota(tile.shape, 1)
-    for s in range(slots):
-        tile = jnp.where(lane == LANES - slots + s, match[s].astype(jnp.float32), tile)
-    out_ref[tag:, :] = tile
+    for d in range(2):
+        for at, v, s, side in stacked(rows_ref, prows):
+            row = ug_ref[v, pl.ds(edge_row(rows_ref, s, side, d, prows), 1), :]
+            for h, part in enumerate(cut(row)):
+                to = STACK * (d * halves + h) + at
+                out_ref[to : to + 1, :] = part
+        for h, part in enumerate(each(lambda u, z: u + z, rim_of(rim_ref, "uk", d), scaled[d])):
+            to = STACK * ((2 + d) * halves + h)
+            out_ref[to : to + STACK, :] = part
+    tile = packed([column_sums(totals[name]) for name in NAMES])
+    out_ref[4 * STACK * halves :, :] = jnp.where(iota(tile.shape, 1) == LANES - 1, label, tile)
 
 
 def apply_kernel(
@@ -454,73 +494,51 @@
             d_ref[v, at, :] = joined(times(prec, cut(kuk_ref[v, at, :])))
 
 
-def strip_of(ref, at, rows, slots):
-    halves = (ref.shape[0] - 8) // (16 * slots)
-    return jnp.concatenate(
-        [ref[h * 16 * slots + at : h * 16 * slots + at + rows, :] for h in range(halves)], axis=1
-    )
-
-
-def wanted_of(ref, slot, slots):
-    tag = ref.shape[0] - 8
-    return ref[tag : tag + 1, LANES - slots + slot : LANES - slots + slot + 1]
-
-
-def line_kernel(slots, *refs):
+def line_parts(ref):
+    halves = (ref.shape[0] // STACK - 1) // 4
+    tag = 4 * STACK * halves
+    return ref[tag:, LANES - 1 :], [sent_stack(ref, kind, d, halves) for kind in range(2) for d in range(2)]
+
+
+def line_kernel(near, *refs):
     line, out_ref = refs[:-2], refs[-1]
-    owners = len(line)
-    tag = line[0].shape[0] - 8
-    me = lax.axis_index("patch")
-    total = line[0][tag:, :]
-    for z in range(1, owners):
-        total = total + line[z][tag:, :]
-    sums = {}
-    for z in range(owners):
-        for s in range(slots):
-            wanted = wanted_of(line[z], s, slots)
-            jumps, slopes = [], []
-            for a in range(4):
-                own = strip_of(line[z], 4 * (4 * s + a), 2, slots)
-                bottom = jnp.zeros_like(own)
-                for near in sorted({(z + 1) % owners, (z - 1) % owners}):
-                    there = lax.rem(me - near + owners, owners)
-                    for t in range(slots):
-                        strip = strip_of(line[near], 4 * (4 * t + a) + 2, 2, slots)
-                        is_it = wanted == (there * slots + t).astype(jnp.float32)
-                        bottom = bottom + jnp.where(is_it, strip, 0.0)
-                jumps.append(own[1:2] - bottom[0:1])
-                slopes.append(own[1:2] - own[0:1] - (bottom[1:2] - bottom[0:1]))
-            for a, b in UU:
-                term = penalty_value * jumps[a] * jumps[b] + penalty_slope * slopes[a] * slopes[b]
-                sums[a, b] = sums[a, b] + term if (a, b) in sums else term
-    out_ref[...] = total + packed([sums[pair] for pair in UU])
-
-
-def join_kernel(slots, rows_ref, matched_ref, prec_ref, *refs):
+    held = [line_parts(ref) for ref in line]
+    sums = [None] * 6
+    for (label, stacks), others in zip(held, near):
+        met = opposite(label, [held[k] for k in others])
+        g, k = (meeting(stacks[2 * i : 2 * i + 2], met[2 * i : 2 * i + 2]) for i in range(2))
+        g_turned, k_turned = [other_vector(w) for w in g], [other_vector(w) for w in k]
+        for i, (p, q) in enumerate(((g, g), (g, g_turned), (g, k), (g, k_turned), (k, k), (k, k_turned))):
+            part = each(
+                lambda a, b, c, d: penalty_value * (a * b) + penalty_slope * (c * d), p[0], q[0], p[1], q[1]
+            )
+            part = sum(part[1:], part[0])
+            sums[i] = part if sums[i] is None else sums[i] + part
+    total = line[0][-STACK:, :]
+    for ref in line[1:]:
+        total = total + ref[-STACK:, :]
+    row = iota(total.shape, 0)
+    masks = [(row % 2 == 1) & (row // 2 % 2 == v) for v in range(2)]
+    rows = {
+        (0, 0): (0, 0), (1, 1): (0, 1), (0, 1): (1, 0), (0, 2): (2, 0), (1, 3): (2, 1), (0, 3): (3, 0), (1, 2): (3, 1),
+        (2, 2): (4, 0), (3, 3): (4, 1), (2, 3): (5, 0),
+    }
+    out_ref[...] = total + packed([column_sums(jnp.where(masks[rows[p][1]], sums[rows[p][0]], 0.0)) for p in UU])
+
+
+def join_kernel(near, rows_ref, prec_ref, *refs):
     line, (c_in, d_in, c_ref, d_ref) = refs[:-4], refs[-4:]
     c_ref[...] = c_in[...]
     d_ref[...] = d_in[...]
-    rows_dev, ncol = c_in.shape[1:]
-    prows = rows_dev // slots
-    owners = len(line)
-    mine, match = place(rows_ref, matched_ref, slots)
-    me = lax.axis_index("patch")
-    for s in range(slots):
-        own_id, want_id = mine[s].astype(jnp.float32), match[s]
-        places = edge_places(rows_ref, s, prows)
-        for a in range(4):
-            own = strip_of(line[0], 4 * (4 * s + a), 4, slots)
-            top = jnp.zeros((2, ncol), jnp.float32)
-            bottom = jnp.zeros((2, ncol), jnp.float32)
-            for near in sorted({1, owners - 1}):
-                there = lax.rem(me - near + owners, owners)
-                for t in range(slots):
-                    strip = strip_of(line[near], 4 * (4 * t + a), 4, slots)
-                    top = top + jnp.where(wanted_of(line[near], t, slots) == own_id, strip[0:2], 0.0)
-                    bottom = bottom + jnp.where(want_id == there * slots + t, strip[2:4], 0.0)
-            ref = c_ref if a < 2 else d_ref
-            for row, added in zip(places, interface_rows(own, top, bottom)):
-                ref[a % 2, pl.ds(row, 1), :] += prec_ref[pl.ds(row, 1), :] * added
+    prows = c_in.shape[1] // 2
+    label, stacks = line_parts(line[0])
+    met = opposite(label, [line_parts(ref) for ref in line[1:]])
+    for i, ref in enumerate((c_ref, d_ref)):
+        added = interface_rows(stacks[2 * i : 2 * i + 2], met[2 * i : 2 * i + 2])
+        for d in range(2):
+            for at, v, s, side in stacked(rows_ref, prows):
+                rows = pl.ds(edge_row(rows_ref, s, side, d, prows), 1)
+                ref[v, rows, :] += prec_ref[rows, :] * joined([p[at : at + 1] for p in added[d]])
 
 
 def form(table, left, right):
@@ -656,31 +674,30 @@
     arrived = lax.all_to_all(
         payload, ("patch", "sub", "half"), split_axis=0, concat_axis=0, tiled=True
     )
-    edge_rows = -(-10 * slots // 8) * 8
-    (edges,) = call(edge_kernel, [((edge_rows, ncol), f32)], "ssv")(patch_rows, matched, vectors)
+    halves = ncol // LANES
+    (edges,) = call(edge_kernel, [(((2 * halves + 1) * STACK, LANES), f32)], "ssv")(patch_rows, matched, vectors)
     below = passed_along(edges, "patch", 1)
     above = passed_along(edges, "patch", -1)
-    k_x, u_k, k_uk, prec, part = call(stiff_kernel, [field, field, field, one, sums], "svvv")(
-        patch_rows, vectors, thickness, foundation
-    )
-    sent_rows = (ncol // LANES) * 16 * slots + 8
+    k_x, u_k, k_uk, prec, part, rim = call(
+        stiff_kernel, [field, field, field, one, sums, ((RIM_STACKS * STACK, ncol), f32)], "svvv"
+    )(patch_rows, vectors, thickness, foundation)
     u_g, u_k, k_uk, stress, sent = call(
         gram_kernel,
-        [field, field, field, ((3, rows_dev, ncol), f32), ((sent_rows, LANES), f32)],
-        "ssvvvvvvvvvvvv",
+        [field, field, field, ((3, rows_dev, ncol), f32), (((4 * halves + 1) * STACK, LANES), f32)],
+        "svvvvvvvvvvvvv",
         [pltpu.VMEM(field[0], f32), pltpu.VMEM(field[0], f32)],
     )(
-        patch_rows, matched, arrived, vectors, thickness, foundation, prec, k_x, u_k, k_uk, part,
+        patch_rows, arrived, vectors, thickness, foundation, prec, k_x, u_k, k_uk, part, rim,
         edges, below, above,
     )
-    line = [sent] + [passed_along(sent, "patch", by) for by in range(1, owners)]
+    line, near = line_shared(sent, "patch")
     a, b, c, d = call(apply_kernel, [field] * 4, "svvvvvvvv")(
         patch_rows, vectors, thickness, foundation, prec, stress, u_g, u_k, k_uk
     )
-    (total,) = call(functools.partial(line_kernel, slots), [tile], "v" * owners + "a")(*line, a)
+    (total,) = call(functools.partial(line_kernel, near), [tile], "v" * owners + "a")(*line, a)
     total = summed_over_both(total, "sub", "half")
-    c, d = call(functools.partial(join_kernel, slots), [field, field], "ssv" + "v" * (owners + 2))(
-        patch_rows, matched, prec, *line, c, d
+    c, d = call(functools.partial(join_kernel, near), [field, field], "sv" + "v" * (len(near[0]) + 3))(
+        patch_rows, prec, line[0], *[line[k] for k in near[0]], c, d
     )
     (modes,) = call(
         functools.partial(final_kernel, cells),

time: 41.2 us -> 39 us (0.947)
  waiting for transfers between devices: 9.7 us -> 7.8 us
    ppermute x5 -> x2, starting transfers between devices: 8.2 us -> 3.78 us  [passed_along(): lax.ppermute(array, axis, [(i, (i + by) % peers) for i in range(peers)])]
    ppermute x0 -> x3, starting transfers between devices: none -> 4.39 us  [line_shared(): lax.ppermute(array, axis, [(i, i ^ k) for i in range(4)])]
    ppermute x5 -> x2, waiting for transfers between devices: 8.42 us -> 6.29 us  [passed_along(): lax.ppermute(array, axis, [(i, (i + by) % peers) for i in range(peers)])]
  transfers between devices with their start and end apart: 9 -> 9, of which waited for: 6 -> 6; matrix products, arithmetic and copies ran while one was open for 0% -> 0% of each run, Pallas kernels for 16% -> 17%
where the time goes in v5:
time: 39 us; the launch traced here: 38.8 us
  starting transfers between devices  17.5 us (45%)
  Pallas kernels  13.2 us (34%)
  waiting for transfers between devices  7.8 us (20%)
    all_to_all x1, starting transfers between devices, per_device(): lax.all_to_all(payload, ('patch', 'sub', 'half'), split_axis=0, concat_ax...  7.5 us
    ppermute x2, waiting for transfers between devices, passed_along(): lax.ppermute(array, axis, [(i, (i + by) % peers) for i in range(peers)])  6.29 us
    ppermute x3, starting transfers between devices, line_shared(): lax.ppermute(array, axis, [(i, i ^ k) for i in range(4)])  4.39 us
    ppermute x2, starting transfers between devices, passed_along(): lax.ppermute(array, axis, [(i, (i + by) % peers) for i in range(peers)])  3.78 us
    pallas_call x1, Pallas kernels, per_device(): call(gram_kernel, [field, field, field, ((3, rows_dev, ncol), f32), (((4...  3.2 us
    pallas_call x1, Pallas kernels, per_device(): call(apply_kernel, [field] * 4, 'svvvvvvvv')  2.7 us
    pallas_call x1, Pallas kernels, per_device(): call(stiff_kernel, [field, field, field, one, sums, ((RIM_STACKS * STACK,...  2.6 us
    ppermute x3, starting transfers between devices, summed_over_both(): total = total + lax.ppermute(array, (outer, inner), pairs)  1.86 us
  transfers between devices with their start and end apart: 9, of which 6 were waited for; matrix products, arithmetic and copies ran while one was open for 0% of the time, Pallas kernels for 17%

profile of v5, /device:TPU:0, one launch (start us, length us, event | category | flops | bytes accessed | tf_op | source)
XLA Modules:
  0.0 38.8 jit_solution(15032346480394761165)
XLA Ops:
  0.0 1.8 %shard_map.73 = bf16[256,896]{1,0:T(8,128)(2,1)} custom-call(bf16[3,256,256]{2,1,0:T(8,128)(2,1)} %bitcast.6, s32[1,256]{1,0:T(1,128)} %bitcast.7), custom_call_target="tpu_custom_call" | custom-call | flops 1000000 | bytes 2000000 | tf_op jit(solution)/shard_map/pallas_call | solution.py:660
  1.8 0.0 copy-start
  1.8 7.5 %all-to-all-start = ((bf16[16,16,896]{2,1,0:T(8,128)(2,1)}), bf16[16,16,896]{2,1,0:T(8,128)(2,1)S(1)}, u32[]{:S(2)}, u32[]{:S(2)}) async-start(bf16[16,16,896]{2,1,0:T(8,128)(2,1)} %bitcast.5), calls=%async_computation | async-start | bytes 917504 | tf_op jit(solution)/shard_map/all_to_all | solution.py:674
  9.4 0.0 copy-start.1
  9.4 0.6 %shard_map.75.edge_ref = f32[40,128]{1,0:T(8,128)S(1)} custom-call(s32[2]{0:T(128)S(1)} %copy-done.3, s32[2]{0:T(128)S(1)} %copy-done.4, f32[2,256,256]{2,1,0:T(8,128)S(1)} %copy-done), custom_call_target="tpu_custom_call" | custom-call | flops 1000000 | bytes 2000000 | tf_op jit(solution)/shard_map/pallas_call | solution.py:678
  10.0 3.8 %collective-permute-start.1 = (f32[40,128]{1,0:T(8,128)S(1)}, f32[40,128]{1,0:T(8,128)S(1)}, u32[]{:S(2)}, u32[]{:S(2)}) collective-permute-start(f32[40,128]{1,0:T(8,128)S(1)} %shard_map.75.edge_ref), channel_id=1, source_target_pairs={{0,12},{4,0},{8,4},{12,8},{1,13},{5,1},{9,5},{13,9},{2,14},{6,2},{... | collective-permute-start | bytes 61448 | tf_op jit(solution)/shard_map/ppermute | solution.py:32
  13.8 2.6 %shard_map.74 = (f32[2,256,256]{2,1,0:T(8,128)S(1)}, f32[2,256,256]{2,1,0:T(8,128)S(1)}, f32[2,256,256]{2,1,0:T(8,128)S(1)}, f32[256,256]{1,0:T(8,128)S(1)}, f32...) custom-call(s32[2]{0:T(128)S(1)} %copy-done.3, f32[2,256,256]{2,1,0:T(8,128)S(1)} %copy-done, f32[256,256]{1,0:T(8,128)S(1)} %copy-done.1, ...), custom_call_target="tpu_custom_call" | custom-call | flops 1000000 | bytes 2000000 | tf_op jit(solution)/shard_map/pallas_call | solution.py:681
  16.4 2.1 %collective-permute-done.1.above_ref = f32[40,128]{1,0:T(8,128)S(1)} collective-permute-done((f32[40,128]{1,0:T(8,128)S(1)}, f32[40,128]{1,0:T(8,128)S(1)}, u32[]{:S(2)}, u32[]{:S(2)}) %collective-permute-start.1) | collective-permute-done | bytes 20512 | tf_op jit(solution)/shard_map/ppermute | solution.py:32
  18.4 4.2 %collective-permute-done.below_ref = f32[40,128]{1,0:T(8,128)S(1)} collective-permute-done((f32[40,128]{1,0:T(8,128)S(1)}, f32[40,128]{1,0:T(8,128)S(1)}, u32[]{:S(2)}, u32[]{:S(2)}) %collective-permute-start) | collective-permute-done | bytes 20512 | tf_op jit(solution)/shard_map/ppermute | solution.py:32
  22.6 0.4 all-to-all-done
  23.0 3.2 %shard_map.76 = (f32[2,256,256]{2,1,0:T(8,128)S(1)}, f32[2,256,256]{2,1,0:T(8,128)S(1)}, f32[2,256,256]{2,1,0:T(8,128)S(1)}, f32[3,256,256]{2,1,0:T(8,128)S(1)}, f32[72,128]{1,0:T(8,128)S(1)}) custom-call(s32[2]{0:T(128)S(1)} %copy-done.3, bf16[256,896]{1,0:T(8,128)(2,1)S(1)} %bitcast.4, f32[2,256,256]{2,1,0:T(8,128)S(1)} %copy-done, ...), custom_call_target="tpu_custom_call" | custom-call | flops 1000000 | bytes 2000000 | tf_op jit(solution)/shard_map/pallas_call | solution.py:684
  26.2 1.4 %collective-permute-start.4 = (f32[72,128]{1,0:T(8,128)S(1)}, f32[72,128]{1,0:T(8,128)S(1)}, u32[]{:S(2)}, u32[]{:S(2)}) collective-permute-start(f32[72,128]{1,0:T(8,128)S(1)} %get-tuple-element.28.refs_0_), channel_id=1, source_target_pairs={{0,12},{4,8},{8,4},{12,0},{1,13},{5,9},{9,5},{13,1},{2,14},{6,10},... | collective-permute-start | bytes 110600 | tf_op jit(solution)/shard_map/ppermute | solution.py:38
  27.6 1.7 %collective-permute-start.3 = (f32[72,128]{1,0:T(8,128)S(1)}, f32[72,128]{1,0:T(8,128)S(1)}, u32[]{:S(2)}, u32[]{:S(2)}) collective-permute-start(f32[72,128]{1,0:T(8,128)S(1)} %get-tuple-element.28.refs_0_), channel_id=1, source_target_pairs={{0,8},{4,12},{8,0},{12,4},{1,9},{5,13},{9,1},{13,5},{2,10},{6,14},... | collective-permute-start | bytes 110600 | tf_op jit(solution)/shard_map/ppermute | solution.py:38
  29.3 1.3 %collective-permute-start.2 = (f32[72,128]{1,0:T(8,128)S(1)}, f32[72,128]{1,0:T(8,128)S(1)}, u32[]{:S(2)}, u32[]{:S(2)}) collective-permute-start(f32[72,128]{1,0:T(8,128)S(1)} %get-tuple-element.28.refs_0_), channel_id=1, source_target_pairs={{0,4},{4,0},{8,12},{12,8},{1,5},{5,1},{9,13},{13,9},{2,6},{6,2},{1... | collective-permute-start | bytes 110600 | tf_op jit(solution)/shard_map/ppermute | solution.py:38
  30.6 2.7 %shard_map.77 = (f32[2,256,256]{2,1,0:T(8,128)S(1)}, f32[2,256,256]{2,1,0:T(8,128)S(1)}, f32[2,256,256]{2,1,0:T(8,128)S(1)}, f32[2,256,256]{2,1,0:T(8,128)S(1)}) custom-call(s32[2]{0:T(128)S(1)} %copy-done.3, f32[2,256,256]{2,1,0:T(8,128)S(1)} %copy-done, f32[256,256]{1,0:T(8,128)S(1)} %copy-done.1, f32[256,256]{1,0:T(8,128)S(1)} %copy-done.2, ...), custom_call_target="tpu_custom_call" | custom-call | flops 1000000 | bytes 2000000 | tf_op jit(solution)/shard_map/pallas_call | solution.py:694
  33.3 0.1 collective-permute-done.2.refs_1_
  33.4 0.3 shard_map.78
  33.7 0.0 collective-permute-start.7
  33.8 1.6 %collective-permute-start.6 = (f32[8,128]{1,0:T(8,128)S(1)}, f32[8,128]{1,0:T(8,128)S(1)}, u32[]{:S(2)}, u32[]{:S(2)}) collective-permute-start(f32[8,128]{1,0:T(8,128)S(1)} %shard_map.78), channel_id=1, source_target_pairs={{0,2},{1,3},{2,0},{3,1},{4,6},{5,7},{6,4},{7,5},{8,10},{9,11},{10,... | collective-permute-start | bytes 12296 | tf_op jit(solution)/shard_map/ppermute | solution.py:52
  35.4 0.3 collective-permute-start.5
  35.6 0.8 %shard_map.79 = (f32[2,256,256]{2,1,0:T(8,128)S(1)}, f32[2,256,256]{2,1,0:T(8,128)S(1)}) custom-call(s32[2]{0:T(128)S(1)} %copy-done.3, f32[256,256]{1,0:T(8,128)S(1)} %get-tuple-element.22.prec_ref, f32[72,128]{1,0:T(8,128)S(1)} %get-tuple-element.28.refs_0_, f32[72,128]{1,0:T(8,128)S(1)} %collective-permute-done.2.refs_1_, ...), custom_call_target="tpu_custom_call" | custom-call | flops 1000000 | bytes 2000000 | tf_op jit(solution)/shard_map/pallas_call | solution.py:699
  36.4 0.4 %collective-permute-done.7 = f32[8,128]{1,0:T(8,128)S(1)} collective-permute-done((f32[8,128]{1,0:T(8,128)S(1)}, f32[8,128]{1,0:T(8,128)S(1)}, u32[]{:S(2)}, u32[]{:S(2)}) %collective-permute-start.7) | collective-permute-done | bytes 4128 | tf_op jit(solution)/shard_map/ppermute | solution.py:52
  36.8 0.6 %collective-permute-done.6 = f32[8,128]{1,0:T(8,128)S(1)} collective-permute-done((f32[8,128]{1,0:T(8,128)S(1)}, f32[8,128]{1,0:T(8,128)S(1)}, u32[]{:S(2)}, u32[]{:S(2)}) %collective-permute-start.6) | collective-permute-done | bytes 4128 | tf_op jit(solution)/shard_map/ppermute | solution.py:52
  37.4 1.3 %shard_map.80 = f32[2,256,256]{2,1,0:T(8,128)} custom-call(f32[8,128]{1,0:T(8,128)S(1)} %add_add_fusion.total_ref, f32[2,256,256]{2,1,0:T(8,128)S(1)} %get-tuple-element.33.refs_4_.a_ref, f32[2,256,256]{2,1,0:T(8,128)S(1)} %get-tuple-element.34.b_ref, f32[2,256,256]{2,1,0:T(8,128)S(1)} %get-tuple-element.37.c_ref, f32[2,256,256]{2,1,0:T(8,128)S(1)} %get-tuple-element.38.d_ref), custom_call_target="tpu_custom_call" | custom-call | flops 1000000 | bytes 2000000 | tf_op jit(solution)/shard_map/pallas_call | solution.py:702
  (13 shorter events, 0.0 us)
Async XLA Ops:
  1.8 7.5 %copy-start = (f32[2,256,256]{2,1,0:T(8,128)S(1)}, f32[2,256,256]{2,1,0:T(8,128)}, u32[]{:S(2)}) copy-start(f32[2,256,256]{2,1,0:T(8,128)} %vec_ref.7) | copy-start | bytes 1572868
  1.8 7.5 %copy-start.3 = (s32[2]{0:T(128)S(1)}, s32[2]{0:T(128)}, u32[]{:S(2)}) copy-start(s32[2]{0:T(128)} %rows_ref.9) | copy-start | bytes 28
  1.8 7.5 %copy-start.4 = (s32[2]{0:T(128)S(1)}, s32[2]{0:T(128)}, u32[]{:S(2)}) copy-start(s32[2]{0:T(128)} %matched_ref.1) | copy-start | bytes 28
  1.8 21.2 %all-to-all-start = ((bf16[16,16,896]{2,1,0:T(8,128)(2,1)}), bf16[16,16,896]{2,1,0:T(8,128)(2,1)S(1)}, u32[]{:S(2)}, u32[]{:S(2)}) async-start(bf16[16,16,896]{2,1,0:T(8,128)(2,1)} %bitcast.5), calls=%async_computation | async-start | bytes 917504 | tf_op jit(solution)/shard_map/all_to_all | solution.py:674
  9.4 4.4 %copy-start.1 = (f32[256,256]{1,0:T(8,128)S(1)}, f32[256,256]{1,0:T(8,128)}, u32[]{:S(2)}) copy-start(f32[256,256]{1,0:T(8,128)} %thick_ref.5) | copy-start | bytes 786436
  9.4 4.4 %copy-start.2 = (f32[256,256]{1,0:T(8,128)S(1)}, f32[256,256]{1,0:T(8,128)}, u32[]{:S(2)}) copy-start(f32[256,256]{1,0:T(8,128)} %support_ref.5) | copy-start | bytes 786436
  10.0 8.5 %collective-permute-start.1 = (f32[40,128]{1,0:T(8,128)S(1)}, f32[40,128]{1,0:T(8,128)S(1)}, u32[]{:S(2)}, u32[]{:S(2)}) collective-permute-start(f32[40,128]{1,0:T(8,128)S(1)} %shard_map.75.edge_ref), channel_id=1, source_target_pairs={{0,12},{4,0},{8,4},{12,8},{1,13},{5,1},{9,5},{13,9},{2,14},{6,2},{... | collective-permute-start | bytes 61448 | tf_op jit(solution)/shard_map/ppermute | solution.py:32
  13.7 8.9 %collective-permute-start = (f32[40,128]{1,0:T(8,128)S(1)}, f32[40,128]{1,0:T(8,128)S(1)}, u32[]{:S(2)}, u32[]{:S(2)}) collective-permute-start(f32[40,128]{1,0:T(8,128)S(1)} %shard_map.75.edge_ref), channel_id=1, source_target_pairs={{0,4},{4,8},{8,12},{12,0},{1,5},{5,9},{9,13},{13,1},{2,6},{6,10},{... | collective-permute-start | bytes 61448 | tf_op jit(solution)/shard_map/ppermute | solution.py:32
  26.2 7.1 %collective-permute-start.4 = (f32[72,128]{1,0:T(8,128)S(1)}, f32[72,128]{1,0:T(8,128)S(1)}, u32[]{:S(2)}, u32[]{:S(2)}) collective-permute-start(f32[72,128]{1,0:T(8,128)S(1)} %get-tuple-element.28.refs_0_), channel_id=1, source_target_pairs={{0,12},{4,8},{8,4},{12,0},{1,13},{5,9},{9,5},{13,1},{2,14},{6,10},... | collective-permute-start | bytes 110600 | tf_op jit(solution)/shard_map/ppermute | solution.py:38
  27.6 5.7 %collective-permute-start.3 = (f32[72,128]{1,0:T(8,128)S(1)}, f32[72,128]{1,0:T(8,128)S(1)}, u32[]{:S(2)}, u32[]{:S(2)}) collective-permute-start(f32[72,128]{1,0:T(8,128)S(1)} %get-tuple-element.28.refs_0_), channel_id=1, source_target_pairs={{0,8},{4,12},{8,0},{12,4},{1,9},{5,13},{9,1},{13,5},{2,10},{6,14},... | collective-permute-start | bytes 110600 | tf_op jit(solution)/shard_map/ppermute | solution.py:38
  29.3 4.1 %collective-permute-start.2 = (f32[72,128]{1,0:T(8,128)S(1)}, f32[72,128]{1,0:T(8,128)S(1)}, u32[]{:S(2)}, u32[]{:S(2)}) collective-permute-start(f32[72,128]{1,0:T(8,128)S(1)} %get-tuple-element.28.refs_0_), channel_id=1, source_target_pairs={{0,4},{4,0},{8,12},{12,8},{1,5},{5,1},{9,13},{13,9},{2,6},{6,2},{1... | collective-permute-start | bytes 110600 | tf_op jit(solution)/shard_map/ppermute | solution.py:38
  33.7 3.0 %collective-permute-start.7 = (f32[8,128]{1,0:T(8,128)S(1)}, f32[8,128]{1,0:T(8,128)S(1)}, u32[]{:S(2)}, u32[]{:S(2)}) collective-permute-start(f32[8,128]{1,0:T(8,128)S(1)} %shard_map.78), channel_id=1, source_target_pairs={{0,3},{1,2},{2,1},{3,0},{4,7},{5,6},{6,5},{7,4},{8,11},{9,10},{10,... | collective-permute-start | bytes 12296 | tf_op jit(solution)/shard_map/ppermute | solution.py:52
  33.8 3.7 %collective-permute-start.6 = (f32[8,128]{1,0:T(8,128)S(1)}, f32[8,128]{1,0:T(8,128)S(1)}, u32[]{:S(2)}, u32[]{:S(2)}) collective-permute-start(f32[8,128]{1,0:T(8,128)S(1)} %shard_map.78), channel_id=1, source_target_pairs={{0,2},{1,3},{2,0},{3,1},{4,6},{5,7},{6,4},{7,5},{8,10},{9,11},{10,... | collective-permute-start | bytes 12296 | tf_op jit(solution)/shard_map/ppermute | solution.py:52
  35.4 2.1 %collective-permute-start.5 = (f32[8,128]{1,0:T(8,128)S(1)}, f32[8,128]{1,0:T(8,128)S(1)}, u32[]{:S(2)}, u32[]{:S(2)}) collective-permute-start(f32[8,128]{1,0:T(8,128)S(1)} %shard_map.78), channel_id=1, source_target_pairs={{0,1},{1,0},{2,3},{3,2},{4,5},{5,4},{6,7},{7,6},{8,9},{9,8},{10,11... | collective-permute-start | bytes 12296 | tf_op jit(solution)/shard_map/ppermute | solution.py:52

commit v6 on v5

--- a/solution.py
+++ b/solution.py
@@ -32,6 +32,12 @@
     return lax.ppermute(array, axis, [(i, (i + by) % peers) for i in range(peers)])
 
 
+def neighbours(array, axis):
+    if lax.axis_size(axis) == 4:
+        return [lax.ppermute(array, axis, [(i, i ^ k) for i in range(4)]) for k in (1, 3)]
+    return [passed_along(array, axis, 1), passed_along(array, axis, -1)]
+
+
 def line_shared(array, axis):
     peers = lax.axis_size(axis)
     if peers == 4:
@@ -228,7 +234,17 @@
     )
 
 
-def pack_kernel(stress_ref, elem_ref, pay_ref, elem, held, sems):
+def local_rows(elem_ref, rows_dev):
+    square = (rows_dev, rows_dev)
+    if rows_dev & (rows_dev - 1) == 0:
+        local = jnp.bitwise_and(elem_ref[...], rows_dev - 1)
+    else:
+        local = lax.rem(elem_ref[...], rows_dev)
+    spread = jnp.broadcast_to(local.astype(jnp.float32), square)
+    return jnp.sum(jnp.where(iota(square, 0) == iota(square, 1), spread, 0.0), axis=1, keepdims=True)
+
+
+def pack_rows_kernel(stress_ref, elem_ref, pay_ref, elem, held, sems):
     rows_dev, ncol = stress_ref.shape[1:]
     get = pltpu.make_async_copy(elem_ref, elem, sems.at[0])
     get.start()
@@ -239,26 +255,58 @@
     for copy in planes:
         copy.start()
     get.wait()
-    square = (rows_dev, rows_dev)
-    if rows_dev & (rows_dev - 1) == 0:
-        local = jnp.bitwise_and(elem[...], rows_dev - 1)
-    else:
-        local = lax.rem(elem[...], rows_dev)
-    spread = jnp.broadcast_to(local.astype(jnp.float32), square)
-    column = jnp.sum(
-        jnp.where(iota(square, 0) == iota(square, 1), spread, 0.0), axis=1, keepdims=True
-    )
+    column = local_rows(elem, rows_dev)
     held[:, 3 * ncol :] = jnp.broadcast_to(column, (rows_dev, LANES)).astype(jnp.bfloat16)
-    tail = pl.ds(3 * ncol, LANES)
-    out = [pltpu.make_async_copy(held.at[:, tail], pay_ref.at[:, tail], sems.at[4])]
-    out[0].start()
-    for j in range(3):
-        planes[j].wait()
-        part = pl.ds(j * ncol, ncol)
-        out.append(pltpu.make_async_copy(held.at[:, part], pay_ref.at[:, part], sems.at[5 + j]))
-        out[-1].start()
-    for copy in out:
+    for copy in planes:
         copy.wait()
+    put = pltpu.make_async_copy(held, pay_ref, sems.at[4])
+    put.start()
+    put.wait()
+
+
+def pack_blocks_kernel(stress_ref, elem_ref, pay_ref, elem, held, get_sem, in_sems, out_sems):
+    blocks, ncol = held.shape[0], stress_ref.shape[3]
+    halves = ncol // LANES
+    get = pltpu.make_async_copy(elem_ref, elem, get_sem)
+    get.start()
+    fetch, put = [], []
+    for t in range(3 * halves):
+        to = held.at[:, pl.ds(16 * t, 16), :]
+        source = stress_ref.at[t // halves, :, :, pl.ds(t % halves * LANES, LANES)]
+        fetch.append(pltpu.make_async_copy(source, to, in_sems.at[t]))
+        put.append(pltpu.make_async_copy(to, pay_ref.at[:, pl.ds(16 * t, 16), :], out_sems.at[t]))
+        fetch[-1].start()
+    get.wait()
+    column = jnp.broadcast_to(local_rows(elem, 16 * blocks), (16 * blocks, LANES))
+    lane = iota((8, LANES), 1)
+    for k in range(blocks):
+        both = jnp.where(lane < LANES // 2, column[16 * k : 16 * k + 8], column[16 * k + 8 : 16 * k + 16])
+        held[k, 48 * halves :, :] = both.astype(jnp.bfloat16)
+    tail = pl.ds(48 * halves, 8)
+    put.append(pltpu.make_async_copy(held.at[:, tail, :], pay_ref.at[:, tail, :], out_sems.at[3 * halves]))
+    put[-1].start()
+    for t in range(3 * halves):
+        fetch[t].wait()
+        put[t].start()
+    for copy in put:
+        copy.wait()
+
+
+def unpacked(arrived_ref, ncol):
+    if len(arrived_ref.shape) == 2:
+        return arrived_ref[:, : 3 * ncol], arrived_ref[:, 3 * ncol :].astype(jnp.float32)
+    blocks, halves = arrived_ref.shape[0], ncol // LANES
+    forces = jnp.concatenate(
+        [
+            jnp.concatenate([arrived_ref[k, 16 * t : 16 * t + 16, :] for k in range(blocks)], axis=0)
+            for t in range(3 * halves)
+        ],
+        axis=1,
+    )
+    tiles = [arrived_ref[k, 48 * halves :, :].astype(jnp.float32) for k in range(blocks)]
+    half = LANES // 2
+    column = jnp.concatenate([t[:, at : at + 1] for t in tiles for at in (0, half)], axis=0)
+    return forces, jnp.broadcast_to(column, (16 * blocks, LANES))
 
 
 def edge_kernel(rows_ref, matched_ref, vec_ref, edge_ref):
@@ -340,7 +388,7 @@
     rows_dev, ncol = prec_ref.shape
     prows = rows_dev // slots
     halves = ncol // LANES
-    index = arrived_ref[:, 3 * ncol :].astype(jnp.float32)
+    forces, index = unpacked(arrived_ref, ncol)
     lane = iota(index.shape, 1).astype(jnp.float32)
     pick = jnp.concatenate(
         [
@@ -350,7 +398,7 @@
         axis=1,
     )
     placed = lax.dot_general(
-        pick, arrived_ref[:, : 3 * ncol], (((0,), (0,)), ((), ())), preferred_element_type=jnp.float32
+        pick, forces, (((0,), (0,)), ((), ())), preferred_element_type=jnp.float32
     )
     for j in range(3):
         stress_ref[j] = placed[:, j * ncol : (j + 1) * ncol]
@@ -471,8 +519,7 @@
 
 
 def apply_kernel(
-    rows_ref, vec_ref, thick_ref, support_ref, prec_ref, stress_ref, ug_ref, uk_ref, kuk_ref,
-    a_ref, b_ref, c_ref, d_ref,
+    rows_ref, vec_ref, thick_ref, support_ref, prec_ref, stress_ref, ug_ref, uk_ref, kuk_ref, a_ref, c_ref, d_ref,
 ):
     slots = rows_ref.shape[0]
     rows_dev, ncol = thick_ref.shape
@@ -486,10 +533,9 @@
         stress = [cut(stress_ref[j, at, :]) for j in range(3)]
         for v in range(2):
             x, ug, uk = masked(live, vec_ref[v, at, :]), cut(ug_ref[v, at, :]), cut(uk_ref[v, at, :])
-            gg, gk = geometric(ug, stress), geometric(uk, stress)
+            gg = geometric(ug, stress)
             kg = stiffness(ug, live_thick, thick, support)
             a_ref[v, at, :] = joined(each(lambda w, u, p, g: w + (u + u) + p * g, x, ug, prec, gg))
-            b_ref[v, at, :] = joined(each(lambda u, p, g: u + p * g, uk, prec, gk))
             c_ref[v, at, :] = joined(each(lambda u, p, k: u + p * k, uk, prec, kg))
             d_ref[v, at, :] = joined(times(prec, cut(kuk_ref[v, at, :])))
 
@@ -526,11 +572,19 @@
     out_ref[...] = total + packed([column_sums(jnp.where(masks[rows[p][1]], sums[rows[p][0]], 0.0)) for p in UU])
 
 
-def join_kernel(near, rows_ref, prec_ref, *refs):
-    line, (c_in, d_in, c_ref, d_ref) = refs[:-4], refs[-4:]
+def join_kernel(near, rows_ref, prec_ref, stress_ref, uk_ref, c_in, d_in, *refs):
+    line, (b_ref, c_ref, d_ref) = refs[:-3], refs[-3:]
     c_ref[...] = c_in[...]
     d_ref[...] = d_in[...]
     prows = c_in.shape[1] // 2
+    for s in range(2):
+        at = slice(s * prows, (s + 1) * prows)
+        prec = cut(prec_ref[at, :])
+        stress = [cut(stress_ref[j, at, :]) for j in range(3)]
+        for v in range(2):
+            uk = cut(uk_ref[v, at, :])
+            gk = geometric(uk, stress)
+            b_ref[v, at, :] = joined(each(lambda u, p, g: u + p * g, uk, prec, gk))
     label, stacks = line_parts(line[0])
     met = opposite(label, [line_parts(ref) for ref in line[1:]])
     for i, ref in enumerate((c_ref, d_ref)):
@@ -559,7 +613,7 @@
 
     def value(*name):
         k = AT[name]
-        return total[k % 8 : k % 8 + 1, k // 8 : k // 8 + 1]
+        return jnp.broadcast_to(total[k % 8 : k % 8 + 1, k // 8 : k // 8 + 1], (8, LANES))
 
     k_table, g_table = {}, {}
 
@@ -614,17 +668,21 @@
         {i: scales[1] * (f - r * new_first[i] if i in new_first else f) for i, f in new_second.items()},
     ]
     copies = []
+    tall = (prows // 8, 8, LANES)
     for s in range(2):
         at = pl.ds(s * prows, prows)
         for v in range(2):
-            acc = None
-            for i in (0, 1):
-                if i in lead[v]:
-                    f, g = lead[v][i], lead[v][4 + i]
-                    term = f * a_ref[i, at, :] + g * b_ref[i, at, :]
-                    term = term - ((mus[v] * f) * c_ref[i, at, :] + (mus[v] * g) * d_ref[i, at, :])
-                    acc = term if acc is None else acc + term
-            held[v, at, :] = acc
+            for h in range(ncol // LANES):
+                cols = pl.ds(h * LANES, LANES)
+                acc = None
+                for i in (0, 1):
+                    if i in lead[v]:
+                        f, g = lead[v][i], lead[v][4 + i]
+                        parts = [ref[i, at, cols].reshape(tall) for ref in (a_ref, b_ref, c_ref, d_ref)]
+                        term = f * parts[0] + g * parts[1]
+                        term = term - ((mus[v] * f) * parts[2] + (mus[v] * g) * parts[3])
+                        acc = term if acc is None else acc + term
+                held[v, at, cols] = acc.reshape(prows, LANES)
             copies.append(pltpu.make_async_copy(held.at[v, at, :], out_ref.at[v, at, :], sems.at[2 * s + v]))
             copies[-1].start()
     for copy in copies:
@@ -657,18 +715,20 @@
     tile = ((8, LANES), f32)
 
     width = 3 * ncol + LANES
-    (payload,) = call(
-        pack_kernel,
-        [((rows_dev, width), bf16)],
-        "hh",
-        [
-            pltpu.VMEM((1, rows_dev), jnp.int32),
-            pltpu.VMEM((rows_dev, width), bf16),
-            pltpu.SemaphoreType.DMA((8,)),
-        ],
-        out_kind="h",
-    )(
-        pltpu.with_memory_space_constraint(jnp.transpose(prestress, (1, 0, 2)), pltpu.HBM),
+    elem = pltpu.VMEM((1, rows_dev), jnp.int32)
+    planes = jnp.transpose(prestress, (1, 0, 2))
+    if rows_dev == 16 * owners * inner:
+        tiles = 3 * (ncol // LANES)
+        shape = (owners * inner, 16 * tiles + 8, LANES)
+        planes = planes.reshape(3, owners * inner, 16, ncol)
+        sems = [pltpu.SemaphoreType.DMA, pltpu.SemaphoreType.DMA((tiles,)), pltpu.SemaphoreType.DMA((tiles + 1,))]
+        pack = pack_blocks_kernel
+    else:
+        shape = (rows_dev, width)
+        sems = [pltpu.SemaphoreType.DMA((5,))]
+        pack = pack_rows_kernel
+    (payload,) = call(pack, [(shape, bf16)], "hh", [elem, pltpu.VMEM(shape, bf16), *sems], out_kind="h")(
+        pltpu.with_memory_space_constraint(planes, pltpu.HBM),
         pltpu.with_memory_space_constraint(elem_row.reshape(1, rows_dev), pltpu.HBM),
     )
     arrived = lax.all_to_all(
@@ -676,8 +736,7 @@
     )
     halves = ncol // LANES
     (edges,) = call(edge_kernel, [(((2 * halves + 1) * STACK, LANES), f32)], "ssv")(patch_rows, matched, vectors)
-    below = passed_along(edges, "patch", 1)
-    above = passed_along(edges, "patch", -1)
+    below, above = neighbours(edges, "patch")
     k_x, u_k, k_uk, prec, part, rim = call(
         stiff_kernel, [field, field, field, one, sums, ((RIM_STACKS * STACK, ncol), f32)], "svvv"
     )(patch_rows, vectors, thickness, foundation)
@@ -691,13 +750,13 @@
         edges, below, above,
     )
     line, near = line_shared(sent, "patch")
-    a, b, c, d = call(apply_kernel, [field] * 4, "svvvvvvvv")(
+    a, c, d = call(apply_kernel, [field] * 3, "svvvvvvvv")(
         patch_rows, vectors, thickness, foundation, prec, stress, u_g, u_k, k_uk
     )
     (total,) = call(functools.partial(line_kernel, near), [tile], "v" * owners + "a")(*line, a)
     total = summed_over_both(total, "sub", "half")
-    c, d = call(functools.partial(join_kernel, near), [field, field], "sv" + "v" * (len(near[0]) + 3))(
-        patch_rows, prec, line[0], *[line[k] for k in near[0]], c, d
+    b, c, d = call(functools.partial(join_kernel, near), [field] * 3, "sv" + "v" * (len(near[0]) + 5))(
+        patch_rows, prec, stress, u_k, c, d, line[0], *[line[k] for k in near[0]]
     )
     (modes,) = call(
         functools.partial(final_kernel, cells),

time: 39 us -> 38.4 us (0.985)
  waiting for transfers between devices: 7.8 us -> 7.36 us
    ppermute x2, waiting for transfers between devices: 6.29 us -> 5.54 us  [neighbours(): lax.ppermute(array, axis, [(i, i ^ k) for i in range(4)])]
    ppermute x3, waiting for transfers between devices: 0.08 us -> 0.67 us  [line_shared(): lax.ppermute(array, axis, [(i, i ^ k) for i in range(4)])]
    ppermute x3, waiting for transfers between devices: 1.06 us -> 0.58 us  [summed_over_both(): total = total + lax.ppermute(array, (outer, inner), pairs)]
  transfers between devices with their start and end apart: 9 -> 9, of which waited for: 6 -> 5; matrix products, arithmetic and copies ran while one was open for 0% -> 0% of each run, Pallas kernels for 17% -> 17%
where the time goes in v6:
time: 38.4 us; the launch traced here: 38 us
  starting transfers between devices  17.6 us (46%)
  Pallas kernels  12.9 us (34%)
  waiting for transfers between devices  7.36 us (19%)
    all_to_all x1, starting transfers between devices, per_device(): lax.all_to_all(payload, ('patch', 'sub', 'half'), split_axis=0, concat_ax...  7.5 us
    ppermute x2, waiting for transfers between devices, neighbours(): lax.ppermute(array, axis, [(i, i ^ k) for i in range(4)])  5.54 us
    ppermute x3, starting transfers between devices, line_shared(): lax.ppermute(array, axis, [(i, i ^ k) for i in range(4)])  4.4 us
    ppermute x2, starting transfers between devices, neighbours(): lax.ppermute(array, axis, [(i, i ^ k) for i in range(4)])  3.79 us
    pallas_call x1, Pallas kernels, per_device(): call(gram_kernel, [field, field, field, ((3, rows_dev, ncol), f32), (((4...  3.18 us
    pallas_call x1, Pallas kernels, per_device(): call(stiff_kernel, [field, field, field, one, sums, ((RIM_STACKS * STACK,...  2.6 us
    pallas_call x1, Pallas kernels, per_device(): call(apply_kernel, [field] * 3, 'svvvvvvvv')  2 us
    ppermute x3, starting transfers between devices, summed_over_both(): total = total + lax.ppermute(array, (outer, inner), pairs)  1.87 us
  transfers between devices with their start and end apart: 9, of which 5 were waited for; matrix products, arithmetic and copies ran while one was open for 0% of the time, Pallas kernels for 17%

profile of v6, /device:TPU:0, one launch (start us, length us, event | category | flops | bytes accessed | tf_op | source)
XLA Modules:
  0.0 38.0 jit_solution(2297119242332222332)
XLA Ops:
  0.0 1.8 %shard_map.73 = bf16[16,104,128]{2,1,0:T(8,128)(2,1)} custom-call(bf16[3,16,16,256]{3,2,1,0:T(8,128)(2,1)} %bitcast.4, s32[1,256]{1,0:T(1,128)} %bitcast.5), custom_call_target="tpu_custom_call" | custom-call | flops 1000000 | bytes 2000000 | tf_op jit(solution)/shard_map/pallas_call | solution.py:730
  1.8 0.0 copy-start
  1.8 0.0 copy-start.3
  1.8 7.5 %all-to-all-start = ((bf16[16,104,128]{2,1,0:T(8,128)(2,1)}), bf16[16,104,128]{2,1,0:T(8,128)(2,1)S(1)}, u32[]{:S(2)}, u32[]{:S(2)}) async-start(bf16[16,104,128]{2,1,0:T(8,128)(2,1)} %shard_map.73), calls=%async_computation | async-start | bytes 851968 | tf_op jit(solution)/shard_map/all_to_all | solution.py:734
  9.3 0.0 copy-start.1
  9.4 0.6 %shard_map.75.edge_ref = f32[40,128]{1,0:T(8,128)S(1)} custom-call(s32[2]{0:T(128)S(1)} %copy-done.3, s32[2]{0:T(128)S(1)} %copy-done.4, f32[2,256,256]{2,1,0:T(8,128)S(1)} %copy-done), custom_call_target="tpu_custom_call" | custom-call | flops 1000000 | bytes 2000000 | tf_op jit(solution)/shard_map/pallas_call | solution.py:738
  10.0 3.8 %collective-permute-start.1 = (f32[40,128]{1,0:T(8,128)S(1)}, f32[40,128]{1,0:T(8,128)S(1)}, u32[]{:S(2)}, u32[]{:S(2)}) collective-permute-start(f32[40,128]{1,0:T(8,128)S(1)} %shard_map.75.edge_ref), channel_id=1, source_target_pairs={{0,12},{4,8},{8,4},{12,0},{1,13},{5,9},{9,5},{13,1},{2,14},{6,10},... | collective-permute-start | bytes 61448 | tf_op jit(solution)/shard_map/ppermute | solution.py:37
  13.8 2.6 %shard_map.74 = (f32[2,256,256]{2,1,0:T(8,128)S(1)}, f32[2,256,256]{2,1,0:T(8,128)S(1)}, f32[2,256,256]{2,1,0:T(8,128)S(1)}, f32[256,256]{1,0:T(8,128)S(1)}, f32...) custom-call(s32[2]{0:T(128)S(1)} %copy-done.3, f32[2,256,256]{2,1,0:T(8,128)S(1)} %copy-done, f32[256,256]{1,0:T(8,128)S(1)} %copy-done.1, ...), custom_call_target="tpu_custom_call" | custom-call | flops 1000000 | bytes 2000000 | tf_op jit(solution)/shard_map/pallas_call | solution.py:740
  16.4 5.5 %collective-permute-done.1.above_ref = f32[40,128]{1,0:T(8,128)S(1)} collective-permute-done((f32[40,128]{1,0:T(8,128)S(1)}, f32[40,128]{1,0:T(8,128)S(1)}, u32[]{:S(2)}, u32[]{:S(2)}) %collective-permute-start.1) | collective-permute-done | bytes 20512 | tf_op jit(solution)/shard_map/ppermute | solution.py:37
  21.9 0.6 %all-to-all-done.arrived_ref = bf16[16,104,128]{2,1,0:T(8,128)(2,1)S(1)} async-done(((bf16[16,104,128]{2,1,0:T(8,128)(2,1)}), bf16[16,104,128]{2,1,0:T(8,128)(2,1)S(1)}, u32[]{:S(2)}, u32[]{:S(2)}) %all-to-all-start) | async-done | bytes 426016 | tf_op jit(solution)/shard_map/all_to_all | solution.py:734
  22.5 3.2 %shard_map.76 = (f32[2,256,256]{2,1,0:T(8,128)S(1)}, f32[2,256,256]{2,1,0:T(8,128)S(1)}, f32[2,256,256]{2,1,0:T(8,128)S(1)}, f32[3,256,256]{2,1,0:T(8,128)S(1)}, f32[72,128]{1,0:T(8,128)S(1)}) custom-call(s32[2]{0:T(128)S(1)} %copy-done.3, bf16[16,104,128]{2,1,0:T(8,128)(2,1)S(1)} %all-to-all-done.arrived_ref, f32[2,256,256]{2,1,0:T(8,128)S(1)} %copy-done, ...), custom_call_target="tpu_custom_call" | custom-call | flops 1000000 | bytes 2000000 | tf_op jit(solution)/shard_map/pallas_call | solution.py:743
  25.7 1.3 %collective-permute-start.4 = (f32[72,128]{1,0:T(8,128)S(1)}, f32[72,128]{1,0:T(8,128)S(1)}, u32[]{:S(2)}, u32[]{:S(2)}) collective-permute-start(f32[72,128]{1,0:T(8,128)S(1)} %get-tuple-element.28.refs_0_), channel_id=1, source_target_pairs={{0,12},{4,8},{8,4},{12,0},{1,13},{5,9},{9,5},{13,1},{2,14},{6,10},... | collective-permute-start | bytes 110600 | tf_op jit(solution)/shard_map/ppermute | solution.py:44
  27.0 1.6 %collective-permute-start.3 = (f32[72,128]{1,0:T(8,128)S(1)}, f32[72,128]{1,0:T(8,128)S(1)}, u32[]{:S(2)}, u32[]{:S(2)}) collective-permute-start(f32[72,128]{1,0:T(8,128)S(1)} %get-tuple-element.28.refs_0_), channel_id=1, source_target_pairs={{0,8},{4,12},{8,0},{12,4},{1,9},{5,13},{9,1},{13,5},{2,10},{6,14},... | collective-permute-start | bytes 110600 | tf_op jit(solution)/shard_map/ppermute | solution.py:44
  28.6 1.5 %collective-permute-start.2 = (f32[72,128]{1,0:T(8,128)S(1)}, f32[72,128]{1,0:T(8,128)S(1)}, u32[]{:S(2)}, u32[]{:S(2)}) collective-permute-start(f32[72,128]{1,0:T(8,128)S(1)} %get-tuple-element.28.refs_0_), channel_id=1, source_target_pairs={{0,4},{4,0},{8,12},{12,8},{1,5},{5,1},{9,13},{13,9},{2,6},{6,2},{1... | collective-permute-start | bytes 110600 | tf_op jit(solution)/shard_map/ppermute | solution.py:44
  30.1 2.0 %shard_map.77 = (f32[2,256,256]{2,1,0:T(8,128)S(1)}, f32[2,256,256]{2,1,0:T(8,128)S(1)}, f32[2,256,256]{2,1,0:T(8,128)S(1)}) custom-call(s32[2]{0:T(128)S(1)} %copy-done.3, f32[2,256,256]{2,1,0:T(8,128)S(1)} %copy-done, f32[256,256]{1,0:T(8,128)S(1)} %copy-done.1, f32[256,256]{1,0:T(8,128)S(1)} %copy-done.2, f32[256,256]{1,0:T(8,128)S(1)} %get-tuple-element.22.prec_ref, ...), custom_call_target="tpu_custom_call" | custom-call | flops 1000000 | bytes 2000000 | tf_op jit(solution)/shard_map/pallas_call | solution.py:753
  32.1 0.2 collective-permute-done.3.refs_2_
  32.3 0.4 %collective-permute-done.2.refs_1_ = f32[72,128]{1,0:T(8,128)S(1)} collective-permute-done((f32[72,128]{1,0:T(8,128)S(1)}, f32[72,128]{1,0:T(8,128)S(1)}, u32[]{:S(2)}, u32[]{:S(2)}) %collective-permute-start.2) | collective-permute-done | bytes 36896 | tf_op jit(solution)/shard_map/ppermute | solution.py:44
  32.7 0.3 shard_map.78
  33.1 0.1 collective-permute-start.7
  33.2 1.5 %collective-permute-start.6 = (f32[8,128]{1,0:T(8,128)S(1)}, f32[8,128]{1,0:T(8,128)S(1)}, u32[]{:S(2)}, u32[]{:S(2)}) collective-permute-start(f32[8,128]{1,0:T(8,128)S(1)} %shard_map.78), channel_id=1, source_target_pairs={{0,2},{1,3},{2,0},{3,1},{4,6},{5,7},{6,4},{7,5},{8,10},{9,11},{10,... | collective-permute-start | bytes 12296 | tf_op jit(solution)/shard_map/ppermute | solution.py:58
  34.7 0.3 collective-permute-start.5
  34.9 1.3 %shard_map.79 = (f32[2,256,256]{2,1,0:T(8,128)S(1)}, f32[2,256,256]{2,1,0:T(8,128)S(1)}, f32[2,256,256]{2,1,0:T(8,128)S(1)}) custom-call(s32[2]{0:T(128)S(1)} %copy-done.3, f32[256,256]{1,0:T(8,128)S(1)} %get-tuple-element.22.prec_ref, f32[3,256,256]{2,1,0:T(8,128)S(1)} %get-tuple-element.29.stress_ref, f32[2,256,256]{2,1,0:T(8,128)S(1)} %get-tuple-element.31.uk_ref, ...), custom_call_target="tpu_custom_call" | custom-call | flops 1000000 | bytes 2000000 | tf_op jit(solution)/shard_map/pallas_call | solution.py:758
  36.3 0.6 %collective-permute-done.6 = f32[8,128]{1,0:T(8,128)S(1)} collective-permute-done((f32[8,128]{1,0:T(8,128)S(1)}, f32[8,128]{1,0:T(8,128)S(1)}, u32[]{:S(2)}, u32[]{:S(2)}) %collective-permute-start.6) | collective-permute-done | bytes 4128 | tf_op jit(solution)/shard_map/ppermute | solution.py:58
  36.8 1.1 %shard_map.80 = f32[2,256,256]{2,1,0:T(8,128)} custom-call(f32[8,128]{1,0:T(8,128)S(1)} %add_add_fusion.total_ref, f32[2,256,256]{2,1,0:T(8,128)S(1)} %get-tuple-element.33.refs_4_.a_ref, f32[2,256,256]{2,1,0:T(8,128)S(1)} %get-tuple-element.36.b_ref, f32[2,256,256]{2,1,0:T(8,128)S(1)} %get-tuple-element.37.c_ref, f32[2,256,256]{2,1,0:T(8,128)S(1)} %get-tuple-element.38.d_ref), custom_call_target="tpu_custom_call" | custom-call | flops 1000000 | bytes 2000000 | tf_op jit(solution)/shard_map/pallas_call | solution.py:761
  (13 shorter events, 0.0 us)
Async XLA Ops:
  1.8 7.5 %copy-start = (f32[2,256,256]{2,1,0:T(8,128)S(1)}, f32[2,256,256]{2,1,0:T(8,128)}, u32[]{:S(2)}) copy-start(f32[2,256,256]{2,1,0:T(8,128)} %vec_ref.7) | copy-start | bytes 1572868
  1.8 7.5 %copy-start.3 = (s32[2]{0:T(128)S(1)}, s32[2]{0:T(128)}, u32[]{:S(2)}) copy-start(s32[2]{0:T(128)} %rows_ref.9) | copy-start | bytes 28
  1.8 7.5 %copy-start.4 = (s32[2]{0:T(128)S(1)}, s32[2]{0:T(128)}, u32[]{:S(2)}) copy-start(s32[2]{0:T(128)} %matched_ref.1) | copy-start | bytes 28
  1.8 20.7 %all-to-all-start = ((bf16[16,104,128]{2,1,0:T(8,128)(2,1)}), bf16[16,104,128]{2,1,0:T(8,128)(2,1)S(1)}, u32[]{:S(2)}, u32[]{:S(2)}) async-start(bf16[16,104,128]{2,1,0:T(8,128)(2,1)} %shard_map.73), calls=%async_computation | async-start | bytes 851968 | tf_op jit(solution)/shard_map/all_to_all | solution.py:734
  9.3 4.4 %copy-start.1 = (f32[256,256]{1,0:T(8,128)S(1)}, f32[256,256]{1,0:T(8,128)}, u32[]{:S(2)}) copy-start(f32[256,256]{1,0:T(8,128)} %thick_ref.5) | copy-start | bytes 786436
  9.4 4.4 %copy-start.2 = (f32[256,256]{1,0:T(8,128)S(1)}, f32[256,256]{1,0:T(8,128)}, u32[]{:S(2)}) copy-start(f32[256,256]{1,0:T(8,128)} %support_ref.5) | copy-start | bytes 786436
  10.0 11.9 %collective-permute-start.1 = (f32[40,128]{1,0:T(8,128)S(1)}, f32[40,128]{1,0:T(8,128)S(1)}, u32[]{:S(2)}, u32[]{:S(2)}) collective-permute-start(f32[40,128]{1,0:T(8,128)S(1)} %shard_map.75.edge_ref), channel_id=1, source_target_pairs={{0,12},{4,8},{8,4},{12,0},{1,13},{5,9},{9,5},{13,1},{2,14},{6,10},... | collective-permute-start | bytes 61448 | tf_op jit(solution)/shard_map/ppermute | solution.py:37
  13.7 8.2 %collective-permute-start = (f32[40,128]{1,0:T(8,128)S(1)}, f32[40,128]{1,0:T(8,128)S(1)}, u32[]{:S(2)}, u32[]{:S(2)}) collective-permute-start(f32[40,128]{1,0:T(8,128)S(1)} %shard_map.75.edge_ref), channel_id=1, source_target_pairs={{0,4},{4,0},{8,12},{12,8},{1,5},{5,1},{9,13},{13,9},{2,6},{6,2},{1... | collective-permute-start | bytes 61448 | tf_op jit(solution)/shard_map/ppermute | solution.py:37
  25.7 6.4 %collective-permute-start.4 = (f32[72,128]{1,0:T(8,128)S(1)}, f32[72,128]{1,0:T(8,128)S(1)}, u32[]{:S(2)}, u32[]{:S(2)}) collective-permute-start(f32[72,128]{1,0:T(8,128)S(1)} %get-tuple-element.28.refs_0_), channel_id=1, source_target_pairs={{0,12},{4,8},{8,4},{12,0},{1,13},{5,9},{9,5},{13,1},{2,14},{6,10},... | collective-permute-start | bytes 110600 | tf_op jit(solution)/shard_map/ppermute | solution.py:44
  27.0 5.3 %collective-permute-start.3 = (f32[72,128]{1,0:T(8,128)S(1)}, f32[72,128]{1,0:T(8,128)S(1)}, u32[]{:S(2)}, u32[]{:S(2)}) collective-permute-start(f32[72,128]{1,0:T(8,128)S(1)} %get-tuple-element.28.refs_0_), channel_id=1, source_target_pairs={{0,8},{4,12},{8,0},{12,4},{1,9},{5,13},{9,1},{13,5},{2,10},{6,14},... | collective-permute-start | bytes 110600 | tf_op jit(solution)/shard_map/ppermute | solution.py:44
  28.6 4.2 %collective-permute-start.2 = (f32[72,128]{1,0:T(8,128)S(1)}, f32[72,128]{1,0:T(8,128)S(1)}, u32[]{:S(2)}, u32[]{:S(2)}) collective-permute-start(f32[72,128]{1,0:T(8,128)S(1)} %get-tuple-element.28.refs_0_), channel_id=1, source_target_pairs={{0,4},{4,0},{8,12},{12,8},{1,5},{5,1},{9,13},{13,9},{2,6},{6,2},{1... | collective-permute-start | bytes 110600 | tf_op jit(solution)/shard_map/ppermute | solution.py:44
  33.1 3.2 %collective-permute-start.7 = (f32[8,128]{1,0:T(8,128)S(1)}, f32[8,128]{1,0:T(8,128)S(1)}, u32[]{:S(2)}, u32[]{:S(2)}) collective-permute-start(f32[8,128]{1,0:T(8,128)S(1)} %shard_map.78), channel_id=1, source_target_pairs={{0,3},{1,2},{2,1},{3,0},{4,7},{5,6},{6,5},{7,4},{8,11},{9,10},{10,... | collective-permute-start | bytes 12296 | tf_op jit(solution)/shard_map/ppermute | solution.py:58
  33.2 3.6 %collective-permute-start.6 = (f32[8,128]{1,0:T(8,128)S(1)}, f32[8,128]{1,0:T(8,128)S(1)}, u32[]{:S(2)}, u32[]{:S(2)}) collective-permute-start(f32[8,128]{1,0:T(8,128)S(1)} %shard_map.78), channel_id=1, source_target_pairs={{0,2},{1,3},{2,0},{3,1},{4,6},{5,7},{6,4},{7,5},{8,10},{9,11},{10,... | collective-permute-start | bytes 12296 | tf_op jit(solution)/shard_map/ppermute | solution.py:58
  34.7 2.1 %collective-permute-start.5 = (f32[8,128]{1,0:T(8,128)S(1)}, f32[8,128]{1,0:T(8,128)S(1)}, u32[]{:S(2)}, u32[]{:S(2)}) collective-permute-start(f32[8,128]{1,0:T(8,128)S(1)} %shard_map.78), channel_id=1, source_target_pairs={{0,1},{1,0},{2,3},{3,2},{4,5},{5,4},{6,7},{7,6},{8,9},{9,8},{10,11... | collective-permute-start | bytes 12296 | tf_op jit(solution)/shard_map/ppermute | solution.py:58

commit v7 on v6

--- a/solution.py
+++ b/solution.py
@@ -13,18 +13,9 @@
 LANES = 128
 
 UU = [(a, b) for a in range(4) for b in range(a, 4)]
-NAMES = (
-    [("kuu", a, b) for a, b in UU]
-    + [("guu", a, b) for a, b in UU]
-    + [("kxx", 0, 0), ("kxx", 0, 1), ("kxx", 1, 1)]
-    + [("gxx", 0, 0), ("gxx", 0, 1), ("gxx", 1, 1)]
-    + [("kpk", 0, 0), ("kpk", 0, 1), ("kpk", 1, 1)]
-    + [("kpg", a, b) for a in range(2) for b in range(2)]
-    + [("gpg", 0, 0), ("gpg", 0, 1), ("gpg", 1, 1)]
-)
+XX = [(0, 0), (0, 1), (1, 1)]
+NAMES = [(kind,) + pair for kind, pairs in (("kuu", UU), ("guu", UU), ("kxx", XX), ("gxx", XX)) for pair in pairs]
 AT = {name: k for k, name in enumerate(NAMES)}
-SUMS = 40
-TILES = SUMS // 8
 
 
 def passed_along(array, axis, by):
@@ -41,8 +32,8 @@
 def line_shared(array, axis):
     peers = lax.axis_size(axis)
     if peers == 4:
-        shared = [lax.ppermute(array, axis, [(i, i ^ k) for i in range(4)]) for k in (1, 2, 3)]
-        return [array] + shared, [(k ^ 1, k ^ 3) for k in range(4)]
+        shared = [lax.ppermute(array, axis, [(i, i ^ k) for i in range(4)]) for k in (3, 2, 1)]
+        return [array] + shared[::-1], [(k ^ 1, k ^ 3) for k in range(4)]
     shared = [passed_along(array, axis, k) for k in range(1, peers)]
     return [array] + shared, [tuple(sorted({(k + 1) % peers, (k - 1) % peers})) for k in range(peers)]
 
@@ -115,17 +106,19 @@
     )
 
 
-def fluxes(w, stress):
-    along_rows = minus(row_after(w), w)
-    along_cols = minus(col_after(w), w)
+def differences(w):
+    return minus(row_after(w), w), minus(col_after(w), w)
+
+
+def membrane(along_rows, along_cols, stress):
     nuu, nvv, nuv = stress
     rows = each(lambda n, r, m, c: n * r + m * c, nuu, along_rows, nuv, along_cols)
     cols = each(lambda n, c, m, r: n * c + m * r, nvv, along_cols, nuv, along_rows)
-    return along_rows, along_cols, rows, cols
+    return rows, cols
 
 
 def geometric(w, stress):
-    _, _, rows, cols = fluxes(w, stress)
+    rows, cols = membrane(*differences(w), stress)
     return each(
         lambda rb, r, cb, c: (rb - r) + (cb - c), row_before(rows), rows, col_before(cols), cols
     )
@@ -321,16 +314,15 @@
     edge_ref[2 * STACK * halves :, :] = labels_of(rows_ref, matched_ref)
 
 
-FIRST = [("kxx", 0, 0), ("kxx", 0, 1), ("kxx", 1, 1), ("kpk", 0, 0), ("kpk", 0, 1), ("kpk", 1, 1)]
-FIRST += [("kuu", 2, 2), ("kuu", 2, 3), ("kuu", 3, 3)]
-
-
-RIM = [("prec", 2), ("thick", 3), ("support", 2), ("k", 2), ("uk", 2), ("kuk", 2)]
+FIRST = [("kxx", 0, 0), ("kxx", 0, 1), ("kxx", 1, 1), ("kuu", 2, 2), ("kuu", 2, 3), ("kuu", 3, 3)]
+
+
+RIM = [("prec", 2), ("thick", 3), ("support", 2), ("uk", 2), ("kuk", 2)]
 RIM_AT = {name: sum(n for _, n in RIM[:i]) for i, (name, _) in enumerate(RIM)}
 RIM_STACKS = sum(n for _, n in RIM)
 
 
-def stiff_kernel(rows_ref, vec_ref, thick_ref, support_ref, k_ref, uk_ref, kuk_ref, prec_ref, sums_ref, rim_ref):
+def stiff_kernel(rows_ref, vec_ref, thick_ref, support_ref, uk_ref, kuk_ref, prec_ref, sums_ref, rim_ref, k_ref):
     slots = rows_ref.shape[0]
     rows_dev, ncol = thick_ref.shape
     prows = rows_dev // slots
@@ -353,14 +345,13 @@
             for b in range(a, 2):
                 for name, product in (
                     (("kxx", a, b), times(wa, cut(k_ref[b, at, :]))),
-                    (("kpk", a, b), times(cut(k_ref[a, at, :]), cut(uk_ref[b, at, :]))),
                     (("kuu", 2 + a, 2 + b), times(cut(uk_ref[a, at, :]), cut(kuk_ref[b, at, :]))),
                 ):
                     part = folded(product)
                     totals[name] = totals[name] + part if s else part
     for k, name in enumerate(FIRST):
         sums_ref[8 * k : 8 * k + 8, :] = totals[name]
-    sources = {"prec": prec_ref, "thick": thick_ref, "support": support_ref, "k": k_ref, "uk": uk_ref, "kuk": kuk_ref}
+    sources = {"prec": prec_ref, "thick": thick_ref, "support": support_ref, "uk": uk_ref, "kuk": kuk_ref}
     for name, depths in RIM:
         for depth in range(depths):
             for at, v, s, side in stacked(rows_ref, prows):
@@ -380,9 +371,12 @@
     return [ref[STACK * (at + h) : STACK * (at + h + 1), :] for h in range(halves)]
 
 
+PIECE = 16
+
+
 def gram_kernel(
-    rows_ref, arrived_ref, vec_ref, thick_ref, support_ref, prec_ref, k_in, uk_in, kuk_in, sums_in, rim_ref,
-    edge_ref, below_ref, above_ref, ug_ref, uk_ref, kuk_ref, stress_ref, out_ref, g_ref, k_ref,
+    rows_ref, arrived_ref, vec_ref, thick_ref, support_ref, prec_ref, uk_in, kuk_in, sums_in, rim_ref,
+    edge_ref, below_ref, above_ref, v_ref, uk_ref, kuk_ref, stress_ref, out_ref,
 ):
     slots = rows_ref.shape[0]
     rows_dev, ncol = prec_ref.shape
@@ -415,7 +409,6 @@
         if second is not None:
             totals[second] = totals[second] + jnp.where(vector == 1, part, 0.0)
 
-    k_ref[...] = k_in[...]
     uk_ref[...] = uk_in[...]
     kuk_ref[...] = kuk_in[...]
     label = edge_ref[2 * STACK * halves :, :]
@@ -447,67 +440,80 @@
     ]
     for d in range(2):
         n, z, e, x = added[d], scaled[d], extra[d], own[d]
-        k, kuk = rim_of(rim_ref, "k", d), rim_of(rim_ref, "kuk", d)
+        kuk = rim_of(rim_ref, "kuk", d)
         add_stack(("kxx", 0, 0), ("kxx", 1, 1), times(x, n))
         add_stack(("kxx", 0, 1), None, times(x, other_vector(n)))
-        z_turned = other_vector(z)
-        for key, base, more in (("kpk", k, n), ("kuu", kuk, e)):
-            lo = 2 if key == "kuu" else 0
-            turned = other_vector(each(lambda p, q: p + q, base, more))
-            add_stack((key, lo, lo), (key, lo + 1, lo + 1), each(lambda r, p, q: r * (p + p + q), z, base, more))
-            add_stack((key, lo, lo + 1), None, each(lambda r, t, p, w: r * t + p * w, z, turned, base, z_turned))
+        add_stack(("kuu", 2, 2), ("kuu", 3, 3), each(lambda r, p, q: r * (p + p + q), z, kuk, e))
+        turned, z_turned = other_vector(each(lambda p, q: p + q, kuk, e)), other_vector(z)
+        add_stack(("kuu", 2, 3), None, each(lambda r, t, p, w: r * t + p * w, z, turned, kuk, z_turned))
     for d in range(4):
         for at, v, s, side in stacked(rows_ref, prows):
             rows = pl.ds(edge_row(rows_ref, s, side, d, prows), 1)
             kuk_ref[v, rows, :] += joined([p[at : at + 1] for p in extra[d]])
             if d < 2:
-                k_ref[v, rows, :] += joined([p[at : at + 1] for p in added[d]])
                 uk_ref[v, rows, :] += joined([p[at : at + 1] for p in scaled[d]])
-    basis = [(ug_ref, 0), (ug_ref, 1), (uk_ref, 0), (uk_ref, 1)]
     for s in range(slots):
         at = slice(s * prows, (s + 1) * prows)
         live = live_of(rows_ref, s, (prows, LANES))
         stress = [cut(stress_ref[j, at, :]) for j in range(3)]
         prec = cut(prec_ref[at, :])
-        gx = []
-        for v in range(2):
-            gx.append(geometric(masked(live, vec_ref[v, at, :]), stress))
-            ug_ref[v, at, :] = joined(times(prec, gx[v]))
-            g_ref[v, at, :] = joined(gx[v])
-        for a in range(2):
-            wa = masked(live, vec_ref[a, at, :])
-            ga, ka, ua = cut(g_ref[a, at, :]), cut(k_ref[a, at, :]), cut(ug_ref[a, at, :])
-            for b in range(2):
-                ub = cut(ug_ref[b, at, :])
-                if b >= a:
-                    add(("gxx", a, b), times(wa, cut(g_ref[b, at, :])))
-                    add(("gpg", a, b), times(ga, ub))
-                add(("kpg", a, b), times(ka, ub))
-                add(("kuu", a, 2 + b), times(ua, cut(kuk_ref[b, at, :])))
+        x = [masked(live, vec_ref[v, at, :]) for v in range(2)]
+        for b in range(2):
+            gx = geometric(x[b], stress)
+            v_ref[b, at, :] = joined(each(lambda w, p, g: w + p * g, x[b], prec, gx))
+            for a in range(b + 1):
+                add(("gxx", a, b), times(x[a], gx))
+    basis = [(v_ref, 0), (v_ref, 1), (uk_ref, 0), (uk_ref, 1)]
+    pieces = [(s, c) for s in range(slots) for c in range(0, prows, PIECE)]
+
+    def piece(ref, v, s, c, low=0, high=0):
+        start, stop = max(c - low, 0), min(c + PIECE + high, prows)
+        parts = cut(ref[v, s * prows + start : s * prows + stop, :])
+        zero = [jnp.zeros((8, LANES), jnp.float32)]
+        head, tail = zero * ((start - c + low) // 8), zero * ((c + PIECE + high - stop) // 8)
+        return [jnp.concatenate([*head, p, *tail], axis=0) if head or tail else p for p in parts]
+
+    for s, c in pieces:
+        stress = [piece(stress_ref, j, s, c) for j in range(3)]
+        first = []
+        for b in range(4):
+            held = piece(*basis[b], s, c, high=8)
+            w = [p[:PIECE] for p in held]
+            along_rows = [pltpu.roll(p, PIECE + 7, 0)[:PIECE] - q for p, q in zip(held, w)]
+            along_cols = minus(col_after(w), w)
+            first.append((along_rows, along_cols))
+            fr, fc = membrane(along_rows, along_cols, stress)
+            for a in range(b + 1):
+                add(("guu", a, b), each(lambda p, x, q, y: p * x + q * y, first[a][0], fr, first[a][1], fc))
+    for s, c in pieces:
+        at = slice(s * prows + c, s * prows + c + PIECE)
+        live = iota((PIECE, LANES), 0) < rows_ref[s] - c
         thick, support = cut(thick_ref[at, :]), cut(support_ref[at, :])
         live_thick = masked(live, thick_ref[at, :])
         bends = []
         for v in range(2):
-            w = cut(ug_ref[v, at, :])
-            bends.append((w, second_rows(w), second_cols(w)))
+            held = piece(v_ref, v, s, c, 8, 8)
+            w = [p[8 : 8 + PIECE] for p in held]
+            rows = [
+                pltpu.roll(p, PIECE + 15, 0)[8 : 8 + PIECE] + pltpu.roll(p, 1, 0)[8 : 8 + PIECE] - (q + q)
+                for p, q in zip(held, w)
+            ]
+            bends.append((w, rows, second_cols(w)))
         for b in range(2):
-            w, r, c = bends[b]
-            sw, tr, tc = times(support, w), times(live_thick, r), times(thick, c)
+            w, rows, cols = bends[b]
+            sw, tr, tc = times(support, w), times(live_thick, rows), times(thick, cols)
             for a in range(b + 1):
                 add(
                     ("kuu", a, b),
                     each(lambda u, x, p, y, q, z: u * x + p * y + q * z, bends[a][0], sw, bends[a][1], tr, bends[a][2], tc),
                 )
-        first = []
-        for b in range(4):
-            ref, v = basis[b]
-            r, c, fr, fc = fluxes(cut(ref[v, at, :]), stress)
-            first.append((r, c))
-            for a in range(b + 1):
-                add(("guu", a, b), each(lambda p, x, q, y: p * x + q * y, first[a][0], fr, first[a][1], fc))
+        for b in range(2):
+            kuk = piece(kuk_ref, b, s, c)
+            for a in range(2):
+                add(("kuu", a, 2 + b), times(bends[a][0], kuk))
     for d in range(2):
         for at, v, s, side in stacked(rows_ref, prows):
-            row = ug_ref[v, pl.ds(edge_row(rows_ref, s, side, d, prows), 1), :]
+            row = v_ref[v, pl.ds(edge_row(rows_ref, s, side, d, prows), 1), :]
             for h, part in enumerate(cut(row)):
                 to = STACK * (d * halves + h) + at
                 out_ref[to : to + 1, :] = part
@@ -518,9 +524,7 @@
     out_ref[4 * STACK * halves :, :] = jnp.where(iota(tile.shape, 1) == LANES - 1, label, tile)
 
 
-def apply_kernel(
-    rows_ref, vec_ref, thick_ref, support_ref, prec_ref, stress_ref, ug_ref, uk_ref, kuk_ref, a_ref, c_ref, d_ref,
-):
+def apply_kernel(rows_ref, thick_ref, support_ref, prec_ref, stress_ref, v_ref, kuk_ref, a_ref, c_ref, d_ref):
     slots = rows_ref.shape[0]
     rows_dev, ncol = thick_ref.shape
     prows = rows_dev // slots
@@ -532,11 +536,9 @@
         prec = cut(prec_ref[at, :])
         stress = [cut(stress_ref[j, at, :]) for j in range(3)]
         for v in range(2):
-            x, ug, uk = masked(live, vec_ref[v, at, :]), cut(ug_ref[v, at, :]), cut(uk_ref[v, at, :])
-            gg = geometric(ug, stress)
-            kg = stiffness(ug, live_thick, thick, support)
-            a_ref[v, at, :] = joined(each(lambda w, u, p, g: w + (u + u) + p * g, x, ug, prec, gg))
-            c_ref[v, at, :] = joined(each(lambda u, p, k: u + p * k, uk, prec, kg))
+            w = cut(v_ref[v, at, :])
+            a_ref[v, at, :] = joined(each(lambda u, p, g: u + p * g, w, prec, geometric(w, stress)))
+            c_ref[v, at, :] = joined(times(prec, stiffness(w, live_thick, thick, support)))
             d_ref[v, at, :] = joined(times(prec, cut(kuk_ref[v, at, :])))
 
 
@@ -573,7 +575,7 @@
 
 
 def join_kernel(near, rows_ref, prec_ref, stress_ref, uk_ref, c_in, d_in, *refs):
-    line, (b_ref, c_ref, d_ref) = refs[:-3], refs[-3:]
+    line, (b_ref, c_ref, d_ref) = refs[:-4], refs[-3:]
     c_ref[...] = c_in[...]
     d_ref[...] = d_in[...]
     prows = c_in.shape[1] // 2
@@ -616,42 +618,19 @@
         return jnp.broadcast_to(total[k % 8 : k % 8 + 1, k // 8 : k // 8 + 1], (8, LANES))
 
     k_table, g_table = {}, {}
-
-    def put(table, i, j, what):
-        table[i, j] = what
-        table[j, i] = what
-
-    for a in range(2):
-        for b in range(2):
-            lo, hi = min(a, b), max(a, b)
-            put(k_table, a, b, value("kxx", lo, hi))
-            put(g_table, a, b, value("gxx", lo, hi))
-            put(k_table, a, 2 + b, value("kpg", a, b))
-            put(k_table, a, 4 + b, value("kpk", lo, hi))
-            put(g_table, a, 2 + b, value("gpg", lo, hi))
-            put(g_table, a, 4 + b, value("kpg", b, a))
     for a, b in UU:
-        put(k_table, 2 + a, 2 + b, value("kuu", a, b))
-        put(g_table, 2 + a, 2 + b, value("guu", a, b))
-
-    first_a, cross_k, second_a = k_table[0, 0], k_table[0, 1], k_table[1, 1]
-    first_g, cross_g, second_g = g_table[0, 0], g_table[0, 1], g_table[1, 1]
+        k_table[a, b] = k_table[b, a] = value("kuu", a, b)
+        g_table[a, b] = g_table[b, a] = value("guu", a, b)
+    first_a, cross_k, second_a = (value("kxx", a, b) for a, b in XX)
+    first_g, cross_g, second_g = (value("gxx", a, b) for a, b in XX)
     ratio = cross_k / first_a
     other_a = second_a - ratio * cross_k
     other_q = second_g - 2.0 * ratio * cross_g + ratio * ratio * first_g
     mu_first = first_g / first_a
     mu_other = other_q / other_a
-    scale_first = jnp.sqrt(norm_scale * cells / first_a)
-    scale_other = jnp.sqrt(norm_scale * cells / other_a)
-    new_first = {0: scale_first, 2: scale_first, 4: -scale_first * mu_first}
-    new_second = {
-        0: -scale_other * ratio,
-        1: scale_other,
-        2: -scale_other * ratio,
-        3: scale_other,
-        4: scale_other * mu_other * ratio,
-        5: -scale_other * mu_other,
-    }
+    one = jnp.ones_like(ratio)
+    new_first = {0: one, 2: -mu_first}
+    new_second = {0: -ratio, 1: one, 2: mu_other * ratio, 3: -mu_other}
     a1 = form(k_table, new_first, new_first)
     c = form(k_table, new_first, new_second)
     a2 = form(k_table, new_second, new_second)
@@ -677,7 +656,7 @@
                 acc = None
                 for i in (0, 1):
                     if i in lead[v]:
-                        f, g = lead[v][i], lead[v][4 + i]
+                        f, g = lead[v][i], lead[v][2 + i]
                         parts = [ref[i, at, cols].reshape(tall) for ref in (a_ref, b_ref, c_ref, d_ref)]
                         term = f * parts[0] + g * parts[1]
                         term = term - ((mus[v] * f) * parts[2] + (mus[v] * g) * parts[3])
@@ -737,26 +716,28 @@
     halves = ncol // LANES
     (edges,) = call(edge_kernel, [(((2 * halves + 1) * STACK, LANES), f32)], "ssv")(patch_rows, matched, vectors)
     below, above = neighbours(edges, "patch")
-    k_x, u_k, k_uk, prec, part, rim = call(
-        stiff_kernel, [field, field, field, one, sums, ((RIM_STACKS * STACK, ncol), f32)], "svvv"
+    u_k, k_uk, prec, part, rim = call(
+        stiff_kernel,
+        [field, field, one, sums, ((RIM_STACKS * STACK, ncol), f32)],
+        "svvv",
+        [pltpu.VMEM(field[0], f32)],
     )(patch_rows, vectors, thickness, foundation)
-    u_g, u_k, k_uk, stress, sent = call(
+    v, u_k, k_uk, stress, sent = call(
         gram_kernel,
         [field, field, field, ((3, rows_dev, ncol), f32), (((4 * halves + 1) * STACK, LANES), f32)],
-        "svvvvvvvvvvvvv",
-        [pltpu.VMEM(field[0], f32), pltpu.VMEM(field[0], f32)],
+        "svvvvvvvvvvvv",
     )(
-        patch_rows, arrived, vectors, thickness, foundation, prec, k_x, u_k, k_uk, part, rim,
+        patch_rows, arrived, vectors, thickness, foundation, prec, u_k, k_uk, part, rim,
         edges, below, above,
     )
     line, near = line_shared(sent, "patch")
-    a, c, d = call(apply_kernel, [field] * 3, "svvvvvvvv")(
-        patch_rows, vectors, thickness, foundation, prec, stress, u_g, u_k, k_uk
+    a, c, d = call(apply_kernel, [field] * 3, "svvvvvv")(
+        patch_rows, thickness, foundation, prec, stress, v, k_uk
     )
     (total,) = call(functools.partial(line_kernel, near), [tile], "v" * owners + "a")(*line, a)
     total = summed_over_both(total, "sub", "half")
-    b, c, d = call(functools.partial(join_kernel, near), [field] * 3, "sv" + "v" * (len(near[0]) + 5))(
-        patch_rows, prec, stress, u_k, c, d, line[0], *[line[k] for k in near[0]]
+    b, c, d = call(functools.partial(join_kernel, near), [field] * 3, "sv" + "v" * (len(near[0]) + 5) + "a")(
+        patch_rows, prec, stress, u_k, c, d, line[0], *[line[k] for k in near[0]], line[2]
     )
     (modes,) = call(
         functools.partial(final_kernel, cells),

time: 38.4 us -> 38.2 us (level)
  no operation moved by 1% of the time
where the time goes in v7:
time: 38.2 us; the launch traced here: 38 us
  starting transfers between devices  17.6 us (46%)
  Pallas kernels  12.6 us (33%)
  waiting for transfers between devices  7.66 us (20%)
    all_to_all x1, starting transfers between devices, per_device(): lax.all_to_all(payload, ('patch', 'sub', 'half'), split_axis=0, concat_ax...  7.5 us
    ppermute x2, waiting for transfers between devices, neighbours(): lax.ppermute(array, axis, [(i, i ^ k) for i in range(4)])  5.52 us
    ppermute x3, starting transfers between devices, line_shared(): lax.ppermute(array, axis, [(i, i ^ k) for i in range(4)])  4.39 us
    ppermute x2, starting transfers between devices, neighbours(): lax.ppermute(array, axis, [(i, i ^ k) for i in range(4)])  3.79 us
    pallas_call x1, Pallas kernels, per_device(): call(gram_kernel, [field, field, field, ((3, rows_dev, ncol), f32), (((4...  2.85 us
    pallas_call x1, Pallas kernels, per_device(): call(stiff_kernel, [field, field, one, sums, ((RIM_STACKS * STACK, ncol),...  2.61 us
    pallas_call x1, Pallas kernels, per_device(): call(apply_kernel, [field] * 3, 'svvvvvv')  2.03 us
    ppermute x3, starting transfers between devices, summed_over_both(): total = total + lax.ppermute(array, (outer, inner), pairs)  1.87 us
  transfers between devices with their start and end apart: 9, of which 5 were waited for; matrix products, arithmetic and copies ran while one was open for 0% of the time, Pallas kernels for 17%

profile of v7, /device:TPU:0, one launch (start us, length us, event | category | flops | bytes accessed | tf_op | source)
XLA Modules:
  0.0 38.0 jit_solution(6445938006948665677)
XLA Ops:
  0.0 1.8 %shard_map.73 = bf16[16,104,128]{2,1,0:T(8,128)(2,1)} custom-call(bf16[3,16,16,256]{3,2,1,0:T(8,128)(2,1)} %bitcast.4, s32[1,256]{1,0:T(1,128)} %bitcast.5), custom_call_target="tpu_custom_call" | custom-call | flops 1000000 | bytes 2000000 | tf_op jit(solution)/shard_map/pallas_call | solution.py:709
  1.8 0.0 copy-start
  1.8 0.0 copy-start.3
  1.8 7.5 %all-to-all-start = ((bf16[16,104,128]{2,1,0:T(8,128)(2,1)}), bf16[16,104,128]{2,1,0:T(8,128)(2,1)S(1)}, u32[]{:S(2)}, u32[]{:S(2)}) async-start(bf16[16,104,128]{2,1,0:T(8,128)(2,1)} %shard_map.73), calls=%async_computation | async-start | bytes 851968 | tf_op jit(solution)/shard_map/all_to_all | solution.py:713
  9.3 0.0 copy-start.1
  9.4 0.6 %shard_map.75.edge_ref = f32[40,128]{1,0:T(8,128)S(1)} custom-call(s32[2]{0:T(128)S(1)} %copy-done.3, s32[2]{0:T(128)S(1)} %copy-done.4, f32[2,256,256]{2,1,0:T(8,128)S(1)} %copy-done), custom_call_target="tpu_custom_call" | custom-call | flops 1000000 | bytes 2000000 | tf_op jit(solution)/shard_map/pallas_call | solution.py:717
  10.0 3.8 %collective-permute-start.1 = (f32[40,128]{1,0:T(8,128)S(1)}, f32[40,128]{1,0:T(8,128)S(1)}, u32[]{:S(2)}, u32[]{:S(2)}) collective-permute-start(f32[40,128]{1,0:T(8,128)S(1)} %shard_map.75.edge_ref), channel_id=1, source_target_pairs={{0,12},{4,8},{8,4},{12,0},{1,13},{5,9},{9,5},{13,1},{2,14},{6,10},... | collective-permute-start | bytes 61448 | tf_op jit(solution)/shard_map/ppermute | solution.py:28
  13.8 2.6 %shard_map.74 = (f32[2,256,256]{2,1,0:T(8,128)S(1)}, f32[2,256,256]{2,1,0:T(8,128)S(1)}, f32[256,256]{1,0:T(8,128)S(1)}, f32[48,128]{1,0:T(8,128)S(1)}, f32[88,256]{1,0:T(8,128)S(1)}) custom-call(s32[2]{0:T(128)S(1)} %copy-done.3, f32[2,256,256]{2,1,0:T(8,128)S(1)} %copy-done, f32[256,256]{1,0:T(8,128)S(1)} %copy-done.1, f32[256,256]{1,0:T(8,128)S(1)} %copy-done.2), custom_call_target="tpu_custom_call" | custom-call | flops 1000000 | bytes 2000000 | tf_op jit(solution)/shard_map/pallas_call | solution.py:719
  16.4 5.5 %collective-permute-done.1.above_ref = f32[40,128]{1,0:T(8,128)S(1)} collective-permute-done((f32[40,128]{1,0:T(8,128)S(1)}, f32[40,128]{1,0:T(8,128)S(1)}, u32[]{:S(2)}, u32[]{:S(2)}) %collective-permute-start.1) | collective-permute-done | bytes 20512 | tf_op jit(solution)/shard_map/ppermute | solution.py:28
  21.9 0.6 %all-to-all-done.arrived_ref = bf16[16,104,128]{2,1,0:T(8,128)(2,1)S(1)} async-done(((bf16[16,104,128]{2,1,0:T(8,128)(2,1)}), bf16[16,104,128]{2,1,0:T(8,128)(2,1)S(1)}, u32[]{:S(2)}, u32[]{:S(2)}) %all-to-all-start) | async-done | bytes 426016 | tf_op jit(solution)/shard_map/all_to_all | solution.py:713
  22.5 2.9 %shard_map.76 = (f32[2,256,256]{2,1,0:T(8,128)S(1)}, f32[2,256,256]{2,1,0:T(8,128)S(1)}, f32[2,256,256]{2,1,0:T(8,128)S(1)}, f32[3,256,256]{2,1,0:T(8,128)S(1)}, f32[72,128]{1,0:T(8,128)S(1)}) custom-call(s32[2]{0:T(128)S(1)} %copy-done.3, bf16[16,104,128]{2,1,0:T(8,128)(2,1)S(1)} %all-to-all-done.arrived_ref, f32[2,256,256]{2,1,0:T(8,128)S(1)} %copy-done, ...), custom_call_target="tpu_custom_call" | custom-call | flops 1000000 | bytes 2000000 | tf_op jit(solution)/shard_map/pallas_call | solution.py:725
  25.3 1.3 %collective-permute-start.4 = (f32[72,128]{1,0:T(8,128)S(1)}, f32[72,128]{1,0:T(8,128)S(1)}, u32[]{:S(2)}, u32[]{:S(2)}) collective-permute-start(f32[72,128]{1,0:T(8,128)S(1)} %get-tuple-element.26.refs_0_), channel_id=1, source_target_pairs={{0,12},{4,8},{8,4},{12,0},{1,13},{5,9},{9,5},{13,1},{2,14},{6,10},... | collective-permute-start | bytes 110600 | tf_op jit(solution)/shard_map/ppermute | solution.py:35
  26.7 1.6 %collective-permute-start.3 = (f32[72,128]{1,0:T(8,128)S(1)}, f32[72,128]{1,0:T(8,128)S(1)}, u32[]{:S(2)}, u32[]{:S(2)}) collective-permute-start(f32[72,128]{1,0:T(8,128)S(1)} %get-tuple-element.26.refs_0_), channel_id=1, source_target_pairs={{0,8},{4,12},{8,0},{12,4},{1,9},{5,13},{9,1},{13,5},{2,10},{6,14},... | collective-permute-start | bytes 110600 | tf_op jit(solution)/shard_map/ppermute | solution.py:35
  28.2 1.5 %collective-permute-start.2 = (f32[72,128]{1,0:T(8,128)S(1)}, f32[72,128]{1,0:T(8,128)S(1)}, u32[]{:S(2)}, u32[]{:S(2)}) collective-permute-start(f32[72,128]{1,0:T(8,128)S(1)} %get-tuple-element.26.refs_0_), channel_id=1, source_target_pairs={{0,4},{4,0},{8,12},{12,8},{1,5},{5,1},{9,13},{13,9},{2,6},{6,2},{1... | collective-permute-start | bytes 110600 | tf_op jit(solution)/shard_map/ppermute | solution.py:35
  29.7 2.0 %shard_map.77 = (f32[2,256,256]{2,1,0:T(8,128)S(1)}, f32[2,256,256]{2,1,0:T(8,128)S(1)}, f32[2,256,256]{2,1,0:T(8,128)S(1)}) custom-call(s32[2]{0:T(128)S(1)} %copy-done.3, f32[256,256]{1,0:T(8,128)S(1)} %copy-done.1, f32[256,256]{1,0:T(8,128)S(1)} %copy-done.2, f32[256,256]{1,0:T(8,128)S(1)} %get-tuple-element.21.prec_ref, ...), custom_call_target="tpu_custom_call" | custom-call | flops 1000000 | bytes 2000000 | tf_op jit(solution)/shard_map/pallas_call | solution.py:734
  31.8 0.2 collective-permute-done.3.refs_2_.refs_3_
  32.0 0.4 %collective-permute-done.2.refs_1_ = f32[72,128]{1,0:T(8,128)S(1)} collective-permute-done((f32[72,128]{1,0:T(8,128)S(1)}, f32[72,128]{1,0:T(8,128)S(1)}, u32[]{:S(2)}, u32[]{:S(2)}) %collective-permute-start.2) | collective-permute-done | bytes 36896 | tf_op jit(solution)/shard_map/ppermute | solution.py:35
  32.4 0.3 shard_map.78
  32.7 0.5 %collective-permute-start.7 = (f32[8,128]{1,0:T(8,128)S(1)}, f32[8,128]{1,0:T(8,128)S(1)}, u32[]{:S(2)}, u32[]{:S(2)}) collective-permute-start(f32[8,128]{1,0:T(8,128)S(1)} %shard_map.78), channel_id=1, source_target_pairs={{0,3},{1,2},{2,1},{3,0},{4,7},{5,6},{6,5},{7,4},{8,11},{9,10},{10,... | collective-permute-start | bytes 12296 | tf_op jit(solution)/shard_map/ppermute | solution.py:49
  33.3 1.1 %collective-permute-start.6 = (f32[8,128]{1,0:T(8,128)S(1)}, f32[8,128]{1,0:T(8,128)S(1)}, u32[]{:S(2)}, u32[]{:S(2)}) collective-permute-start(f32[8,128]{1,0:T(8,128)S(1)} %shard_map.78), channel_id=1, source_target_pairs={{0,2},{1,3},{2,0},{3,1},{4,6},{5,7},{6,4},{7,5},{8,10},{9,11},{10,... | collective-permute-start | bytes 12296 | tf_op jit(solution)/shard_map/ppermute | solution.py:49
  34.3 0.2 collective-permute-start.5
  34.6 1.3 %shard_map.79 = (f32[2,256,256]{2,1,0:T(8,128)S(1)}, f32[2,256,256]{2,1,0:T(8,128)S(1)}, f32[2,256,256]{2,1,0:T(8,128)S(1)}) custom-call(s32[2]{0:T(128)S(1)} %copy-done.3, f32[256,256]{1,0:T(8,128)S(1)} %get-tuple-element.21.prec_ref, f32[3,256,256]{2,1,0:T(8,128)S(1)} %get-tuple-element.27.stress_ref, f32[2,256,256]{2,1,0:T(8,128)S(1)} %get-tuple-element.31.uk_ref, ...), custom_call_target="tpu_custom_call" | custom-call | flops 1000000 | bytes 2000000 | tf_op jit(solution)/shard_map/pallas_call | solution.py:739
  35.9 0.9 %collective-permute-done.6 = f32[8,128]{1,0:T(8,128)S(1)} collective-permute-done((f32[8,128]{1,0:T(8,128)S(1)}, f32[8,128]{1,0:T(8,128)S(1)}, u32[]{:S(2)}, u32[]{:S(2)}) %collective-permute-start.6) | collective-permute-done | bytes 4128 | tf_op jit(solution)/shard_map/ppermute | solution.py:49
  36.9 1.1 %shard_map.80 = f32[2,256,256]{2,1,0:T(8,128)} custom-call(f32[8,128]{1,0:T(8,128)S(1)} %add_add_fusion.total_ref, f32[2,256,256]{2,1,0:T(8,128)S(1)} %get-tuple-element.30.refs_4_.a_ref, f32[2,256,256]{2,1,0:T(8,128)S(1)} %get-tuple-element.34.b_ref, f32[2,256,256]{2,1,0:T(8,128)S(1)} %get-tuple-element.35.c_ref, f32[2,256,256]{2,1,0:T(8,128)S(1)} %get-tuple-element.36.d_ref), custom_call_target="tpu_custom_call" | custom-call | flops 1000000 | bytes 2000000 | tf_op jit(solution)/shard_map/pallas_call | solution.py:742
  (13 shorter events, 0.0 us)
Async XLA Ops:
  1.8 7.5 %copy-start = (f32[2,256,256]{2,1,0:T(8,128)S(1)}, f32[2,256,256]{2,1,0:T(8,128)}, u32[]{:S(2)}) copy-start(f32[2,256,256]{2,1,0:T(8,128)} %vec_ref.5) | copy-start | bytes 1572868
  1.8 7.5 %copy-start.3 = (s32[2]{0:T(128)S(1)}, s32[2]{0:T(128)}, u32[]{:S(2)}) copy-start(s32[2]{0:T(128)} %rows_ref.9) | copy-start | bytes 28
  1.8 7.5 %copy-start.4 = (s32[2]{0:T(128)S(1)}, s32[2]{0:T(128)}, u32[]{:S(2)}) copy-start(s32[2]{0:T(128)} %matched_ref.1) | copy-start | bytes 28
  1.8 20.7 %all-to-all-start = ((bf16[16,104,128]{2,1,0:T(8,128)(2,1)}), bf16[16,104,128]{2,1,0:T(8,128)(2,1)S(1)}, u32[]{:S(2)}, u32[]{:S(2)}) async-start(bf16[16,104,128]{2,1,0:T(8,128)(2,1)} %shard_map.73), calls=%async_computation | async-start | bytes 851968 | tf_op jit(solution)/shard_map/all_to_all | solution.py:713
  9.3 4.4 %copy-start.1 = (f32[256,256]{1,0:T(8,128)S(1)}, f32[256,256]{1,0:T(8,128)}, u32[]{:S(2)}) copy-start(f32[256,256]{1,0:T(8,128)} %thick_ref.5) | copy-start | bytes 786436
  9.4 4.4 %copy-start.2 = (f32[256,256]{1,0:T(8,128)S(1)}, f32[256,256]{1,0:T(8,128)}, u32[]{:S(2)}) copy-start(f32[256,256]{1,0:T(8,128)} %support_ref.5) | copy-start | bytes 786436
  10.0 11.9 %collective-permute-start.1 = (f32[40,128]{1,0:T(8,128)S(1)}, f32[40,128]{1,0:T(8,128)S(1)}, u32[]{:S(2)}, u32[]{:S(2)}) collective-permute-start(f32[40,128]{1,0:T(8,128)S(1)} %shard_map.75.edge_ref), channel_id=1, source_target_pairs={{0,12},{4,8},{8,4},{12,0},{1,13},{5,9},{9,5},{13,1},{2,14},{6,10},... | collective-permute-start | bytes 61448 | tf_op jit(solution)/shard_map/ppermute | solution.py:28
  13.7 8.2 %collective-permute-start = (f32[40,128]{1,0:T(8,128)S(1)}, f32[40,128]{1,0:T(8,128)S(1)}, u32[]{:S(2)}, u32[]{:S(2)}) collective-permute-start(f32[40,128]{1,0:T(8,128)S(1)} %shard_map.75.edge_ref), channel_id=1, source_target_pairs={{0,4},{4,0},{8,12},{12,8},{1,5},{5,1},{9,13},{13,9},{2,6},{6,2},{1... | collective-permute-start | bytes 61448 | tf_op jit(solution)/shard_map/ppermute | solution.py:28
  25.3 6.4 %collective-permute-start.4 = (f32[72,128]{1,0:T(8,128)S(1)}, f32[72,128]{1,0:T(8,128)S(1)}, u32[]{:S(2)}, u32[]{:S(2)}) collective-permute-start(f32[72,128]{1,0:T(8,128)S(1)} %get-tuple-element.26.refs_0_), channel_id=1, source_target_pairs={{0,12},{4,8},{8,4},{12,0},{1,13},{5,9},{9,5},{13,1},{2,14},{6,10},... | collective-permute-start | bytes 110600 | tf_op jit(solution)/shard_map/ppermute | solution.py:35
  26.7 5.3 %collective-permute-start.3 = (f32[72,128]{1,0:T(8,128)S(1)}, f32[72,128]{1,0:T(8,128)S(1)}, u32[]{:S(2)}, u32[]{:S(2)}) collective-permute-start(f32[72,128]{1,0:T(8,128)S(1)} %get-tuple-element.26.refs_0_), channel_id=1, source_target_pairs={{0,8},{4,12},{8,0},{12,4},{1,9},{5,13},{9,1},{13,5},{2,10},{6,14},... | collective-permute-start | bytes 110600 | tf_op jit(solution)/shard_map/ppermute | solution.py:35
  28.2 4.2 %collective-permute-start.2 = (f32[72,128]{1,0:T(8,128)S(1)}, f32[72,128]{1,0:T(8,128)S(1)}, u32[]{:S(2)}, u32[]{:S(2)}) collective-permute-start(f32[72,128]{1,0:T(8,128)S(1)} %get-tuple-element.26.refs_0_), channel_id=1, source_target_pairs={{0,4},{4,0},{8,12},{12,8},{1,5},{5,1},{9,13},{13,9},{2,6},{6,2},{1... | collective-permute-start | bytes 110600 | tf_op jit(solution)/shard_map/ppermute | solution.py:35
  32.7 3.2 %collective-permute-start.7 = (f32[8,128]{1,0:T(8,128)S(1)}, f32[8,128]{1,0:T(8,128)S(1)}, u32[]{:S(2)}, u32[]{:S(2)}) collective-permute-start(f32[8,128]{1,0:T(8,128)S(1)} %shard_map.78), channel_id=1, source_target_pairs={{0,3},{1,2},{2,1},{3,0},{4,7},{5,6},{6,5},{7,4},{8,11},{9,10},{10,... | collective-permute-start | bytes 12296 | tf_op jit(solution)/shard_map/ppermute | solution.py:49
  33.3 3.6 %collective-permute-start.6 = (f32[8,128]{1,0:T(8,128)S(1)}, f32[8,128]{1,0:T(8,128)S(1)}, u32[]{:S(2)}, u32[]{:S(2)}) collective-permute-start(f32[8,128]{1,0:T(8,128)S(1)} %shard_map.78), channel_id=1, source_target_pairs={{0,2},{1,3},{2,0},{3,1},{4,6},{5,7},{6,4},{7,5},{8,10},{9,11},{10,... | collective-permute-start | bytes 12296 | tf_op jit(solution)/shard_map/ppermute | solution.py:49
  34.3 2.5 %collective-permute-start.5 = (f32[8,128]{1,0:T(8,128)S(1)}, f32[8,128]{1,0:T(8,128)S(1)}, u32[]{:S(2)}, u32[]{:S(2)}) collective-permute-start(f32[8,128]{1,0:T(8,128)S(1)} %shard_map.78), channel_id=1, source_target_pairs={{0,1},{1,0},{2,3},{3,2},{4,5},{5,4},{6,7},{7,6},{8,9},{9,8},{10,11... | collective-permute-start | bytes 12296 | tf_op jit(solution)/shard_map/ppermute | solution.py:49

commit v8 on v7

--- a/solution.py
+++ b/solution.py
@@ -257,30 +257,29 @@
     put.wait()
 
 
-def pack_blocks_kernel(stress_ref, elem_ref, pay_ref, elem, held, get_sem, in_sems, out_sems):
+def pack_blocks_kernel(stress_ref, elem_ref, pay_ref, elem, planes, held, get_sem, in_sems, out_sems):
     blocks, ncol = held.shape[0], stress_ref.shape[3]
     halves = ncol // LANES
     get = pltpu.make_async_copy(elem_ref, elem, get_sem)
     get.start()
-    fetch, put = [], []
-    for t in range(3 * halves):
-        to = held.at[:, pl.ds(16 * t, 16), :]
-        source = stress_ref.at[t // halves, :, :, pl.ds(t % halves * LANES, LANES)]
-        fetch.append(pltpu.make_async_copy(source, to, in_sems.at[t]))
-        put.append(pltpu.make_async_copy(to, pay_ref.at[:, pl.ds(16 * t, 16), :], out_sems.at[t]))
-        fetch[-1].start()
+    fetch = [pltpu.make_async_copy(stress_ref.at[j], planes.at[j], in_sems.at[j]) for j in range(3)]
+    for copy in fetch:
+        copy.start()
+    put = []
     get.wait()
     column = jnp.broadcast_to(local_rows(elem, 16 * blocks), (16 * blocks, LANES))
     lane = iota((8, LANES), 1)
     for k in range(blocks):
         both = jnp.where(lane < LANES // 2, column[16 * k : 16 * k + 8], column[16 * k + 8 : 16 * k + 16])
-        held[k, 48 * halves :, :] = both.astype(jnp.bfloat16)
-    tail = pl.ds(48 * halves, 8)
-    put.append(pltpu.make_async_copy(held.at[:, tail, :], pay_ref.at[:, tail, :], out_sems.at[3 * halves]))
-    put[-1].start()
+        held[k] = both.astype(jnp.bfloat16)
+    put.append(pltpu.make_async_copy(held, pay_ref.at[:, pl.ds(48 * halves, 8), :], out_sems.at[3 * halves]))
+    put[0].start()
     for t in range(3 * halves):
-        fetch[t].wait()
-        put[t].start()
+        if t % halves == 0:
+            fetch[t // halves].wait()
+        source = planes.at[t // halves, :, :, pl.ds(t % halves * LANES, LANES)]
+        put.append(pltpu.make_async_copy(source, pay_ref.at[:, pl.ds(16 * t, 16), :], out_sems.at[t]))
+        put[-1].start()
     for copy in put:
         copy.wait()
 
@@ -702,11 +701,13 @@
         planes = planes.reshape(3, owners * inner, 16, ncol)
         sems = [pltpu.SemaphoreType.DMA, pltpu.SemaphoreType.DMA((tiles,)), pltpu.SemaphoreType.DMA((tiles + 1,))]
         pack = pack_blocks_kernel
+        scratch = [pltpu.VMEM(planes.shape, bf16), pltpu.VMEM((owners * inner, 8, LANES), bf16)]
     else:
         shape = (rows_dev, width)
         sems = [pltpu.SemaphoreType.DMA((5,))]
         pack = pack_rows_kernel
-    (payload,) = call(pack, [(shape, bf16)], "hh", [elem, pltpu.VMEM(shape, bf16), *sems], out_kind="h")(
+        scratch = [pltpu.VMEM(shape, bf16)]
+    (payload,) = call(pack, [(shape, bf16)], "hh", [elem, *scratch, *sems], out_kind="h")(
         pltpu.with_memory_space_constraint(planes, pltpu.HBM),
         pltpu.with_memory_space_constraint(elem_row.reshape(1, rows_dev), pltpu.HBM),
     )

time: 38.2 us -> 38.1 us (level)
  no operation moved by 1% of the time
where the time goes in v8:
time: 38.1 us; the launch traced here: 38 us
  starting transfers between devices  17.6 us (46%)
  Pallas kernels  12.6 us (33%)
  waiting for transfers between devices  7.66 us (20%)
    all_to_all x1, starting transfers between devices, per_device(): lax.all_to_all(payload, ('patch', 'sub', 'half'), split_axis=0, concat_ax...  7.5 us
    ppermute x2, waiting for transfers between devices, neighbours(): lax.ppermute(array, axis, [(i, i ^ k) for i in range(4)])  5.52 us
    ppermute x3, starting transfers between devices, line_shared(): lax.ppermute(array, axis, [(i, i ^ k) for i in range(4)])  4.39 us
    ppermute x2, starting transfers between devices, neighbours(): lax.ppermute(array, axis, [(i, i ^ k) for i in range(4)])  3.79 us
    pallas_call x1, Pallas kernels, per_device(): call(gram_kernel, [field, field, field, ((3, rows_dev, ncol), f32), (((4...  2.85 us
    pallas_call x1, Pallas kernels, per_device(): call(stiff_kernel, [field, field, one, sums, ((RIM_STACKS * STACK, ncol),...  2.61 us
    pallas_call x1, Pallas kernels, per_device(): call(apply_kernel, [field] * 3, 'svvvvvv')  2.03 us
    ppermute x3, starting transfers between devices, summed_over_both(): total = total + lax.ppermute(array, (outer, inner), pairs)  1.87 us
  transfers between devices with their start and end apart: 9, of which 5 were waited for; matrix products, arithmetic and copies ran while one was open for 0% of the time, Pallas kernels for 17%

profile of v8, /device:TPU:0, one launch (start us, length us, event | category | flops | bytes accessed | tf_op | source)
XLA Modules:
  0.0 38.0 jit_solution(5192445202515365882)
XLA Ops:
  0.0 1.8 %shard_map.73 = bf16[16,104,128]{2,1,0:T(8,128)(2,1)} custom-call(bf16[3,16,16,256]{3,2,1,0:T(8,128)(2,1)} %bitcast.4, s32[1,256]{1,0:T(1,128)} %bitcast.5), custom_call_target="tpu_custom_call" | custom-call | flops 1000000 | bytes 2000000 | tf_op jit(solution)/shard_map/pallas_call | solution.py:710
  1.8 0.0 copy-start
  1.9 0.0 copy-start.4
  1.9 7.5 %all-to-all-start = ((bf16[16,104,128]{2,1,0:T(8,128)(2,1)}), bf16[16,104,128]{2,1,0:T(8,128)(2,1)S(1)}, u32[]{:S(2)}, u32[]{:S(2)}) async-start(bf16[16,104,128]{2,1,0:T(8,128)(2,1)} %shard_map.73), calls=%async_computation | async-start | bytes 851968 | tf_op jit(solution)/shard_map/all_to_all | solution.py:714
  9.4 0.0 copy-start.1
  9.4 0.6 %shard_map.75.edge_ref = f32[40,128]{1,0:T(8,128)S(1)} custom-call(s32[2]{0:T(128)S(1)} %copy-done.3, s32[2]{0:T(128)S(1)} %copy-done.4, f32[2,256,256]{2,1,0:T(8,128)S(1)} %copy-done), custom_call_target="tpu_custom_call" | custom-call | flops 1000000 | bytes 2000000 | tf_op jit(solution)/shard_map/pallas_call | solution.py:718
  10.0 3.8 %collective-permute-start.1 = (f32[40,128]{1,0:T(8,128)S(1)}, f32[40,128]{1,0:T(8,128)S(1)}, u32[]{:S(2)}, u32[]{:S(2)}) collective-permute-start(f32[40,128]{1,0:T(8,128)S(1)} %shard_map.75.edge_ref), channel_id=1, source_target_pairs={{0,12},{4,8},{8,4},{12,0},{1,13},{5,9},{9,5},{13,1},{2,14},{6,10},... | collective-permute-start | bytes 61448 | tf_op jit(solution)/shard_map/ppermute | solution.py:28
  13.8 2.6 %shard_map.74 = (f32[2,256,256]{2,1,0:T(8,128)S(1)}, f32[2,256,256]{2,1,0:T(8,128)S(1)}, f32[256,256]{1,0:T(8,128)S(1)}, f32[48,128]{1,0:T(8,128)S(1)}, f32[88,256]{1,0:T(8,128)S(1)}) custom-call(s32[2]{0:T(128)S(1)} %copy-done.3, f32[2,256,256]{2,1,0:T(8,128)S(1)} %copy-done, f32[256,256]{1,0:T(8,128)S(1)} %copy-done.1, f32[256,256]{1,0:T(8,128)S(1)} %copy-done.2), custom_call_target="tpu_custom_call" | custom-call | flops 1000000 | bytes 2000000 | tf_op jit(solution)/shard_map/pallas_call | solution.py:720
  16.4 5.5 %collective-permute-done.1.above_ref = f32[40,128]{1,0:T(8,128)S(1)} collective-permute-done((f32[40,128]{1,0:T(8,128)S(1)}, f32[40,128]{1,0:T(8,128)S(1)}, u32[]{:S(2)}, u32[]{:S(2)}) %collective-permute-start.1) | collective-permute-done | bytes 20512 | tf_op jit(solution)/shard_map/ppermute | solution.py:28
  22.0 0.6 %all-to-all-done.arrived_ref = bf16[16,104,128]{2,1,0:T(8,128)(2,1)S(1)} async-done(((bf16[16,104,128]{2,1,0:T(8,128)(2,1)}), bf16[16,104,128]{2,1,0:T(8,128)(2,1)S(1)}, u32[]{:S(2)}, u32[]{:S(2)}) %all-to-all-start) | async-done | bytes 426016 | tf_op jit(solution)/shard_map/all_to_all | solution.py:714
  22.5 2.8 %shard_map.76 = (f32[2,256,256]{2,1,0:T(8,128)S(1)}, f32[2,256,256]{2,1,0:T(8,128)S(1)}, f32[2,256,256]{2,1,0:T(8,128)S(1)}, f32[3,256,256]{2,1,0:T(8,128)S(1)}, f32[72,128]{1,0:T(8,128)S(1)}) custom-call(s32[2]{0:T(128)S(1)} %copy-done.3, bf16[16,104,128]{2,1,0:T(8,128)(2,1)S(1)} %all-to-all-done.arrived_ref, f32[2,256,256]{2,1,0:T(8,128)S(1)} %copy-done, ...), custom_call_target="tpu_custom_call" | custom-call | flops 1000000 | bytes 2000000 | tf_op jit(solution)/shard_map/pallas_call | solution.py:726
  25.4 1.3 %collective-permute-start.4 = (f32[72,128]{1,0:T(8,128)S(1)}, f32[72,128]{1,0:T(8,128)S(1)}, u32[]{:S(2)}, u32[]{:S(2)}) collective-permute-start(f32[72,128]{1,0:T(8,128)S(1)} %get-tuple-element.26.refs_0_), channel_id=1, source_target_pairs={{0,12},{4,8},{8,4},{12,0},{1,13},{5,9},{9,5},{13,1},{2,14},{6,10},... | collective-permute-start | bytes 110600 | tf_op jit(solution)/shard_map/ppermute | solution.py:35
  26.7 1.6 %collective-permute-start.3 = (f32[72,128]{1,0:T(8,128)S(1)}, f32[72,128]{1,0:T(8,128)S(1)}, u32[]{:S(2)}, u32[]{:S(2)}) collective-permute-start(f32[72,128]{1,0:T(8,128)S(1)} %get-tuple-element.26.refs_0_), channel_id=1, source_target_pairs={{0,8},{4,12},{8,0},{12,4},{1,9},{5,13},{9,1},{13,5},{2,10},{6,14},... | collective-permute-start | bytes 110600 | tf_op jit(solution)/shard_map/ppermute | solution.py:35
  28.3 1.5 %collective-permute-start.2 = (f32[72,128]{1,0:T(8,128)S(1)}, f32[72,128]{1,0:T(8,128)S(1)}, u32[]{:S(2)}, u32[]{:S(2)}) collective-permute-start(f32[72,128]{1,0:T(8,128)S(1)} %get-tuple-element.26.refs_0_), channel_id=1, source_target_pairs={{0,4},{4,0},{8,12},{12,8},{1,5},{5,1},{9,13},{13,9},{2,6},{6,2},{1... | collective-permute-start | bytes 110600 | tf_op jit(solution)/shard_map/ppermute | solution.py:35
  29.8 2.0 %shard_map.77 = (f32[2,256,256]{2,1,0:T(8,128)S(1)}, f32[2,256,256]{2,1,0:T(8,128)S(1)}, f32[2,256,256]{2,1,0:T(8,128)S(1)}) custom-call(s32[2]{0:T(128)S(1)} %copy-done.3, f32[256,256]{1,0:T(8,128)S(1)} %copy-done.1, f32[256,256]{1,0:T(8,128)S(1)} %copy-done.2, f32[256,256]{1,0:T(8,128)S(1)} %get-tuple-element.21.prec_ref, ...), custom_call_target="tpu_custom_call" | custom-call | flops 1000000 | bytes 2000000 | tf_op jit(solution)/shard_map/pallas_call | solution.py:735
  31.8 0.2 collective-permute-done.3.refs_2_.refs_3_
  32.0 0.4 %collective-permute-done.2.refs_1_ = f32[72,128]{1,0:T(8,128)S(1)} collective-permute-done((f32[72,128]{1,0:T(8,128)S(1)}, f32[72,128]{1,0:T(8,128)S(1)}, u32[]{:S(2)}, u32[]{:S(2)}) %collective-permute-start.2) | collective-permute-done | bytes 36896 | tf_op jit(solution)/shard_map/ppermute | solution.py:35
  32.5 0.3 shard_map.78
  32.8 0.5 %collective-permute-start.7 = (f32[8,128]{1,0:T(8,128)S(1)}, f32[8,128]{1,0:T(8,128)S(1)}, u32[]{:S(2)}, u32[]{:S(2)}) collective-permute-start(f32[8,128]{1,0:T(8,128)S(1)} %shard_map.78), channel_id=1, source_target_pairs={{0,3},{1,2},{2,1},{3,0},{4,7},{5,6},{6,5},{7,4},{8,11},{9,10},{10,... | collective-permute-start | bytes 12296 | tf_op jit(solution)/shard_map/ppermute | solution.py:49
  33.3 1.1 %collective-permute-start.6 = (f32[8,128]{1,0:T(8,128)S(1)}, f32[8,128]{1,0:T(8,128)S(1)}, u32[]{:S(2)}, u32[]{:S(2)}) collective-permute-start(f32[8,128]{1,0:T(8,128)S(1)} %shard_map.78), channel_id=1, source_target_pairs={{0,2},{1,3},{2,0},{3,1},{4,6},{5,7},{6,4},{7,5},{8,10},{9,11},{10,... | collective-permute-start | bytes 12296 | tf_op jit(solution)/shard_map/ppermute | solution.py:49
  34.4 0.3 collective-permute-start.5
  34.6 1.3 %shard_map.79 = (f32[2,256,256]{2,1,0:T(8,128)S(1)}, f32[2,256,256]{2,1,0:T(8,128)S(1)}, f32[2,256,256]{2,1,0:T(8,128)S(1)}) custom-call(s32[2]{0:T(128)S(1)} %copy-done.3, f32[256,256]{1,0:T(8,128)S(1)} %get-tuple-element.21.prec_ref, f32[3,256,256]{2,1,0:T(8,128)S(1)} %get-tuple-element.27.stress_ref, f32[2,256,256]{2,1,0:T(8,128)S(1)} %get-tuple-element.31.uk_ref, ...), custom_call_target="tpu_custom_call" | custom-call | flops 1000000 | bytes 2000000 | tf_op jit(solution)/shard_map/pallas_call | solution.py:740
  36.0 0.9 %collective-permute-done.6 = f32[8,128]{1,0:T(8,128)S(1)} collective-permute-done((f32[8,128]{1,0:T(8,128)S(1)}, f32[8,128]{1,0:T(8,128)S(1)}, u32[]{:S(2)}, u32[]{:S(2)}) %collective-permute-start.6) | collective-permute-done | bytes 4128 | tf_op jit(solution)/shard_map/ppermute | solution.py:49
  36.9 1.1 %shard_map.80 = f32[2,256,256]{2,1,0:T(8,128)} custom-call(f32[8,128]{1,0:T(8,128)S(1)} %add_add_fusion.total_ref, f32[2,256,256]{2,1,0:T(8,128)S(1)} %get-tuple-element.30.refs_4_.a_ref, f32[2,256,256]{2,1,0:T(8,128)S(1)} %get-tuple-element.34.b_ref, f32[2,256,256]{2,1,0:T(8,128)S(1)} %get-tuple-element.35.c_ref, f32[2,256,256]{2,1,0:T(8,128)S(1)} %get-tuple-element.36.d_ref), custom_call_target="tpu_custom_call" | custom-call | flops 1000000 | bytes 2000000 | tf_op jit(solution)/shard_map/pallas_call | solution.py:743
  (13 shorter events, 0.0 us)
Async XLA Ops:
  1.8 7.5 %copy-start = (f32[2,256,256]{2,1,0:T(8,128)S(1)}, f32[2,256,256]{2,1,0:T(8,128)}, u32[]{:S(2)}) copy-start(f32[2,256,256]{2,1,0:T(8,128)} %vec_ref.5) | copy-start | bytes 1572868
  1.8 7.5 %copy-start.3 = (s32[2]{0:T(128)S(1)}, s32[2]{0:T(128)}, u32[]{:S(2)}) copy-start(s32[2]{0:T(128)} %rows_ref.9) | copy-start | bytes 28
  1.9 7.5 %copy-start.4 = (s32[2]{0:T(128)S(1)}, s32[2]{0:T(128)}, u32[]{:S(2)}) copy-start(s32[2]{0:T(128)} %matched_ref.1) | copy-start | bytes 28
  1.9 20.7 %all-to-all-start = ((bf16[16,104,128]{2,1,0:T(8,128)(2,1)}), bf16[16,104,128]{2,1,0:T(8,128)(2,1)S(1)}, u32[]{:S(2)}, u32[]{:S(2)}) async-start(bf16[16,104,128]{2,1,0:T(8,128)(2,1)} %shard_map.73), calls=%async_computation | async-start | bytes 851968 | tf_op jit(solution)/shard_map/all_to_all | solution.py:714
  9.4 4.4 %copy-start.1 = (f32[256,256]{1,0:T(8,128)S(1)}, f32[256,256]{1,0:T(8,128)}, u32[]{:S(2)}) copy-start(f32[256,256]{1,0:T(8,128)} %thick_ref.5) | copy-start | bytes 786436
  9.4 4.4 %copy-start.2 = (f32[256,256]{1,0:T(8,128)S(1)}, f32[256,256]{1,0:T(8,128)}, u32[]{:S(2)}) copy-start(f32[256,256]{1,0:T(8,128)} %support_ref.5) | copy-start | bytes 786436
  10.0 11.9 %collective-permute-start.1 = (f32[40,128]{1,0:T(8,128)S(1)}, f32[40,128]{1,0:T(8,128)S(1)}, u32[]{:S(2)}, u32[]{:S(2)}) collective-permute-start(f32[40,128]{1,0:T(8,128)S(1)} %shard_map.75.edge_ref), channel_id=1, source_target_pairs={{0,12},{4,8},{8,4},{12,0},{1,13},{5,9},{9,5},{13,1},{2,14},{6,10},... | collective-permute-start | bytes 61448 | tf_op jit(solution)/shard_map/ppermute | solution.py:28
  13.8 8.2 %collective-permute-start = (f32[40,128]{1,0:T(8,128)S(1)}, f32[40,128]{1,0:T(8,128)S(1)}, u32[]{:S(2)}, u32[]{:S(2)}) collective-permute-start(f32[40,128]{1,0:T(8,128)S(1)} %shard_map.75.edge_ref), channel_id=1, source_target_pairs={{0,4},{4,0},{8,12},{12,8},{1,5},{5,1},{9,13},{13,9},{2,6},{6,2},{1... | collective-permute-start | bytes 61448 | tf_op jit(solution)/shard_map/ppermute | solution.py:28
  25.4 6.4 %collective-permute-start.4 = (f32[72,128]{1,0:T(8,128)S(1)}, f32[72,128]{1,0:T(8,128)S(1)}, u32[]{:S(2)}, u32[]{:S(2)}) collective-permute-start(f32[72,128]{1,0:T(8,128)S(1)} %get-tuple-element.26.refs_0_), channel_id=1, source_target_pairs={{0,12},{4,8},{8,4},{12,0},{1,13},{5,9},{9,5},{13,1},{2,14},{6,10},... | collective-permute-start | bytes 110600 | tf_op jit(solution)/shard_map/ppermute | solution.py:35
  26.7 5.3 %collective-permute-start.3 = (f32[72,128]{1,0:T(8,128)S(1)}, f32[72,128]{1,0:T(8,128)S(1)}, u32[]{:S(2)}, u32[]{:S(2)}) collective-permute-start(f32[72,128]{1,0:T(8,128)S(1)} %get-tuple-element.26.refs_0_), channel_id=1, source_target_pairs={{0,8},{4,12},{8,0},{12,4},{1,9},{5,13},{9,1},{13,5},{2,10},{6,14},... | collective-permute-start | bytes 110600 | tf_op jit(solution)/shard_map/ppermute | solution.py:35
  28.3 4.2 %collective-permute-start.2 = (f32[72,128]{1,0:T(8,128)S(1)}, f32[72,128]{1,0:T(8,128)S(1)}, u32[]{:S(2)}, u32[]{:S(2)}) collective-permute-start(f32[72,128]{1,0:T(8,128)S(1)} %get-tuple-element.26.refs_0_), channel_id=1, source_target_pairs={{0,4},{4,0},{8,12},{12,8},{1,5},{5,1},{9,13},{13,9},{2,6},{6,2},{1... | collective-permute-start | bytes 110600 | tf_op jit(solution)/shard_map/ppermute | solution.py:35
  32.8 3.2 %collective-permute-start.7 = (f32[8,128]{1,0:T(8,128)S(1)}, f32[8,128]{1,0:T(8,128)S(1)}, u32[]{:S(2)}, u32[]{:S(2)}) collective-permute-start(f32[8,128]{1,0:T(8,128)S(1)} %shard_map.78), channel_id=1, source_target_pairs={{0,3},{1,2},{2,1},{3,0},{4,7},{5,6},{6,5},{7,4},{8,11},{9,10},{10,... | collective-permute-start | bytes 12296 | tf_op jit(solution)/shard_map/ppermute | solution.py:49
  33.3 3.6 %collective-permute-start.6 = (f32[8,128]{1,0:T(8,128)S(1)}, f32[8,128]{1,0:T(8,128)S(1)}, u32[]{:S(2)}, u32[]{:S(2)}) collective-permute-start(f32[8,128]{1,0:T(8,128)S(1)} %shard_map.78), channel_id=1, source_target_pairs={{0,2},{1,3},{2,0},{3,1},{4,6},{5,7},{6,4},{7,5},{8,10},{9,11},{10,... | collective-permute-start | bytes 12296 | tf_op jit(solution)/shard_map/ppermute | solution.py:49
  34.4 2.5 %collective-permute-start.5 = (f32[8,128]{1,0:T(8,128)S(1)}, f32[8,128]{1,0:T(8,128)S(1)}, u32[]{:S(2)}, u32[]{:S(2)}) collective-permute-start(f32[8,128]{1,0:T(8,128)S(1)} %shard_map.78), channel_id=1, source_target_pairs={{0,1},{1,0},{2,3},{3,2},{4,5},{5,4},{6,7},{7,6},{8,9},{9,8},{10,11... | collective-permute-start | bytes 12296 | tf_op jit(solution)/shard_map/ppermute | solution.py:49

commit v9 on v8

--- a/solution.py
+++ b/solution.py
@@ -257,21 +257,35 @@
     put.wait()
 
 
-def pack_blocks_kernel(stress_ref, elem_ref, pay_ref, elem, planes, held, get_sem, in_sems, out_sems):
+LABEL_LANE = 32
+
+
+def neighbour_labels(arrived_ref, back, halves):
+    me, peers, inner = lax.axis_index("patch"), lax.axis_size("patch"), lax.axis_size(("sub", "half"))
+    there = jnp.bitwise_xor(me, back) if peers == 4 else lax.rem(me - back + peers, peers)
+    block = there * inner + lax.axis_index(("sub", "half"))
+    return arrived_ref[block, 48 * halves :, :].astype(jnp.float32)[:, LABEL_LANE : LABEL_LANE + 1]
+
+
+def pack_blocks_kernel(stress_ref, elem_ref, matched_ref, pay_ref, elem, planes, held, match, get_sem, in_sems, out_sems):
     blocks, ncol = held.shape[0], stress_ref.shape[3]
     halves = ncol // LANES
     get = pltpu.make_async_copy(elem_ref, elem, get_sem)
     get.start()
+    ask = pltpu.make_async_copy(matched_ref, match, out_sems.at[0])
+    ask.start()
     fetch = [pltpu.make_async_copy(stress_ref.at[j], planes.at[j], in_sems.at[j]) for j in range(3)]
     for copy in fetch:
         copy.start()
     put = []
     get.wait()
     column = jnp.broadcast_to(local_rows(elem, 16 * blocks), (16 * blocks, LANES))
+    ask.wait()
+    labels = labels_of(None, match)
     lane = iota((8, LANES), 1)
     for k in range(blocks):
         both = jnp.where(lane < LANES // 2, column[16 * k : 16 * k + 8], column[16 * k + 8 : 16 * k + 16])
-        held[k] = both.astype(jnp.bfloat16)
+        held[k] = jnp.where(lane == LABEL_LANE, labels, both).astype(jnp.bfloat16)
     put.append(pltpu.make_async_copy(held, pay_ref.at[:, pl.ds(48 * halves, 8), :], out_sems.at[3 * halves]))
     put[0].start()
     for t in range(3 * halves):
@@ -416,7 +430,12 @@
         return [[ref[STACK * (d * halves + h) : STACK * (d * halves + h + 1), :] for h in range(halves)] for d in range(2)]
 
     own = depths_of(edge_ref)
-    met = opposite(label, [(ref[2 * STACK * halves :, :], depths_of(ref)) for ref in (below_ref, above_ref)])
+    if len(arrived_ref.shape) == 2:
+        labels = [ref[2 * STACK * halves :, :] for ref in (below_ref, above_ref)]
+    else:
+        backs = (1, 3) if lax.axis_size("patch") == 4 else (1, -1)
+        labels = [neighbour_labels(arrived_ref, back, halves) for back in backs]
+    met = opposite(label, [(near, depths_of(ref)) for near, ref in zip(labels, (below_ref, above_ref))])
     added = interface_rows(own, met)
     scaled = [times(rim_of(rim_ref, "prec", d), added[d]) for d in range(2)]
     bend = [
@@ -701,22 +720,24 @@
         planes = planes.reshape(3, owners * inner, 16, ncol)
         sems = [pltpu.SemaphoreType.DMA, pltpu.SemaphoreType.DMA((tiles,)), pltpu.SemaphoreType.DMA((tiles + 1,))]
         pack = pack_blocks_kernel
-        scratch = [pltpu.VMEM(planes.shape, bf16), pltpu.VMEM((owners * inner, 8, LANES), bf16)]
+        scratch = [pltpu.VMEM(planes.shape, bf16), pltpu.VMEM((owners * inner, 8, LANES), bf16), pltpu.SMEM(matched.shape, jnp.int32)]
+        extra = [pltpu.with_memory_space_constraint(matched, pltpu.HBM)]
     else:
         shape = (rows_dev, width)
         sems = [pltpu.SemaphoreType.DMA((5,))]
         pack = pack_rows_kernel
-        scratch = [pltpu.VMEM(shape, bf16)]
-    (payload,) = call(pack, [(shape, bf16)], "hh", [elem, *scratch, *sems], out_kind="h")(
+        scratch, extra = [pltpu.VMEM(shape, bf16)], []
+    (payload,) = call(pack, [(shape, bf16)], "h" * (2 + len(extra)), [elem, *scratch, *sems], out_kind="h")(
         pltpu.with_memory_space_constraint(planes, pltpu.HBM),
         pltpu.with_memory_space_constraint(elem_row.reshape(1, rows_dev), pltpu.HBM),
+        *extra,
     )
     arrived = lax.all_to_all(
         payload, ("patch", "sub", "half"), split_axis=0, concat_axis=0, tiled=True
     )
     halves = ncol // LANES
     (edges,) = call(edge_kernel, [(((2 * halves + 1) * STACK, LANES), f32)], "ssv")(patch_rows, matched, vectors)
-    below, above = neighbours(edges, "patch")
+    below, above = neighbours(edges[: 2 * STACK * halves] if extra else edges, "patch")
     u_k, k_uk, prec, part, rim = call(
         stiff_kernel,
         [field, field, one, sums, ((RIM_STACKS * STACK, ncol), f32)],

time: 38.1 us -> 38.1 us (level)
  no operation moved by 1% of the time
where the time goes in v9:
time: 38.1 us; the launch traced here: 37.9 us
  starting transfers between devices  17.6 us (46%)
  Pallas kernels  12.5 us (33%)
  waiting for transfers between devices  7.61 us (20%)
    all_to_all x1, starting transfers between devices, per_device(): lax.all_to_all(payload, ('patch', 'sub', 'half'), split_axis=0, concat_ax...  7.5 us
    ppermute x2, waiting for transfers between devices, neighbours(): lax.ppermute(array, axis, [(i, i ^ k) for i in range(4)])  5.32 us
    ppermute x3, starting transfers between devices, line_shared(): lax.ppermute(array, axis, [(i, i ^ k) for i in range(4)])  4.39 us
    ppermute x2, starting transfers between devices, neighbours(): lax.ppermute(array, axis, [(i, i ^ k) for i in range(4)])  3.79 us
    pallas_call x1, Pallas kernels, per_device(): call(gram_kernel, [field, field, field, ((3, rows_dev, ncol), f32), (((4...  2.8 us
    pallas_call x1, Pallas kernels, per_device(): call(stiff_kernel, [field, field, one, sums, ((RIM_STACKS * STACK, ncol),...  2.67 us
    pallas_call x1, Pallas kernels, per_device(): call(apply_kernel, [field] * 3, 'svvvvvv')  1.97 us
    ppermute x3, starting transfers between devices, summed_over_both(): total = total + lax.ppermute(array, (outer, inner), pairs)  1.87 us
  transfers between devices with their start and end apart: 9, of which 5 were waited for; matrix products, arithmetic and copies ran while one was open for 0% of the time, Pallas kernels for 17%

profile of v9, /device:TPU:0, one launch (start us, length us, event | category | flops | bytes accessed | tf_op | source)
XLA Modules:
  0.0 37.9 jit_solution(17807148499473975869)
XLA Ops:
  0.0 1.8 %shard_map.73 = bf16[16,104,128]{2,1,0:T(8,128)(2,1)} custom-call(bf16[3,16,16,256]{3,2,1,0:T(8,128)(2,1)} %bitcast.4, s32[1,256]{1,0:T(1,128)} %bitcast.5, s32[2]{0:T(128)} %matched_ref.3), custom_call_target="tpu_custom_call" | custom-call | flops 1000000 | bytes 2000000 | tf_op jit(solution)/shard_map/pallas_call | solution.py:730
  1.8 0.0 copy-start
  1.8 0.0 copy-start.3
  1.9 0.0 copy-start.4
  1.9 7.5 %all-to-all-start = ((bf16[16,104,128]{2,1,0:T(8,128)(2,1)}), bf16[16,104,128]{2,1,0:T(8,128)(2,1)S(1)}, u32[]{:S(2)}, u32[]{:S(2)}) async-start(bf16[16,104,128]{2,1,0:T(8,128)(2,1)} %shard_map.73), calls=%async_computation | async-start | bytes 851968 | tf_op jit(solution)/shard_map/all_to_all | solution.py:735
  9.4 0.6 %shard_map.75.edge_ref = f32[40,128]{1,0:T(8,128)S(1)} custom-call(s32[2]{0:T(128)S(1)} %copy-done.3, s32[2]{0:T(128)S(1)} %copy-done.4, f32[2,256,256]{2,1,0:T(8,128)S(1)} %copy-done), custom_call_target="tpu_custom_call" | custom-call | flops 1000000 | bytes 2000000 | tf_op jit(solution)/shard_map/pallas_call | solution.py:739
  10.0 3.8 %collective-permute-start.1 = (f32[32,128]{1,0:T(8,128)S(1)}, f32[32,128]{1,0:T(8,128)S(1)}, u32[]{:S(2)}, u32[]{:S(2)}) collective-permute-start(f32[32,128]{1,0:T(8,128)S(1)} %slice.4), channel_id=1, source_target_pairs={{0,12},{4,8},{8,4},{12,0},{1,13},{5,9},{9,5},{13,1},{2,14},{6,10},... | collective-permute-start | bytes 49160 | tf_op jit(solution)/shard_map/ppermute | solution.py:28
  13.8 2.7 %shard_map.74 = (f32[2,256,256]{2,1,0:T(8,128)S(1)}, f32[2,256,256]{2,1,0:T(8,128)S(1)}, f32[256,256]{1,0:T(8,128)S(1)}, f32[48,128]{1,0:T(8,128)S(1)}, f32[88,256]{1,0:T(8,128)S(1)}) custom-call(s32[2]{0:T(128)S(1)} %copy-done.3, f32[2,256,256]{2,1,0:T(8,128)S(1)} %copy-done, f32[256,256]{1,0:T(8,128)S(1)} %copy-done.1, f32[256,256]{1,0:T(8,128)S(1)} %copy-done.2), custom_call_target="tpu_custom_call" | custom-call | flops 1000000 | bytes 2000000 | tf_op jit(solution)/shard_map/pallas_call | solution.py:741
  16.5 5.3 %collective-permute-done.1.above_ref = f32[32,128]{1,0:T(8,128)S(1)} collective-permute-done((f32[32,128]{1,0:T(8,128)S(1)}, f32[32,128]{1,0:T(8,128)S(1)}, u32[]{:S(2)}, u32[]{:S(2)}) %collective-permute-start.1) | collective-permute-done | bytes 16416 | tf_op jit(solution)/shard_map/ppermute | solution.py:28
  21.8 0.6 %all-to-all-done.arrived_ref = bf16[16,104,128]{2,1,0:T(8,128)(2,1)S(1)} async-done(((bf16[16,104,128]{2,1,0:T(8,128)(2,1)}), bf16[16,104,128]{2,1,0:T(8,128)(2,1)S(1)}, u32[]{:S(2)}, u32[]{:S(2)}) %all-to-all-start) | async-done | bytes 426016 | tf_op jit(solution)/shard_map/all_to_all | solution.py:735
  22.4 2.8 %shard_map.76 = (f32[2,256,256]{2,1,0:T(8,128)S(1)}, f32[2,256,256]{2,1,0:T(8,128)S(1)}, f32[2,256,256]{2,1,0:T(8,128)S(1)}, f32[3,256,256]{2,1,0:T(8,128)S(1)}, f32[72,128]{1,0:T(8,128)S(1)}) custom-call(s32[2]{0:T(128)S(1)} %copy-done.3, bf16[16,104,128]{2,1,0:T(8,128)(2,1)S(1)} %all-to-all-done.arrived_ref, f32[2,256,256]{2,1,0:T(8,128)S(1)} %copy-done, ...), custom_call_target="tpu_custom_call" | custom-call | flops 1000000 | bytes 2000000 | tf_op jit(solution)/shard_map/pallas_call | solution.py:747
  25.3 1.3 %collective-permute-start.4 = (f32[72,128]{1,0:T(8,128)S(1)}, f32[72,128]{1,0:T(8,128)S(1)}, u32[]{:S(2)}, u32[]{:S(2)}) collective-permute-start(f32[72,128]{1,0:T(8,128)S(1)} %get-tuple-element.26.refs_0_), channel_id=1, source_target_pairs={{0,12},{4,8},{8,4},{12,0},{1,13},{5,9},{9,5},{13,1},{2,14},{6,10},... | collective-permute-start | bytes 110600 | tf_op jit(solution)/shard_map/ppermute | solution.py:35
  26.6 1.5 %collective-permute-start.3 = (f32[72,128]{1,0:T(8,128)S(1)}, f32[72,128]{1,0:T(8,128)S(1)}, u32[]{:S(2)}, u32[]{:S(2)}) collective-permute-start(f32[72,128]{1,0:T(8,128)S(1)} %get-tuple-element.26.refs_0_), channel_id=1, source_target_pairs={{0,8},{4,12},{8,0},{12,4},{1,9},{5,13},{9,1},{13,5},{2,10},{6,14},... | collective-permute-start | bytes 110600 | tf_op jit(solution)/shard_map/ppermute | solution.py:35
  28.1 1.6 %collective-permute-start.2 = (f32[72,128]{1,0:T(8,128)S(1)}, f32[72,128]{1,0:T(8,128)S(1)}, u32[]{:S(2)}, u32[]{:S(2)}) collective-permute-start(f32[72,128]{1,0:T(8,128)S(1)} %get-tuple-element.26.refs_0_), channel_id=1, source_target_pairs={{0,4},{4,0},{8,12},{12,8},{1,5},{5,1},{9,13},{13,9},{2,6},{6,2},{1... | collective-permute-start | bytes 110600 | tf_op jit(solution)/shard_map/ppermute | solution.py:35
  29.6 2.0 %shard_map.77 = (f32[2,256,256]{2,1,0:T(8,128)S(1)}, f32[2,256,256]{2,1,0:T(8,128)S(1)}, f32[2,256,256]{2,1,0:T(8,128)S(1)}) custom-call(s32[2]{0:T(128)S(1)} %copy-done.3, f32[256,256]{1,0:T(8,128)S(1)} %copy-done.1, f32[256,256]{1,0:T(8,128)S(1)} %copy-done.2, f32[256,256]{1,0:T(8,128)S(1)} %get-tuple-element.21.prec_ref, ...), custom_call_target="tpu_custom_call" | custom-call | flops 1000000 | bytes 2000000 | tf_op jit(solution)/shard_map/pallas_call | solution.py:756
  31.6 0.3 collective-permute-done.3.refs_2_.refs_3_
  31.9 0.4 %collective-permute-done.2.refs_1_ = f32[72,128]{1,0:T(8,128)S(1)} collective-permute-done((f32[72,128]{1,0:T(8,128)S(1)}, f32[72,128]{1,0:T(8,128)S(1)}, u32[]{:S(2)}, u32[]{:S(2)}) %collective-permute-start.2) | collective-permute-done | bytes 36896 | tf_op jit(solution)/shard_map/ppermute | solution.py:35
  32.3 0.3 shard_map.78
  32.6 0.6 %collective-permute-start.7 = (f32[8,128]{1,0:T(8,128)S(1)}, f32[8,128]{1,0:T(8,128)S(1)}, u32[]{:S(2)}, u32[]{:S(2)}) collective-permute-start(f32[8,128]{1,0:T(8,128)S(1)} %shard_map.78), channel_id=1, source_target_pairs={{0,3},{1,2},{2,1},{3,0},{4,7},{5,6},{6,5},{7,4},{8,11},{9,10},{10,... | collective-permute-start | bytes 12296 | tf_op jit(solution)/shard_map/ppermute | solution.py:49
  33.2 1.1 %collective-permute-start.6 = (f32[8,128]{1,0:T(8,128)S(1)}, f32[8,128]{1,0:T(8,128)S(1)}, u32[]{:S(2)}, u32[]{:S(2)}) collective-permute-start(f32[8,128]{1,0:T(8,128)S(1)} %shard_map.78), channel_id=1, source_target_pairs={{0,2},{1,3},{2,0},{3,1},{4,6},{5,7},{6,4},{7,5},{8,10},{9,11},{10,... | collective-permute-start | bytes 12296 | tf_op jit(solution)/shard_map/ppermute | solution.py:49
  34.3 0.2 collective-permute-start.5
  34.5 1.3 %shard_map.79 = (f32[2,256,256]{2,1,0:T(8,128)S(1)}, f32[2,256,256]{2,1,0:T(8,128)S(1)}, f32[2,256,256]{2,1,0:T(8,128)S(1)}) custom-call(s32[2]{0:T(128)S(1)} %copy-done.3, f32[256,256]{1,0:T(8,128)S(1)} %get-tuple-element.21.prec_ref, f32[3,256,256]{2,1,0:T(8,128)S(1)} %get-tuple-element.27.stress_ref, f32[2,256,256]{2,1,0:T(8,128)S(1)} %get-tuple-element.31.uk_ref, ...), custom_call_target="tpu_custom_call" | custom-call | flops 1000000 | bytes 2000000 | tf_op jit(solution)/shard_map/pallas_call | solution.py:761
  35.8 1.0 %collective-permute-done.6 = f32[8,128]{1,0:T(8,128)S(1)} collective-permute-done((f32[8,128]{1,0:T(8,128)S(1)}, f32[8,128]{1,0:T(8,128)S(1)}, u32[]{:S(2)}, u32[]{:S(2)}) %collective-permute-start.6) | collective-permute-done | bytes 4128 | tf_op jit(solution)/shard_map/ppermute | solution.py:49
  36.8 1.1 %shard_map.80 = f32[2,256,256]{2,1,0:T(8,128)} custom-call(f32[8,128]{1,0:T(8,128)S(1)} %add_add_fusion.total_ref, f32[2,256,256]{2,1,0:T(8,128)S(1)} %get-tuple-element.30.refs_4_.a_ref, f32[2,256,256]{2,1,0:T(8,128)S(1)} %get-tuple-element.34.b_ref, f32[2,256,256]{2,1,0:T(8,128)S(1)} %get-tuple-element.35.c_ref, f32[2,256,256]{2,1,0:T(8,128)S(1)} %get-tuple-element.36.d_ref), custom_call_target="tpu_custom_call" | custom-call | flops 1000000 | bytes 2000000 | tf_op jit(solution)/shard_map/pallas_call | solution.py:764
  (14 shorter events, 0.0 us)
Async XLA Ops:
  1.8 7.5 %copy-start = (f32[2,256,256]{2,1,0:T(8,128)S(1)}, f32[2,256,256]{2,1,0:T(8,128)}, u32[]{:S(2)}) copy-start(f32[2,256,256]{2,1,0:T(8,128)} %vec_ref.5) | copy-start | bytes 1572868
  1.8 7.5 %copy-start.3 = (s32[2]{0:T(128)S(1)}, s32[2]{0:T(128)}, u32[]{:S(2)}) copy-start(s32[2]{0:T(128)} %rows_ref.9) | copy-start | bytes 28
  1.9 7.5 %copy-start.4 = (s32[2]{0:T(128)S(1)}, s32[2]{0:T(128)}, u32[]{:S(2)}) copy-start(s32[2]{0:T(128)} %matched_ref.3) | copy-start | bytes 28
  1.9 20.6 %all-to-all-start = ((bf16[16,104,128]{2,1,0:T(8,128)(2,1)}), bf16[16,104,128]{2,1,0:T(8,128)(2,1)S(1)}, u32[]{:S(2)}, u32[]{:S(2)}) async-start(bf16[16,104,128]{2,1,0:T(8,128)(2,1)} %shard_map.73), calls=%async_computation | async-start | bytes 851968 | tf_op jit(solution)/shard_map/all_to_all | solution.py:735
  9.4 4.4 %copy-start.1 = (f32[256,256]{1,0:T(8,128)S(1)}, f32[256,256]{1,0:T(8,128)}, u32[]{:S(2)}) copy-start(f32[256,256]{1,0:T(8,128)} %thick_ref.5) | copy-start | bytes 786436
  9.4 4.4 %copy-start.2 = (f32[256,256]{1,0:T(8,128)S(1)}, f32[256,256]{1,0:T(8,128)}, u32[]{:S(2)}) copy-start(f32[256,256]{1,0:T(8,128)} %support_ref.5) | copy-start | bytes 786436
  10.0 11.8 %collective-permute-start.1 = (f32[32,128]{1,0:T(8,128)S(1)}, f32[32,128]{1,0:T(8,128)S(1)}, u32[]{:S(2)}, u32[]{:S(2)}) collective-permute-start(f32[32,128]{1,0:T(8,128)S(1)} %slice.4), channel_id=1, source_target_pairs={{0,12},{4,8},{8,4},{12,0},{1,13},{5,9},{9,5},{13,1},{2,14},{6,10},... | collective-permute-start | bytes 49160 | tf_op jit(solution)/shard_map/ppermute | solution.py:28
  13.8 8.0 %collective-permute-start = (f32[32,128]{1,0:T(8,128)S(1)}, f32[32,128]{1,0:T(8,128)S(1)}, u32[]{:S(2)}, u32[]{:S(2)}) collective-permute-start(f32[32,128]{1,0:T(8,128)S(1)} %slice.4), channel_id=1, source_target_pairs={{0,4},{4,0},{8,12},{12,8},{1,5},{5,1},{9,13},{13,9},{2,6},{6,2},{1... | collective-permute-start | bytes 49160 | tf_op jit(solution)/shard_map/ppermute | solution.py:28
  25.3 6.4 %collective-permute-start.4 = (f32[72,128]{1,0:T(8,128)S(1)}, f32[72,128]{1,0:T(8,128)S(1)}, u32[]{:S(2)}, u32[]{:S(2)}) collective-permute-start(f32[72,128]{1,0:T(8,128)S(1)} %get-tuple-element.26.refs_0_), channel_id=1, source_target_pairs={{0,12},{4,8},{8,4},{12,0},{1,13},{5,9},{9,5},{13,1},{2,14},{6,10},... | collective-permute-start | bytes 110600 | tf_op jit(solution)/shard_map/ppermute | solution.py:35
  26.6 5.3 %collective-permute-start.3 = (f32[72,128]{1,0:T(8,128)S(1)}, f32[72,128]{1,0:T(8,128)S(1)}, u32[]{:S(2)}, u32[]{:S(2)}) collective-permute-start(f32[72,128]{1,0:T(8,128)S(1)} %get-tuple-element.26.refs_0_), channel_id=1, source_target_pairs={{0,8},{4,12},{8,0},{12,4},{1,9},{5,13},{9,1},{13,5},{2,10},{6,14},... | collective-permute-start | bytes 110600 | tf_op jit(solution)/shard_map/ppermute | solution.py:35
  28.1 4.2 %collective-permute-start.2 = (f32[72,128]{1,0:T(8,128)S(1)}, f32[72,128]{1,0:T(8,128)S(1)}, u32[]{:S(2)}, u32[]{:S(2)}) collective-permute-start(f32[72,128]{1,0:T(8,128)S(1)} %get-tuple-element.26.refs_0_), channel_id=1, source_target_pairs={{0,4},{4,0},{8,12},{12,8},{1,5},{5,1},{9,13},{13,9},{2,6},{6,2},{1... | collective-permute-start | bytes 110600 | tf_op jit(solution)/shard_map/ppermute | solution.py:35
  32.6 3.2 %collective-permute-start.7 = (f32[8,128]{1,0:T(8,128)S(1)}, f32[8,128]{1,0:T(8,128)S(1)}, u32[]{:S(2)}, u32[]{:S(2)}) collective-permute-start(f32[8,128]{1,0:T(8,128)S(1)} %shard_map.78), channel_id=1, source_target_pairs={{0,3},{1,2},{2,1},{3,0},{4,7},{5,6},{6,5},{7,4},{8,11},{9,10},{10,... | collective-permute-start | bytes 12296 | tf_op jit(solution)/shard_map/ppermute | solution.py:49
  33.2 3.6 %collective-permute-start.6 = (f32[8,128]{1,0:T(8,128)S(1)}, f32[8,128]{1,0:T(8,128)S(1)}, u32[]{:S(2)}, u32[]{:S(2)}) collective-permute-start(f32[8,128]{1,0:T(8,128)S(1)} %shard_map.78), channel_id=1, source_target_pairs={{0,2},{1,3},{2,0},{3,1},{4,6},{5,7},{6,4},{7,5},{8,10},{9,11},{10,... | collective-permute-start | bytes 12296 | tf_op jit(solution)/shard_map/ppermute | solution.py:49
  34.3 2.5 %collective-permute-start.5 = (f32[8,128]{1,0:T(8,128)S(1)}, f32[8,128]{1,0:T(8,128)S(1)}, u32[]{:S(2)}, u32[]{:S(2)}) collective-permute-start(f32[8,128]{1,0:T(8,128)S(1)} %shard_map.78), channel_id=1, source_target_pairs={{0,1},{1,0},{2,3},{3,2},{4,5},{5,4},{6,7},{7,6},{8,9},{9,8},{10,11... | collective-permute-start | bytes 12296 | tf_op jit(solution)/shard_map/ppermute | solution.py:49

commit v10 on v9

--- a/solution.py
+++ b/solution.py
@@ -384,7 +384,7 @@
     return [ref[STACK * (at + h) : STACK * (at + h + 1), :] for h in range(halves)]
 
 
-PIECE = 16
+PIECE = 32
 
 
 def gram_kernel(

time: 38.1 us -> 38.2 us (level)
  no operation moved by 1% of the time
where the time goes in v10:
time: 38.2 us; the launch traced here: 37.9 us
  starting transfers between devices  17.6 us (46%)
  Pallas kernels  12.6 us (33%)
  waiting for transfers between devices  7.6 us (20%)
    all_to_all x1, starting transfers between devices, per_device(): lax.all_to_all(payload, ('patch', 'sub', 'half'), split_axis=0, concat_ax...  7.5 us
    ppermute x2, waiting for transfers between devices, neighbours(): lax.ppermute(array, axis, [(i, i ^ k) for i in range(4)])  5.32 us
    ppermute x3, starting transfers between devices, line_shared(): lax.ppermute(array, axis, [(i, i ^ k) for i in range(4)])  4.39 us
    ppermute x2, starting transfers between devices, neighbours(): lax.ppermute(array, axis, [(i, i ^ k) for i in range(4)])  3.79 us
    pallas_call x1, Pallas kernels, per_device(): call(gram_kernel, [field, field, field, ((3, rows_dev, ncol), f32), (((4...  2.84 us
    pallas_call x1, Pallas kernels, per_device(): call(stiff_kernel, [field, field, one, sums, ((RIM_STACKS * STACK, ncol),...  2.68 us
    pallas_call x1, Pallas kernels, per_device(): call(apply_kernel, [field] * 3, 'svvvvvv')  1.97 us
    ppermute x3, starting transfers between devices, summed_over_both(): total = total + lax.ppermute(array, (outer, inner), pairs)  1.87 us
  transfers between devices with their start and end apart: 9, of which 5 were waited for; matrix products, arithmetic and copies ran while one was open for 0% of the time, Pallas kernels for 17%

profile of v10, /device:TPU:0, one launch (start us, length us, event | category | flops | bytes accessed | tf_op | source)
XLA Modules:
  0.0 37.9 jit_solution(50109983371948152)
XLA Ops:
  0.0 1.8 %shard_map.73 = bf16[16,104,128]{2,1,0:T(8,128)(2,1)} custom-call(bf16[3,16,16,256]{3,2,1,0:T(8,128)(2,1)} %bitcast.4, s32[1,256]{1,0:T(1,128)} %bitcast.5, s32[2]{0:T(128)} %matched_ref.3), custom_call_target="tpu_custom_call" | custom-call | flops 1000000 | bytes 2000000 | tf_op jit(solution)/shard_map/pallas_call | solution.py:730
  1.8 0.0 copy-start
  1.9 7.5 %all-to-all-start = ((bf16[16,104,128]{2,1,0:T(8,128)(2,1)}), bf16[16,104,128]{2,1,0:T(8,128)(2,1)S(1)}, u32[]{:S(2)}, u32[]{:S(2)}) async-start(bf16[16,104,128]{2,1,0:T(8,128)(2,1)} %shard_map.73), calls=%async_computation | async-start | bytes 851968 | tf_op jit(solution)/shard_map/all_to_all | solution.py:735
  9.4 0.0 copy-start.1
  9.4 0.0 copy-start.2
  9.4 0.6 %shard_map.75.edge_ref = f32[40,128]{1,0:T(8,128)S(1)} custom-call(s32[2]{0:T(128)S(1)} %copy-done.3, s32[2]{0:T(128)S(1)} %copy-done.4, f32[2,256,256]{2,1,0:T(8,128)S(1)} %copy-done), custom_call_target="tpu_custom_call" | custom-call | flops 1000000 | bytes 2000000 | tf_op jit(solution)/shard_map/pallas_call | solution.py:739
  10.0 3.8 %collective-permute-start.1 = (f32[32,128]{1,0:T(8,128)S(1)}, f32[32,128]{1,0:T(8,128)S(1)}, u32[]{:S(2)}, u32[]{:S(2)}) collective-permute-start(f32[32,128]{1,0:T(8,128)S(1)} %slice.4), channel_id=1, source_target_pairs={{0,12},{4,8},{8,4},{12,0},{1,13},{5,9},{9,5},{13,1},{2,14},{6,10},... | collective-permute-start | bytes 49160 | tf_op jit(solution)/shard_map/ppermute | solution.py:28
  13.8 2.7 %shard_map.74 = (f32[2,256,256]{2,1,0:T(8,128)S(1)}, f32[2,256,256]{2,1,0:T(8,128)S(1)}, f32[256,256]{1,0:T(8,128)S(1)}, f32[48,128]{1,0:T(8,128)S(1)}, f32[88,256]{1,0:T(8,128)S(1)}) custom-call(s32[2]{0:T(128)S(1)} %copy-done.3, f32[2,256,256]{2,1,0:T(8,128)S(1)} %copy-done, f32[256,256]{1,0:T(8,128)S(1)} %copy-done.1, f32[256,256]{1,0:T(8,128)S(1)} %copy-done.2), custom_call_target="tpu_custom_call" | custom-call | flops 1000000 | bytes 2000000 | tf_op jit(solution)/shard_map/pallas_call | solution.py:741
  16.5 5.3 %collective-permute-done.1.above_ref = f32[32,128]{1,0:T(8,128)S(1)} collective-permute-done((f32[32,128]{1,0:T(8,128)S(1)}, f32[32,128]{1,0:T(8,128)S(1)}, u32[]{:S(2)}, u32[]{:S(2)}) %collective-permute-start.1) | collective-permute-done | bytes 16416 | tf_op jit(solution)/shard_map/ppermute | solution.py:28
  21.8 0.6 %all-to-all-done.arrived_ref = bf16[16,104,128]{2,1,0:T(8,128)(2,1)S(1)} async-done(((bf16[16,104,128]{2,1,0:T(8,128)(2,1)}), bf16[16,104,128]{2,1,0:T(8,128)(2,1)S(1)}, u32[]{:S(2)}, u32[]{:S(2)}) %all-to-all-start) | async-done | bytes 426016 | tf_op jit(solution)/shard_map/all_to_all | solution.py:735
  22.4 2.8 %shard_map.76 = (f32[2,256,256]{2,1,0:T(8,128)S(1)}, f32[2,256,256]{2,1,0:T(8,128)S(1)}, f32[2,256,256]{2,1,0:T(8,128)S(1)}, f32[3,256,256]{2,1,0:T(8,128)S(1)}, f32[72,128]{1,0:T(8,128)S(1)}) custom-call(s32[2]{0:T(128)S(1)} %copy-done.3, bf16[16,104,128]{2,1,0:T(8,128)(2,1)S(1)} %all-to-all-done.arrived_ref, f32[2,256,256]{2,1,0:T(8,128)S(1)} %copy-done, ...), custom_call_target="tpu_custom_call" | custom-call | flops 1000000 | bytes 2000000 | tf_op jit(solution)/shard_map/pallas_call | solution.py:747
  25.3 1.3 %collective-permute-start.4 = (f32[72,128]{1,0:T(8,128)S(1)}, f32[72,128]{1,0:T(8,128)S(1)}, u32[]{:S(2)}, u32[]{:S(2)}) collective-permute-start(f32[72,128]{1,0:T(8,128)S(1)} %get-tuple-element.26.refs_0_), channel_id=1, source_target_pairs={{0,12},{4,8},{8,4},{12,0},{1,13},{5,9},{9,5},{13,1},{2,14},{6,10},... | collective-permute-start | bytes 110600 | tf_op jit(solution)/shard_map/ppermute | solution.py:35
  26.6 1.5 %collective-permute-start.3 = (f32[72,128]{1,0:T(8,128)S(1)}, f32[72,128]{1,0:T(8,128)S(1)}, u32[]{:S(2)}, u32[]{:S(2)}) collective-permute-start(f32[72,128]{1,0:T(8,128)S(1)} %get-tuple-element.26.refs_0_), channel_id=1, source_target_pairs={{0,8},{4,12},{8,0},{12,4},{1,9},{5,13},{9,1},{13,5},{2,10},{6,14},... | collective-permute-start | bytes 110600 | tf_op jit(solution)/shard_map/ppermute | solution.py:35
  28.1 1.6 %collective-permute-start.2 = (f32[72,128]{1,0:T(8,128)S(1)}, f32[72,128]{1,0:T(8,128)S(1)}, u32[]{:S(2)}, u32[]{:S(2)}) collective-permute-start(f32[72,128]{1,0:T(8,128)S(1)} %get-tuple-element.26.refs_0_), channel_id=1, source_target_pairs={{0,4},{4,0},{8,12},{12,8},{1,5},{5,1},{9,13},{13,9},{2,6},{6,2},{1... | collective-permute-start | bytes 110600 | tf_op jit(solution)/shard_map/ppermute | solution.py:35
  29.7 2.0 %shard_map.77 = (f32[2,256,256]{2,1,0:T(8,128)S(1)}, f32[2,256,256]{2,1,0:T(8,128)S(1)}, f32[2,256,256]{2,1,0:T(8,128)S(1)}) custom-call(s32[2]{0:T(128)S(1)} %copy-done.3, f32[256,256]{1,0:T(8,128)S(1)} %copy-done.1, f32[256,256]{1,0:T(8,128)S(1)} %copy-done.2, f32[256,256]{1,0:T(8,128)S(1)} %get-tuple-element.21.prec_ref, ...), custom_call_target="tpu_custom_call" | custom-call | flops 1000000 | bytes 2000000 | tf_op jit(solution)/shard_map/pallas_call | solution.py:756
  31.7 0.3 collective-permute-done.3.refs_2_.refs_3_
  31.9 0.4 %collective-permute-done.2.refs_1_ = f32[72,128]{1,0:T(8,128)S(1)} collective-permute-done((f32[72,128]{1,0:T(8,128)S(1)}, f32[72,128]{1,0:T(8,128)S(1)}, u32[]{:S(2)}, u32[]{:S(2)}) %collective-permute-start.2) | collective-permute-done | bytes 36896 | tf_op jit(solution)/shard_map/ppermute | solution.py:35
  32.3 0.3 shard_map.78
  32.7 0.5 %collective-permute-start.7 = (f32[8,128]{1,0:T(8,128)S(1)}, f32[8,128]{1,0:T(8,128)S(1)}, u32[]{:S(2)}, u32[]{:S(2)}) collective-permute-start(f32[8,128]{1,0:T(8,128)S(1)} %shard_map.78), channel_id=1, source_target_pairs={{0,3},{1,2},{2,1},{3,0},{4,7},{5,6},{6,5},{7,4},{8,11},{9,10},{10,... | collective-permute-start | bytes 12296 | tf_op jit(solution)/shard_map/ppermute | solution.py:49
  33.2 1.1 %collective-permute-start.6 = (f32[8,128]{1,0:T(8,128)S(1)}, f32[8,128]{1,0:T(8,128)S(1)}, u32[]{:S(2)}, u32[]{:S(2)}) collective-permute-start(f32[8,128]{1,0:T(8,128)S(1)} %shard_map.78), channel_id=1, source_target_pairs={{0,2},{1,3},{2,0},{3,1},{4,6},{5,7},{6,4},{7,5},{8,10},{9,11},{10,... | collective-permute-start | bytes 12296 | tf_op jit(solution)/shard_map/ppermute | solution.py:49
  34.3 0.3 collective-permute-start.5
  34.5 1.3 %shard_map.79 = (f32[2,256,256]{2,1,0:T(8,128)S(1)}, f32[2,256,256]{2,1,0:T(8,128)S(1)}, f32[2,256,256]{2,1,0:T(8,128)S(1)}) custom-call(s32[2]{0:T(128)S(1)} %copy-done.3, f32[256,256]{1,0:T(8,128)S(1)} %get-tuple-element.21.prec_ref, f32[3,256,256]{2,1,0:T(8,128)S(1)} %get-tuple-element.27.stress_ref, f32[2,256,256]{2,1,0:T(8,128)S(1)} %get-tuple-element.31.uk_ref, ...), custom_call_target="tpu_custom_call" | custom-call | flops 1000000 | bytes 2000000 | tf_op jit(solution)/shard_map/pallas_call | solution.py:761
  35.9 1.0 %collective-permute-done.6 = f32[8,128]{1,0:T(8,128)S(1)} collective-permute-done((f32[8,128]{1,0:T(8,128)S(1)}, f32[8,128]{1,0:T(8,128)S(1)}, u32[]{:S(2)}, u32[]{:S(2)}) %collective-permute-start.6) | collective-permute-done | bytes 4128 | tf_op jit(solution)/shard_map/ppermute | solution.py:49
  36.8 1.1 %shard_map.80 = f32[2,256,256]{2,1,0:T(8,128)} custom-call(f32[8,128]{1,0:T(8,128)S(1)} %add_add_fusion.total_ref, f32[2,256,256]{2,1,0:T(8,128)S(1)} %get-tuple-element.30.refs_4_.a_ref, f32[2,256,256]{2,1,0:T(8,128)S(1)} %get-tuple-element.34.b_ref, f32[2,256,256]{2,1,0:T(8,128)S(1)} %get-tuple-element.35.c_ref, f32[2,256,256]{2,1,0:T(8,128)S(1)} %get-tuple-element.36.d_ref), custom_call_target="tpu_custom_call" | custom-call | flops 1000000 | bytes 2000000 | tf_op jit(solution)/shard_map/pallas_call | solution.py:764
  (14 shorter events, 0.0 us)
Async XLA Ops:
  1.8 7.5 %copy-start = (f32[2,256,256]{2,1,0:T(8,128)S(1)}, f32[2,256,256]{2,1,0:T(8,128)}, u32[]{:S(2)}) copy-start(f32[2,256,256]{2,1,0:T(8,128)} %vec_ref.5) | copy-start | bytes 1572868
  1.8 7.5 %copy-start.3 = (s32[2]{0:T(128)S(1)}, s32[2]{0:T(128)}, u32[]{:S(2)}) copy-start(s32[2]{0:T(128)} %rows_ref.9) | copy-start | bytes 28
  1.9 7.5 %copy-start.4 = (s32[2]{0:T(128)S(1)}, s32[2]{0:T(128)}, u32[]{:S(2)}) copy-start(s32[2]{0:T(128)} %matched_ref.3) | copy-start | bytes 28
  1.9 20.6 %all-to-all-start = ((bf16[16,104,128]{2,1,0:T(8,128)(2,1)}), bf16[16,104,128]{2,1,0:T(8,128)(2,1)S(1)}, u32[]{:S(2)}, u32[]{:S(2)}) async-start(bf16[16,104,128]{2,1,0:T(8,128)(2,1)} %shard_map.73), calls=%async_computation | async-start | bytes 851968 | tf_op jit(solution)/shard_map/all_to_all | solution.py:735
  9.4 4.4 %copy-start.1 = (f32[256,256]{1,0:T(8,128)S(1)}, f32[256,256]{1,0:T(8,128)}, u32[]{:S(2)}) copy-start(f32[256,256]{1,0:T(8,128)} %thick_ref.5) | copy-start | bytes 786436
  9.4 4.4 %copy-start.2 = (f32[256,256]{1,0:T(8,128)S(1)}, f32[256,256]{1,0:T(8,128)}, u32[]{:S(2)}) copy-start(f32[256,256]{1,0:T(8,128)} %support_ref.5) | copy-start | bytes 786436
  10.0 11.8 %collective-permute-start.1 = (f32[32,128]{1,0:T(8,128)S(1)}, f32[32,128]{1,0:T(8,128)S(1)}, u32[]{:S(2)}, u32[]{:S(2)}) collective-permute-start(f32[32,128]{1,0:T(8,128)S(1)} %slice.4), channel_id=1, source_target_pairs={{0,12},{4,8},{8,4},{12,0},{1,13},{5,9},{9,5},{13,1},{2,14},{6,10},... | collective-permute-start | bytes 49160 | tf_op jit(solution)/shard_map/ppermute | solution.py:28
  13.8 8.0 %collective-permute-start = (f32[32,128]{1,0:T(8,128)S(1)}, f32[32,128]{1,0:T(8,128)S(1)}, u32[]{:S(2)}, u32[]{:S(2)}) collective-permute-start(f32[32,128]{1,0:T(8,128)S(1)} %slice.4), channel_id=1, source_target_pairs={{0,4},{4,0},{8,12},{12,8},{1,5},{5,1},{9,13},{13,9},{2,6},{6,2},{1... | collective-permute-start | bytes 49160 | tf_op jit(solution)/shard_map/ppermute | solution.py:28
  25.3 6.4 %collective-permute-start.4 = (f32[72,128]{1,0:T(8,128)S(1)}, f32[72,128]{1,0:T(8,128)S(1)}, u32[]{:S(2)}, u32[]{:S(2)}) collective-permute-start(f32[72,128]{1,0:T(8,128)S(1)} %get-tuple-element.26.refs_0_), channel_id=1, source_target_pairs={{0,12},{4,8},{8,4},{12,0},{1,13},{5,9},{9,5},{13,1},{2,14},{6,10},... | collective-permute-start | bytes 110600 | tf_op jit(solution)/shard_map/ppermute | solution.py:35
  26.6 5.3 %collective-permute-start.3 = (f32[72,128]{1,0:T(8,128)S(1)}, f32[72,128]{1,0:T(8,128)S(1)}, u32[]{:S(2)}, u32[]{:S(2)}) collective-permute-start(f32[72,128]{1,0:T(8,128)S(1)} %get-tuple-element.26.refs_0_), channel_id=1, source_target_pairs={{0,8},{4,12},{8,0},{12,4},{1,9},{5,13},{9,1},{13,5},{2,10},{6,14},... | collective-permute-start | bytes 110600 | tf_op jit(solution)/shard_map/ppermute | solution.py:35
  28.1 4.2 %collective-permute-start.2 = (f32[72,128]{1,0:T(8,128)S(1)}, f32[72,128]{1,0:T(8,128)S(1)}, u32[]{:S(2)}, u32[]{:S(2)}) collective-permute-start(f32[72,128]{1,0:T(8,128)S(1)} %get-tuple-element.26.refs_0_), channel_id=1, source_target_pairs={{0,4},{4,0},{8,12},{12,8},{1,5},{5,1},{9,13},{13,9},{2,6},{6,2},{1... | collective-permute-start | bytes 110600 | tf_op jit(solution)/shard_map/ppermute | solution.py:35
  32.7 3.2 %collective-permute-start.7 = (f32[8,128]{1,0:T(8,128)S(1)}, f32[8,128]{1,0:T(8,128)S(1)}, u32[]{:S(2)}, u32[]{:S(2)}) collective-permute-start(f32[8,128]{1,0:T(8,128)S(1)} %shard_map.78), channel_id=1, source_target_pairs={{0,3},{1,2},{2,1},{3,0},{4,7},{5,6},{6,5},{7,4},{8,11},{9,10},{10,... | collective-permute-start | bytes 12296 | tf_op jit(solution)/shard_map/ppermute | solution.py:49
  33.2 3.6 %collective-permute-start.6 = (f32[8,128]{1,0:T(8,128)S(1)}, f32[8,128]{1,0:T(8,128)S(1)}, u32[]{:S(2)}, u32[]{:S(2)}) collective-permute-start(f32[8,128]{1,0:T(8,128)S(1)} %shard_map.78), channel_id=1, source_target_pairs={{0,2},{1,3},{2,0},{3,1},{4,6},{5,7},{6,4},{7,5},{8,10},{9,11},{10,... | collective-permute-start | bytes 12296 | tf_op jit(solution)/shard_map/ppermute | solution.py:49
  34.3 2.5 %collective-permute-start.5 = (f32[8,128]{1,0:T(8,128)S(1)}, f32[8,128]{1,0:T(8,128)S(1)}, u32[]{:S(2)}, u32[]{:S(2)}) collective-permute-start(f32[8,128]{1,0:T(8,128)S(1)} %shard_map.78), channel_id=1, source_target_pairs={{0,1},{1,0},{2,3},{3,2},{4,5},{5,4},{6,7},{7,6},{8,9},{9,8},{10,11... | collective-permute-start | bytes 12296 | tf_op jit(solution)/shard_map/ppermute | solution.py:49
